TPU v7x, 32 devices: a whole 2x2x4 slice. The times are simulated.
32 devices in a mesh: groups: 2 (over x), seq: 8 (over z, y), exp: 2 (over core).
Axes of the slice: x: 2, y: 2, z: 4, core: 2. Of those that a mesh axis runs over, the one named last changes fastest.
Arguments:
- queries: bfloat16 [2048, 6144], P(('groups', 'seq'), 'exp'), parts along dimension 0, may hold values from -6 to 6
- key_rows: bfloat16 [2048, 6144], P(('groups', 'seq'), 'exp'), parts along dimension 0, may hold values from -18 to 18
- values: bfloat16 [2048, 6144], P(('groups', 'seq'), 'exp'), parts along dimension 0, may hold values from -18 to 18
- log_decay: float32 [2048, 48], P(('groups', 'seq'), 'exp'), parts along dimension 0, may hold values from -2.2 to 0, as said below
- residual: bfloat16 [2048, 6144], P(('groups', 'seq'), 'exp'), parts along dimension 0, may hold values from -6 to 6
- attn_gain: float32 [6144], P('exp'), may hold values from 0.25 to 1.75
- moe_gain: float32 [6144], replicated, may hold values from 0.25 to 1.75
- router: bfloat16 [6144, 32], replicated, may hold values from -0.3125 to 0.3125
- routes: int32 [2048, 2], P(('groups', 'seq')), parts along dimension 0, may hold values from 0 to 31, as said below
- slot_pos: int32 [2048, 2], P(('groups', 'seq')), parts along dimension 0, may hold values from 0 to 16, as said below
- gate_weight: bfloat16 [2, 6144, 6144], P('exp', None, 'seq'), may hold values from -0.078125 to 0.078125
- up_weight: bfloat16 [2, 6144, 6144], P('exp', None, 'seq'), may hold values from -0.078125 to 0.078125
- down_weight: bfloat16 [2, 6144, 6144], P('exp', 'seq'), may hold values from -0.15625 to 0.15625
Outputs:
- mixed: bfloat16 [2048, 6144], P(('groups', 'seq'), 'exp'), parts along dimension 0
There are 2 independent parts, one for each index of `groups`. A program takes and returns all parts, laid end to end along the dimension named above; an argument that names none is the same for every part. Nothing has to cross between parts.
Inputs may be any that keep to these rules, and one draw needn't show every extreme that they name: log_decay is at most 0 everywhere. `routes`: the two entries of a row differ. Experts 0 to 1 are the present ones. In each block of 128 rows each present expert is named by at most 16 rows, and by exactly 16 rows in some block. Where routes[t, j] < 2, slot_pos[t, j] counts the earlier rows of t's block that name the same expert; elsewhere it is 16.
All inputs are finite; a program needn't handle non-finite values.
Results may differ from a plain program's by a relative error of at most 0.0052.
Values may be sent and summed in bfloat16 or wider, within the bound.
No kernel may reach another device: no remote copies, remote signals or barrier semaphores. Data moves between devices by JAX's collectives and lax.ppermute only.
A program may use at most 192 MiB of HBM per device.

v0:
```python
import jax
import jax.numpy as jnp
from jax import lax
from jax.sharding import PartitionSpec as P

CAP = 16


def carried_in(value, axis, join, neutral):
    count, mine = (lax.axis_size(axis), lax.axis_index(axis))
    pieces = jax.tree.map(lambda part: lax.all_gather(part, axis), value)
    subtotal = jax.tree.map(
        lambda part, zero: jnp.full_like(part, 0) + jnp.asarray(zero, part.dtype), value, neutral
    )

    def hop(position, subtotal):
        longer = join(subtotal, jax.tree.map(lambda part: part[position], pieces))
        return jax.tree.map(lambda new, old: jnp.where(position < mine, new, old), longer, subtotal)

    return lax.fori_loop(0, count - 1, hop, subtotal)


def slot_table(routes, slot_pos, expert, capacity):
    matches = (routes == expert)[None] & (slot_pos[None] == jnp.arange(capacity)[:, None, None])
    return jnp.sum(jnp.where(matches, 1.0, 0.0), axis=2)


def mixing_table(routes, slot_pos, shares, expert, capacity):
    matches = (routes == expert)[:, :, None] & (
        slot_pos[:, :, None] == jnp.arange(capacity)[None, None, :]
    )
    return jnp.sum(jnp.where(matches, shares[:, :, None], 0.0), axis=1)


def shards(
    queries,
    key_rows,
    values,
    log_decay,
    residual,
    attn_gain,
    moe_gain,
    router,
    routes,
    slot_pos,
    gate_weight,
    up_weight,
    down_weight,
):
    length = queries.shape[0]
    heads_here = log_decay.shape[1]
    head_width = queries.shape[1] // heads_here
    query_heads = queries.reshape(length, heads_here, head_width)
    key_heads = key_rows.reshape(length, heads_here, head_width)
    value_heads = values.reshape(length, heads_here, head_width)
    running = jnp.cumsum(log_decay, axis=0)
    block_total = running[-1]
    scaled = (
        key_heads.astype(jnp.float32) * jnp.exp(block_total[None, :] - running)[:, :, None]
    ).astype(jnp.bfloat16)
    local_state = jnp.einsum(
        "shd,she->hde", scaled, value_heads, preferred_element_type=jnp.float32
    )

    def combine(earlier, latter):
        return (earlier[0] + latter[0], jnp.exp(latter[0])[:, None, None] * earlier[1] + latter[1])

    entering = carried_in(
        (block_total, local_state),
        "seq",
        combine,
        (jnp.zeros_like(block_total), jnp.zeros_like(local_state)),
    )[1]
    router_scores = jnp.einsum(
        "thd,shd->hts", query_heads, key_heads, preferred_element_type=jnp.float32
    )
    spread = running.T[:, :, None] - running.T[:, None, :]
    causal = (jnp.arange(length)[:, None] >= jnp.arange(length)[None, :])[None]
    mixing = jnp.where(causal, router_scores * jnp.exp(jnp.where(causal, spread, 0.0)), 0.0).astype(
        jnp.bfloat16
    )
    within_part = jnp.einsum(
        "hts,shd->thd", mixing, value_heads, preferred_element_type=jnp.float32
    )
    carried_part = jnp.einsum(
        "thd,hde->the",
        query_heads,
        entering.astype(jnp.bfloat16),
        preferred_element_type=jnp.float32,
    )
    raw = within_part + carried_part * jnp.exp(running)[:, :, None]
    normed = raw * lax.rsqrt(jnp.mean(raw * raw, axis=2, keepdims=True) + 1e-05)
    hidden_half = (residual.astype(jnp.float32) + normed.reshape(length, -1) * attn_gain).astype(
        jnp.bfloat16
    )
    expert_present = lax.axis_index("exp")
    hidden_full = lax.all_gather(hidden_half, "exp", axis=1, tiled=True)
    hidden_float = hidden_full.astype(jnp.float32)
    inverse = lax.rsqrt(jnp.mean(hidden_float * hidden_float, axis=1) + 1e-06)
    moe_in = (hidden_float * inverse[:, None] * moe_gain).astype(jnp.bfloat16)
    logits = (
        jnp.dot(
            hidden_float * moe_gain, router.astype(jnp.float32), precision=lax.Precision.HIGHEST
        )
        * inverse[:, None]
    )
    table = slot_table(routes, slot_pos, expert_present, CAP).astype(jnp.bfloat16)
    buffer = jnp.dot(table, moe_in, preferred_element_type=jnp.float32).astype(jnp.bfloat16)
    picked = jnp.sum(
        jnp.where(
            routes[:, :, None] == jnp.arange(router.shape[1])[None, None, :],
            logits[:, None, :],
            0.0,
        ),
        axis=2,
    )
    gates = jax.nn.sigmoid(picked)
    shares = gates / jnp.sum(gates, axis=1, keepdims=True)
    segment = lax.all_gather(buffer, "seq", axis=0, tiled=True)
    gate_part = jnp.dot(segment, gate_weight[0], preferred_element_type=jnp.float32)
    up_part = jnp.dot(segment, up_weight[0], preferred_element_type=jnp.float32)
    hidden_rows = (jax.nn.silu(gate_part) * up_part).astype(jnp.bfloat16)
    segment = hidden_rows
    expert_out = lax.psum_scatter(
        jnp.dot(segment, down_weight[0], preferred_element_type=jnp.float32).astype(jnp.bfloat16),
        "seq",
        scatter_dimension=0,
        tiled=True,
    )
    weighting = mixing_table(routes, slot_pos, shares, expert_present, CAP)
    contribution = jnp.dot(
        weighting, expert_out.astype(jnp.float32), precision=lax.Precision.HIGHEST
    )
    expert_sum = lax.psum_scatter(
        contribution.astype(jnp.bfloat16), "exp", scatter_dimension=1, tiled=True
    ).astype(jnp.float32)
    return (hidden_half.astype(jnp.float32) + expert_sum).astype(jnp.bfloat16)


def solution(mesh):
    placed = (
        P(("groups", "seq"), "exp"),
        P(("groups", "seq"), "exp"),
        P(("groups", "seq"), "exp"),
        P(("groups", "seq"), "exp"),
        P(("groups", "seq"), "exp"),
        P("exp"),
        P(),
        P(),
        P(("groups", "seq"), None),
        P(("groups", "seq"), None),
        P("exp", None, "seq"),
        P("exp", None, "seq"),
        P("exp", "seq", None),
    )
    return jax.shard_map(
        shards, mesh=mesh, in_specs=placed, out_specs=P(("groups", "seq"), "exp"), check_vma=False
    )
```

profile of v0, /device:TPU:0, one launch (start us, length us, event | category | flops | bytes accessed | tf_op | source)
XLA Modules:
  0.0 367.1 jit_solution(16911909510126246500)
XLA Ops:
  11.0 22.4 %all-gather.1 = f32[8,1,24]{2,1,0:T(1,128)S(1)} all-gather(f32[1,1,24]{2,1,0:T(1,128)S(1)} %get-tuple-element.131), channel_id=1, replica_groups=mesh['groups'=2,'seq'=8,'exp'=2] {'seq'}, dimensions={0}, use_global_device_ids=true | all-gather | bytes 864 | tf_op jit(solution)/shard_map/all_gather | solution.py:11
  33.4 3.3 fusion.19
  36.7 153.4 %all-gather.10.cloned.1.call-done = f32[192,128,128]{2,1,0:T(8,128)} async-done(((f32[24,128,128]{2,1,0:T(8,128)}), f32[192,128,128]{2,1,0:T(8,128)}) %all-gather.10.cloned.1.call-update) | async-done | bytes 12582928 | tf_op jit(solution)/shard_map/all_gather | solution.py:11
  190.1 12.7 %while.14 = (s32[]{:T(128)}, f32[24,128,128]{2,1,0:T(8,128)S(1)}, s32[]{:T(128)}, f32[8,24]{1,0:T(8,128)S(1)}, f32[8,24,128,128]{3,2,1,0:T(8,128)}, /*index=5*/s32[]{:T(128)}, s32[]{:T(128)}) while((s32[]{:T(128)}, f32[24,128,128]{2,1,0:T(8,128)S(1)}, s32[]{:T(128)}, f32[8,24]{1,0:T(8,128)S(1)}, f32[8,24,128,128]{3,2,1,0:T(8,128)}, ...), condition=%wide.region_2.3_spmd.clone, body=%wide.region_1.2_spmd.clone.sunk | while | flops 1572868 | bytes 4718993 | solution.py:20
  190.1 1.8 fusion.69
  191.9 1.8 fusion.69
  193.8 1.8 fusion.69
  195.6 1.8 fusion.69
  197.4 1.8 fusion.69
  199.2 1.8 fusion.69
  201.0 1.8 fusion.69
  202.8 2.1 multiply_reduce_fusion
  205.1 1.6 copy.60
  206.8 2.5 add_convert_fusion.1
  209.4 8.0 %all-gather.6.cloned.1.call-done = bf16[128,6144]{1,0:T(8,128)(2,1)} async-done(((bf16[128,3072]{1,0:T(8,128)(2,1)}), bf16[128,6144]{1,0:T(8,128)(2,1)}) %all-gather.6.cloned.1.call-update) | async-done | bytes 1572880 | tf_op jit(solution)/shard_map/all_gather | solution.py:97
  217.4 1.9 fusion.11
  220.7 45.5 %all-gather.8.cloned.1.call-done = bf16[128,6144]{1,0:T(8,128)(2,1)} async-done(((bf16[16,6144]{1,0:T(8,128)(2,1)}), bf16[128,6144]{1,0:T(8,128)(2,1)}) %all-gather.8.cloned.1.call-update) | async-done | bytes 1572880 | tf_op jit(solution)/shard_map/all_gather | solution.py:119
  266.1 5.7 %fusion.5 = f32[128,768]{1,0:T(8,128)S(1)} fusion(bf16[128,6144]{1,0:T(8,128)(2,1)} %all-gather.8.cloned.1.call-done, bf16[1,6144,768]{2,1,0:T(8,128)(2,1)} %param.25), kind=kOutput, calls=%fused_computation.7 | convolution fusion | flops 1207959552 | bytes 11403264 | tf_op jit(solution)/shard_map/dot_general | solution.py:120
  271.8 11.1 %fusion.7 = bf16[128,6144]{1,0:T(8,128)(2,1)} fusion(bf16[1,768,6144]{2,1,0:T(8,128)(2,1)} %param.27, bf16[128,6144]{1,0:T(8,128)(2,1)S(1)} %copy-done.1, bf16[1,6144,768]{2,1,0:T(8,128)(2,1)} %param.26, f32[128,768]{1,0:T(8,128)S(1)} %fusion.5), kind=kOutput, calls=%fused_computation.9 | convolution fusion | flops 2417295360 | bytes 22413312 | tf_op jit(solution)/shard_map/dot_general | solution.py:125
  284.3 1.9 fusion.26
  286.3 60.3 %reduce-scatter.3.cloned.1.call-done = bf16[16,6144]{1,0:T(8,128)(2,1)} async-done(((bf16[128,6144]{1,0:T(8,128)(2,1)}), bf16[16,6144]{1,0:T(8,128)(2,1)}) %reduce-scatter.3.cloned.1.call-update) | async-done | bytes 196624 | tf_op jit(solution)/shard_map/reduce_scatter | solution.py:124
  346.7 3.5 convolution_convert_fusion
  350.2 8.1 %reduce-scatter.5.cloned.1.call-done = bf16[128,3072]{1,0:T(8,128)(2,1)} async-done(((bf16[128,6144]{1,0:T(8,128)(2,1)}), bf16[128,3072]{1,0:T(8,128)(2,1)}) %reduce-scatter.5.cloned.1.call-update) | async-done | bytes 786448 | tf_op jit(solution)/shard_map/reduce_scatter | solution.py:134
  358.4 2.2 add_convert_fusion
  (62 shorter events, 7.5 us)
Async XLA Ops:
  6.5 26.9 %copy-start = (bf16[128,3072]{1,0:T(8,128)(2,1)S(1)}, bf16[128,3072]{1,0:T(8,128)(2,1)}, u32[]{:S(2)}) copy-start(bf16[128,3072]{1,0:T(8,128)(2,1)} %param.15) | copy-start | bytes 2359300
  6.5 2.7 copy-start.5
  6.5 183.6 %all-gather.10.cloned.1.call-start = ((), (), s32[]{:S(2)}) async-start(), calls=%async_computation.6 | async-start | bytes 14155776 | tf_op jit(solution)/shard_map/all_gather | solution.py:11
  10.8 206.6 %all-gather.6.cloned.1.call-start = ((), (), s32[]{:S(2)}) async-start(), calls=%async_computation.2 | async-start | bytes 2359296 | tf_op jit(solution)/shard_map/all_gather | solution.py:97
  205.1 1.7 copy-start.6
  205.1 1.7 copy-start.9
  206.7 2.6 copy-start.10
  206.7 2.6 copy-start.11
  209.3 10.1 %copy-start.8 = (f32[6144]{0:T(1024)S(1)}, f32[6144]{0:T(1024)}, u32[]{:S(2)}) copy-start(f32[6144]{0:T(1024)} %param.21) | copy-start | bytes 73732
  209.3 56.8 %all-gather.8.cloned.1.call-start = ((), (), s32[]{:S(2)}) async-start(), calls=%async_computation.3 | async-start | bytes 1769472 | tf_op jit(solution)/shard_map/all_gather | solution.py:119
  217.4 1.9 copy-start.3
  220.6 126.0 %reduce-scatter.3.cloned.1.call-start = ((), (), s32[]{:S(2)}) async-start(), calls=%async_computation.4 | async-start | bytes 1769472 | tf_op jit(solution)/shard_map/reduce_scatter | solution.py:124
  266.1 5.7 %copy-start.1 = (bf16[128,6144]{1,0:T(8,128)(2,1)S(1)}, bf16[128,6144]{1,0:T(8,128)(2,1)}, u32[]{:S(2)}) copy-start(bf16[128,6144]{1,0:T(8,128)(2,1)} %all-gather.8.cloned.1.call-done) | copy-start | bytes 4718596
  271.8 11.3 %copy-start.7 = (bf16[6144,32]{0,1:T(8,128)(2,1)S(1)}, bf16[6144,32]{0,1:T(8,128)(2,1)}, u32[]{:S(2)}) copy-start(bf16[6144,32]{0,1:T(8,128)(2,1)} %param.22) | copy-start | bytes 1179652
  282.9 1.4 copy-start.4
  282.9 75.5 %reduce-scatter.5.cloned.1.call-start = ((), (), s32[]{:S(2)}) async-start(), calls=%async_computation.5 | async-start | bytes 2359296 | tf_op jit(solution)/shard_map/reduce_scatter | solution.py:134
  286.3 72.0 %copy-start.2 = (bf16[128,3072]{1,0:T(8,128)(2,1)S(1)}, bf16[128,3072]{1,0:T(8,128)(2,1)}, u32[]{:S(2)}) copy-start(bf16[128,3072]{1,0:T(8,128)(2,1)} %add_convert_fusion.1) | copy-start | bytes 2359300
Sparse Core Ops, SparseCore 0:
  10.9 179.1 all-gather.9
  209.4 7.9 all-gather.5
  220.7 45.3 all-gather.7
  283.0 63.5 reduce-scatter.2
  350.3 7.9 reduce-scatter.4
where the time goes:
time: 368 us; the launch traced here: 367 us
  waiting for transfers between devices  275 us (75%)
  matrix products  30.3 us (8%)
  blocking collectives  22.4 us (6%)
  other arithmetic  19.5 us (5%)
  between operations  13.3 us (4%)
  local copies, waits for them, and re-layouts  5.5 us (1%)
    all_gather x1, waiting for transfers between devices, carried_in(): pieces = jax.tree.map(lambda part: lax.all_gather(part, axis), value)  153 us
    reduce_scatter x1, waiting for transfers between devices, shards(): lax.psum_scatter(jnp.dot(segment, down_weight[0], preferred_element_type=...  60.3 us
    all_gather x1, waiting for transfers between devices, shards(): segment = lax.all_gather(buffer, 'seq', axis=0, tiled=True)  45.5 us
    all_gather x1, blocking collectives, carried_in(): pieces = jax.tree.map(lambda part: lax.all_gather(part, axis), value)  22.4 us
    select_n x7, other arithmetic, hop(): jnp.where(position < mine, new, old)  12.4 us
    dot_general x1, matrix products, shards(): jnp.dot(segment, down_weight[0], preferred_element_type=jnp.float32)  11.1 us
    reduce_scatter x1, waiting for transfers between devices, shards(): lax.psum_scatter(contribution.astype(jnp.bfloat16), 'exp', scatter_dimens...  8.14 us
    all_gather x1, waiting for transfers between devices, shards(): hidden_full = lax.all_gather(hidden_half, 'exp', axis=1, tiled=True)  8.04 us
  transfers between devices with their start and end apart: 5, of which 5 were waited for; matrix products, arithmetic and copies ran while one was open for 1% of the time, Pallas kernels for 0%

commit v1 on v0

v1 whole, which is shorter than its diff:
```python
import jax
import jax.numpy as jnp
from jax import lax
from jax.sharding import PartitionSpec as P

CAP = 16
CHUNKS = 2


def slot_matches(routes, slot_pos, expert, capacity):
    return (routes == expert)[:, :, None] & (
        slot_pos[:, :, None] == jnp.arange(capacity)[None, None, :]
    )


def entering_state(local_state, block_total):
    count, mine = (lax.axis_size("seq"), lax.axis_index("seq"))
    odd = mine % 2 == 1
    swap = [(i, i ^ 1) for i in range(count)]
    heads = local_state.shape[0]
    half = heads // 2
    part = half // CHUNKS
    total_other = lax.ppermute(block_total[None], "seq", swap)[0]

    def pick(array, first):
        return lax.dynamic_slice_in_dim(array, jnp.where(odd, half, 0) + first, part, axis=0)

    def pick_other(array, first):
        return lax.dynamic_slice_in_dim(array, jnp.where(odd, 0, half) + first, part, axis=0)

    kept, swapped = ([], [])
    for chunk in range(CHUNKS):
        own = pick(local_state, chunk * part)
        arrived = lax.ppermute(
            pick_other(local_state, chunk * part).astype(jnp.bfloat16), "seq", swap
        ).astype(jnp.float32)
        own_decay = jnp.exp(pick(block_total, chunk * part))[:, None, None]
        other_decay = jnp.exp(pick(total_other, chunk * part))[:, None, None]
        even_state = jnp.where(odd, arrived, own)
        odd_state = jnp.where(odd, own, arrived)
        even_decay = jnp.where(odd, other_decay, own_decay)
        odd_decay = jnp.where(odd, own_decay, other_decay)
        pair_state = odd_decay * even_state + odd_state
        pair_decay = even_decay * odd_decay
        before = jnp.zeros_like(own)
        for hop in range(count // 2 - 1):
            pairs = [(2 * hop + k, 2 * hop + 2 + k) for k in range(2)]
            sent = (pair_decay * before + pair_state).astype(jnp.bfloat16)
            before = before + lax.ppermute(sent, "seq", pairs).astype(jnp.float32)
        between = even_decay * before + even_state
        kept.append(jnp.where(odd, between, before).astype(jnp.bfloat16))
        swapped.append(
            lax.ppermute(jnp.where(odd, before, between).astype(jnp.bfloat16), "seq", swap)
        )
    kept, swapped = (jnp.concatenate(kept), jnp.concatenate(swapped))
    return jnp.where(odd, jnp.concatenate([swapped, kept]), jnp.concatenate([kept, swapped]))


def ring_pairs(count):
    order = list(range(0, count, 2)) + list(range(count - 1, 0, -2))
    right = [(order[i], order[(i + 1) % count]) for i in range(count)]
    return (right, [(b, a) for a, b in right])


def ring_gather(unit):
    count = lax.axis_size("seq")
    right, left = ring_pairs(count)
    middle = unit.shape[1] // 2
    from_left, from_right = ([], [])
    moving_right, moving_left = (unit, unit)
    for _ in range(count // 2 - 1):
        moving_right = lax.ppermute(moving_right, "seq", right)
        moving_left = lax.ppermute(moving_left, "seq", left)
        from_left.append(moving_right)
        from_right.append(moving_left)
    far = jnp.concatenate(
        [
            lax.ppermute(moving_right[:, :middle], "seq", right),
            lax.ppermute(moving_left[:, middle:], "seq", left),
        ],
        axis=1,
    )
    return jnp.concatenate([unit] + from_left + [far] + from_right, axis=0)


def ring_scatter(partial, rows):
    count = lax.axis_size("seq")
    right, left = ring_pairs(count)
    middle = partial.shape[1] // 2
    steps = count // 2

    def piece(position):
        return partial[position * rows : (position + 1) * rows]

    far = piece(steps).astype(jnp.bfloat16)
    moving_left = lax.ppermute(far[:, :middle], "seq", left).astype(jnp.float32)
    moving_right = lax.ppermute(far[:, middle:], "seq", right).astype(jnp.float32)
    for step in range(steps - 1, 0, -1):
        to_left, to_right = (piece(step), piece(steps + step))
        if step == steps - 1:
            to_left = jnp.concatenate(
                [to_left[:, :middle] + moving_left, to_left[:, middle:]], axis=1
            )
            to_right = jnp.concatenate(
                [to_right[:, :middle], to_right[:, middle:] + moving_right], axis=1
            )
        else:
            to_left, to_right = (to_left + moving_left, to_right + moving_right)
        moving_left = lax.ppermute(to_left.astype(jnp.bfloat16), "seq", left).astype(jnp.float32)
        moving_right = lax.ppermute(to_right.astype(jnp.bfloat16), "seq", right).astype(
            jnp.float32
        )
    return piece(0) + moving_left + moving_right


def shards(
    queries,
    key_rows,
    values,
    log_decay,
    residual,
    attn_gain,
    moe_gain,
    router,
    routes,
    slot_pos,
    gate_weight,
    up_weight,
    down_weight,
):
    length, width = queries.shape
    heads_here = log_decay.shape[1]
    head_width = width // heads_here
    core = lax.axis_index("exp")
    exchange = [(0, 1), (1, 0)]
    query_heads = queries.reshape(length, heads_here, head_width)
    key_heads = key_rows.reshape(length, heads_here, head_width)
    value_heads = values.reshape(length, heads_here, head_width)
    running = jnp.cumsum(log_decay, axis=0)
    block_total = running[-1]
    scaled = (
        key_heads.astype(jnp.float32) * jnp.exp(block_total[None, :] - running)[:, :, None]
    ).astype(jnp.bfloat16)
    local_state = jnp.einsum(
        "shd,she->hde", scaled, value_heads, preferred_element_type=jnp.float32
    )
    entering = entering_state(local_state, block_total)
    scores = jnp.einsum("thd,shd->hts", query_heads, key_heads, preferred_element_type=jnp.float32)
    spread = running.T[:, :, None] - running.T[:, None, :]
    causal = (jnp.arange(length)[:, None] >= jnp.arange(length)[None, :])[None]
    mixing = jnp.where(causal, scores * jnp.exp(jnp.where(causal, spread, 0.0)), 0.0).astype(
        jnp.bfloat16
    )
    within_part = jnp.einsum(
        "hts,shd->thd", mixing, value_heads, preferred_element_type=jnp.float32
    )
    carried_part = jnp.einsum(
        "thd,hde->the", query_heads, entering, preferred_element_type=jnp.float32
    )
    raw = within_part + carried_part * jnp.exp(running)[:, :, None]
    normed = raw * lax.rsqrt(jnp.mean(raw * raw, axis=2, keepdims=True) + 1e-05)
    hidden_half = (residual.astype(jnp.float32) + normed.reshape(length, -1) * attn_gain).astype(
        jnp.bfloat16
    )

    matches = [slot_matches(routes, slot_pos, expert, CAP) for expert in range(2)]
    tables = [jnp.any(match, axis=1).astype(jnp.bfloat16).T for match in matches]
    table = jnp.concatenate(tables, axis=0)
    rows = jnp.dot(table, hidden_half, preferred_element_type=jnp.float32).astype(jnp.bfloat16)
    rows_own = jnp.where(core == 0, rows[:CAP], rows[CAP:])
    rows_other = lax.ppermute(jnp.where(core == 0, rows[CAP:], rows[:CAP]), "exp", exchange)
    rows_whole = jnp.where(
        core == 0,
        jnp.concatenate([rows_own, rows_other], axis=1),
        jnp.concatenate([rows_other, rows_own], axis=1),
    ).astype(jnp.float32)
    rows_inverse = lax.rsqrt(jnp.mean(rows_whole * rows_whole, axis=1, keepdims=True) + 1e-06)
    buffer = (rows_whole * rows_inverse * moe_gain).astype(jnp.bfloat16)

    segment = ring_gather(buffer)
    gate_part = jnp.dot(segment, gate_weight[0], preferred_element_type=jnp.float32)
    up_part = jnp.dot(segment, up_weight[0], preferred_element_type=jnp.float32)
    hidden_rows = (jax.nn.silu(gate_part) * up_part).astype(jnp.bfloat16)
    partial = jnp.dot(hidden_rows, down_weight[0], preferred_element_type=jnp.float32)
    expert_out = ring_scatter(partial, CAP).astype(jnp.bfloat16)

    hidden_float = hidden_half.astype(jnp.float32)
    gain_half = lax.dynamic_slice_in_dim(moe_gain, core * width, width)
    router_half = lax.dynamic_slice_in_dim(router, core * width, width, axis=0)
    logits_half = jnp.dot(
        hidden_float * gain_half, router_half.astype(jnp.float32), precision=lax.Precision.HIGHEST
    )
    picked_half = jnp.sum(
        jnp.where(
            routes[:, :, None] == jnp.arange(router.shape[1])[None, None, :],
            logits_half[:, None, :],
            0.0,
        ),
        axis=2,
    )
    square_half = jnp.sum(hidden_float * hidden_float, axis=1, keepdims=True)
    sums_half = jnp.concatenate([picked_half, square_half], axis=1)
    sums = sums_half + lax.ppermute(sums_half, "exp", exchange)
    inverse = lax.rsqrt(sums[:, 2:] / (2 * width) + 1e-06)
    gates = jax.nn.sigmoid(sums[:, :2] * inverse)
    shares = gates / jnp.sum(gates, axis=1, keepdims=True)
    weighting = jnp.concatenate(
        [jnp.sum(jnp.where(match, shares[:, :, None], 0.0), axis=1) for match in matches], axis=1
    )

    out_low, out_high = (expert_out[:, :width], expert_out[:, width:])
    out_own = jnp.where(core == 0, out_low, out_high)
    out_other = lax.ppermute(jnp.where(core == 0, out_high, out_low), "exp", exchange)
    outs = jnp.where(
        core == 0,
        jnp.concatenate([out_own, out_other], axis=0),
        jnp.concatenate([out_other, out_own], axis=0),
    ).astype(jnp.float32)
    expert_sum = jnp.dot(weighting, outs, precision=lax.Precision.HIGHEST)
    return (hidden_float + expert_sum).astype(jnp.bfloat16)


def solution(mesh):
    placed = (
        P(("groups", "seq"), "exp"),
        P(("groups", "seq"), "exp"),
        P(("groups", "seq"), "exp"),
        P(("groups", "seq"), "exp"),
        P(("groups", "seq"), "exp"),
        P("exp"),
        P(),
        P(),
        P(("groups", "seq"), None),
        P(("groups", "seq"), None),
        P("exp", None, "seq"),
        P("exp", None, "seq"),
        P("exp", "seq", None),
    )
    return jax.shard_map(
        shards, mesh=mesh, in_specs=placed, out_specs=P(("groups", "seq"), "exp"), check_vma=False
    )
```

time: 368 us -> 148 us (0.40)
  waiting for transfers between devices: 275 us -> 57.1 us
  starting transfers between devices: 0.35 us -> 42.2 us
  blocking collectives: 22.4 us -> 0 us
  between operations: 13.3 us -> 0.46 us
  other arithmetic: 19.5 us -> 11 us
    all_gather x3 -> x0, waiting for transfers between devices: 207 us -> none  [the longest x1 153 us: carried_in(): pieces = jax.tree.map(lambda part: lax.all_gather(part, axis), value)]
    reduce_scatter x2 -> x0, waiting for transfers between devices: 68.5 us -> none  [the longest x1 60.3 us: shards(): lax.psum_scatter(jnp.dot(segment, down_weight[0], preferred_element_type=...]
    ppermute x0 -> x30, waiting for transfers between devices: none -> 57.1 us  [the longest x3 9.77 us: ring_scatter(): lax.ppermute(to_left.astype(jnp.bfloat16), 'seq', left).astype(jnp.float32)]
    ppermute x0 -> x30, starting transfers between devices: none -> 42.2 us  [the longest x6 13.5 us: entering_state(): before = before + lax.ppermute(sent, 'seq', pairs).astype(jnp.float32)]
    all_gather x1 -> x0, blocking collectives: 22.4 us -> none  [carried_in(): pieces = jax.tree.map(lambda part: lax.all_gather(part, axis), value)]
    select_n x7 -> x2, other arithmetic: 12.4 us -> 0.04 us  [the longest x1 0.02 us: shards(): jnp.where(core == 0, rows[CAP:], rows[:CAP])]
  transfers between devices with their start and end apart: 5 -> 30, of which waited for: 5 -> 21; matrix products, arithmetic and copies ran while one was open for 1% -> 8% of each run, Pallas kernels for 0% -> 0%
where the time goes in v1:
time: 148 us
  waiting for transfers between devices  57.1 us (39%)
  starting transfers between devices  42.2 us (29%)
  matrix products  28.3 us (19%)
  other arithmetic  11 us (7%)
  local copies, waits for them, and re-layouts  8.44 us (6%)
    ppermute x6, starting transfers between devices, entering_state(): before = before + lax.ppermute(sent, 'seq', pairs).astype(jnp.float32)  13.5 us
    dot_general x1, matrix products, shards(): jnp.dot(hidden_rows, down_weight[0], preferred_element_type=jnp.float32)  12.1 us
    ppermute x3, starting transfers between devices, ring_gather(): moving_right = lax.ppermute(moving_right, 'seq', right)  10.6 us
    ppermute x3, waiting for transfers between devices, ring_scatter(): lax.ppermute(to_left.astype(jnp.bfloat16), 'seq', left).astype(jnp.float32)  9.77 us
    ppermute x3, waiting for transfers between devices, ring_scatter(): lax.ppermute(to_right.astype(jnp.bfloat16), 'seq', right)  9.19 us
    ppermute x3, waiting for transfers between devices, ring_gather(): moving_left = lax.ppermute(moving_left, 'seq', left)  6.29 us
    ppermute x3, starting transfers between devices, ring_scatter(): lax.ppermute(to_left.astype(jnp.bfloat16), 'seq', left).astype(jnp.float32)  6.13 us
    ppermute x3, waiting for transfers between devices, ring_gather(): moving_right = lax.ppermute(moving_right, 'seq', right)  5.66 us
  transfers between devices with their start and end apart: 30, of which 21 were waited for; matrix products, arithmetic and copies ran while one was open for 8% of the time, Pallas kernels for 0%

profile of v1, /device:TPU:0, one launch (start us, length us, event | category | flops | bytes accessed | tf_op | source)
XLA Modules:
  0.0 147.5 jit_solution(1501743910170487850)
XLA Ops:
  5.6 3.0 %collective-permute-start.1 = (bf16[6,128,128]{2,1,0:T(8,128)(2,1)S(1)}, bf16[6,128,128]{2,1,0:T(8,128)(2,1)S(1)}, u32[]{:S(2)}, u32[]{:S(2)}) collective-permute-start(bf16[6,128,128]{2,1,0:T(8,128)(2,1)S(1)} %get-tuple-element.36), channel_id=1, source_target_pairs={{0,2},{2,0},{4,6},{6,4},{8,10},{10,8},{12,14},{14,12},{1,3},{3,1},... | collective-permute-start | bytes 589832 | tf_op jit(solution)/shard_map/ppermute | solution.py:34
  8.6 4.9 %collective-permute-done = f32[1,24]{1,0:T(1,128)S(1)} collective-permute-done((f32[1,24]{1,0:T(1,128)S(1)}, f32[1,24]{1,0:T(1,128)S(1)}, u32[]{:S(2)}, u32[]{:S(2)}) %collective-permute-start) | collective-permute-done | bytes 128 | tf_op jit(solution)/shard_map/ppermute | solution.py:23
  14.3 3.7 %collective-permute-start.2 = (bf16[6,128,128]{2,1,0:T(8,128)(2,1)S(1)}, bf16[6,128,128]{2,1,0:T(8,128)(2,1)S(1)}, u32[]{:S(2)}, u32[]{:S(2)}) collective-permute-start(bf16[6,128,128]{2,1,0:T(8,128)(2,1)S(1)} %add_convert_fusion.4), channel_id=1, source_target_pairs={{0,4},{2,6},{1,5},{3,7},{16,20},{18,22},{17,21},{19,23}} | collective-permute-start | bytes 589832 | tf_op jit(solution)/shard_map/ppermute | solution.py:49
  25.0 6.3 %collective-permute-start.7 = (bf16[6,128,128]{2,1,0:T(8,128)(2,1)S(1)}, bf16[6,128,128]{2,1,0:T(8,128)(2,1)S(1)}, u32[]{:S(2)}, u32[]{:S(2)}) collective-permute-start(bf16[6,128,128]{2,1,0:T(8,128)(2,1)S(1)} %get-tuple-element.35), channel_id=1, source_target_pairs={{0,4},{2,6},{1,5},{3,7},{16,20},{18,22},{17,21},{19,23}} | collective-permute-start | bytes 589832 | tf_op jit(solution)/shard_map/ppermute | solution.py:49
  31.3 3.1 %collective-permute-done.7 = bf16[6,128,128]{2,1,0:T(8,128)(2,1)S(1)} collective-permute-done((bf16[6,128,128]{2,1,0:T(8,128)(2,1)S(1)}, bf16[6,128,128]{2,1,0:T(8,128)(2,1)S(1)}, u32[]{:S(2)}, u32[]{:S(2)}) %collective-permute-start.7) | collective-permute-done | bytes 196640 | tf_op jit(solution)/shard_map/ppermute | solution.py:49
  41.7 3.3 %fusion.10 = f32[24,128,128]{1,2,0:T(8,128)} fusion(bf16[128,24,128]{0,2,1:T(8,128)(2,1)S(1)} %bitcast.79, f32[24,128]{1,0:T(8,128)} %copy.51, pred[128,128]{1,0:T(8,128)(4,1)S(1)} %iota_compare_fusion, bf16[128,3072]{1,0:T(8,128)(2,1)} %param.15, bf16[128,3072]{1,0:T(8,128)(2,1)S(1)} %copy-done), kind=kOutput, calls=%fused_computation.19 | convolution fusion | flops 203292672 | bytes 3960832 | tf_op jit(solution)/shard_map/hts,shd->thd/dot_general | solution.py:154
  48.5 2.6 %collective-permute-done.5 = bf16[6,128,128]{2,1,0:T(8,128)(2,1)} collective-permute-done((bf16[6,128,128]{2,1,0:T(8,128)(2,1)}, bf16[6,128,128]{2,1,0:T(8,128)(2,1)}, u32[]{:S(2)}, u32[]{:S(2)}) %collective-permute-start.5) | collective-permute-done | bytes 196640 | tf_op jit(solution)/shard_map/ppermute | solution.py:53
  51.1 2.5 %collective-permute-done.10 = bf16[6,128,128]{2,1,0:T(8,128)(2,1)S(1)} collective-permute-done((bf16[6,128,128]{2,1,0:T(8,128)(2,1)S(1)}, bf16[6,128,128]{2,1,0:T(8,128)(2,1)S(1)}, u32[]{:S(2)}, u32[]{:S(2)}) %collective-permute-start.10) | collective-permute-done | bytes 196640 | tf_op jit(solution)/shard_map/ppermute | solution.py:53
  53.5 2.4 %multiply_reduce_fusion = (f32[128,24]{0,1:T(8,128)S(1)}, f32[128,24,128]{0,2,1:T(8,128)S(1)}) fusion(f32[128,24]{0,1:T(8,128)S(1)} %copy.59, bf16[6,128,128]{2,1,0:T(8,128)(2,1)S(1)} %get-tuple-element.28, bf16[6,128,128]{2,1,0:T(8,128)(2,1)S(1)} %copy-done.8, bf16[6,128,128]{2,1,0:T(8,128)(2,1)S(1)} %collective-permute-done.10, ...), kind=kOutput, calls=%fused_computation.16 | convolution fusion | flops 104985600 | bytes 4743169 | tf_op jit(solution)/shard_map/thd,hde->the/dot_general | solution.py:157
  61.5 5.1 %collective-permute-start.13 = (bf16[16,6144]{1,0:T(8,128)(2,1)S(1)}, bf16[16,6144]{1,0:T(8,128)(2,1)S(1)}, u32[]{:S(2)}, u32[]{:S(2)}) collective-permute-start(bf16[16,6144]{1,0:T(8,128)(2,1)S(1)} %get-tuple-element.12), channel_id=1, source_target_pairs={{0,4},{4,8},{8,12},{12,14},{14,10},{10,6},{6,2},{2,0},{1,5},{5,9},... | collective-permute-start | bytes 589832 | tf_op jit(solution)/shard_map/ppermute | solution.py:72
  68.6 2.5 %collective-permute-done.13 = bf16[16,6144]{1,0:T(8,128)(2,1)S(1)} collective-permute-done((bf16[16,6144]{1,0:T(8,128)(2,1)S(1)}, bf16[16,6144]{1,0:T(8,128)(2,1)S(1)}, u32[]{:S(2)}, u32[]{:S(2)}) %collective-permute-start.13) | collective-permute-done | bytes 196640 | tf_op jit(solution)/shard_map/ppermute | solution.py:72
  71.1 3.0 %collective-permute-start.14 = (bf16[16,6144]{1,0:T(8,128)(2,1)S(1)}, bf16[16,6144]{1,0:T(8,128)(2,1)S(1)}, u32[]{:S(2)}, u32[]{:S(2)}) collective-permute-start(bf16[16,6144]{1,0:T(8,128)(2,1)S(1)} %collective-permute-done.13), channel_id=1, source_target_pairs={{0,4},{4,8},{8,12},{12,14},{14,10},{10,6},{6,2},{2,0},{1,5},{5,9},... | collective-permute-start | bytes 589832 | tf_op jit(solution)/shard_map/ppermute | solution.py:72
  74.6 3.2 %collective-permute-done.14 = bf16[16,6144]{1,0:T(8,128)(2,1)S(1)} collective-permute-done((bf16[16,6144]{1,0:T(8,128)(2,1)S(1)}, bf16[16,6144]{1,0:T(8,128)(2,1)S(1)}, u32[]{:S(2)}, u32[]{:S(2)}) %collective-permute-start.14) | collective-permute-done | bytes 196640 | tf_op jit(solution)/shard_map/ppermute | solution.py:72
  77.8 2.5 %collective-permute-start.15 = (bf16[16,6144]{1,0:T(8,128)(2,1)S(1)}, bf16[16,6144]{1,0:T(8,128)(2,1)S(1)}, u32[]{:S(2)}, u32[]{:S(2)}) collective-permute-start(bf16[16,6144]{1,0:T(8,128)(2,1)S(1)} %collective-permute-done.14), channel_id=1, source_target_pairs={{0,4},{4,8},{8,12},{12,14},{14,10},{10,6},{6,2},{2,0},{1,5},{5,9},... | collective-permute-start | bytes 589832 | tf_op jit(solution)/shard_map/ppermute | solution.py:72
  81.0 5.4 %collective-permute-done.19 = bf16[16,6144]{1,0:T(8,128)(2,1)S(1)} collective-permute-done((bf16[16,6144]{1,0:T(8,128)(2,1)S(1)}, bf16[16,6144]{1,0:T(8,128)(2,1)S(1)}, u32[]{:S(2)}, u32[]{:S(2)}) %collective-permute-start.19) | collective-permute-done | bytes 196640 | tf_op jit(solution)/shard_map/ppermute | solution.py:73
  88.8 2.3 %collective-permute-done.20 = bf16[16,3072]{1,0:T(8,128)(2,1)S(1)} collective-permute-done((bf16[16,3072]{1,0:T(8,128)(2,1)S(1)}, bf16[16,3072]{1,0:T(8,128)(2,1)S(1)}, u32[]{:S(2)}, u32[]{:S(2)}) %collective-permute-start.20) | collective-permute-done | bytes 98336 | tf_op jit(solution)/shard_map/ppermute | solution.py:79
  91.7 5.1 %fusion.2 = f32[128,768]{1,0:T(8,128)S(1)} fusion(bf16[128,6144]{1,0:T(8,128)(2,1)S(1)} %constant_dynamic-update-slice_fusion, bf16[1,6144,768]{2,1,0:T(8,128)(2,1)} %param.24), kind=kOutput, calls=%fused_computation.2 | convolution fusion | flops 1207959552 | bytes 11403264 | tf_op jit(solution)/shard_map/dot_general | solution.py:182
  96.8 12.1 %fusion.104 = (bf16[128,6144]{1,0:T(8,128)(2,1)}, f32[128,6144]{1,0:T(8,128)}) fusion(bf16[1,768,6144]{2,1,0:T(8,128)(2,1)} %param.25, f32[128,768]{1,0:T(8,128)S(1)} %fusion.2, bf16[128,6144]{1,0:T(8,128)(2,1)S(1)} %constant_dynamic-update-slice_fusion, bf16[1,6144,768]{2,1,0:T(8,128)(2,1)} %param.23), kind=kOutput, calls=%fused_computation.179 | convolution fusion | flops 2417295360 | bytes 25559040 | tf_op jit(solution)/shard_map/dot_general | solution.py:184
  112.2 2.6 %collective-permute-done.21 = bf16[16,3072]{1,0:T(8,128)(2,1)S(1)} collective-permute-done((bf16[16,3072]{1,0:T(8,128)(2,1)S(1)}, bf16[16,3072]{1,0:T(8,128)(2,1)S(1)}, u32[]{:S(2)}, u32[]{:S(2)}) %collective-permute-start.21) | collective-permute-done | bytes 98336 | tf_op jit(solution)/shard_map/ppermute | solution.py:96
  119.6 4.4 %collective-permute-done.22 = bf16[16,6144]{1,0:T(8,128)(2,1)S(1)} collective-permute-done((bf16[16,6144]{1,0:T(8,128)(2,1)S(1)}, bf16[16,6144]{1,0:T(8,128)(2,1)S(1)}, u32[]{:S(2)}, u32[]{:S(2)}) %collective-permute-start.22) | collective-permute-done | bytes 196640 | tf_op jit(solution)/shard_map/ppermute | solution.py:109
  125.0 2.3 %collective-permute-start.23 = (bf16[16,6144]{1,0:T(8,128)(2,1)S(1)}, bf16[16,6144]{1,0:T(8,128)(2,1)S(1)}, u32[]{:S(2)}, u32[]{:S(2)}) collective-permute-start(bf16[16,6144]{1,0:T(8,128)(2,1)S(1)} %fusion.53), channel_id=1, source_target_pairs={{4,0},{8,4},{12,8},{14,12},{10,14},{6,10},{2,6},{0,2},{5,1},{9,5},... | collective-permute-start | bytes 589832 | tf_op jit(solution)/shard_map/ppermute | solution.py:109
  127.4 5.4 %collective-permute-done.23 = bf16[16,6144]{1,0:T(8,128)(2,1)S(1)} collective-permute-done((bf16[16,6144]{1,0:T(8,128)(2,1)S(1)}, bf16[16,6144]{1,0:T(8,128)(2,1)S(1)}, u32[]{:S(2)}, u32[]{:S(2)}) %collective-permute-start.23) | collective-permute-done | bytes 196640 | tf_op jit(solution)/shard_map/ppermute | solution.py:109
  135.0 3.6 %collective-permute-done.27 = bf16[16,6144]{1,0:T(8,128)(2,1)S(1)} collective-permute-done((bf16[16,6144]{1,0:T(8,128)(2,1)S(1)}, bf16[16,6144]{1,0:T(8,128)(2,1)S(1)}, u32[]{:S(2)}, u32[]{:S(2)}) %collective-permute-start.27) | collective-permute-done | bytes 196640 | tf_op jit(solution)/shard_map/ppermute | solution.py:110
  138.7 5.6 %collective-permute-done.28 = bf16[16,6144]{1,0:T(8,128)(2,1)S(1)} collective-permute-done((bf16[16,6144]{1,0:T(8,128)(2,1)S(1)}, bf16[16,6144]{1,0:T(8,128)(2,1)S(1)}, u32[]{:S(2)}, u32[]{:S(2)}) %collective-permute-start.28) | collective-permute-done | bytes 196640 | tf_op jit(solution)/shard_map/ppermute | solution.py:110
  (131 shorter events, 50.4 us)
Async XLA Ops:
  5.6 8.6 %collective-permute-start.1 = (bf16[6,128,128]{2,1,0:T(8,128)(2,1)S(1)}, bf16[6,128,128]{2,1,0:T(8,128)(2,1)S(1)}, u32[]{:S(2)}, u32[]{:S(2)}) collective-permute-start(bf16[6,128,128]{2,1,0:T(8,128)(2,1)S(1)} %get-tuple-element.36), channel_id=1, source_target_pairs={{0,2},{2,0},{4,6},{6,4},{8,10},{10,8},{12,14},{14,12},{1,3},{3,1},... | collective-permute-start | bytes 589832 | tf_op jit(solution)/shard_map/ppermute | solution.py:34
  8.5 5.0 %collective-permute-start = (f32[1,24]{1,0:T(1,128)S(1)}, f32[1,24]{1,0:T(1,128)S(1)}, u32[]{:S(2)}, u32[]{:S(2)}) collective-permute-start(f32[1,24]{1,0:T(1,128)S(1)} %get-tuple-element.45), channel_id=1, source_target_pairs={{0,2},{2,0},{4,6},{6,4},{8,10},{10,8},{12,14},{14,12},{1,3},{3,1},... | collective-permute-start | bytes 296 | tf_op jit(solution)/shard_map/ppermute | solution.py:23
  14.3 6.9 %collective-permute-start.2 = (bf16[6,128,128]{2,1,0:T(8,128)(2,1)S(1)}, bf16[6,128,128]{2,1,0:T(8,128)(2,1)S(1)}, u32[]{:S(2)}, u32[]{:S(2)}) collective-permute-start(bf16[6,128,128]{2,1,0:T(8,128)(2,1)S(1)} %add_convert_fusion.4), channel_id=1, source_target_pairs={{0,4},{2,6},{1,5},{3,7},{16,20},{18,22},{17,21},{19,23}} | collective-permute-start | bytes 589832 | tf_op jit(solution)/shard_map/ppermute | solution.py:49
  18.0 5.9 %collective-permute-start.6 = (bf16[6,128,128]{2,1,0:T(8,128)(2,1)}, bf16[6,128,128]{2,1,0:T(8,128)(2,1)S(1)}, u32[]{:S(2)}, u32[]{:S(2)}) collective-permute-start(bf16[6,128,128]{2,1,0:T(8,128)(2,1)} %get-tuple-element.37), channel_id=1, source_target_pairs={{0,2},{2,0},{4,6},{6,4},{8,10},{10,8},{12,14},{14,12},{1,3},{3,1},... | collective-permute-start | bytes 589832 | tf_op jit(solution)/shard_map/ppermute | solution.py:34
  24.3 7.0 %collective-permute-start.4 = (bf16[6,128,128]{2,1,0:T(8,128)(2,1)S(1)}, bf16[6,128,128]{2,1,0:T(8,128)(2,1)S(1)}, u32[]{:S(2)}, u32[]{:S(2)}) collective-permute-start(bf16[6,128,128]{2,1,0:T(8,128)(2,1)S(1)} %get-tuple-element.34), channel_id=1, source_target_pairs={{8,12},{10,14},{9,13},{11,15},{24,28},{26,30},{25,29},{27,31}} | collective-permute-start | bytes 589832 | tf_op jit(solution)/shard_map/ppermute | solution.py:49
  25.0 9.4 %collective-permute-start.7 = (bf16[6,128,128]{2,1,0:T(8,128)(2,1)S(1)}, bf16[6,128,128]{2,1,0:T(8,128)(2,1)S(1)}, u32[]{:S(2)}, u32[]{:S(2)}) collective-permute-start(bf16[6,128,128]{2,1,0:T(8,128)(2,1)S(1)} %get-tuple-element.35), channel_id=1, source_target_pairs={{0,4},{2,6},{1,5},{3,7},{16,20},{18,22},{17,21},{19,23}} | collective-permute-start | bytes 589832 | tf_op jit(solution)/shard_map/ppermute | solution.py:49
  40.2 6.4 %collective-permute-start.9 = (bf16[6,128,128]{2,1,0:T(8,128)(2,1)}, bf16[6,128,128]{2,1,0:T(8,128)(2,1)}, u32[]{:S(2)}, u32[]{:S(2)}) collective-permute-start(bf16[6,128,128]{2,1,0:T(8,128)(2,1)} %add_convert_fusion.1), channel_id=1, source_target_pairs={{8,12},{10,14},{9,13},{11,15},{24,28},{26,30},{25,29},{27,31}} | collective-permute-start | bytes 589832 | tf_op jit(solution)/shard_map/ppermute | solution.py:49
  45.0 6.1 %collective-permute-start.5 = (bf16[6,128,128]{2,1,0:T(8,128)(2,1)}, bf16[6,128,128]{2,1,0:T(8,128)(2,1)}, u32[]{:S(2)}, u32[]{:S(2)}) collective-permute-start(bf16[6,128,128]{2,1,0:T(8,128)(2,1)} %get-tuple-element.25), channel_id=1, source_target_pairs={{0,2},{2,0},{4,6},{6,4},{8,10},{10,8},{12,14},{14,12},{1,3},{3,1},... | collective-permute-start | bytes 589832 | tf_op jit(solution)/shard_map/ppermute | solution.py:53
  47.8 5.7 %collective-permute-start.10 = (bf16[6,128,128]{2,1,0:T(8,128)(2,1)S(1)}, bf16[6,128,128]{2,1,0:T(8,128)(2,1)S(1)}, u32[]{:S(2)}, u32[]{:S(2)}) collective-permute-start(bf16[6,128,128]{2,1,0:T(8,128)(2,1)S(1)} %get-tuple-element.27), channel_id=1, source_target_pairs={{0,2},{2,0},{4,6},{6,4},{8,10},{10,8},{12,14},{14,12},{1,3},{3,1},... | collective-permute-start | bytes 589832 | tf_op jit(solution)/shard_map/ppermute | solution.py:53
  61.5 9.6 %collective-permute-start.13 = (bf16[16,6144]{1,0:T(8,128)(2,1)S(1)}, bf16[16,6144]{1,0:T(8,128)(2,1)S(1)}, u32[]{:S(2)}, u32[]{:S(2)}) collective-permute-start(bf16[16,6144]{1,0:T(8,128)(2,1)S(1)} %get-tuple-element.12), channel_id=1, source_target_pairs={{0,4},{4,8},{8,12},{12,14},{14,10},{10,6},{6,2},{2,0},{1,5},{5,9},... | collective-permute-start | bytes 589832 | tf_op jit(solution)/shard_map/ppermute | solution.py:72
  66.6 7.9 %collective-permute-start.17 = (bf16[16,6144]{1,0:T(8,128)(2,1)S(1)}, bf16[16,6144]{1,0:T(8,128)(2,1)S(1)}, u32[]{:S(2)}, u32[]{:S(2)}) collective-permute-start(bf16[16,6144]{1,0:T(8,128)(2,1)S(1)} %get-tuple-element.12), channel_id=1, source_target_pairs={{4,0},{8,4},{12,8},{14,12},{10,14},{6,10},{2,6},{0,2},{5,1},{9,5},... | collective-permute-start | bytes 589832 | tf_op jit(solution)/shard_map/ppermute | solution.py:73
  71.1 6.7 %collective-permute-start.14 = (bf16[16,6144]{1,0:T(8,128)(2,1)S(1)}, bf16[16,6144]{1,0:T(8,128)(2,1)S(1)}, u32[]{:S(2)}, u32[]{:S(2)}) collective-permute-start(bf16[16,6144]{1,0:T(8,128)(2,1)S(1)} %collective-permute-done.13), channel_id=1, source_target_pairs={{0,4},{4,8},{8,12},{12,14},{14,10},{10,6},{6,2},{2,0},{1,5},{5,9},... | collective-permute-start | bytes 589832 | tf_op jit(solution)/shard_map/ppermute | solution.py:72
  74.6 6.1 %collective-permute-start.18 = (bf16[16,6144]{1,0:T(8,128)(2,1)S(1)}, bf16[16,6144]{1,0:T(8,128)(2,1)S(1)}, u32[]{:S(2)}, u32[]{:S(2)}) collective-permute-start(bf16[16,6144]{1,0:T(8,128)(2,1)S(1)} %collective-permute-done.17), channel_id=1, source_target_pairs={{4,0},{8,4},{12,8},{14,12},{10,14},{6,10},{2,6},{0,2},{5,1},{9,5},... | collective-permute-start | bytes 589832 | tf_op jit(solution)/shard_map/ppermute | solution.py:73
  77.8 9.0 %collective-permute-start.15 = (bf16[16,6144]{1,0:T(8,128)(2,1)S(1)}, bf16[16,6144]{1,0:T(8,128)(2,1)S(1)}, u32[]{:S(2)}, u32[]{:S(2)}) collective-permute-start(bf16[16,6144]{1,0:T(8,128)(2,1)S(1)} %collective-permute-done.14), channel_id=1, source_target_pairs={{0,4},{4,8},{8,12},{12,14},{14,10},{10,6},{6,2},{2,0},{1,5},{5,9},... | collective-permute-start | bytes 589832 | tf_op jit(solution)/shard_map/ppermute | solution.py:72
  80.7 5.7 %collective-permute-start.19 = (bf16[16,6144]{1,0:T(8,128)(2,1)S(1)}, bf16[16,6144]{1,0:T(8,128)(2,1)S(1)}, u32[]{:S(2)}, u32[]{:S(2)}) collective-permute-start(bf16[16,6144]{1,0:T(8,128)(2,1)S(1)} %collective-permute-done.18), channel_id=1, source_target_pairs={{4,0},{8,4},{12,8},{14,12},{10,14},{6,10},{2,6},{0,2},{5,1},{9,5},... | collective-permute-start | bytes 589832 | tf_op jit(solution)/shard_map/ppermute | solution.py:73
  86.4 4.7 %collective-permute-start.20 = (bf16[16,3072]{1,0:T(8,128)(2,1)S(1)}, bf16[16,3072]{1,0:T(8,128)(2,1)S(1)}, u32[]{:S(2)}, u32[]{:S(2)}) collective-permute-start(bf16[16,3072]{1,0:T(8,128)(2,1)S(1)} %slice.98), channel_id=1, source_target_pairs={{4,0},{8,4},{12,8},{14,12},{10,14},{6,10},{2,6},{0,2},{5,1},{9,5},... | collective-permute-start | bytes 294920 | tf_op jit(solution)/shard_map/ppermute | solution.py:79
  86.7 4.8 %collective-permute-start.16 = (bf16[16,3072]{1,0:T(8,128)(2,1)S(1)}, bf16[16,3072]{1,0:T(8,128)(2,1)S(1)}, u32[]{:S(2)}, u32[]{:S(2)}) collective-permute-start(bf16[16,3072]{1,0:T(8,128)(2,1)S(1)} %slice.97), channel_id=1, source_target_pairs={{0,4},{4,8},{8,12},{12,14},{14,10},{10,6},{6,2},{2,0},{1,5},{5,9},... | collective-permute-start | bytes 294920 | tf_op jit(solution)/shard_map/ppermute | solution.py:78
  112.2 15.2 %collective-permute-start.11 = (f32[128,3]{0,1:T(4,128)S(1)}, f32[128,3]{0,1:T(4,128)S(1)}, u32[]{:S(2)}, u32[]{:S(2)}) collective-permute-start(f32[128,3]{0,1:T(4,128)S(1)} %pad_maximum_fusion.2), channel_id=1, source_target_pairs={{0,1},{1,0},{2,3},{3,2},{4,5},{5,4},{6,7},{7,6},{8,9},{9,8},{10,11... | collective-permute-start | bytes 4616 | tf_op jit(solution)/shard_map/ppermute | solution.py:203
  117.5 6.5 %collective-permute-start.22 = (bf16[16,6144]{1,0:T(8,128)(2,1)S(1)}, bf16[16,6144]{1,0:T(8,128)(2,1)S(1)}, u32[]{:S(2)}, u32[]{:S(2)}) collective-permute-start(bf16[16,6144]{1,0:T(8,128)(2,1)S(1)} %pad_maximum_fusion), channel_id=1, source_target_pairs={{4,0},{8,4},{12,8},{14,12},{10,14},{6,10},{2,6},{0,2},{5,1},{9,5},... | collective-permute-start | bytes 589832 | tf_op jit(solution)/shard_map/ppermute | solution.py:109
  119.3 8.1 %collective-permute-start.26 = (bf16[16,6144]{1,0:T(8,128)(2,1)S(1)}, bf16[16,6144]{1,0:T(8,128)(2,1)S(1)}, u32[]{:S(2)}, u32[]{:S(2)}) collective-permute-start(bf16[16,6144]{1,0:T(8,128)(2,1)S(1)} %pad_maximum_fusion.1), channel_id=1, source_target_pairs={{0,4},{4,8},{8,12},{12,14},{14,10},{10,6},{6,2},{2,0},{1,5},{5,9},... | collective-permute-start | bytes 589832 | tf_op jit(solution)/shard_map/ppermute | solution.py:110
  125.0 7.7 %collective-permute-start.23 = (bf16[16,6144]{1,0:T(8,128)(2,1)S(1)}, bf16[16,6144]{1,0:T(8,128)(2,1)S(1)}, u32[]{:S(2)}, u32[]{:S(2)}) collective-permute-start(bf16[16,6144]{1,0:T(8,128)(2,1)S(1)} %fusion.53), channel_id=1, source_target_pairs={{4,0},{8,4},{12,8},{14,12},{10,14},{6,10},{2,6},{0,2},{5,1},{9,5},... | collective-permute-start | bytes 589832 | tf_op jit(solution)/shard_map/ppermute | solution.py:109
  132.8 5.7 %collective-permute-start.27 = (bf16[16,6144]{1,0:T(8,128)(2,1)S(1)}, bf16[16,6144]{1,0:T(8,128)(2,1)S(1)}, u32[]{:S(2)}, u32[]{:S(2)}) collective-permute-start(bf16[16,6144]{1,0:T(8,128)(2,1)S(1)} %get-tuple-element.22), channel_id=1, source_target_pairs={{0,4},{4,8},{8,12},{12,14},{14,10},{10,6},{6,2},{2,0},{1,5},{5,9},... | collective-permute-start | bytes 589832 | tf_op jit(solution)/shard_map/ppermute | solution.py:110
  132.9 5.7 %collective-permute-start.24 = (bf16[16,6144]{1,0:T(8,128)(2,1)S(1)}, bf16[16,6144]{1,0:T(8,128)(2,1)S(1)}, u32[]{:S(2)}, u32[]{:S(2)}) collective-permute-start(bf16[16,6144]{1,0:T(8,128)(2,1)S(1)} %get-tuple-element.21), channel_id=1, source_target_pairs={{4,0},{8,4},{12,8},{14,12},{10,14},{6,10},{2,6},{0,2},{5,1},{9,5},... | collective-permute-start | bytes 589832 | tf_op jit(solution)/shard_map/ppermute | solution.py:109
  138.6 5.7 %collective-permute-start.28 = (bf16[16,6144]{1,0:T(8,128)(2,1)S(1)}, bf16[16,6144]{1,0:T(8,128)(2,1)S(1)}, u32[]{:S(2)}, u32[]{:S(2)}) collective-permute-start(bf16[16,6144]{1,0:T(8,128)(2,1)S(1)} %fusion.52), channel_id=1, source_target_pairs={{0,4},{4,8},{8,12},{12,14},{14,10},{10,6},{6,2},{2,0},{1,5},{5,9},... | collective-permute-start | bytes 589832 | tf_op jit(solution)/shard_map/ppermute | solution.py:110
  (23 other events, 183.8 us)

commit v2 on v1

--- a/solution.py
+++ b/solution.py
@@ -1,10 +1,222 @@
+import functools
+
 import jax
 import jax.numpy as jnp
 from jax import lax
+from jax.experimental import pallas as pl
+from jax.experimental.pallas import tpu as pltpu
 from jax.sharding import PartitionSpec as P
 
 CAP = 16
 CHUNKS = 2
+VMEM = pl.BlockSpec(memory_space=pltpu.VMEM)
+SMEM = pl.BlockSpec(memory_space=pltpu.SMEM)
+HBM = pl.BlockSpec(memory_space=pl.ANY)
+F32, BF16 = (jnp.float32, jnp.bfloat16)
+
+
+def grant(mebibytes):
+    return pltpu.CompilerParams(vmem_limit_bytes=mebibytes * 2**20)
+
+
+def triangle(length):
+    rows = lax.broadcasted_iota(jnp.int32, (length, length), 0)
+    columns = lax.broadcasted_iota(jnp.int32, (length, length), 1)
+    return rows >= columns
+
+
+def as_columns(table):
+    heads, length = table.shape
+    return jnp.concatenate([table, jnp.zeros((length - heads, length), F32)], axis=0).T
+
+
+def state_kernel(odd_ref, log_ref, key_ref, value_ref, run_ref, full_ref, narrow_ref):
+    heads, length = log_ref.shape
+    width = key_ref.shape[1] // heads
+    half = heads // 2
+    running = lax.dot_general(
+        log_ref[...],
+        jnp.where(triangle(length), 1.0, 0.0),
+        (((1,), (1,)), ((), ())),
+        precision=lax.Precision.HIGHEST,
+        preferred_element_type=F32,
+    )
+    run_ref[...] = running
+    rest = as_columns(jnp.exp(running[:, length - 1 :] - running))
+    for head in range(heads):
+        lanes = slice(head * width, (head + 1) * width)
+        scaled = (key_ref[:, lanes].astype(F32) * rest[:, head : head + 1]).astype(BF16)
+        state = lax.dot_general(
+            scaled, value_ref[:, lanes], (((0,), (0,)), ((), ())), preferred_element_type=F32
+        )
+        side = odd_ref[0] if head < half else 1 - odd_ref[0]
+        place = side * half + head % half
+        full_ref[place] = state
+        narrow_ref[place] = state.astype(BF16)
+
+
+def block_state(odd, log_rows, key_rows, value_rows):
+    heads, length = log_rows.shape
+    width = key_rows.shape[1] // heads
+    return pl.pallas_call(
+        state_kernel,
+        out_shape=(
+            jax.ShapeDtypeStruct((heads, length), F32),
+            jax.ShapeDtypeStruct((heads, width, width), F32),
+            jax.ShapeDtypeStruct((heads, width, width), BF16),
+        ),
+        in_specs=[SMEM, VMEM, VMEM, VMEM],
+        out_specs=(VMEM, VMEM, VMEM),
+        compiler_params=grant(16),
+        cost_estimate=pl.CostEstimate(
+            flops=2 * length * width * width * heads,
+            bytes_accessed=4 * length * width * heads + 6 * heads * width * width,
+            transcendentals=0,
+        ),
+    )(odd, log_rows, key_rows, value_rows)
+
+
+def within_kernel(run_ref, query_ref, key_ref, value_ref, out_ref):
+    heads, length = run_ref.shape
+    width = key_ref.shape[1] // heads
+    causal = triangle(length)
+    running = run_ref[...]
+    columns = as_columns(running)
+    for head in range(heads):
+        lanes = slice(head * width, (head + 1) * width)
+        scores = lax.dot_general(
+            query_ref[:, lanes],
+            key_ref[:, lanes],
+            (((1,), (1,)), ((), ())),
+            preferred_element_type=F32,
+        )
+        spread = columns[:, head : head + 1] - running[head : head + 1, :]
+        decay = jnp.exp(jnp.where(causal, spread, 0.0))
+        mixing = jnp.where(causal, scores * decay, 0.0).astype(BF16)
+        out_ref[:, lanes] = jnp.dot(mixing, value_ref[:, lanes], preferred_element_type=F32)
+
+
+def within_block(running, query_rows, key_rows, value_rows):
+    heads, length = running.shape
+    width = key_rows.shape[1] // heads
+    return pl.pallas_call(
+        within_kernel,
+        out_shape=jax.ShapeDtypeStruct(query_rows.shape, F32),
+        in_specs=[VMEM] * 4,
+        out_specs=VMEM,
+        compiler_params=grant(16),
+        cost_estimate=pl.CostEstimate(
+            flops=4 * length * length * width * heads,
+            bytes_accessed=10 * length * width * heads,
+            transcendentals=heads * length * length,
+        ),
+    )(running, query_rows, key_rows, value_rows)
+
+
+def hidden_kernel(odd_ref, run_ref, query_ref, within_ref, residual_ref, gain_ref, table_ref, *refs):
+    states, (hidden_ref, own_ref, other_ref) = (refs[:-3], refs[-3:])
+    heads, length = run_ref.shape
+    width = query_ref.shape[1] // heads
+    half, part = (heads // 2, states[0].shape[0])
+    grown = as_columns(jnp.exp(run_ref[...]))
+    even = odd_ref[0] == 0
+    for head in range(heads):
+        lanes = slice(head * width, (head + 1) * width)
+        chunk, place = divmod(head % half, part)
+        kept, swapped = (states[chunk][place], states[CHUNKS + chunk][place])
+        state = jnp.where(even, kept, swapped) if head < half else jnp.where(even, swapped, kept)
+        carried = jnp.dot(query_ref[:, lanes], state, preferred_element_type=F32)
+        raw = within_ref[:, lanes] + carried * grown[:, head : head + 1]
+        normed = raw * lax.rsqrt(jnp.mean(raw * raw, axis=1, keepdims=True) + 1e-05)
+        hidden_ref[:, lanes] = (
+            residual_ref[:, lanes].astype(F32) + normed * gain_ref[:, lanes]
+        ).astype(BF16)
+    rows = jnp.dot(table_ref[...], hidden_ref[...], preferred_element_type=F32).astype(BF16)
+    own_ref[...] = rows[: own_ref.shape[0]]
+    other_ref[...] = rows[own_ref.shape[0] :]
+
+
+def hidden_rows(odd, running, query_rows, within, residual, gain, table, kept, swapped):
+    heads, length = running.shape
+    capacity = table.shape[0] // 2
+    wide = query_rows.shape[1]
+    return pl.pallas_call(
+        hidden_kernel,
+        out_shape=(
+            jax.ShapeDtypeStruct((length, wide), BF16),
+            jax.ShapeDtypeStruct((capacity, wide), BF16),
+            jax.ShapeDtypeStruct((capacity, wide), BF16),
+        ),
+        in_specs=[SMEM] + [VMEM] * (6 + 2 * CHUNKS),
+        out_specs=(VMEM, VMEM, VMEM),
+        compiler_params=grant(16),
+        cost_estimate=pl.CostEstimate(
+            flops=2 * length * wide * (wide // heads),
+            bytes_accessed=12 * length * wide,
+            transcendentals=0,
+        ),
+    )(odd, running, query_rows, within, residual, gain, table, *kept, *swapped)
+
+
+def expert_kernel(
+    deep, wide, row_ref, gate_ref, up_ref, down_ref, out_ref, gate, up, down, gate_sem, up_sem, down_sem
+):
+    width, units = gate_ref.shape
+    copies = []
+    for step in range(width // deep):
+        rows = pl.ds(step * deep, deep)
+        pair = (
+            pltpu.make_async_copy(gate_ref.at[rows], gate.at[rows], gate_sem.at[step]),
+            pltpu.make_async_copy(up_ref.at[rows], up.at[rows], up_sem.at[step]),
+        )
+        for copy in pair:
+            copy.start()
+        copies.append(pair)
+    downs = []
+    for step in range(width // wide):
+        lanes = pl.ds(step * wide, wide)
+        downs.append(
+            pltpu.make_async_copy(down_ref.at[:, lanes], down.at[:, lanes], down_sem.at[step])
+        )
+        downs[-1].start()
+    gate_part = jnp.zeros((row_ref.shape[0], units), F32)
+    up_part = jnp.zeros((row_ref.shape[0], units), F32)
+    for step, pair in enumerate(copies):
+        lanes = slice(step * deep, (step + 1) * deep)
+        for copy in pair:
+            copy.wait()
+        gate_part += jnp.dot(row_ref[:, lanes], gate[lanes], preferred_element_type=F32)
+        up_part += jnp.dot(row_ref[:, lanes], up[lanes], preferred_element_type=F32)
+    hidden = (jax.nn.silu(gate_part) * up_part).astype(BF16)
+    for step, copy in enumerate(downs):
+        lanes = slice(step * wide, (step + 1) * wide)
+        copy.wait()
+        out_ref[:, lanes] = jnp.dot(hidden, down[:, lanes], preferred_element_type=F32)
+
+
+def expert_rows(segment, gate_weight, up_weight, down_weight):
+    width, units = gate_weight.shape
+    deep = wide = width // 6
+    return pl.pallas_call(
+        functools.partial(expert_kernel, deep, wide),
+        out_shape=jax.ShapeDtypeStruct((segment.shape[0], width), F32),
+        in_specs=[VMEM, HBM, HBM, HBM],
+        out_specs=VMEM,
+        scratch_shapes=[
+            pltpu.VMEM((width, units), BF16),
+            pltpu.VMEM((width, units), BF16),
+            pltpu.VMEM((units, width), BF16),
+            pltpu.SemaphoreType.DMA((width // deep,)),
+            pltpu.SemaphoreType.DMA((width // deep,)),
+            pltpu.SemaphoreType.DMA((width // wide,)),
+        ],
+        compiler_params=grant(48),
+        cost_estimate=pl.CostEstimate(
+            flops=6 * segment.shape[0] * width * units,
+            bytes_accessed=6 * width * units,
+            transcendentals=0,
+        ),
+    )(segment, gate_weight, up_weight, down_weight)
 
 
 def slot_matches(routes, slot_pos, expert, capacity):
@@ -13,47 +225,36 @@
     )
 
 
-def entering_state(local_state, block_total):
-    count, mine = (lax.axis_size("seq"), lax.axis_index("seq"))
-    odd = mine % 2 == 1
+def entering_state(odd, full, narrow, block_total):
+    count = lax.axis_size("seq")
     swap = [(i, i ^ 1) for i in range(count)]
-    heads = local_state.shape[0]
-    half = heads // 2
+    half = full.shape[0] // 2
     part = half // CHUNKS
-    total_other = lax.ppermute(block_total[None], "seq", swap)[0]
-
-    def pick(array, first):
-        return lax.dynamic_slice_in_dim(array, jnp.where(odd, half, 0) + first, part, axis=0)
-
-    def pick_other(array, first):
-        return lax.dynamic_slice_in_dim(array, jnp.where(odd, 0, half) + first, part, axis=0)
-
+    low, high = (block_total[:half], block_total[half:])
+    total_own = jnp.where(odd, high, low)
+    total_other = lax.ppermute(jnp.where(odd, low, high)[None], "seq", swap)[0]
+    even_decay = jnp.exp(jnp.where(odd, total_other, total_own))[:, None, None]
+    odd_decay = jnp.exp(jnp.where(odd, total_own, total_other))[:, None, None]
+    pair_decay = even_decay * odd_decay
     kept, swapped = ([], [])
     for chunk in range(CHUNKS):
-        own = pick(local_state, chunk * part)
+        here = slice(chunk * part, (chunk + 1) * part)
+        own = full[here]
         arrived = lax.ppermute(
-            pick_other(local_state, chunk * part).astype(jnp.bfloat16), "seq", swap
-        ).astype(jnp.float32)
-        own_decay = jnp.exp(pick(block_total, chunk * part))[:, None, None]
-        other_decay = jnp.exp(pick(total_other, chunk * part))[:, None, None]
+            narrow[half + chunk * part : half + (chunk + 1) * part], "seq", swap
+        ).astype(F32)
         even_state = jnp.where(odd, arrived, own)
         odd_state = jnp.where(odd, own, arrived)
-        even_decay = jnp.where(odd, other_decay, own_decay)
-        odd_decay = jnp.where(odd, own_decay, other_decay)
-        pair_state = odd_decay * even_state + odd_state
-        pair_decay = even_decay * odd_decay
+        pair_state = odd_decay[here] * even_state + odd_state
         before = jnp.zeros_like(own)
         for hop in range(count // 2 - 1):
             pairs = [(2 * hop + k, 2 * hop + 2 + k) for k in range(2)]
-            sent = (pair_decay * before + pair_state).astype(jnp.bfloat16)
-            before = before + lax.ppermute(sent, "seq", pairs).astype(jnp.float32)
-        between = even_decay * before + even_state
-        kept.append(jnp.where(odd, between, before).astype(jnp.bfloat16))
-        swapped.append(
-            lax.ppermute(jnp.where(odd, before, between).astype(jnp.bfloat16), "seq", swap)
-        )
-    kept, swapped = (jnp.concatenate(kept), jnp.concatenate(swapped))
-    return jnp.where(odd, jnp.concatenate([swapped, kept]), jnp.concatenate([kept, swapped]))
+            sent = (pair_decay[here] * before + pair_state).astype(BF16)
+            before = before + lax.ppermute(sent, "seq", pairs).astype(F32)
+        between = even_decay[here] * before + even_state
+        kept.append(jnp.where(odd, between, before).astype(BF16))
+        swapped.append(lax.ppermute(jnp.where(odd, before, between).astype(BF16), "seq", swap))
+    return (kept, swapped)
 
 
 def ring_pairs(count):
@@ -129,46 +330,21 @@
     down_weight,
 ):
     length, width = queries.shape
-    heads_here = log_decay.shape[1]
-    head_width = width // heads_here
     core = lax.axis_index("exp")
     exchange = [(0, 1), (1, 0)]
-    query_heads = queries.reshape(length, heads_here, head_width)
-    key_heads = key_rows.reshape(length, heads_here, head_width)
-    value_heads = values.reshape(length, heads_here, head_width)
-    running = jnp.cumsum(log_decay, axis=0)
-    block_total = running[-1]
-    scaled = (
-        key_heads.astype(jnp.float32) * jnp.exp(block_total[None, :] - running)[:, :, None]
-    ).astype(jnp.bfloat16)
-    local_state = jnp.einsum(
-        "shd,she->hde", scaled, value_heads, preferred_element_type=jnp.float32
-    )
-    entering = entering_state(local_state, block_total)
-    scores = jnp.einsum("thd,shd->hts", query_heads, key_heads, preferred_element_type=jnp.float32)
-    spread = running.T[:, :, None] - running.T[:, None, :]
-    causal = (jnp.arange(length)[:, None] >= jnp.arange(length)[None, :])[None]
-    mixing = jnp.where(causal, scores * jnp.exp(jnp.where(causal, spread, 0.0)), 0.0).astype(
-        jnp.bfloat16
-    )
-    within_part = jnp.einsum(
-        "hts,shd->thd", mixing, value_heads, preferred_element_type=jnp.float32
-    )
-    carried_part = jnp.einsum(
-        "thd,hde->the", query_heads, entering, preferred_element_type=jnp.float32
-    )
-    raw = within_part + carried_part * jnp.exp(running)[:, :, None]
-    normed = raw * lax.rsqrt(jnp.mean(raw * raw, axis=2, keepdims=True) + 1e-05)
-    hidden_half = (residual.astype(jnp.float32) + normed.reshape(length, -1) * attn_gain).astype(
-        jnp.bfloat16
-    )
+    odd = lax.axis_index("seq") % 2
+    odd_scalar = odd.astype(jnp.int32)[None]
+    running, full, narrow = block_state(odd_scalar, log_decay.T, key_rows, values)
+    kept, swapped = entering_state(odd == 1, full, narrow, running[:, -1])
+    within = within_block(running, queries, key_rows, values)
 
     matches = [slot_matches(routes, slot_pos, expert, CAP) for expert in range(2)]
-    tables = [jnp.any(match, axis=1).astype(jnp.bfloat16).T for match in matches]
-    table = jnp.concatenate(tables, axis=0)
-    rows = jnp.dot(table, hidden_half, preferred_element_type=jnp.float32).astype(jnp.bfloat16)
-    rows_own = jnp.where(core == 0, rows[:CAP], rows[CAP:])
-    rows_other = lax.ppermute(jnp.where(core == 0, rows[CAP:], rows[:CAP]), "exp", exchange)
+    tables = [jnp.any(match, axis=1).astype(BF16).T for match in matches]
+    table = jnp.where(core == 0, jnp.concatenate(tables), jnp.concatenate(tables[::-1]))
+    hidden_half, rows_own, rows_sent = hidden_rows(
+        odd_scalar, running, queries, within, residual, attn_gain[None], table, kept, swapped
+    )
+    rows_other = lax.ppermute(rows_sent, "exp", exchange)
     rows_whole = jnp.where(
         core == 0,
         jnp.concatenate([rows_own, rows_other], axis=1),
@@ -178,10 +354,7 @@
     buffer = (rows_whole * rows_inverse * moe_gain).astype(jnp.bfloat16)
 
     segment = ring_gather(buffer)
-    gate_part = jnp.dot(segment, gate_weight[0], preferred_element_type=jnp.float32)
-    up_part = jnp.dot(segment, up_weight[0], preferred_element_type=jnp.float32)
-    hidden_rows = (jax.nn.silu(gate_part) * up_part).astype(jnp.bfloat16)
-    partial = jnp.dot(hidden_rows, down_weight[0], preferred_element_type=jnp.float32)
+    partial = expert_rows(segment, gate_weight[0], up_weight[0], down_weight[0])
     expert_out = ring_scatter(partial, CAP).astype(jnp.bfloat16)
 
     hidden_float = hidden_half.astype(jnp.float32)

time: 148 us -> 134 us (0.905)
  matrix products: 28.3 us -> 2.77 us
  Pallas kernels: 0 us -> 20 us
  other arithmetic: 11 us -> 4.74 us
  local copies, waits for them, and re-layouts: 8.44 us -> 3.93 us
  starting transfers between devices: 42.2 us -> 45.6 us
    dot_general x6 -> x0, matrix products: 24.6 us -> none  [the longest x1 12.1 us: shards(): jnp.dot(hidden_rows, down_weight[0], preferred_element_type=jnp.float32)]
    pallas_call x0 -> x4, Pallas kernels: none -> 20 us  [the longest x1 11.7 us: expert_rows(): pl.pallas_call(functools.partial(expert_kernel, deep, wide), out_shape=ja...]
    ppermute x12, waiting for transfers between devices: 17.9 us -> 12.7 us  [the longest x6 6.18 us: entering_state(): before = before + lax.ppermute(sent, 'seq', pairs).astype(F32)]
    reshape x2 -> x0, local copies, waits for them, and re-layouts: 3.14 us -> none  [the longest x1 1.64 us: shards(): normed.reshape(length, -1) * attn_gain]
    ppermute x3, starting transfers between devices: 10.6 us -> 13.2 us  [ring_gather(): moving_right = lax.ppermute(moving_right, 'seq', right)]
    unnamed x40 -> x43, local copies, waits for them, and re-layouts: 1.68 us -> 3.7 us
    ppermute x3, waiting for transfers between devices: 5.66 us -> 7.62 us  [ring_gather(): moving_right = lax.ppermute(moving_right, 'seq', right)]
    reduce_sum x1, other arithmetic: 1.79 us -> 0.24 us  [shards(): square_half = jnp.sum(hidden_float * hidden_float, axis=1, keepdims=True)]
  transfers between devices with their start and end apart: 30 -> 30, of which waited for: 21 -> 19; matrix products, arithmetic and copies ran while one was open for 8% -> 3% of each run, Pallas kernels for 0% -> 3%
where the time goes in v2:
time: 134 us; the launch traced here: 133 us
  waiting for transfers between devices  55.7 us (42%)
  starting transfers between devices  45.6 us (34%)
  Pallas kernels  20 us (15%)
  other arithmetic  4.74 us (4%)
  local copies, waits for them, and re-layouts  3.93 us (3%)
  matrix products  2.77 us (2%)
    ppermute x6, starting transfers between devices, entering_state(): before = before + lax.ppermute(sent, 'seq', pairs).astype(F32)  14.5 us
    ppermute x3, starting transfers between devices, ring_gather(): moving_right = lax.ppermute(moving_right, 'seq', right)  13.2 us
    pallas_call x1, Pallas kernels, expert_rows(): pl.pallas_call(functools.partial(expert_kernel, deep, wide), out_shape=ja...  11.7 us
    ppermute x3, waiting for transfers between devices, ring_scatter(): lax.ppermute(to_left.astype(jnp.bfloat16), 'seq', left).astype(jnp.float32)  10.9 us
    ppermute x3, waiting for transfers between devices, ring_scatter(): lax.ppermute(to_right.astype(jnp.bfloat16), 'seq', right)  9.19 us
    ppermute x3, waiting for transfers between devices, ring_gather(): moving_right = lax.ppermute(moving_right, 'seq', right)  7.62 us
    ppermute x3, waiting for transfers between devices, ring_gather(): moving_left = lax.ppermute(moving_left, 'seq', left)  7.3 us
    ppermute x6, waiting for transfers between devices, entering_state(): before = before + lax.ppermute(sent, 'seq', pairs).astype(F32)  6.18 us
  transfers between devices with their start and end apart: 30, of which 19 were waited for; matrix products, arithmetic and copies ran while one was open for 3% of the time, Pallas kernels for 3%

profile of v2, /device:TPU:0, one launch (start us, length us, event | category | flops | bytes accessed | tf_op | source)
XLA Modules:
  0.0 133.2 jit_solution(2042027907508219445)
XLA Ops:
  5.0 3.0 %collective-permute-start = (f32[1,12]{1,0:T(1,128)S(1)}, f32[1,12]{1,0:T(1,128)S(1)}, u32[]{:S(2)}, u32[]{:S(2)}) collective-permute-start(f32[1,12]{1,0:T(1,128)S(1)} %bitcast.36), channel_id=1, source_target_pairs={{0,2},{2,0},{4,6},{6,4},{8,10},{10,8},{12,14},{14,12},{1,3},{3,1},... | collective-permute-start | bytes 152 | tf_op jit(solution)/shard_map/ppermute | solution.py:235
  8.1 2.0 %collective-permute-start.1 = (bf16[6,128,128]{2,1,0:T(8,128)(2,1)S(1)}, bf16[6,128,128]{2,1,0:T(8,128)(2,1)S(1)}, u32[]{:S(2)}, u32[]{:S(2)}) collective-permute-start(bf16[6,128,128]{2,1,0:T(8,128)(2,1)S(1)} %get-tuple-element.41), channel_id=1, source_target_pairs={{0,2},{2,0},{4,6},{6,4},{8,10},{10,8},{12,14},{14,12},{1,3},{3,1},... | collective-permute-start | bytes 589832 | tf_op jit(solution)/shard_map/ppermute | solution.py:243
  10.2 5.7 %collective-permute-done.5 = bf16[6,128,128]{2,1,0:T(8,128)(2,1)S(1)} collective-permute-done((bf16[6,128,128]{2,1,0:T(8,128)(2,1)S(1)}, bf16[6,128,128]{2,1,0:T(8,128)(2,1)S(1)}, u32[]{:S(2)}, u32[]{:S(2)}) %collective-permute-start.5) | collective-permute-done | bytes 196640 | tf_op jit(solution)/shard_map/ppermute | solution.py:243
  16.1 3.5 %collective-permute-start.6 = (bf16[6,128,128]{2,1,0:T(8,128)(2,1)S(1)}, bf16[6,128,128]{2,1,0:T(8,128)(2,1)S(1)}, u32[]{:S(2)}, u32[]{:S(2)}) collective-permute-start(bf16[6,128,128]{2,1,0:T(8,128)(2,1)S(1)} %add_convert_fusion.1), channel_id=1, source_target_pairs={{0,4},{2,6},{1,5},{3,7},{16,20},{18,22},{17,21},{19,23}} | collective-permute-start | bytes 589832 | tf_op jit(solution)/shard_map/ppermute | solution.py:253
  19.7 3.1 %collective-permute-done.6 = bf16[6,128,128]{2,1,0:T(8,128)(2,1)S(1)} collective-permute-done((bf16[6,128,128]{2,1,0:T(8,128)(2,1)S(1)}, bf16[6,128,128]{2,1,0:T(8,128)(2,1)S(1)}, u32[]{:S(2)}, u32[]{:S(2)}) %collective-permute-start.6) | collective-permute-done | bytes 196640 | tf_op jit(solution)/shard_map/ppermute | solution.py:253
  24.6 8.2 %collective-permute-start.2 = (bf16[6,128,128]{2,1,0:T(8,128)(2,1)S(1)}, bf16[6,128,128]{2,1,0:T(8,128)(2,1)S(1)}, u32[]{:S(2)}, u32[]{:S(2)}) collective-permute-start(bf16[6,128,128]{2,1,0:T(8,128)(2,1)S(1)} %get-tuple-element.39), channel_id=1, source_target_pairs={{0,4},{2,6},{1,5},{3,7},{16,20},{18,22},{17,21},{19,23}} | collective-permute-start | bytes 589832 | tf_op jit(solution)/shard_map/ppermute | solution.py:253
  32.9 3.1 %collective-permute-done.2 = bf16[6,128,128]{2,1,0:T(8,128)(2,1)S(1)} collective-permute-done((bf16[6,128,128]{2,1,0:T(8,128)(2,1)S(1)}, bf16[6,128,128]{2,1,0:T(8,128)(2,1)S(1)}, u32[]{:S(2)}, u32[]{:S(2)}) %collective-permute-start.2) | collective-permute-done | bytes 196640 | tf_op jit(solution)/shard_map/ppermute | solution.py:253
  42.8 3.9 %shard_map.128.within_ref = f32[128,3072]{1,0:T(8,128)S(1)} custom-call(f32[24,128]{1,0:T(8,128)S(1)} %get-tuple-element.11.run_ref, bf16[128,3072]{1,0:T(8,128)(2,1)S(1)} %copy-done.5, bf16[128,3072]{1,0:T(8,128)(2,1)S(1)} %copy-done.2, bf16[128,3072]{1,0:T(8,128)(2,1)S(1)} %copy-done.4), custom_call_target="tpu_custom_call" | custom-call | flops 201326592 | bytes 3932160 | tf_op jit(solution)/shard_map/pallas_call | solution.py:102
  47.3 2.7 %shard_map.129 = (bf16[128,3072]{1,0:T(8,128)(2,1)S(1)}, bf16[16,3072]{1,0:T(8,128)(2,1)S(1)}, bf16[16,3072]{1,0:T(8,128)(2,1)S(1)}) custom-call(s32[1]{0:T(128)} %bitcast.odd_ref, f32[24,128]{1,0:T(8,128)S(1)} %get-tuple-element.11.run_ref, bf16[128,3072]{1,0:T(8,128)(2,1)S(1)} %copy-done.5, f32[128,3072]{1,0:T(8,128)S(1)} %shard_map.128.within_ref, ...), custom_call_target="tpu_custom_call" | custom-call | flops 100663296 | bytes 4718592 | tf_op jit(solution)/shard_map/pallas_call | solution.py:143
  51.6 6.3 %collective-permute-start.13 = (bf16[16,6144]{1,0:T(8,128)(2,1)S(1)}, bf16[16,6144]{1,0:T(8,128)(2,1)S(1)}, u32[]{:S(2)}, u32[]{:S(2)}) collective-permute-start(bf16[16,6144]{1,0:T(8,128)(2,1)S(1)} %get-tuple-element.24), channel_id=1, source_target_pairs={{0,4},{4,8},{8,12},{12,14},{14,10},{10,6},{6,2},{2,0},{1,5},{5,9},... | collective-permute-start | bytes 589832 | tf_op jit(solution)/shard_map/ppermute | solution.py:273
  58.2 4.3 %collective-permute-done.13 = bf16[16,6144]{1,0:T(8,128)(2,1)S(1)} collective-permute-done((bf16[16,6144]{1,0:T(8,128)(2,1)S(1)}, bf16[16,6144]{1,0:T(8,128)(2,1)S(1)}, u32[]{:S(2)}, u32[]{:S(2)}) %collective-permute-start.13) | collective-permute-done | bytes 196640 | tf_op jit(solution)/shard_map/ppermute | solution.py:273
  62.5 4.4 %collective-permute-start.14 = (bf16[16,6144]{1,0:T(8,128)(2,1)S(1)}, bf16[16,6144]{1,0:T(8,128)(2,1)S(1)}, u32[]{:S(2)}, u32[]{:S(2)}) collective-permute-start(bf16[16,6144]{1,0:T(8,128)(2,1)S(1)} %collective-permute-done.13), channel_id=1, source_target_pairs={{0,4},{4,8},{8,12},{12,14},{14,10},{10,6},{6,2},{2,0},{1,5},{5,9},... | collective-permute-start | bytes 589832 | tf_op jit(solution)/shard_map/ppermute | solution.py:273
  67.4 3.3 %collective-permute-done.14 = bf16[16,6144]{1,0:T(8,128)(2,1)S(1)} collective-permute-done((bf16[16,6144]{1,0:T(8,128)(2,1)S(1)}, bf16[16,6144]{1,0:T(8,128)(2,1)S(1)}, u32[]{:S(2)}, u32[]{:S(2)}) %collective-permute-start.14) | collective-permute-done | bytes 196640 | tf_op jit(solution)/shard_map/ppermute | solution.py:273
  70.7 2.5 %collective-permute-start.15 = (bf16[16,6144]{1,0:T(8,128)(2,1)S(1)}, bf16[16,6144]{1,0:T(8,128)(2,1)S(1)}, u32[]{:S(2)}, u32[]{:S(2)}) collective-permute-start(bf16[16,6144]{1,0:T(8,128)(2,1)S(1)} %collective-permute-done.14), channel_id=1, source_target_pairs={{0,4},{4,8},{8,12},{12,14},{14,10},{10,6},{6,2},{2,0},{1,5},{5,9},... | collective-permute-start | bytes 589832 | tf_op jit(solution)/shard_map/ppermute | solution.py:273
  74.4 5.6 %collective-permute-done.19 = bf16[16,6144]{1,0:T(8,128)(2,1)S(1)} collective-permute-done((bf16[16,6144]{1,0:T(8,128)(2,1)S(1)}, bf16[16,6144]{1,0:T(8,128)(2,1)S(1)}, u32[]{:S(2)}, u32[]{:S(2)}) %collective-permute-start.19) | collective-permute-done | bytes 196640 | tf_op jit(solution)/shard_map/ppermute | solution.py:274
  80.4 2.0 %collective-permute-start.16 = (bf16[16,3072]{1,0:T(8,128)(2,1)S(1)}, bf16[16,3072]{1,0:T(8,128)(2,1)S(1)}, u32[]{:S(2)}, u32[]{:S(2)}) collective-permute-start(bf16[16,3072]{1,0:T(8,128)(2,1)S(1)} %slice.141), channel_id=1, source_target_pairs={{0,4},{4,8},{8,12},{12,14},{14,10},{10,6},{6,2},{2,0},{1,5},{5,9},... | collective-permute-start | bytes 294920 | tf_op jit(solution)/shard_map/ppermute | solution.py:279
  82.4 2.3 %collective-permute-done.20 = bf16[16,3072]{1,0:T(8,128)(2,1)S(1)} collective-permute-done((bf16[16,3072]{1,0:T(8,128)(2,1)S(1)}, bf16[16,3072]{1,0:T(8,128)(2,1)S(1)}, u32[]{:S(2)}, u32[]{:S(2)}) %collective-permute-start.20) | collective-permute-done | bytes 98336 | tf_op jit(solution)/shard_map/ppermute | solution.py:280
  85.4 11.7 %shard_map.130 = f32[128,6144]{1,0:T(8,128)S(1)} custom-call(bf16[128,6144]{1,0:T(8,128)(2,1)S(1)} %constant_dynamic-update-slice_fusion.row_ref, bf16[6144,768]{1,0:T(8,128)(2,1)} %bitcast.31, bf16[6144,768]{1,0:T(8,128)(2,1)} %bitcast.32, bf16[768,6144]{1,0:T(8,128)(2,1)} %bitcast.33), custom_call_target="tpu_custom_call" | custom-call | flops 3623878656 | bytes 28311552 | tf_op jit(solution)/shard_map/pallas_call | solution.py:200
  99.4 2.6 %collective-permute-done.21 = bf16[16,3072]{1,0:T(8,128)(2,1)S(1)} collective-permute-done((bf16[16,3072]{1,0:T(8,128)(2,1)S(1)}, bf16[16,3072]{1,0:T(8,128)(2,1)S(1)}, u32[]{:S(2)}, u32[]{:S(2)}) %collective-permute-start.21) | collective-permute-done | bytes 98336 | tf_op jit(solution)/shard_map/ppermute | solution.py:297
  105.6 5.4 %collective-permute-done.22 = bf16[16,6144]{1,0:T(8,128)(2,1)S(1)} collective-permute-done((bf16[16,6144]{1,0:T(8,128)(2,1)S(1)}, bf16[16,6144]{1,0:T(8,128)(2,1)S(1)}, u32[]{:S(2)}, u32[]{:S(2)}) %collective-permute-start.22) | collective-permute-done | bytes 196640 | tf_op jit(solution)/shard_map/ppermute | solution.py:310
  113.0 5.5 %collective-permute-done.23 = bf16[16,6144]{1,0:T(8,128)(2,1)S(1)} collective-permute-done((bf16[16,6144]{1,0:T(8,128)(2,1)S(1)}, bf16[16,6144]{1,0:T(8,128)(2,1)S(1)}, u32[]{:S(2)}, u32[]{:S(2)}) %collective-permute-start.23) | collective-permute-done | bytes 196640 | tf_op jit(solution)/shard_map/ppermute | solution.py:310
  118.7 2.1 %collective-permute-start.24 = (bf16[16,6144]{1,0:T(8,128)(2,1)S(1)}, bf16[16,6144]{1,0:T(8,128)(2,1)S(1)}, u32[]{:S(2)}, u32[]{:S(2)}) collective-permute-start(bf16[16,6144]{1,0:T(8,128)(2,1)S(1)} %get-tuple-element.25), channel_id=1, source_target_pairs={{4,0},{8,4},{12,8},{14,12},{10,14},{6,10},{2,6},{0,2},{5,1},{9,5},... | collective-permute-start | bytes 589832 | tf_op jit(solution)/shard_map/ppermute | solution.py:310
  120.7 3.6 %collective-permute-done.27 = bf16[16,6144]{1,0:T(8,128)(2,1)S(1)} collective-permute-done((bf16[16,6144]{1,0:T(8,128)(2,1)S(1)}, bf16[16,6144]{1,0:T(8,128)(2,1)S(1)}, u32[]{:S(2)}, u32[]{:S(2)}) %collective-permute-start.27) | collective-permute-done | bytes 196640 | tf_op jit(solution)/shard_map/ppermute | solution.py:311
  124.4 5.6 %collective-permute-done.28 = bf16[16,6144]{1,0:T(8,128)(2,1)S(1)} collective-permute-done((bf16[16,6144]{1,0:T(8,128)(2,1)S(1)}, bf16[16,6144]{1,0:T(8,128)(2,1)S(1)}, u32[]{:S(2)}, u32[]{:S(2)}) %collective-permute-start.28) | collective-permute-done | bytes 196640 | tf_op jit(solution)/shard_map/ppermute | solution.py:311
  (129 shorter events, 30.4 us)
Async XLA Ops:
  5.0 5.2 %collective-permute-start = (f32[1,12]{1,0:T(1,128)S(1)}, f32[1,12]{1,0:T(1,128)S(1)}, u32[]{:S(2)}, u32[]{:S(2)}) collective-permute-start(f32[1,12]{1,0:T(1,128)S(1)} %bitcast.36), channel_id=1, source_target_pairs={{0,2},{2,0},{4,6},{6,4},{8,10},{10,8},{12,14},{14,12},{1,3},{3,1},... | collective-permute-start | bytes 152 | tf_op jit(solution)/shard_map/ppermute | solution.py:235
  8.0 7.9 %collective-permute-start.5 = (bf16[6,128,128]{2,1,0:T(8,128)(2,1)S(1)}, bf16[6,128,128]{2,1,0:T(8,128)(2,1)S(1)}, u32[]{:S(2)}, u32[]{:S(2)}) collective-permute-start(bf16[6,128,128]{2,1,0:T(8,128)(2,1)S(1)} %get-tuple-element.40), channel_id=1, source_target_pairs={{0,2},{2,0},{4,6},{6,4},{8,10},{10,8},{12,14},{14,12},{1,3},{3,1},... | collective-permute-start | bytes 589832 | tf_op jit(solution)/shard_map/ppermute | solution.py:243
  8.1 15.5 %collective-permute-start.1 = (bf16[6,128,128]{2,1,0:T(8,128)(2,1)S(1)}, bf16[6,128,128]{2,1,0:T(8,128)(2,1)S(1)}, u32[]{:S(2)}, u32[]{:S(2)}) collective-permute-start(bf16[6,128,128]{2,1,0:T(8,128)(2,1)S(1)} %get-tuple-element.41), channel_id=1, source_target_pairs={{0,2},{2,0},{4,6},{6,4},{8,10},{10,8},{12,14},{14,12},{1,3},{3,1},... | collective-permute-start | bytes 589832 | tf_op jit(solution)/shard_map/ppermute | solution.py:243
  16.1 6.7 %collective-permute-start.6 = (bf16[6,128,128]{2,1,0:T(8,128)(2,1)S(1)}, bf16[6,128,128]{2,1,0:T(8,128)(2,1)S(1)}, u32[]{:S(2)}, u32[]{:S(2)}) collective-permute-start(bf16[6,128,128]{2,1,0:T(8,128)(2,1)S(1)} %add_convert_fusion.1), channel_id=1, source_target_pairs={{0,4},{2,6},{1,5},{3,7},{16,20},{18,22},{17,21},{19,23}} | collective-permute-start | bytes 589832 | tf_op jit(solution)/shard_map/ppermute | solution.py:253
  24.0 8.9 %collective-permute-start.8 = (bf16[6,128,128]{2,1,0:T(8,128)(2,1)S(1)}, bf16[6,128,128]{2,1,0:T(8,128)(2,1)S(1)}, u32[]{:S(2)}, u32[]{:S(2)}) collective-permute-start(bf16[6,128,128]{2,1,0:T(8,128)(2,1)S(1)} %get-tuple-element.38), channel_id=1, source_target_pairs={{8,12},{10,14},{9,13},{11,15},{24,28},{26,30},{25,29},{27,31}} | collective-permute-start | bytes 589832 | tf_op jit(solution)/shard_map/ppermute | solution.py:253
  24.6 11.3 %collective-permute-start.2 = (bf16[6,128,128]{2,1,0:T(8,128)(2,1)S(1)}, bf16[6,128,128]{2,1,0:T(8,128)(2,1)S(1)}, u32[]{:S(2)}, u32[]{:S(2)}) collective-permute-start(bf16[6,128,128]{2,1,0:T(8,128)(2,1)S(1)} %get-tuple-element.39), channel_id=1, source_target_pairs={{0,4},{2,6},{1,5},{3,7},{16,20},{18,22},{17,21},{19,23}} | collective-permute-start | bytes 589832 | tf_op jit(solution)/shard_map/ppermute | solution.py:253
  39.3 7.4 %collective-permute-start.10 = (bf16[6,128,128]{2,1,0:T(8,128)(2,1)}, bf16[6,128,128]{2,1,0:T(8,128)(2,1)S(1)}, u32[]{:S(2)}, u32[]{:S(2)}) collective-permute-start(bf16[6,128,128]{2,1,0:T(8,128)(2,1)} %get-tuple-element.29), channel_id=1, source_target_pairs={{0,2},{2,0},{4,6},{6,4},{8,10},{10,8},{12,14},{14,12},{1,3},{3,1},... | collective-permute-start | bytes 589832 | tf_op jit(solution)/shard_map/ppermute | solution.py:256
  40.7 6.6 %collective-permute-start.9 = (bf16[6,128,128]{2,1,0:T(8,128)(2,1)}, bf16[6,128,128]{2,1,0:T(8,128)(2,1)S(1)}, u32[]{:S(2)}, u32[]{:S(2)}) collective-permute-start(bf16[6,128,128]{2,1,0:T(8,128)(2,1)} %get-tuple-element.31), channel_id=1, source_target_pairs={{0,2},{2,0},{4,6},{6,4},{8,10},{10,8},{12,14},{14,12},{1,3},{3,1},... | collective-permute-start | bytes 589832 | tf_op jit(solution)/shard_map/ppermute | solution.py:256
  51.6 10.9 %collective-permute-start.13 = (bf16[16,6144]{1,0:T(8,128)(2,1)S(1)}, bf16[16,6144]{1,0:T(8,128)(2,1)S(1)}, u32[]{:S(2)}, u32[]{:S(2)}) collective-permute-start(bf16[16,6144]{1,0:T(8,128)(2,1)S(1)} %get-tuple-element.24), channel_id=1, source_target_pairs={{0,4},{4,8},{8,12},{12,14},{14,10},{10,6},{6,2},{2,0},{1,5},{5,9},... | collective-permute-start | bytes 589832 | tf_op jit(solution)/shard_map/ppermute | solution.py:273
  57.9 9.5 %collective-permute-start.17 = (bf16[16,6144]{1,0:T(8,128)(2,1)S(1)}, bf16[16,6144]{1,0:T(8,128)(2,1)S(1)}, u32[]{:S(2)}, u32[]{:S(2)}) collective-permute-start(bf16[16,6144]{1,0:T(8,128)(2,1)S(1)} %get-tuple-element.24), channel_id=1, source_target_pairs={{4,0},{8,4},{12,8},{14,12},{10,14},{6,10},{2,6},{0,2},{5,1},{9,5},... | collective-permute-start | bytes 589832 | tf_op jit(solution)/shard_map/ppermute | solution.py:274
  62.5 8.2 %collective-permute-start.14 = (bf16[16,6144]{1,0:T(8,128)(2,1)S(1)}, bf16[16,6144]{1,0:T(8,128)(2,1)S(1)}, u32[]{:S(2)}, u32[]{:S(2)}) collective-permute-start(bf16[16,6144]{1,0:T(8,128)(2,1)S(1)} %collective-permute-done.13), channel_id=1, source_target_pairs={{0,4},{4,8},{8,12},{12,14},{14,10},{10,6},{6,2},{2,0},{1,5},{5,9},... | collective-permute-start | bytes 589832 | tf_op jit(solution)/shard_map/ppermute | solution.py:273
  67.4 7.0 %collective-permute-start.18 = (bf16[16,6144]{1,0:T(8,128)(2,1)S(1)}, bf16[16,6144]{1,0:T(8,128)(2,1)S(1)}, u32[]{:S(2)}, u32[]{:S(2)}) collective-permute-start(bf16[16,6144]{1,0:T(8,128)(2,1)S(1)} %collective-permute-done.17), channel_id=1, source_target_pairs={{4,0},{8,4},{12,8},{14,12},{10,14},{6,10},{2,6},{0,2},{5,1},{9,5},... | collective-permute-start | bytes 589832 | tf_op jit(solution)/shard_map/ppermute | solution.py:274
  70.7 9.7 %collective-permute-start.15 = (bf16[16,6144]{1,0:T(8,128)(2,1)S(1)}, bf16[16,6144]{1,0:T(8,128)(2,1)S(1)}, u32[]{:S(2)}, u32[]{:S(2)}) collective-permute-start(bf16[16,6144]{1,0:T(8,128)(2,1)S(1)} %collective-permute-done.14), channel_id=1, source_target_pairs={{0,4},{4,8},{8,12},{12,14},{14,10},{10,6},{6,2},{2,0},{1,5},{5,9},... | collective-permute-start | bytes 589832 | tf_op jit(solution)/shard_map/ppermute | solution.py:273
  74.4 5.7 %collective-permute-start.19 = (bf16[16,6144]{1,0:T(8,128)(2,1)S(1)}, bf16[16,6144]{1,0:T(8,128)(2,1)S(1)}, u32[]{:S(2)}, u32[]{:S(2)}) collective-permute-start(bf16[16,6144]{1,0:T(8,128)(2,1)S(1)} %collective-permute-done.18), channel_id=1, source_target_pairs={{4,0},{8,4},{12,8},{14,12},{10,14},{6,10},{2,6},{0,2},{5,1},{9,5},... | collective-permute-start | bytes 589832 | tf_op jit(solution)/shard_map/ppermute | solution.py:274
  80.1 4.7 %collective-permute-start.20 = (bf16[16,3072]{1,0:T(8,128)(2,1)S(1)}, bf16[16,3072]{1,0:T(8,128)(2,1)S(1)}, u32[]{:S(2)}, u32[]{:S(2)}) collective-permute-start(bf16[16,3072]{1,0:T(8,128)(2,1)S(1)} %slice.142), channel_id=1, source_target_pairs={{4,0},{8,4},{12,8},{14,12},{10,14},{6,10},{2,6},{0,2},{5,1},{9,5},... | collective-permute-start | bytes 294920 | tf_op jit(solution)/shard_map/ppermute | solution.py:280
  80.4 4.8 %collective-permute-start.16 = (bf16[16,3072]{1,0:T(8,128)(2,1)S(1)}, bf16[16,3072]{1,0:T(8,128)(2,1)S(1)}, u32[]{:S(2)}, u32[]{:S(2)}) collective-permute-start(bf16[16,3072]{1,0:T(8,128)(2,1)S(1)} %slice.141), channel_id=1, source_target_pairs={{0,4},{4,8},{8,12},{12,14},{14,10},{10,6},{6,2},{2,0},{1,5},{5,9},... | collective-permute-start | bytes 294920 | tf_op jit(solution)/shard_map/ppermute | solution.py:279
  97.3 4.7 %collective-permute-start.21 = (bf16[16,3072]{1,0:T(8,128)(2,1)S(1)}, bf16[16,3072]{1,0:T(8,128)(2,1)S(1)}, u32[]{:S(2)}, u32[]{:S(2)}) collective-permute-start(bf16[16,3072]{1,0:T(8,128)(2,1)S(1)} %get-tuple-element.33), channel_id=1, source_target_pairs={{4,0},{8,4},{12,8},{14,12},{10,14},{6,10},{2,6},{0,2},{5,1},{9,5},... | collective-permute-start | bytes 294920 | tf_op jit(solution)/shard_map/ppermute | solution.py:297
  99.4 13.6 %collective-permute-start.11 = (f32[128,3]{0,1:T(4,128)S(1)}, f32[128,3]{0,1:T(4,128)S(1)}, u32[]{:S(2)}, u32[]{:S(2)}) collective-permute-start(f32[128,3]{0,1:T(4,128)S(1)} %pad_maximum_fusion.2), channel_id=1, source_target_pairs={{0,1},{1,0},{2,3},{3,2},{4,5},{5,4},{6,7},{7,6},{8,9},{9,8},{10,11... | collective-permute-start | bytes 4616 | tf_op jit(solution)/shard_map/ppermute | solution.py:376
  103.5 7.6 %collective-permute-start.22 = (bf16[16,6144]{1,0:T(8,128)(2,1)S(1)}, bf16[16,6144]{1,0:T(8,128)(2,1)S(1)}, u32[]{:S(2)}, u32[]{:S(2)}) collective-permute-start(bf16[16,6144]{1,0:T(8,128)(2,1)S(1)} %pad_maximum_fusion), channel_id=1, source_target_pairs={{4,0},{8,4},{12,8},{14,12},{10,14},{6,10},{2,6},{0,2},{5,1},{9,5},... | collective-permute-start | bytes 589832 | tf_op jit(solution)/shard_map/ppermute | solution.py:310
  105.3 7.7 %collective-permute-start.26 = (bf16[16,6144]{1,0:T(8,128)(2,1)S(1)}, bf16[16,6144]{1,0:T(8,128)(2,1)S(1)}, u32[]{:S(2)}, u32[]{:S(2)}) collective-permute-start(bf16[16,6144]{1,0:T(8,128)(2,1)S(1)} %pad_maximum_fusion.1), channel_id=1, source_target_pairs={{0,4},{4,8},{8,12},{12,14},{14,10},{10,6},{6,2},{2,0},{1,5},{5,9},... | collective-permute-start | bytes 589832 | tf_op jit(solution)/shard_map/ppermute | solution.py:311
  111.1 7.4 %collective-permute-start.23 = (bf16[16,6144]{1,0:T(8,128)(2,1)S(1)}, bf16[16,6144]{1,0:T(8,128)(2,1)S(1)}, u32[]{:S(2)}, u32[]{:S(2)}) collective-permute-start(bf16[16,6144]{1,0:T(8,128)(2,1)S(1)} %fusion.15), channel_id=1, source_target_pairs={{4,0},{8,4},{12,8},{14,12},{10,14},{6,10},{2,6},{0,2},{5,1},{9,5},... | collective-permute-start | bytes 589832 | tf_op jit(solution)/shard_map/ppermute | solution.py:310
  118.6 5.7 %collective-permute-start.27 = (bf16[16,6144]{1,0:T(8,128)(2,1)S(1)}, bf16[16,6144]{1,0:T(8,128)(2,1)S(1)}, u32[]{:S(2)}, u32[]{:S(2)}) collective-permute-start(bf16[16,6144]{1,0:T(8,128)(2,1)S(1)} %get-tuple-element.26), channel_id=1, source_target_pairs={{0,4},{4,8},{8,12},{12,14},{14,10},{10,6},{6,2},{2,0},{1,5},{5,9},... | collective-permute-start | bytes 589832 | tf_op jit(solution)/shard_map/ppermute | solution.py:311
  118.7 5.7 %collective-permute-start.24 = (bf16[16,6144]{1,0:T(8,128)(2,1)S(1)}, bf16[16,6144]{1,0:T(8,128)(2,1)S(1)}, u32[]{:S(2)}, u32[]{:S(2)}) collective-permute-start(bf16[16,6144]{1,0:T(8,128)(2,1)S(1)} %get-tuple-element.25), channel_id=1, source_target_pairs={{4,0},{8,4},{12,8},{14,12},{10,14},{6,10},{2,6},{0,2},{5,1},{9,5},... | collective-permute-start | bytes 589832 | tf_op jit(solution)/shard_map/ppermute | solution.py:310
  124.3 5.7 %collective-permute-start.28 = (bf16[16,6144]{1,0:T(8,128)(2,1)S(1)}, bf16[16,6144]{1,0:T(8,128)(2,1)S(1)}, u32[]{:S(2)}, u32[]{:S(2)}) collective-permute-start(bf16[16,6144]{1,0:T(8,128)(2,1)S(1)} %fusion.14), channel_id=1, source_target_pairs={{0,4},{4,8},{8,12},{12,14},{14,10},{10,6},{6,2},{2,0},{1,5},{5,9},... | collective-permute-start | bytes 589832 | tf_op jit(solution)/shard_map/ppermute | solution.py:311
  (26 other events, 167.1 us)

commit v3 on v2

--- a/solution.py
+++ b/solution.py
@@ -8,7 +8,7 @@
 from jax.sharding import PartitionSpec as P
 
 CAP = 16
-CHUNKS = 2
+CHUNKS = 3
 VMEM = pl.BlockSpec(memory_space=pltpu.VMEM)
 SMEM = pl.BlockSpec(memory_space=pltpu.SMEM)
 HBM = pl.BlockSpec(memory_space=pl.ANY)
@@ -158,40 +158,45 @@
     )(odd, running, query_rows, within, residual, gain, table, *kept, *swapped)
 
 
-def expert_kernel(
-    deep, wide, row_ref, gate_ref, up_ref, down_ref, out_ref, gate, up, down, gate_sem, up_sem, down_sem
-):
+def buffer_kernel(core_ref, own_ref, other_ref, gain_ref, out_ref):
+    width = own_ref.shape[1]
+    own, other = (own_ref[...].astype(F32), other_ref[...].astype(F32))
+    first = core_ref[0] == 0
+    low, high = (jnp.where(first, own, other), jnp.where(first, other, own))
+    squares = jnp.sum(low * low + high * high, axis=1, keepdims=True)
+    inverse = lax.rsqrt(squares / (2 * width) + 1e-06)
+    out_ref[:, :width] = (low * inverse * gain_ref[:, :width]).astype(BF16)
+    out_ref[:, width:] = (high * inverse * gain_ref[:, width:]).astype(BF16)
+
+
+def buffer_rows(core, own, other, gain, weights):
+    capacity, width = own.shape
+    return pl.pallas_call(
+        buffer_kernel,
+        out_shape=jax.ShapeDtypeStruct((capacity, 2 * width), BF16),
+        in_specs=[SMEM, VMEM, VMEM, VMEM],
+        out_specs=VMEM,
+        compiler_params=grant(4),
+        cost_estimate=pl.CostEstimate(
+            flops=1500 * sum(weight.size for weight in weights),
+            bytes_accessed=8 * capacity * width,
+            transcendentals=0,
+        ),
+    )(core, own, other, gain)
+
+
+def expert_kernel(deep, wide, row_ref, gate_ref, up_ref, down_ref, out_ref):
     width, units = gate_ref.shape
-    copies = []
-    for step in range(width // deep):
-        rows = pl.ds(step * deep, deep)
-        pair = (
-            pltpu.make_async_copy(gate_ref.at[rows], gate.at[rows], gate_sem.at[step]),
-            pltpu.make_async_copy(up_ref.at[rows], up.at[rows], up_sem.at[step]),
-        )
-        for copy in pair:
-            copy.start()
-        copies.append(pair)
-    downs = []
-    for step in range(width // wide):
-        lanes = pl.ds(step * wide, wide)
-        downs.append(
-            pltpu.make_async_copy(down_ref.at[:, lanes], down.at[:, lanes], down_sem.at[step])
-        )
-        downs[-1].start()
     gate_part = jnp.zeros((row_ref.shape[0], units), F32)
     up_part = jnp.zeros((row_ref.shape[0], units), F32)
-    for step, pair in enumerate(copies):
+    for step in range(width // deep):
         lanes = slice(step * deep, (step + 1) * deep)
-        for copy in pair:
-            copy.wait()
-        gate_part += jnp.dot(row_ref[:, lanes], gate[lanes], preferred_element_type=F32)
-        up_part += jnp.dot(row_ref[:, lanes], up[lanes], preferred_element_type=F32)
+        gate_part += jnp.dot(row_ref[:, lanes], gate_ref[lanes], preferred_element_type=F32)
+        up_part += jnp.dot(row_ref[:, lanes], up_ref[lanes], preferred_element_type=F32)
     hidden = (jax.nn.silu(gate_part) * up_part).astype(BF16)
-    for step, copy in enumerate(downs):
+    for step in range(width // wide):
         lanes = slice(step * wide, (step + 1) * wide)
-        copy.wait()
-        out_ref[:, lanes] = jnp.dot(hidden, down[:, lanes], preferred_element_type=F32)
+        out_ref[:, lanes] = jnp.dot(hidden, down_ref[:, lanes], preferred_element_type=F32)
 
 
 def expert_rows(segment, gate_weight, up_weight, down_weight):
@@ -200,17 +205,9 @@
     return pl.pallas_call(
         functools.partial(expert_kernel, deep, wide),
         out_shape=jax.ShapeDtypeStruct((segment.shape[0], width), F32),
-        in_specs=[VMEM, HBM, HBM, HBM],
+        in_specs=[VMEM] * 4,
         out_specs=VMEM,
-        scratch_shapes=[
-            pltpu.VMEM((width, units), BF16),
-            pltpu.VMEM((width, units), BF16),
-            pltpu.VMEM((units, width), BF16),
-            pltpu.SemaphoreType.DMA((width // deep,)),
-            pltpu.SemaphoreType.DMA((width // deep,)),
-            pltpu.SemaphoreType.DMA((width // wide,)),
-        ],
-        compiler_params=grant(48),
+        compiler_params=grant(8),
         cost_estimate=pl.CostEstimate(
             flops=6 * segment.shape[0] * width * units,
             bytes_accessed=6 * width * units,
@@ -225,7 +222,11 @@
     )
 
 
-def entering_state(odd, full, narrow, block_total):
+def after(value, *others):
+    return lax.optimization_barrier((value, *others))[0]
+
+
+def entering_state(odd, full, narrow, block_total, aside):
     count = lax.axis_size("seq")
     swap = [(i, i ^ 1) for i in range(count)]
     half = full.shape[0] // 2
@@ -236,25 +237,39 @@
     even_decay = jnp.exp(jnp.where(odd, total_other, total_own))[:, None, None]
     odd_decay = jnp.exp(jnp.where(odd, total_own, total_other))[:, None, None]
     pair_decay = even_decay * odd_decay
-    kept, swapped = ([], [])
-    for chunk in range(CHUNKS):
-        here = slice(chunk * part, (chunk + 1) * part)
-        own = full[here]
+    places = [slice(chunk * part, (chunk + 1) * part) for chunk in range(CHUNKS)]
+    even_states, pair_states = ([], [])
+    for place in places:
+        own = full[place]
         arrived = lax.ppermute(
-            narrow[half + chunk * part : half + (chunk + 1) * part], "seq", swap
+            narrow[half + place.start : half + place.stop], "seq", swap
         ).astype(F32)
-        even_state = jnp.where(odd, arrived, own)
+        even_states.append(jnp.where(odd, arrived, own))
         odd_state = jnp.where(odd, own, arrived)
-        pair_state = odd_decay[here] * even_state + odd_state
-        before = jnp.zeros_like(own)
-        for hop in range(count // 2 - 1):
-            pairs = [(2 * hop + k, 2 * hop + 2 + k) for k in range(2)]
-            sent = (pair_decay[here] * before + pair_state).astype(BF16)
-            before = before + lax.ppermute(sent, "seq", pairs).astype(F32)
-        between = even_decay[here] * before + even_state
-        kept.append(jnp.where(odd, between, before).astype(BF16))
-        swapped.append(lax.ppermute(jnp.where(odd, before, between).astype(BF16), "seq", swap))
-    return (kept, swapped)
+        pair_states.append(odd_decay[place] * even_states[-1] + odd_state)
+    links = count // 2 - 1
+    befores = [jnp.zeros_like(state) for state in pair_states]
+    sents = [state.astype(BF16) for state in pair_states]
+    kept, swapped = ([None] * CHUNKS, [None] * CHUNKS)
+    marks, result = ([sents[-1]], None)
+    for link in range(links):
+        pairs = [(2 * link + k, 2 * link + 2 + k) for k in range(2)]
+        gots = [lax.ppermute(sent, "seq", pairs) for sent in sents]
+        if link == links - 1:
+            result = aside(sents[-1])
+            marks = [*marks, *result]
+        for chunk, place in enumerate(places):
+            got = after(gots[chunk], *marks).astype(F32)
+            before = befores[chunk] = befores[chunk] + got
+            if link < links - 1:
+                sents[chunk] = (pair_decay[place] * before + pair_states[chunk]).astype(BF16)
+                marks = [sents[chunk]]
+            else:
+                between = even_decay[place] * before + even_states[chunk]
+                kept[chunk] = jnp.where(odd, between, before).astype(BF16)
+                marks = [jnp.where(odd, before, between).astype(BF16)]
+                swapped[chunk] = lax.ppermute(marks[0], "seq", swap)
+    return (kept, swapped, result)
 
 
 def ring_pairs(count):
@@ -270,18 +285,14 @@
     from_left, from_right = ([], [])
     moving_right, moving_left = (unit, unit)
     for _ in range(count // 2 - 1):
-        moving_right = lax.ppermute(moving_right, "seq", right)
-        moving_left = lax.ppermute(moving_left, "seq", left)
+        moving_right = after(lax.ppermute(moving_right, "seq", right), moving_left)
+        moving_left = after(lax.ppermute(moving_left, "seq", left), moving_right)
         from_left.append(moving_right)
         from_right.append(moving_left)
-    far = jnp.concatenate(
-        [
-            lax.ppermute(moving_right[:, :middle], "seq", right),
-            lax.ppermute(moving_left[:, middle:], "seq", left),
-        ],
-        axis=1,
-    )
-    return jnp.concatenate([unit] + from_left + [far] + from_right, axis=0)
+    far_left = after(lax.ppermute(moving_right[:, :middle], "seq", right), moving_left)
+    far_right = lax.ppermute(moving_left[:, middle:], "seq", left)
+    far = jnp.concatenate([far_left, far_right], axis=1)
+    return (jnp.concatenate([unit] + from_left + [far] + from_right, axis=0), from_right[0])
 
 
 def ring_scatter(partial, rows):
@@ -293,25 +304,29 @@
     def piece(position):
         return partial[position * rows : (position + 1) * rows]
 
-    far = piece(steps).astype(jnp.bfloat16)
-    moving_left = lax.ppermute(far[:, :middle], "seq", left).astype(jnp.float32)
-    moving_right = lax.ppermute(far[:, middle:], "seq", right).astype(jnp.float32)
-    for step in range(steps - 1, 0, -1):
+    far = piece(steps)
+    to_left, to_right = (far[:, :middle].astype(BF16), far[:, middle:].astype(BF16))
+    for step in range(steps - 1, -1, -1):
+        moving_left = after(lax.ppermute(to_left, "seq", left), to_right).astype(F32)
+        arriving = lax.ppermute(to_right, "seq", right)
+        if step == 0:
+            return piece(0) + moving_left + arriving.astype(F32)
         to_left, to_right = (piece(step), piece(steps + step))
         if step == steps - 1:
             to_left = jnp.concatenate(
                 [to_left[:, :middle] + moving_left, to_left[:, middle:]], axis=1
             )
+        else:
+            to_left = to_left + moving_left
+        to_left = to_left.astype(BF16)
+        moving_right = after(arriving, to_left).astype(F32)
+        if step == steps - 1:
             to_right = jnp.concatenate(
                 [to_right[:, :middle], to_right[:, middle:] + moving_right], axis=1
             )
         else:
-            to_left, to_right = (to_left + moving_left, to_right + moving_right)
-        moving_left = lax.ppermute(to_left.astype(jnp.bfloat16), "seq", left).astype(jnp.float32)
-        moving_right = lax.ppermute(to_right.astype(jnp.bfloat16), "seq", right).astype(
-            jnp.float32
-        )
-    return piece(0) + moving_left + moving_right
+            to_right = to_right + moving_right
+        to_right = to_right.astype(BF16)
 
 
 def shards(
@@ -335,29 +350,34 @@
     odd = lax.axis_index("seq") % 2
     odd_scalar = odd.astype(jnp.int32)[None]
     running, full, narrow = block_state(odd_scalar, log_decay.T, key_rows, values)
-    kept, swapped = entering_state(odd == 1, full, narrow, running[:, -1])
-    within = within_block(running, queries, key_rows, values)
-
-    matches = [slot_matches(routes, slot_pos, expert, CAP) for expert in range(2)]
-    tables = [jnp.any(match, axis=1).astype(BF16).T for match in matches]
-    table = jnp.where(core == 0, jnp.concatenate(tables), jnp.concatenate(tables[::-1]))
+
+    def aside(mark):
+        experts = jnp.stack([core, 1 - core])
+        matches = [slot_matches(after(routes, mark), slot_pos, expert, CAP) for expert in experts]
+        table = jnp.concatenate([jnp.any(match, axis=1).T for match in matches]).astype(BF16)
+        return (within_block(running, after(queries, mark), key_rows, values), table)
+
+    kept, swapped, (within, table) = entering_state(
+        odd == 1, full, narrow, running[:, -1], aside
+    )
+
     hidden_half, rows_own, rows_sent = hidden_rows(
         odd_scalar, running, queries, within, residual, attn_gain[None], table, kept, swapped
     )
     rows_other = lax.ppermute(rows_sent, "exp", exchange)
-    rows_whole = jnp.where(
-        core == 0,
-        jnp.concatenate([rows_own, rows_other], axis=1),
-        jnp.concatenate([rows_other, rows_own], axis=1),
-    ).astype(jnp.float32)
-    rows_inverse = lax.rsqrt(jnp.mean(rows_whole * rows_whole, axis=1, keepdims=True) + 1e-06)
-    buffer = (rows_whole * rows_inverse * moe_gain).astype(jnp.bfloat16)
-
-    segment = ring_gather(buffer)
+    buffer = buffer_rows(
+        core.astype(jnp.int32)[None],
+        rows_own,
+        rows_other,
+        moe_gain[None],
+        (gate_weight, up_weight, down_weight),
+    )
+
+    segment, mark = ring_gather(buffer)
     partial = expert_rows(segment, gate_weight[0], up_weight[0], down_weight[0])
     expert_out = ring_scatter(partial, CAP).astype(jnp.bfloat16)
 
-    hidden_float = hidden_half.astype(jnp.float32)
+    hidden_float = after(hidden_half, mark).astype(jnp.float32)
     gain_half = lax.dynamic_slice_in_dim(moe_gain, core * width, width)
     router_half = lax.dynamic_slice_in_dim(router, core * width, width, axis=0)
     logits_half = jnp.dot(
@@ -377,6 +397,7 @@
     inverse = lax.rsqrt(sums[:, 2:] / (2 * width) + 1e-06)
     gates = jax.nn.sigmoid(sums[:, :2] * inverse)
     shares = gates / jnp.sum(gates, axis=1, keepdims=True)
+    matches = [slot_matches(routes, slot_pos, expert, CAP) for expert in range(2)]
     weighting = jnp.concatenate(
         [jnp.sum(jnp.where(match, shares[:, :, None], 0.0), axis=1) for match in matches], axis=1
     )

time: 134 us -> 114 us (0.85)
  Pallas kernels: 20 us -> 12.4 us
  waiting for transfers between devices: 55.7 us -> 49.4 us
  starting transfers between devices: 45.6 us -> 42.7 us
  other arithmetic: 4.74 us -> 2.4 us
    ppermute x25 -> x30, waiting for transfers between devices: 53.8 us -> 40 us  [the longest x4 15.6 us: ring_scatter(): lax.ppermute(to_left, 'seq', left)]
    pallas_call x1, Pallas kernels: 11.7 us -> 3.92 us  [expert_rows(): pl.pallas_call(functools.partial(expert_kernel, deep, wide), out_shape=ja...]
    ppermute x1, waiting for transfers between devices: 0.51 us -> 3.74 us  [ring_gather(): lax.ppermute(moving_right[:, :middle], 'seq', right)]
    ppermute x1, starting transfers between devices: 3.03 us -> 0.08 us  [entering_state(): total_other = lax.ppermute(jnp.where(odd, low, high)[None], 'seq', swap)[0]]
    ppermute x1, waiting for transfers between devices: 0.01 us -> 2.04 us  [entering_state(): total_other = lax.ppermute(jnp.where(odd, low, high)[None], 'seq', swap)[0]]
    convert_element_type x10 -> x15, other arithmetic: 3.45 us -> 1.49 us  [the longest x6 0.78 us: entering_state(): (pair_decay[place] * before + pair_states[chunk]).astype(BF16)]
    ppermute x25 -> x30, starting transfers between devices: 40.4 us -> 41.6 us  [the longest x9 13.8 us: entering_state(): gots = [lax.ppermute(sent, 'seq', pairs) for sent in sents]]
    unnamed x43 -> x48, local copies, waits for them, and re-layouts: 3.7 us -> 3.2 us
  transfers between devices with their start and end apart: 30 -> 35, of which waited for: 19 -> 22; matrix products, arithmetic and copies ran while one was open for 3% -> 3% of each run, Pallas kernels for 3% -> 3%
where the time goes in v3:
time: 114 us
  waiting for transfers between devices  49.4 us (43%)
  starting transfers between devices  42.7 us (37%)
  Pallas kernels  12.4 us (11%)
  local copies, waits for them, and re-layouts  3.52 us (3%)
  matrix products  2.77 us (2%)
  other arithmetic  2.4 us (2%)
    ppermute x4, waiting for transfers between devices, ring_scatter(): lax.ppermute(to_left, 'seq', left)  15.6 us
    ppermute x9, starting transfers between devices, entering_state(): gots = [lax.ppermute(sent, 'seq', pairs) for sent in sents]  13.8 us
    ppermute x3, waiting for transfers between devices, ring_gather(): moving_right = after(lax.ppermute(moving_right, 'seq', right), moving_left)  11.5 us
    ppermute x4, starting transfers between devices, ring_scatter(): lax.ppermute(to_left, 'seq', left)  7.19 us
    ppermute x3, starting transfers between devices, entering_state(): lax.ppermute(narrow[half + place.start:half + place.stop], 'seq', swap)  5.12 us
    ppermute x3, starting transfers between devices, ring_gather(): moving_right = after(lax.ppermute(moving_right, 'seq', right), moving_left)  4.73 us
    ppermute x3, starting transfers between devices, ring_gather(): moving_left = after(lax.ppermute(moving_left, 'seq', left), moving_right)  4.24 us
    ppermute x3, waiting for transfers between devices, entering_state(): swapped[chunk] = lax.ppermute(marks[0], 'seq', swap)  4.13 us
  transfers between devices with their start and end apart: 35, of which 22 were waited for; matrix products, arithmetic and copies ran while one was open for 3% of the time, Pallas kernels for 3%

profile of v3, /device:TPU:0, one launch (start us, length us, event | category | flops | bytes accessed | tf_op | source)
XLA Modules:
  0.0 113.9 jit_solution(5299966131793165057)
XLA Ops:
  4.8 3.0 %collective-permute-start.5 = (bf16[4,128,128]{2,1,0:T(8,128)(2,1)S(1)}, bf16[4,128,128]{2,1,0:T(8,128)(2,1)S(1)}, u32[]{:S(2)}, u32[]{:S(2)}) collective-permute-start(bf16[4,128,128]{2,1,0:T(8,128)(2,1)S(1)} %get-tuple-element.89), channel_id=1, source_target_pairs={{0,2},{2,0},{4,6},{6,4},{8,10},{10,8},{12,14},{14,12},{1,3},{3,1},... | collective-permute-start | bytes 393224 | tf_op jit(solution)/shard_map/ppermute | solution.py:244
  8.1 2.0 %collective-permute-start.1 = (bf16[4,128,128]{2,1,0:T(8,128)(2,1)S(1)}, bf16[4,128,128]{2,1,0:T(8,128)(2,1)S(1)}, u32[]{:S(2)}, u32[]{:S(2)}) collective-permute-start(bf16[4,128,128]{2,1,0:T(8,128)(2,1)S(1)} %get-tuple-element.91), channel_id=1, source_target_pairs={{0,2},{2,0},{4,6},{6,4},{8,10},{10,8},{12,14},{14,12},{1,3},{3,1},... | collective-permute-start | bytes 393224 | tf_op jit(solution)/shard_map/ppermute | solution.py:244
  10.2 2.0 %collective-permute-done = f32[1,12]{1,0:T(1,128)S(1)} collective-permute-done((f32[1,12]{1,0:T(1,128)S(1)}, f32[1,12]{1,0:T(1,128)S(1)}, u32[]{:S(2)}, u32[]{:S(2)}) %collective-permute-start) | collective-permute-done | bytes 80 | tf_op jit(solution)/shard_map/ppermute | solution.py:236
  12.4 2.7 %collective-permute-done.1 = bf16[4,128,128]{2,1,0:T(8,128)(2,1)S(1)} collective-permute-done((bf16[4,128,128]{2,1,0:T(8,128)(2,1)S(1)}, bf16[4,128,128]{2,1,0:T(8,128)(2,1)S(1)}, u32[]{:S(2)}, u32[]{:S(2)}) %collective-permute-start.1) | collective-permute-done | bytes 131104 | tf_op jit(solution)/shard_map/ppermute | solution.py:244
  15.2 4.0 %collective-permute-start.6 = (bf16[4,128,128]{2,1,0:T(8,128)(2,1)S(1)}, bf16[4,128,128]{2,1,0:T(8,128)(2,1)S(1)}, u32[]{:S(2)}, u32[]{:S(2)}) collective-permute-start(bf16[4,128,128]{2,1,0:T(8,128)(2,1)S(1)} %get-tuple-element.87), channel_id=1, source_target_pairs={{0,4},{2,6},{1,5},{3,7},{16,20},{18,22},{17,21},{19,23}} | collective-permute-start | bytes 393224 | tf_op jit(solution)/shard_map/ppermute | solution.py:257
  19.2 2.4 %collective-permute-done.6 = bf16[4,128,128]{2,1,0:T(8,128)(2,1)S(1)} collective-permute-done((bf16[4,128,128]{2,1,0:T(8,128)(2,1)S(1)}, bf16[4,128,128]{2,1,0:T(8,128)(2,1)S(1)}, u32[]{:S(2)}, u32[]{:S(2)}) %collective-permute-start.6) | collective-permute-done | bytes 131104 | tf_op jit(solution)/shard_map/ppermute | solution.py:257
  21.8 4.4 %collective-permute-start.4 = (bf16[4,128,128]{2,1,0:T(8,128)(2,1)S(1)}, bf16[4,128,128]{2,1,0:T(8,128)(2,1)S(1)}, u32[]{:S(2)}, u32[]{:S(2)}) collective-permute-start(bf16[4,128,128]{2,1,0:T(8,128)(2,1)S(1)} %get-tuple-element.86), channel_id=1, source_target_pairs={{0,4},{2,6},{1,5},{3,7},{16,20},{18,22},{17,21},{19,23}} | collective-permute-start | bytes 393224 | tf_op jit(solution)/shard_map/ppermute | solution.py:257
  33.4 3.9 %shard_map.128.within_ref = f32[128,3072]{1,0:T(8,128)S(1)} custom-call(f32[24,128]{1,0:T(8,128)S(1)} %get-tuple-element.37.run_ref, bf16[128,3072]{1,0:T(8,128)(2,1)S(1)} %copy-done.5, bf16[128,3072]{1,0:T(8,128)(2,1)S(1)} %copy-done.2, bf16[128,3072]{1,0:T(8,128)(2,1)S(1)} %copy-done.4), custom_call_target="tpu_custom_call" | custom-call | flops 201326592 | bytes 3932160 | tf_op jit(solution)/shard_map/pallas_call | solution.py:102
  45.6 2.7 %shard_map.129 = (bf16[128,3072]{1,0:T(8,128)(2,1)S(1)}, bf16[16,3072]{1,0:T(8,128)(2,1)S(1)}, bf16[16,3072]{1,0:T(8,128)(2,1)S(1)}) custom-call(s32[1]{0:T(128)} %bitcast.odd_ref, f32[24,128]{1,0:T(8,128)S(1)} %get-tuple-element.37.run_ref, bf16[128,3072]{1,0:T(8,128)(2,1)S(1)} %copy-done.5, f32[128,3072]{1,0:T(8,128)S(1)} %shard_map.128.within_ref, ...), custom_call_target="tpu_custom_call" | custom-call | flops 100663296 | bytes 4718592 | tf_op jit(solution)/shard_map/pallas_call | solution.py:143
  51.1 3.1 %collective-permute-start.18 = (bf16[16,6144]{1,0:T(8,128)(2,1)S(1)}, bf16[16,6144]{1,0:T(8,128)(2,1)S(1)}, u32[]{:S(2)}, u32[]{:S(2)}) collective-permute-start(bf16[16,6144]{1,0:T(8,128)(2,1)S(1)} %shard_map.130), channel_id=1, source_target_pairs={{0,4},{4,8},{8,12},{12,14},{14,10},{10,6},{6,2},{2,0},{1,5},{5,9},... | collective-permute-start | bytes 589832 | tf_op jit(solution)/shard_map/ppermute | solution.py:288
  54.2 6.0 %collective-permute-done.18 = bf16[16,6144]{1,0:T(8,128)(2,1)S(1)} collective-permute-done((bf16[16,6144]{1,0:T(8,128)(2,1)S(1)}, bf16[16,6144]{1,0:T(8,128)(2,1)S(1)}, u32[]{:S(2)}, u32[]{:S(2)}) %collective-permute-start.18) | collective-permute-done | bytes 196640 | tf_op jit(solution)/shard_map/ppermute | solution.py:288
  65.9 1.8 %collective-permute-done.20 = bf16[16,6144]{1,0:T(8,128)(2,1)S(1)} collective-permute-done((bf16[16,6144]{1,0:T(8,128)(2,1)S(1)}, bf16[16,6144]{1,0:T(8,128)(2,1)S(1)}, u32[]{:S(2)}, u32[]{:S(2)}) %collective-permute-start.20) | collective-permute-done | bytes 196640 | tf_op jit(solution)/shard_map/ppermute | solution.py:288
  69.8 3.6 %collective-permute-done.21 = bf16[16,6144]{1,0:T(8,128)(2,1)S(1)} collective-permute-done((bf16[16,6144]{1,0:T(8,128)(2,1)S(1)}, bf16[16,6144]{1,0:T(8,128)(2,1)S(1)}, u32[]{:S(2)}, u32[]{:S(2)}) %collective-permute-start.21) | collective-permute-done | bytes 196640 | tf_op jit(solution)/shard_map/ppermute | solution.py:288
  76.4 3.7 %collective-permute-done.23 = bf16[16,3072]{1,0:T(8,128)(2,1)S(1)} collective-permute-done((bf16[16,3072]{1,0:T(8,128)(2,1)S(1)}, bf16[16,3072]{1,0:T(8,128)(2,1)S(1)}, u32[]{:S(2)}, u32[]{:S(2)}) %collective-permute-start.23) | collective-permute-done | bytes 98336 | tf_op jit(solution)/shard_map/ppermute | solution.py:292
  80.3 3.9 %shard_map.131 = f32[128,6144]{1,0:T(8,128)S(1)} custom-call(bf16[128,6144]{1,0:T(8,128)(2,1)S(1)} %constant_dynamic-update-slice_fusion.row_ref, bf16[6144,768]{1,0:T(8,128)(2,1)S(1)} %bitcast.29, bf16[6144,768]{1,0:T(8,128)(2,1)S(1)} %bitcast.32, bf16[768,6144]{1,0:T(8,128)(2,1)S(1)} %bitcast.35), custom_call_target="tpu_custom_call" | custom-call | flops 3623878656 | bytes 28311552 | tf_op jit(solution)/shard_map/pallas_call | solution.py:205
  84.5 1.8 %collective-permute-start.26 = (bf16[16,3072]{1,0:T(8,128)(2,1)S(1)}, bf16[16,3072]{1,0:T(8,128)(2,1)S(1)}, u32[]{:S(2)}, u32[]{:S(2)}) collective-permute-start(bf16[16,3072]{1,0:T(8,128)(2,1)S(1)} %get-tuple-element.84), channel_id=1, source_target_pairs={{4,0},{8,4},{12,8},{14,12},{10,14},{6,10},{2,6},{0,2},{5,1},{9,5},... | collective-permute-start | bytes 294920 | tf_op jit(solution)/shard_map/ppermute | solution.py:310
  86.6 3.5 %collective-permute-done.26 = bf16[16,3072]{1,0:T(8,128)(2,1)S(1)} collective-permute-done((bf16[16,3072]{1,0:T(8,128)(2,1)S(1)}, bf16[16,3072]{1,0:T(8,128)(2,1)S(1)}, u32[]{:S(2)}, u32[]{:S(2)}) %collective-permute-start.26) | collective-permute-done | bytes 98336 | tf_op jit(solution)/shard_map/ppermute | solution.py:310
  90.2 1.8 %collective-permute-start.27 = (bf16[16,6144]{1,0:T(8,128)(2,1)S(1)}, bf16[16,6144]{1,0:T(8,128)(2,1)S(1)}, u32[]{:S(2)}, u32[]{:S(2)}) collective-permute-start(bf16[16,6144]{1,0:T(8,128)(2,1)S(1)} %pad_maximum_fusion), channel_id=1, source_target_pairs={{4,0},{8,4},{12,8},{14,12},{10,14},{6,10},{2,6},{0,2},{5,1},{9,5},... | collective-permute-start | bytes 589832 | tf_op jit(solution)/shard_map/ppermute | solution.py:310
  92.4 4.7 %collective-permute-done.27 = bf16[16,6144]{1,0:T(8,128)(2,1)S(1)} collective-permute-done((bf16[16,6144]{1,0:T(8,128)(2,1)S(1)}, bf16[16,6144]{1,0:T(8,128)(2,1)S(1)}, u32[]{:S(2)}, u32[]{:S(2)}) %collective-permute-start.27) | collective-permute-done | bytes 196640 | tf_op jit(solution)/shard_map/ppermute | solution.py:310
  97.1 1.8 %collective-permute-start.29 = (bf16[16,6144]{1,0:T(8,128)(2,1)S(1)}, bf16[16,6144]{1,0:T(8,128)(2,1)S(1)}, u32[]{:S(2)}, u32[]{:S(2)}) collective-permute-start(bf16[16,6144]{1,0:T(8,128)(2,1)S(1)} %fusion.6), channel_id=1, source_target_pairs={{4,0},{8,4},{12,8},{14,12},{10,14},{6,10},{2,6},{0,2},{5,1},{9,5},... | collective-permute-start | bytes 589832 | tf_op jit(solution)/shard_map/ppermute | solution.py:310
  99.2 3.8 %collective-permute-done.29 = bf16[16,6144]{1,0:T(8,128)(2,1)S(1)} collective-permute-done((bf16[16,6144]{1,0:T(8,128)(2,1)S(1)}, bf16[16,6144]{1,0:T(8,128)(2,1)S(1)}, u32[]{:S(2)}, u32[]{:S(2)}) %collective-permute-start.29) | collective-permute-done | bytes 196640 | tf_op jit(solution)/shard_map/ppermute | solution.py:310
  103.1 1.8 %collective-permute-start.31 = (bf16[16,6144]{1,0:T(8,128)(2,1)S(1)}, bf16[16,6144]{1,0:T(8,128)(2,1)S(1)}, u32[]{:S(2)}, u32[]{:S(2)}) collective-permute-start(bf16[16,6144]{1,0:T(8,128)(2,1)S(1)} %fusion.7), channel_id=1, source_target_pairs={{4,0},{8,4},{12,8},{14,12},{10,14},{6,10},{2,6},{0,2},{5,1},{9,5},... | collective-permute-start | bytes 589832 | tf_op jit(solution)/shard_map/ppermute | solution.py:310
  105.3 3.5 %collective-permute-done.31 = bf16[16,6144]{1,0:T(8,128)(2,1)S(1)} collective-permute-done((bf16[16,6144]{1,0:T(8,128)(2,1)S(1)}, bf16[16,6144]{1,0:T(8,128)(2,1)S(1)}, u32[]{:S(2)}, u32[]{:S(2)}) %collective-permute-start.31) | collective-permute-done | bytes 196640 | tf_op jit(solution)/shard_map/ppermute | solution.py:310
  108.8 1.8 %collective-permute-done.33 = bf16[16,6144]{1,0:T(8,128)(2,1)S(1)} collective-permute-done((bf16[16,6144]{1,0:T(8,128)(2,1)S(1)}, bf16[16,6144]{1,0:T(8,128)(2,1)S(1)}, u32[]{:S(2)}, u32[]{:S(2)}) %collective-permute-start.33) | collective-permute-done | bytes 196640 | tf_op jit(solution)/shard_map/ppermute | solution.py:311
  (150 shorter events, 39.4 us)
Async XLA Ops:
  4.8 7.5 %collective-permute-start.5 = (bf16[4,128,128]{2,1,0:T(8,128)(2,1)S(1)}, bf16[4,128,128]{2,1,0:T(8,128)(2,1)S(1)}, u32[]{:S(2)}, u32[]{:S(2)}) collective-permute-start(bf16[4,128,128]{2,1,0:T(8,128)(2,1)S(1)} %get-tuple-element.89), channel_id=1, source_target_pairs={{0,2},{2,0},{4,6},{6,4},{8,10},{10,8},{12,14},{14,12},{1,3},{3,1},... | collective-permute-start | bytes 393224 | tf_op jit(solution)/shard_map/ppermute | solution.py:244
  8.1 6.9 %collective-permute-start.1 = (bf16[4,128,128]{2,1,0:T(8,128)(2,1)S(1)}, bf16[4,128,128]{2,1,0:T(8,128)(2,1)S(1)}, u32[]{:S(2)}, u32[]{:S(2)}) collective-permute-start(bf16[4,128,128]{2,1,0:T(8,128)(2,1)S(1)} %get-tuple-element.91), channel_id=1, source_target_pairs={{0,2},{2,0},{4,6},{6,4},{8,10},{10,8},{12,14},{14,12},{1,3},{3,1},... | collective-permute-start | bytes 393224 | tf_op jit(solution)/shard_map/ppermute | solution.py:244
  10.1 11.5 %collective-permute-start.3 = (bf16[4,128,128]{2,1,0:T(8,128)(2,1)S(1)}, bf16[4,128,128]{2,1,0:T(8,128)(2,1)S(1)}, u32[]{:S(2)}, u32[]{:S(2)}) collective-permute-start(bf16[4,128,128]{2,1,0:T(8,128)(2,1)S(1)} %get-tuple-element.90), channel_id=1, source_target_pairs={{0,2},{2,0},{4,6},{6,4},{8,10},{10,8},{12,14},{14,12},{1,3},{3,1},... | collective-permute-start | bytes 393224 | tf_op jit(solution)/shard_map/ppermute | solution.py:244
  15.2 6.5 %collective-permute-start.6 = (bf16[4,128,128]{2,1,0:T(8,128)(2,1)S(1)}, bf16[4,128,128]{2,1,0:T(8,128)(2,1)S(1)}, u32[]{:S(2)}, u32[]{:S(2)}) collective-permute-start(bf16[4,128,128]{2,1,0:T(8,128)(2,1)S(1)} %get-tuple-element.87), channel_id=1, source_target_pairs={{0,4},{2,6},{1,5},{3,7},{16,20},{18,22},{17,21},{19,23}} | collective-permute-start | bytes 393224 | tf_op jit(solution)/shard_map/ppermute | solution.py:257
  21.8 6.9 %collective-permute-start.4 = (bf16[4,128,128]{2,1,0:T(8,128)(2,1)S(1)}, bf16[4,128,128]{2,1,0:T(8,128)(2,1)S(1)}, u32[]{:S(2)}, u32[]{:S(2)}) collective-permute-start(bf16[4,128,128]{2,1,0:T(8,128)(2,1)S(1)} %get-tuple-element.86), channel_id=1, source_target_pairs={{0,4},{2,6},{1,5},{3,7},{16,20},{18,22},{17,21},{19,23}} | collective-permute-start | bytes 393224 | tf_op jit(solution)/shard_map/ppermute | solution.py:257
  31.0 6.3 %collective-permute-start.10 = (bf16[4,128,128]{2,1,0:T(8,128)(2,1)S(1)}, bf16[4,128,128]{2,1,0:T(8,128)(2,1)S(1)}, u32[]{:S(2)}, u32[]{:S(2)}) collective-permute-start(bf16[4,128,128]{2,1,0:T(8,128)(2,1)S(1)} %add_convert_fusion.2), channel_id=1, source_target_pairs={{8,12},{10,14},{9,13},{11,15},{24,28},{26,30},{25,29},{27,31}} | collective-permute-start | bytes 393224 | tf_op jit(solution)/shard_map/ppermute | solution.py:257
  31.8 7.2 %collective-permute-start.11 = (bf16[4,128,128]{2,1,0:T(8,128)(2,1)S(1)}, bf16[4,128,128]{2,1,0:T(8,128)(2,1)S(1)}, u32[]{:S(2)}, u32[]{:S(2)}) collective-permute-start(bf16[4,128,128]{2,1,0:T(8,128)(2,1)S(1)} %add_convert_fusion.1), channel_id=1, source_target_pairs={{8,12},{10,14},{9,13},{11,15},{24,28},{26,30},{25,29},{27,31}} | collective-permute-start | bytes 393224 | tf_op jit(solution)/shard_map/ppermute | solution.py:257
  32.6 7.1 %collective-permute-start.12 = (bf16[4,128,128]{2,1,0:T(8,128)(2,1)S(1)}, bf16[4,128,128]{2,1,0:T(8,128)(2,1)S(1)}, u32[]{:S(2)}, u32[]{:S(2)}) collective-permute-start(bf16[4,128,128]{2,1,0:T(8,128)(2,1)S(1)} %add_convert_fusion), channel_id=1, source_target_pairs={{8,12},{10,14},{9,13},{11,15},{24,28},{26,30},{25,29},{27,31}} | collective-permute-start | bytes 393224 | tf_op jit(solution)/shard_map/ppermute | solution.py:257
  39.9 5.7 %collective-permute-start.15 = (bf16[4,128,128]{2,1,0:T(8,128)(2,1)S(1)}, bf16[4,128,128]{2,1,0:T(8,128)(2,1)S(1)}, u32[]{:S(2)}, u32[]{:S(2)}) collective-permute-start(bf16[4,128,128]{2,1,0:T(8,128)(2,1)S(1)} %get-tuple-element.75), channel_id=1, source_target_pairs={{0,2},{2,0},{4,6},{6,4},{8,10},{10,8},{12,14},{14,12},{1,3},{3,1},... | collective-permute-start | bytes 393224 | tf_op jit(solution)/shard_map/ppermute | solution.py:271
  49.9 11.9 %collective-permute-start.17 = (bf16[16,6144]{1,0:T(8,128)(2,1)S(1)}, bf16[16,6144]{1,0:T(8,128)(2,1)S(1)}, u32[]{:S(2)}, u32[]{:S(2)}) collective-permute-start(bf16[16,6144]{1,0:T(8,128)(2,1)S(1)} %shard_map.130), channel_id=1, source_target_pairs={{4,0},{8,4},{12,8},{14,12},{10,14},{6,10},{2,6},{0,2},{5,1},{9,5},... | collective-permute-start | bytes 589832 | tf_op jit(solution)/shard_map/ppermute | solution.py:289
  51.1 9.1 %collective-permute-start.18 = (bf16[16,6144]{1,0:T(8,128)(2,1)S(1)}, bf16[16,6144]{1,0:T(8,128)(2,1)S(1)}, u32[]{:S(2)}, u32[]{:S(2)}) collective-permute-start(bf16[16,6144]{1,0:T(8,128)(2,1)S(1)} %shard_map.130), channel_id=1, source_target_pairs={{0,4},{4,8},{8,12},{12,14},{14,10},{10,6},{6,2},{2,0},{1,5},{5,9},... | collective-permute-start | bytes 589832 | tf_op jit(solution)/shard_map/ppermute | solution.py:288
  60.3 7.5 %collective-permute-start.20 = (bf16[16,6144]{1,0:T(8,128)(2,1)S(1)}, bf16[16,6144]{1,0:T(8,128)(2,1)S(1)}, u32[]{:S(2)}, u32[]{:S(2)}) collective-permute-start(bf16[16,6144]{1,0:T(8,128)(2,1)S(1)} %collective-permute-done.18), channel_id=1, source_target_pairs={{0,4},{4,8},{8,12},{12,14},{14,10},{10,6},{6,2},{2,0},{1,5},{5,9},... | collective-permute-start | bytes 589832 | tf_op jit(solution)/shard_map/ppermute | solution.py:288
  61.8 6.6 %collective-permute-start.22 = (bf16[16,6144]{1,0:T(8,128)(2,1)S(1)}, bf16[16,6144]{1,0:T(8,128)(2,1)S(1)}, u32[]{:S(2)}, u32[]{:S(2)}) collective-permute-start(bf16[16,6144]{1,0:T(8,128)(2,1)S(1)} %collective-permute-done.17), channel_id=1, source_target_pairs={{4,0},{8,4},{12,8},{14,12},{10,14},{6,10},{2,6},{0,2},{5,1},{9,5},... | collective-permute-start | bytes 589832 | tf_op jit(solution)/shard_map/ppermute | solution.py:289
  67.7 5.7 %collective-permute-start.21 = (bf16[16,6144]{1,0:T(8,128)(2,1)S(1)}, bf16[16,6144]{1,0:T(8,128)(2,1)S(1)}, u32[]{:S(2)}, u32[]{:S(2)}) collective-permute-start(bf16[16,6144]{1,0:T(8,128)(2,1)S(1)} %collective-permute-done.20), channel_id=1, source_target_pairs={{0,4},{4,8},{8,12},{12,14},{14,10},{10,6},{6,2},{2,0},{1,5},{5,9},... | collective-permute-start | bytes 589832 | tf_op jit(solution)/shard_map/ppermute | solution.py:288
  68.4 5.7 %collective-permute-start.24 = (bf16[16,6144]{1,0:T(8,128)(2,1)S(1)}, bf16[16,6144]{1,0:T(8,128)(2,1)S(1)}, u32[]{:S(2)}, u32[]{:S(2)}) collective-permute-start(bf16[16,6144]{1,0:T(8,128)(2,1)S(1)} %collective-permute-done.22), channel_id=1, source_target_pairs={{4,0},{8,4},{12,8},{14,12},{10,14},{6,10},{2,6},{0,2},{5,1},{9,5},... | collective-permute-start | bytes 589832 | tf_op jit(solution)/shard_map/ppermute | solution.py:289
  74.0 6.1 %collective-permute-start.25 = (bf16[16,3072]{1,0:T(8,128)(2,1)S(1)}, bf16[16,3072]{1,0:T(8,128)(2,1)S(1)}, u32[]{:S(2)}, u32[]{:S(2)}) collective-permute-start(bf16[16,3072]{1,0:T(8,128)(2,1)S(1)} %slice.149), channel_id=1, source_target_pairs={{4,0},{8,4},{12,8},{14,12},{10,14},{6,10},{2,6},{0,2},{5,1},{9,5},... | collective-permute-start | bytes 294920 | tf_op jit(solution)/shard_map/ppermute | solution.py:293
  84.5 5.6 %collective-permute-start.26 = (bf16[16,3072]{1,0:T(8,128)(2,1)S(1)}, bf16[16,3072]{1,0:T(8,128)(2,1)S(1)}, u32[]{:S(2)}, u32[]{:S(2)}) collective-permute-start(bf16[16,3072]{1,0:T(8,128)(2,1)S(1)} %get-tuple-element.84), channel_id=1, source_target_pairs={{4,0},{8,4},{12,8},{14,12},{10,14},{6,10},{2,6},{0,2},{5,1},{9,5},... | collective-permute-start | bytes 294920 | tf_op jit(solution)/shard_map/ppermute | solution.py:310
  86.3 5.7 %collective-permute-start.28 = (bf16[16,3072]{1,0:T(8,128)(2,1)S(1)}, bf16[16,3072]{1,0:T(8,128)(2,1)S(1)}, u32[]{:S(2)}, u32[]{:S(2)}) collective-permute-start(bf16[16,3072]{1,0:T(8,128)(2,1)S(1)} %get-tuple-element.83), channel_id=1, source_target_pairs={{0,4},{4,8},{8,12},{12,14},{14,10},{10,6},{6,2},{2,0},{1,5},{5,9},... | collective-permute-start | bytes 294920 | tf_op jit(solution)/shard_map/ppermute | solution.py:311
  90.2 6.9 %collective-permute-start.27 = (bf16[16,6144]{1,0:T(8,128)(2,1)S(1)}, bf16[16,6144]{1,0:T(8,128)(2,1)S(1)}, u32[]{:S(2)}, u32[]{:S(2)}) collective-permute-start(bf16[16,6144]{1,0:T(8,128)(2,1)S(1)} %pad_maximum_fusion), channel_id=1, source_target_pairs={{4,0},{8,4},{12,8},{14,12},{10,14},{6,10},{2,6},{0,2},{5,1},{9,5},... | collective-permute-start | bytes 589832 | tf_op jit(solution)/shard_map/ppermute | solution.py:310
  92.0 6.9 %collective-permute-start.30 = (bf16[16,6144]{1,0:T(8,128)(2,1)S(1)}, bf16[16,6144]{1,0:T(8,128)(2,1)S(1)}, u32[]{:S(2)}, u32[]{:S(2)}) collective-permute-start(bf16[16,6144]{1,0:T(8,128)(2,1)S(1)} %pad_maximum_fusion.1), channel_id=1, source_target_pairs={{0,4},{4,8},{8,12},{12,14},{14,10},{10,6},{6,2},{2,0},{1,5},{5,9},... | collective-permute-start | bytes 589832 | tf_op jit(solution)/shard_map/ppermute | solution.py:311
  97.1 6.0 %collective-permute-start.29 = (bf16[16,6144]{1,0:T(8,128)(2,1)S(1)}, bf16[16,6144]{1,0:T(8,128)(2,1)S(1)}, u32[]{:S(2)}, u32[]{:S(2)}) collective-permute-start(bf16[16,6144]{1,0:T(8,128)(2,1)S(1)} %fusion.6), channel_id=1, source_target_pairs={{4,0},{8,4},{12,8},{14,12},{10,14},{6,10},{2,6},{0,2},{5,1},{9,5},... | collective-permute-start | bytes 589832 | tf_op jit(solution)/shard_map/ppermute | solution.py:310
  98.9 6.0 %collective-permute-start.32 = (bf16[16,6144]{1,0:T(8,128)(2,1)S(1)}, bf16[16,6144]{1,0:T(8,128)(2,1)S(1)}, u32[]{:S(2)}, u32[]{:S(2)}) collective-permute-start(bf16[16,6144]{1,0:T(8,128)(2,1)S(1)} %fusion.5), channel_id=1, source_target_pairs={{0,4},{4,8},{8,12},{12,14},{14,10},{10,6},{6,2},{2,0},{1,5},{5,9},... | collective-permute-start | bytes 589832 | tf_op jit(solution)/shard_map/ppermute | solution.py:311
  103.1 5.7 %collective-permute-start.31 = (bf16[16,6144]{1,0:T(8,128)(2,1)S(1)}, bf16[16,6144]{1,0:T(8,128)(2,1)S(1)}, u32[]{:S(2)}, u32[]{:S(2)}) collective-permute-start(bf16[16,6144]{1,0:T(8,128)(2,1)S(1)} %fusion.7), channel_id=1, source_target_pairs={{4,0},{8,4},{12,8},{14,12},{10,14},{6,10},{2,6},{0,2},{5,1},{9,5},... | collective-permute-start | bytes 589832 | tf_op jit(solution)/shard_map/ppermute | solution.py:310
  105.0 5.7 %collective-permute-start.33 = (bf16[16,6144]{1,0:T(8,128)(2,1)S(1)}, bf16[16,6144]{1,0:T(8,128)(2,1)S(1)}, u32[]{:S(2)}, u32[]{:S(2)}) collective-permute-start(bf16[16,6144]{1,0:T(8,128)(2,1)S(1)} %fusion.4), channel_id=1, source_target_pairs={{0,4},{4,8},{8,12},{12,14},{14,10},{10,6},{6,2},{2,0},{1,5},{5,9},... | collective-permute-start | bytes 589832 | tf_op jit(solution)/shard_map/ppermute | solution.py:311
  (32 other events, 418.8 us)

commit v4 on v3

v4 whole, which is shorter than its diff:
```python
import functools

import jax
import jax.numpy as jnp
from jax import lax
from jax.experimental import pallas as pl
from jax.experimental.pallas import tpu as pltpu
from jax.sharding import PartitionSpec as P

CAP = 16
CHUNKS = 3
VMEM = pl.BlockSpec(memory_space=pltpu.VMEM)
SMEM = pl.BlockSpec(memory_space=pltpu.SMEM)
HBM = pl.BlockSpec(memory_space=pl.ANY)
F32, BF16 = (jnp.float32, jnp.bfloat16)


def grant(mebibytes):
    return pltpu.CompilerParams(vmem_limit_bytes=mebibytes * 2**20)


def triangle(length):
    rows = lax.broadcasted_iota(jnp.int32, (length, length), 0)
    columns = lax.broadcasted_iota(jnp.int32, (length, length), 1)
    return rows >= columns


def as_columns(table):
    heads, length = table.shape
    return jnp.concatenate([table, jnp.zeros((length - heads, length), F32)], axis=0).T


def running_sums(log_rows):
    return lax.dot_general(
        log_rows,
        jnp.where(triangle(log_rows.shape[1]), 1.0, 0.0),
        (((1,), (1,)), ((), ())),
        precision=lax.Precision.HIGHEST,
        preferred_element_type=F32,
    )


def state_kernel(sent, log_ref, key_ref, value_ref, *refs):
    outs, (log, key, value, sems) = (refs[:-4], refs[-4:])
    heads, length = log_ref.shape
    width = key_ref.shape[1] // heads
    half = heads // 2
    part = half // CHUNKS
    side = (lax.axis_index("seq") + sent) % 2
    log_copy = pltpu.make_async_copy(log_ref, log, sems.at[2 * CHUNKS])
    log_copy.start()
    copies = []
    for chunk in range(CHUNKS):
        lanes = pl.ds(pl.multiple_of((side * half + chunk * part) * width, width), part * width)
        here = pl.ds(chunk * part * width, part * width)
        pair = (
            pltpu.make_async_copy(key_ref.at[:, lanes], key.at[:, here], sems.at[2 * chunk]),
            pltpu.make_async_copy(value_ref.at[:, lanes], value.at[:, here], sems.at[2 * chunk + 1]),
        )
        for copy in pair:
            copy.start()
        copies.append(pair)
    log_copy.wait()
    running = running_sums(log[...])
    total = running[:, length - 1 :]
    rest = as_columns(jnp.exp(total - running))
    rest = jnp.where(side == 0, rest[:, :half], rest[:, half:heads])
    for head in range(half):
        chunk, place = divmod(head, part)
        if place == 0:
            for copy in copies[chunk]:
                copy.wait()
        lanes = slice(head * width, (head + 1) * width)
        scaled = (key[:, lanes].astype(F32) * rest[:, head : head + 1]).astype(BF16)
        state = lax.dot_general(
            scaled, value[:, lanes], (((0,), (0,)), ((), ())), preferred_element_type=F32
        )
        rows = slice(place * width, (place + 1) * width)
        outs[chunk][rows, :] = state.astype(outs[chunk].dtype)
    if sent:
        totals = as_columns(jnp.broadcast_to(total, (heads, length)))[:1]
        totals = jnp.where(side == 0, totals[:, :half], totals[:, half:heads])
        first = totals.astype(BF16).astype(F32)
        second = (totals - first).astype(BF16).astype(F32)
        third = totals - first - second
        rows = jnp.concatenate([first, second, third, jnp.zeros((13, half), F32)], axis=0)
        rows = jnp.concatenate([rows, jnp.zeros((16, width - half), F32)], axis=1)
        outs[0][part * width :, :] = rows.astype(BF16)
    else:
        outs[CHUNKS][...] = running


def half_state(sent, log_rows, key_rows, value_rows):
    heads, length = log_rows.shape
    width = key_rows.shape[1] // heads
    rows = heads // 2 // CHUNKS * width
    shapes = [jax.ShapeDtypeStruct((rows, width), BF16 if sent else F32)] * CHUNKS
    if sent:
        shapes[0] = jax.ShapeDtypeStruct((rows + 16, width), BF16)
    else:
        shapes.append(jax.ShapeDtypeStruct((heads, length), F32))
    return pl.pallas_call(
        functools.partial(state_kernel, sent),
        out_shape=tuple(shapes),
        in_specs=[HBM, HBM, HBM],
        out_specs=(VMEM,) * len(shapes),
        scratch_shapes=[
            pltpu.VMEM((heads, length), F32),
            pltpu.VMEM((length, heads // 2 * width), BF16),
            pltpu.VMEM((length, heads // 2 * width), BF16),
            pltpu.SemaphoreType.DMA((2 * CHUNKS + 1,)),
        ],
        compiler_params=grant(60 if sent else 8),
        cost_estimate=pl.CostEstimate(
            flops=length * width * width * heads,
            bytes_accessed=2 * length * width * heads,
            transcendentals=0,
        ),
    )(log_rows, key_rows, value_rows)


def slots_of(route_ref, slot_ref, capacity, values):
    shape = (2 * capacity, route_ref.shape[1])
    place = lax.broadcasted_iota(jnp.int32, shape, 0)
    expert = jnp.where(place < capacity, lax.axis_index("exp"), 1 - lax.axis_index("exp"))
    slot = place % capacity
    table = jnp.zeros(shape, F32)
    for choice, value in enumerate(values):
        here = slice(choice, choice + 1)
        match = (route_ref[here, :] == expert) & (slot_ref[here, :] == slot)
        table += jnp.where(match, value, 0.0)
    return table


def within_kernel(
    sent, run_ref, query_ref, key_ref, value_ref, residual_ref, route_ref, slot_ref, out_ref, pack_ref
):
    heads, length = run_ref.shape
    width = key_ref.shape[1] // heads
    half = heads // 2
    span = half * width
    causal = triangle(length)
    side = (lax.axis_index("seq") + sent) % 2
    running = jnp.where(side == 0, run_ref[:half, :], run_ref[half:, :])
    columns = as_columns(running)
    for head in range(half):
        lanes = pl.ds(pl.multiple_of((side * half + head) * width, width), width)
        scores = lax.dot_general(
            query_ref[:, lanes],
            key_ref[:, lanes],
            (((1,), (1,)), ((), ())),
            preferred_element_type=F32,
        )
        spread = columns[:, head : head + 1] - running[head : head + 1, :]
        mixing = jnp.where(causal, scores * jnp.exp(spread), 0.0).astype(BF16)
        out_ref[:, head * width : (head + 1) * width] = jnp.dot(
            mixing, value_ref[:, lanes], preferred_element_type=F32
        )

    table = slots_of(route_ref, slot_ref, pack_ref.shape[0] // 2, (1.0, 1.0)).astype(BF16)

    def routed(array):
        return jnp.dot(table, array, preferred_element_type=F32).astype(BF16)

    grown = jnp.exp(columns)
    high = grown.astype(BF16)
    low = (grown - high.astype(F32)).astype(BF16)
    lanes = pl.ds(pl.multiple_of(side * span, span), span)
    pack_ref[:, :span] = routed(query_ref[:, lanes])
    pack_ref[:, span : 2 * span] = routed(residual_ref[:, lanes])
    pack_ref[:, 2 * span : 3 * span] = routed(out_ref[...].astype(BF16))
    blank = jnp.zeros((table.shape[0], width // 2 - half), BF16)
    pack_ref[:, 3 * span :] = jnp.concatenate(
        [routed(high)[:, :half], blank, routed(low)[:, :half], blank], axis=1
    )


def within_block(sent, running, query_rows, key_rows, value_rows, residual, routes, slots):
    heads, length = running.shape
    width = key_rows.shape[1] // heads
    span = heads // 2 * width
    return pl.pallas_call(
        functools.partial(within_kernel, sent),
        out_shape=(
            jax.ShapeDtypeStruct((length, span), F32),
            jax.ShapeDtypeStruct((2 * CAP, 3 * span + width), BF16),
        ),
        in_specs=[VMEM] * 7,
        out_specs=(VMEM, VMEM),
        compiler_params=grant(16),
        cost_estimate=pl.CostEstimate(
            flops=4 * length * length * span,
            bytes_accessed=12 * length * span,
            transcendentals=heads // 2 * length * length,
        ),
    )(running, query_rows, key_rows, value_rows, residual, routes, slots)


def rows_kernel(chunk, own_ref, got_ref, gain_ref, kept_ref, moved_ref, mine_ref, theirs_ref):
    part, width, _ = kept_ref.shape
    half = part * CHUNKS
    span = half * width
    odd = lax.axis_index("seq") % 2
    capacity = own_ref.shape[0] // 2
    for pack, state_ref, moved in ((own_ref, kept_ref, 0), (got_ref, moved_ref, 1)):
        tail = pack[:, 3 * span :].astype(F32)
        grown = tail[:, :half] + tail[:, width // 2 : width // 2 + half]
        place = pl.ds(pl.multiple_of((odd ^ moved) * capacity, capacity), capacity)
        for index in range(part):
            head = chunk * part + index
            lanes = [slice(k * span + head * width, k * span + (head + 1) * width) for k in range(3)]
            gain = jnp.where(odd == 0, gain_ref[:, lanes[0]], gain_ref[:, lanes[1]])
            query, residual, within = [pack[:, lane] for lane in lanes]
            carried = jnp.dot(query, state_ref[index], preferred_element_type=F32)
            raw = within.astype(F32) + carried * grown[:, head : head + 1]
            normed = raw * lax.rsqrt(jnp.mean(raw * raw, axis=1, keepdims=True) + 1e-05)
            hidden = (residual.astype(F32) + normed * gain).astype(BF16)
            here = slice(index * width, (index + 1) * width)
            mine_ref[place, here] = hidden[:capacity]
            theirs_ref[place, here] = hidden[capacity:]


def pair_rows(chunk, own, got, gain, kept, moved, weights):
    part, width, _ = kept.shape
    rows = own.shape[0]
    shape = jax.ShapeDtypeStruct((rows, part * width), BF16)
    flops = 4 * rows * part * width * width
    if chunk == CHUNKS - 1:
        flops = 1500 * sum(weight.size for weight in weights)
    return pl.pallas_call(
        functools.partial(rows_kernel, chunk),
        out_shape=(shape, shape),
        in_specs=[VMEM] * 5,
        out_specs=(VMEM, VMEM),
        compiler_params=grant(8),
        cost_estimate=pl.CostEstimate(
            flops=flops, bytes_accessed=12 * own.size, transcendentals=0
        ),
    )(own, got, gain, kept, moved)


def hidden_kernel(
    run_ref,
    query_ref,
    own_ref,
    other_ref,
    residual_ref,
    gain_ref,
    moe_gain_ref,
    router_ref,
    route_ref,
    *refs,
):
    *state_refs, hidden_ref, sums_ref = refs
    heads, length = run_ref.shape
    span = query_ref.shape[1]
    width = span // heads
    half, part = (heads // 2, state_refs[0].shape[0])
    grown = as_columns(jnp.exp(run_ref[...]))
    even = lax.axis_index("seq") % 2 == 0
    squares = jnp.zeros((length, width), F32)
    for head in range(heads):
        lanes = slice(head * width, (head + 1) * width)
        chunk, place = divmod(head % half, part)
        kept, swapped = (state_refs[chunk][place], state_refs[CHUNKS + chunk][place])
        here = slice(head % half * width, (head % half + 1) * width)
        own, other = (own_ref[:, here], other_ref[:, here])
        if head >= half:
            kept, swapped, own, other = (swapped, kept, other, own)
        state, within = (jnp.where(even, kept, swapped), jnp.where(even, own, other))
        carried = jnp.dot(query_ref[:, lanes], state, preferred_element_type=F32)
        raw = within + carried * grown[:, head : head + 1]
        normed = raw * lax.rsqrt(jnp.mean(raw * raw, axis=1, keepdims=True) + 1e-05)
        hidden = (residual_ref[:, lanes].astype(F32) + normed * gain_ref[:, lanes]).astype(BF16)
        hidden_ref[:, lanes] = hidden
        value = hidden.astype(F32)
        squares += value * value
    here = pl.ds(pl.multiple_of(lax.axis_index("exp") * span, span), span)
    weights = router_ref[:, here].astype(F32) * moe_gain_ref[:, here]
    first = weights.astype(BF16)
    second = (weights - first.astype(F32)).astype(BF16)
    third = (weights - first.astype(F32) - second.astype(F32)).astype(BF16)
    products = lax.dot_general(
        hidden_ref[...],
        jnp.concatenate([first, second, third, jnp.zeros_like(first)], axis=0),
        (((1,), (1,)), ((), ())),
        preferred_element_type=F32,
    ).T
    count = weights.shape[0]
    logits = products[:count] + products[count : 2 * count] + products[2 * count : 3 * count]
    expert = lax.broadcasted_iota(jnp.int32, logits.shape, 0)
    for choice in range(2):
        here = slice(choice, choice + 1)
        chosen = jnp.where(route_ref[here, :] == expert, logits, 0.0)
        sums_ref[here, :] = jnp.sum(chosen, axis=0, keepdims=True)
    sums_ref[2:3, :] = jnp.sum(squares.T, axis=0, keepdims=True)
    sums_ref[3:, :] = jnp.zeros((sums_ref.shape[0] - 3, length), F32)


def hidden_block(
    running, query_rows, own, other, residual, gain, moe_gain, router, routes, kept, swapped
):
    heads, length = running.shape
    wide = query_rows.shape[1]
    return pl.pallas_call(
        hidden_kernel,
        out_shape=(
            jax.ShapeDtypeStruct((length, wide), BF16),
            jax.ShapeDtypeStruct((8, length), F32),
        ),
        in_specs=[VMEM] * (9 + 2 * CHUNKS),
        out_specs=(VMEM, VMEM),
        compiler_params=grant(16),
        cost_estimate=pl.CostEstimate(
            flops=2 * length * wide * (wide // heads),
            bytes_accessed=12 * length * wide,
            transcendentals=0,
        ),
    )(
        running, query_rows, own, other, residual, gain, moe_gain, router, routes, *kept, *swapped
    )


def expert_kernel(order_ref, gain_ref, gate_ref, up_ref, down_ref, *refs):
    *units, out_ref, square_ref, scaled_ref, hidden_ref = refs
    width = gate_ref.shape[0]
    count = order_ref.shape[0]
    steps = count // 2
    capacity = scaled_ref.shape[0] // count
    quarter = width // 4

    pieces = [(steps, 0, units[steps]), (steps, 1, units[steps + 1])]
    for position, unit in [*enumerate(units[:steps]), *enumerate(units[steps + 2 :], steps + 1)]:
        for side in range(2):
            pieces.append((position, side, unit.at[:, side * quarter : (side + 1) * quarter]))

    def block_of(position):
        return order_ref[lax.axis_index("seq"), position]

    def rows_of(position):
        first = block_of(position) // 2 * (2 * capacity)
        return pl.ds(pl.multiple_of(first, 2 * capacity), 2 * capacity)

    square_ref[...] = jnp.zeros_like(square_ref)
    for position, side, piece in pieces:
        value = piece[...].astype(F32)
        square = jnp.sum(value * value, axis=1, keepdims=True)
        square_ref[rows_of(position), :] += jnp.broadcast_to(square, (2 * capacity, 128))
        first = ((lax.axis_index("exp") ^ side) * 2 + block_of(position) % 2) * quarter
        lanes = pl.ds(pl.multiple_of(first, quarter), quarter)
        scaled_ref[rows_of(position), lanes] = (value * gain_ref[:, lanes]).astype(BF16)
    inverse = lax.rsqrt(square_ref[...][:, :1] / width + 1e-06)

    chunks = [slice(part * quarter, (part + 1) * quarter) for part in range(4)]
    gate_part, up_part = (0.0, 0.0)
    for lanes in chunks:
        rows = scaled_ref[:, lanes]
        gate_part += jnp.dot(rows, gate_ref[lanes], preferred_element_type=F32)
        up_part += jnp.dot(rows, up_ref[lanes], preferred_element_type=F32)
    gate_part, up_part = (gate_part * inverse, up_part * inverse)
    hidden_ref[...] = (jax.nn.silu(gate_part) * up_part).astype(BF16)
    hidden = jnp.concatenate(
        [
            hidden_ref[pl.ds(pl.multiple_of(block_of(position) * capacity, capacity), capacity)]
            for position in range(count)
        ],
        axis=0,
    )
    for lanes in chunks:
        out_ref[:, lanes] = jnp.dot(hidden, down_ref[:, lanes], preferred_element_type=F32)


def expert_rows(order, gain, units, gate_weight, up_weight, down_weight):
    width, hidden_units = gate_weight.shape
    rows = order.shape[0] * CAP
    return pl.pallas_call(
        expert_kernel,
        out_shape=jax.ShapeDtypeStruct((rows, width), F32),
        in_specs=[SMEM] + [VMEM] * (4 + len(units)),
        out_specs=VMEM,
        scratch_shapes=[
            pltpu.VMEM((rows, 128), F32),
            pltpu.VMEM((rows, width), BF16),
            pltpu.VMEM((rows, hidden_units), BF16),
        ],
        compiler_params=grant(max(16, rows // 16)),
        cost_estimate=pl.CostEstimate(
            flops=6 * rows * width * hidden_units,
            bytes_accessed=6 * width * hidden_units,
            transcendentals=0,
        ),
    )(order, gain, gate_weight, up_weight, down_weight, *units)


def total_kernel(own_ref, left_ref, right_ref, kept_ref, sent_ref):
    span = kept_ref.shape[1]
    for side, out_ref in enumerate((kept_ref, sent_ref)):
        lanes = pl.ds(pl.multiple_of((lax.axis_index("exp") ^ side) * span, span), span)
        total = own_ref[:, lanes] + left_ref[:, lanes].astype(F32) + right_ref[:, lanes].astype(F32)
        out_ref[...] = total.astype(BF16)


def expert_total(own, from_left, from_right):
    rows, width = own.shape
    shape = jax.ShapeDtypeStruct((rows, width // 2), BF16)
    return pl.pallas_call(
        total_kernel,
        out_shape=(shape, shape),
        in_specs=[VMEM] * 3,
        out_specs=(VMEM, VMEM),
        compiler_params=grant(4),
        cost_estimate=pl.CostEstimate(
            flops=2 * rows * width, bytes_accessed=10 * rows * width, transcendentals=0
        ),
    )(own, from_left, from_right)


def share_kernel(span, sums_ref, got_sums_ref, route_ref, slot_ref, table_ref):
    capacity = table_ref.shape[1] // 4
    sums = sums_ref[...] + got_sums_ref[...]
    inverse = lax.rsqrt(sums[2:3] / (2 * span) + 1e-06)
    gates = jax.nn.sigmoid(sums[:2] * inverse)
    shares = gates / jnp.sum(gates, axis=0, keepdims=True)
    table = slots_of(route_ref, slot_ref, capacity, (shares[:1], shares[1:]))
    table = as_columns(table)[:, : 2 * capacity]
    high = table.astype(BF16)
    low = (table - high.astype(F32)).astype(BF16)
    table_ref[...] = jnp.concatenate([high, low], axis=1)


def share_table(span, sums, got_sums, routes, slots):
    return pl.pallas_call(
        functools.partial(share_kernel, span),
        out_shape=jax.ShapeDtypeStruct((routes.shape[1], 4 * CAP), BF16),
        in_specs=[VMEM] * 4,
        out_specs=VMEM,
        compiler_params=grant(4),
    )(sums, got_sums, routes, slots)


def mixed_kernel(table_ref, hidden_ref, own_ref, got_ref, out_ref, held_ref, sems):
    span = own_ref.shape[1]
    copies = []
    for part in range(4):
        lanes = slice(part * span // 4, (part + 1) * span // 4)
        outs = jnp.concatenate([own_ref[:, lanes], got_ref[:, lanes]] * 2, axis=0)
        mixed = jnp.dot(table_ref[...], outs, preferred_element_type=F32)
        held_ref[:, lanes] = (hidden_ref[:, lanes].astype(F32) + mixed).astype(BF16)
        copies.append(
            pltpu.make_async_copy(held_ref.at[:, lanes], out_ref.at[:, lanes], sems.at[part])
        )
        copies[-1].start()
    for copy in copies:
        copy.wait()


def mixed_block(table, hidden, own, got):
    return pl.pallas_call(
        mixed_kernel,
        out_shape=jax.ShapeDtypeStruct(hidden.shape, BF16),
        in_specs=[VMEM] * 4,
        out_specs=HBM,
        scratch_shapes=[pltpu.VMEM(hidden.shape, BF16), pltpu.SemaphoreType.DMA((4,))],
        compiler_params=grant(8),
        cost_estimate=pl.CostEstimate(
            flops=8 * hidden.size * own.shape[0],
            bytes_accessed=4 * hidden.size,
            transcendentals=0,
        ),
    )(table, hidden, own, got)


def after(value, *others):
    return lax.optimization_barrier((value, *others))[0]


def entering_state(odd, states, sending, block_total, aside, share, finish):
    count = lax.axis_size("seq")
    swap = [(i, i ^ 1) for i in range(count)]
    rows, width = states[0].shape
    part = rows // width
    half = part * CHUNKS
    total_own = jnp.where(odd, block_total[half:], block_total[:half])
    even_decays, pair_decays, even_states, pair_states, sents, marks = ([], [], [], [], [], [])
    for chunk in range(CHUNKS):
        arrived = after(lax.ppermute(sending[chunk], "seq", swap), *marks)
        if chunk == 0:
            total_other = jnp.sum(arrived[rows : rows + 3, :half].astype(F32), axis=0)
            even_decay = jnp.exp(jnp.where(odd, total_other, total_own))[:, None, None]
            odd_decay = jnp.exp(jnp.where(odd, total_own, total_other))[:, None, None]
        place = slice(chunk * part, (chunk + 1) * part)
        own = states[chunk].reshape(part, width, width)
        arrived = arrived[:rows].astype(F32).reshape(part, width, width)
        even_states.append(jnp.where(odd, arrived, own))
        odd_state = jnp.where(odd, own, arrived)
        even_decays.append(even_decay[place])
        pair_decays.append(even_decay[place] * odd_decay[place])
        pair_states.append(odd_decay[place] * even_states[-1] + odd_state)
        sents.append(pair_states[-1].astype(BF16))
        marks = [sents[-1]]
        if chunk == 0:
            shared = share(sents[-1])
            marks = [*marks, *shared]
    shared = (after(shared[0], sents[-1]), shared[1])
    swapped = lax.ppermute(shared[0], "seq", swap)
    marks = [sents[-1], shared[0]]
    links = count // 2 - 1
    turn = max(links - 2, 0)
    befores = [jnp.zeros_like(state) for state in pair_states]
    finished = []
    for link in range(links):
        pairs = [(2 * link + k, 2 * link + 2 + k) for k in range(2)]
        gots = [lax.ppermute(sent, "seq", pairs) for sent in sents]
        if link == turn:
            result = aside(sents[-1])
            marks = [*marks, *result]
        for chunk in range(CHUNKS):
            got = after(gots[chunk], *marks).astype(F32)
            before = befores[chunk] = befores[chunk] + got
            if link < links - 1:
                sents[chunk] = (pair_decays[chunk] * before + pair_states[chunk]).astype(BF16)
                marks = [sents[chunk]]
            else:
                between = even_decays[chunk] * before + even_states[chunk]
                kept = jnp.where(odd, between, before).astype(BF16)
                moved = jnp.where(odd, before, between).astype(BF16)
                marks = [kept, moved]
            if link == links - 1:
                finished.append(finish(chunk, kept, moved, result[0], swapped))
                marks = [*marks, *finished[-1][:2]]
    return (finished, result[1], shared[1])


def ring_order(count):
    return list(range(0, count, 2)) + list(range(count - 1, 0, -2))


def ring_pairs(count):
    order = ring_order(count)
    right = [(order[i], order[(i + 1) % count]) for i in range(count)]
    return (right, [(b, a) for a, b in right])


def ring_blocks(count):
    order = ring_order(count)
    steps = count // 2
    offsets = [-k for k in range(steps + 1)] + list(range(1, steps))
    return jnp.array(
        [
            [order[(order.index(block) + offset) % count] for offset in offsets]
            for block in range(count)
        ],
        jnp.int32,
    )


def ring_gather(unit, *holds):
    count = lax.axis_size("seq")
    right, left = ring_pairs(count)
    middle = unit.shape[1] // 2
    from_left, from_right = ([], [])
    moving_right, moving_left = (unit, unit)
    for step in range(count // 2 - 1):
        hold = holds[step](moving_right) if step < len(holds) else ()
        moving_right = after(lax.ppermute(moving_right, "seq", right), moving_left, *hold)
        moving_left = after(lax.ppermute(moving_left, "seq", left), moving_right)
        from_left.append(moving_right)
        from_right.append(moving_left)
    far_left = after(lax.ppermute(moving_right[:, :middle], "seq", right), moving_left)
    far_right = lax.ppermute(moving_left[:, middle:], "seq", left)
    return [unit, *from_left, far_left, far_right, *from_right]


def ring_scatter(partial, rows, hold):
    count = lax.axis_size("seq")
    right, left = ring_pairs(count)
    middle = partial.shape[1] // 2
    steps = count // 2

    def piece(position):
        return partial[position * rows : (position + 1) * rows]

    far = piece(steps)
    to_left, to_right = (far[:, :middle].astype(BF16), far[:, middle:].astype(BF16))
    for step in range(steps - 1, -1, -1):
        marks = (to_right, hold) if step == steps - 1 else (to_right,)
        moving_left = after(lax.ppermute(to_left, "seq", left), *marks)
        arriving = lax.ppermute(to_right, "seq", right)
        if step == 0:
            return (piece(0), moving_left, arriving)
        to_left, to_right = (piece(step), piece(steps + step))
        if step == steps - 1:
            to_left = jnp.concatenate(
                [to_left[:, :middle] + moving_left.astype(F32), to_left[:, middle:]], axis=1
            )
        else:
            to_left = to_left + moving_left.astype(F32)
        to_left = to_left.astype(BF16)
        moving_right = after(arriving, to_left).astype(F32)
        if step == steps - 1:
            to_right = jnp.concatenate(
                [to_right[:, :middle], to_right[:, middle:] + moving_right], axis=1
            )
        else:
            to_right = to_right + moving_right
        to_right = to_right.astype(BF16)


def shards(
    queries,
    key_rows,
    values,
    log_decay,
    residual,
    attn_gain,
    moe_gain,
    router,
    routes,
    slot_pos,
    gate_weight,
    up_weight,
    down_weight,
):
    count = lax.axis_size("seq")
    exchange = [(0, 1), (1, 0)]
    swap = [(i, i ^ 1) for i in range(count)]
    log_rows, route_rows, slot_rows = (log_decay.T, routes.T, slot_pos.T)
    attn_gain, moe_gain = (attn_gain[None], moe_gain[None])
    odd = lax.axis_index("seq") % 2 == 1
    sending = half_state(True, after(log_rows, odd), key_rows, values)
    *states, running = half_state(False, after(log_rows, sending[0]), key_rows, values)

    def routed(sent, mark):
        within, pack = within_block(
            sent,
            running,
            after(queries, mark),
            key_rows,
            values,
            residual,
            route_rows,
            slot_rows,
        )
        return (pack, within)

    weights = (gate_weight, up_weight, down_weight)

    def finish(chunk, kept, moved, own, got):
        rows = pair_rows(chunk, own, got, attn_gain, kept, moved, weights)
        return (*rows, kept, lax.ppermute(moved, "seq", swap))

    finished, within_own, within_other = entering_state(
        odd,
        states,
        sending,
        running[:, -1],
        functools.partial(routed, False),
        functools.partial(routed, True),
        finish,
    )
    rows_mine, rows_sent, kept, swapped = zip(*finished, strict=True)
    rows_got = lax.ppermute(jnp.concatenate(rows_sent, axis=1), "exp", exchange)
    unit = jnp.concatenate([*rows_mine, after(rows_got, *swapped[:3])], axis=1)

    held = []

    def hold_hidden(mark):
        held.extend(
            hidden_block(
                running,
                queries,
                within_own,
                within_other,
                after(residual, mark),
                attn_gain,
                moe_gain,
                router.T,
                route_rows,
                kept,
                swapped,
            )
        )
        return held

    def hold_sums(mark):
        held.append(lax.ppermute(after(held[1], mark), "exp", exchange))
        return held[2:]

    units = ring_gather(unit, hold_hidden, hold_sums)
    hidden_half, sums, got_sums = held
    partial = expert_rows(
        ring_blocks(count), moe_gain, units, gate_weight[0], up_weight[0], down_weight[0]
    )
    table = share_table(queries.shape[1], sums, got_sums, route_rows, slot_rows)
    own, from_right, from_left = ring_scatter(partial, CAP, table)
    out_own, out_sent = expert_total(own, from_right, from_left)
    out_got = lax.ppermute(out_sent, "exp", exchange)
    return mixed_block(table, hidden_half, out_own, out_got)


def solution(mesh):
    placed = (
        P(("groups", "seq"), "exp"),
        P(("groups", "seq"), "exp"),
        P(("groups", "seq"), "exp"),
        P(("groups", "seq"), "exp"),
        P(("groups", "seq"), "exp"),
        P("exp"),
        P(),
        P(),
        P(("groups", "seq"), None),
        P(("groups", "seq"), None),
        P("exp", None, "seq"),
        P("exp", None, "seq"),
        P("exp", "seq", None),
    )
    return jax.shard_map(
        shards, mesh=mesh, in_specs=placed, out_specs=P(("groups", "seq"), "exp"), check_vma=False
    )
```

time: 114 us -> 99.7 us (0.87)
  waiting for transfers between devices: 49.4 us -> 34.8 us
  Pallas kernels: 12.4 us -> 20.2 us
  starting transfers between devices: 42.7 us -> 38.2 us
  matrix products: 2.77 us -> 0 us
    ppermute x17, waiting for transfers between devices: 39.5 us -> 26.8 us  [the longest x4 12.6 us: ring_scatter(): moving_left = after(lax.ppermute(to_left, 'seq', left), *marks)]
    pallas_call x5 -> x12, Pallas kernels: 12.4 us -> 20.2 us  [the longest x1 5.28 us: expert_rows(): pl.pallas_call(expert_kernel, out_shape=jax.ShapeDtypeStruct((rows, width...]
    ppermute x3, starting transfers between devices: 4.24 us -> 0.01 us  [ring_gather(): moving_left = after(lax.ppermute(moving_left, 'seq', left), moving_right)]
    ppermute x9, starting transfers between devices: 13.8 us -> 10.1 us  [entering_state(): gots = [lax.ppermute(sent, 'seq', pairs) for sent in sents]]
    ppermute x4, starting transfers between devices: 1.32 us -> 4.22 us  [ring_scatter(): arriving = lax.ppermute(to_right, 'seq', right)]
    dot_general x2 -> x0, matrix products: 2.77 us -> none  [the longest x1 1.73 us: shards(): expert_sum = jnp.dot(weighting, outs, precision=lax.Precision.HIGHEST)]
    ppermute x9, waiting for transfers between devices: 3.26 us -> 1.17 us  [entering_state(): gots = [lax.ppermute(sent, 'seq', pairs) for sent in sents]]
    ppermute x1, waiting for transfers between devices: 3.74 us -> 2.35 us  [ring_gather(): lax.ppermute(moving_right[:, :middle], 'seq', right)]
  transfers between devices with their start and end apart: 35 -> 35, of which waited for: 22 -> 20; matrix products, arithmetic and copies ran while one was open for 3% -> 2% of each run, Pallas kernels for 3% -> 11%
where the time goes in v4:
time: 99.7 us; the launch traced here: 99.3 us
  starting transfers between devices  38.2 us (38%)
  waiting for transfers between devices  34.8 us (35%)
  Pallas kernels  20.2 us (20%)
  local copies, waits for them, and re-layouts  3.12 us (3%)
  other arithmetic  2.24 us (2%)
    ppermute x4, waiting for transfers between devices, ring_scatter(): moving_left = after(lax.ppermute(to_left, 'seq', left), *marks)  12.6 us
    ppermute x9, starting transfers between devices, entering_state(): gots = [lax.ppermute(sent, 'seq', pairs) for sent in sents]  10.1 us
    ppermute x3, starting transfers between devices, ring_gather(): lax.ppermute(moving_right, 'seq', right)  8.12 us
    ppermute x3, waiting for transfers between devices, ring_gather(): lax.ppermute(moving_right, 'seq', right)  6.95 us
    pallas_call x1, Pallas kernels, expert_rows(): pl.pallas_call(expert_kernel, out_shape=jax.ShapeDtypeStruct((rows, width...  5.28 us
    ppermute x3, starting transfers between devices, entering_state(): arrived = after(lax.ppermute(sending[chunk], 'seq', swap), *marks)  5.08 us
    ppermute x4, starting transfers between devices, ring_scatter(): moving_left = after(lax.ppermute(to_left, 'seq', left), *marks)  4.98 us
    pallas_call x2, Pallas kernels, half_state(): pl.pallas_call(functools.partial(state_kernel, sent), out_shape=tuple(sha...  4.83 us
  transfers between devices with their start and end apart: 35, of which 20 were waited for; matrix products, arithmetic and copies ran while one was open for 2% of the time, Pallas kernels for 11%

profile of v4, /device:TPU:0, one launch (start us, length us, event | category | flops | bytes accessed | tf_op | source)
XLA Modules:
  0.0 99.3 jit_solution(13546128099956837865)
XLA Ops:
  0.0 3.1 %shard_map.136 = (bf16[528,128]{1,0:T(8,128)(2,1)}, bf16[512,128]{1,0:T(8,128)(2,1)}, bf16[512,128]{1,0:T(8,128)(2,1)}) custom-call(f32[24,128]{1,0:T(8,128)} %bitcast.31, bf16[128,3072]{1,0:T(8,128)(2,1)} %key_ref.7, bf16[128,3072]{1,0:T(8,128)(2,1)} %value_ref.7), custom_call_target="tpu_custom_call" | custom-call | flops 50331648 | bytes 786432 | tf_op jit(solution)/shard_map/pallas_call | solution.py:102
  3.1 3.1 %collective-permute-start = (bf16[528,128]{1,0:T(8,128)(2,1)}, bf16[528,128]{1,0:T(8,128)(2,1)S(1)}, u32[]{:S(2)}, u32[]{:S(2)}) collective-permute-start(bf16[528,128]{1,0:T(8,128)(2,1)} %get-tuple-element.60), channel_id=1, source_target_pairs={{0,2},{2,0},{4,6},{6,4},{8,10},{10,8},{12,14},{14,12},{1,3},{3,1},... | collective-permute-start | bytes 405512 | tf_op jit(solution)/shard_map/ppermute | solution.py:486
  6.2 1.9 %collective-permute-start.1 = (bf16[512,128]{1,0:T(8,128)(2,1)}, bf16[512,128]{1,0:T(8,128)(2,1)S(1)}, u32[]{:S(2)}, u32[]{:S(2)}) collective-permute-start(bf16[512,128]{1,0:T(8,128)(2,1)} %get-tuple-element.63), channel_id=1, source_target_pairs={{0,2},{2,0},{4,6},{6,4},{8,10},{10,8},{12,14},{14,12},{1,3},{3,1},... | collective-permute-start | bytes 393224 | tf_op jit(solution)/shard_map/ppermute | solution.py:486
  11.2 1.7 %shard_map.137 = (f32[512,128]{1,0:T(8,128)S(1)}, f32[512,128]{1,0:T(8,128)S(1)}, f32[512,128]{1,0:T(8,128)S(1)}, f32[24,128]{1,0:T(8,128)S(1)}) custom-call(f32[24,128]{1,0:T(8,128)S(1)} %bitcast.32, bf16[128,3072]{1,0:T(8,128)(2,1)S(1)} %copy-done, bf16[128,3072]{1,0:T(8,128)(2,1)S(1)} %copy-done.2), custom_call_target="tpu_custom_call" | custom-call | flops 50331648 | bytes 786432 | tf_op jit(solution)/shard_map/pallas_call | solution.py:102
  13.4 3.5 %collective-permute-start.5 = (bf16[4,128,128]{2,1,0:T(8,128)(2,1)S(1)}, bf16[4,128,128]{2,1,0:T(8,128)(2,1)S(1)}, u32[]{:S(2)}, u32[]{:S(2)}) collective-permute-start(bf16[4,128,128]{2,1,0:T(8,128)(2,1)S(1)} %get-tuple-element.117), channel_id=1, source_target_pairs={{0,4},{2,6},{1,5},{3,7},{16,20},{18,22},{17,21},{19,23}} | collective-permute-start | bytes 393224 | tf_op jit(solution)/shard_map/ppermute | solution.py:513
  16.9 2.2 %shard_map.138 = (f32[128,1536]{1,0:T(8,128)S(1)}, bf16[32,4736]{1,0:T(8,128)(2,1)S(1)}) custom-call(f32[24,128]{1,0:T(8,128)S(1)} %get-tuple-element.62.run_ref, bf16[128,3072]{1,0:T(8,128)(2,1)S(1)} %copy-done.4, bf16[128,3072]{1,0:T(8,128)(2,1)S(1)} %copy-done.1, bf16[128,3072]{1,0:T(8,128)(2,1)S(1)} %copy-done.3, bf16[128,3072]{1,0:T(8,128)(2,1)S(1)} %copy-done.5, ...), custom_call_target="tpu_custom_call" | custom-call | flops 100663296 | bytes 2359296 | tf_op jit(solution)/shard_map/pallas_call | solution.py:182
  26.2 2.2 %shard_map.139 = (f32[128,1536]{1,0:T(8,128)S(1)}, bf16[32,4736]{1,0:T(8,128)(2,1)S(1)}) custom-call(f32[24,128]{1,0:T(8,128)S(1)} %get-tuple-element.62.run_ref, bf16[128,3072]{1,0:T(8,128)(2,1)S(1)} %copy-done.4, bf16[128,3072]{1,0:T(8,128)(2,1)S(1)} %copy-done.1, bf16[128,3072]{1,0:T(8,128)(2,1)S(1)} %copy-done.3, bf16[128,3072]{1,0:T(8,128)(2,1)S(1)} %copy-done.5, ...), custom_call_target="tpu_custom_call" | custom-call | flops 100663296 | bytes 2359296 | tf_op jit(solution)/shard_map/pallas_call | solution.py:182
  32.1 1.6 %collective-permute-start.15 = (bf16[4,128,128]{2,1,0:T(8,128)(2,1)S(1)}, bf16[4,128,128]{2,1,0:T(8,128)(2,1)S(1)}, u32[]{:S(2)}, u32[]{:S(2)}) collective-permute-start(bf16[4,128,128]{2,1,0:T(8,128)(2,1)S(1)} %get-tuple-element.127.moved_ref), channel_id=1, source_target_pairs={{0,2},{2,0},{4,6},{6,4},{8,10},{10,8},{12,14},{14,12},{1,3},{3,1},... | collective-permute-start | bytes 393224 | tf_op jit(solution)/shard_map/ppermute | solution.py:650
  36.8 3.5 %collective-permute-done.16.refs_5_ = bf16[4,128,128]{2,1,0:T(8,128)(2,1)S(1)} collective-permute-done((bf16[4,128,128]{2,1,0:T(8,128)(2,1)S(1)}, bf16[4,128,128]{2,1,0:T(8,128)(2,1)S(1)}, u32[]{:S(2)}, u32[]{:S(2)}) %collective-permute-start.16) | collective-permute-done | bytes 131104 | tf_op jit(solution)/shard_map/ppermute | solution.py:650
  40.4 3.2 %collective-permute-start.17 = (bf16[32,3072]{1,0:T(8,128)(2,1)S(1)}, bf16[32,3072]{1,0:T(8,128)(2,1)S(1)}, u32[]{:S(2)}, u32[]{:S(2)}) collective-permute-start(bf16[32,3072]{1,0:T(8,128)(2,1)S(1)} %constant_dynamic-update-slice_fusion.refs_0_), channel_id=1, source_target_pairs={{0,4},{4,8},{8,12},{12,14},{14,10},{10,6},{6,2},{2,0},{1,5},{5,9},... | collective-permute-start | bytes 589832 | tf_op jit(solution)/shard_map/ppermute | solution.py:565
  43.5 2.9 %shard_map.143 = (bf16[128,3072]{1,0:T(8,128)(2,1)S(1)}, f32[8,128]{1,0:T(8,128)S(1)}) custom-call(f32[24,128]{1,0:T(8,128)S(1)} %get-tuple-element.62.run_ref, bf16[128,3072]{1,0:T(8,128)(2,1)S(1)} %copy-done.4, f32[128,1536]{1,0:T(8,128)S(1)} %get-tuple-element.78.own_ref, f32[128,1536]{1,0:T(8,128)S(1)} %get-tuple-element.68.other_ref, ...), custom_call_target="tpu_custom_call" | custom-call | flops 100663296 | bytes 4718592 | tf_op jit(solution)/shard_map/pallas_call | solution.py:305
  46.4 1.5 %collective-permute-done.17.refs_1_ = bf16[32,3072]{1,0:T(8,128)(2,1)S(1)} collective-permute-done((bf16[32,3072]{1,0:T(8,128)(2,1)S(1)}, bf16[32,3072]{1,0:T(8,128)(2,1)S(1)}, u32[]{:S(2)}, u32[]{:S(2)}) %collective-permute-start.17) | collective-permute-done | bytes 196640 | tf_op jit(solution)/shard_map/ppermute | solution.py:565
  47.9 2.5 %collective-permute-start.19 = (bf16[32,3072]{1,0:T(8,128)(2,1)S(1)}, bf16[32,3072]{1,0:T(8,128)(2,1)S(1)}, u32[]{:S(2)}, u32[]{:S(2)}) collective-permute-start(bf16[32,3072]{1,0:T(8,128)(2,1)S(1)} %collective-permute-done.17.refs_1_), channel_id=1, source_target_pairs={{0,4},{4,8},{8,12},{12,14},{14,10},{10,6},{6,2},{2,0},{1,5},{5,9},... | collective-permute-start | bytes 589832 | tf_op jit(solution)/shard_map/ppermute | solution.py:565
  51.6 2.0 %collective-permute-done.19.refs_2_ = bf16[32,3072]{1,0:T(8,128)(2,1)S(1)} collective-permute-done((bf16[32,3072]{1,0:T(8,128)(2,1)S(1)}, bf16[32,3072]{1,0:T(8,128)(2,1)S(1)}, u32[]{:S(2)}, u32[]{:S(2)}) %collective-permute-start.19) | collective-permute-done | bytes 196640 | tf_op jit(solution)/shard_map/ppermute | solution.py:565
  53.6 2.5 %collective-permute-start.21 = (bf16[32,3072]{1,0:T(8,128)(2,1)S(1)}, bf16[32,3072]{1,0:T(8,128)(2,1)S(1)}, u32[]{:S(2)}, u32[]{:S(2)}) collective-permute-start(bf16[32,3072]{1,0:T(8,128)(2,1)S(1)} %collective-permute-done.19.refs_2_), channel_id=1, source_target_pairs={{0,4},{4,8},{8,12},{12,14},{14,10},{10,6},{6,2},{2,0},{1,5},{5,9},... | collective-permute-start | bytes 589832 | tf_op jit(solution)/shard_map/ppermute | solution.py:565
  56.1 3.4 %collective-permute-done.21.refs_3_ = bf16[32,3072]{1,0:T(8,128)(2,1)S(1)} collective-permute-done((bf16[32,3072]{1,0:T(8,128)(2,1)S(1)}, bf16[32,3072]{1,0:T(8,128)(2,1)S(1)}, u32[]{:S(2)}, u32[]{:S(2)}) %collective-permute-start.21) | collective-permute-done | bytes 196640 | tf_op jit(solution)/shard_map/ppermute | solution.py:565
  59.5 2.3 %collective-permute-done.24.refs_8_ = bf16[32,3072]{1,0:T(8,128)(2,1)S(1)} collective-permute-done((bf16[32,3072]{1,0:T(8,128)(2,1)S(1)}, bf16[32,3072]{1,0:T(8,128)(2,1)S(1)}, u32[]{:S(2)}, u32[]{:S(2)}) %collective-permute-start.24) | collective-permute-done | bytes 196640 | tf_op jit(solution)/shard_map/ppermute | solution.py:566
  64.0 2.4 %collective-permute-done.23.refs_4_ = bf16[32,1536]{1,0:T(8,128)(2,1)S(1)} collective-permute-done((bf16[32,1536]{1,0:T(8,128)(2,1)S(1)}, bf16[32,1536]{1,0:T(8,128)(2,1)S(1)}, u32[]{:S(2)}, u32[]{:S(2)}) %collective-permute-start.23) | collective-permute-done | bytes 98336 | tf_op jit(solution)/shard_map/ppermute | solution.py:569
  67.6 5.3 %shard_map.145 = f32[128,6144]{1,0:T(8,128)S(1)} custom-call(s32[8,8]{1,0:T(8,128)S(1)} %copy-done.12, f32[1,6144]{1,0:T(1,128)S(1)} %bitcast.30, bf16[6144,768]{1,0:T(8,128)(2,1)S(1)} %bitcast.17, bf16[6144,768]{1,0:T(8,128)(2,1)S(1)} %bitcast.20, bf16[768,6144]{1,0:T(8,128)(2,1)S(1)} %bitcast.23, ...), custom_call_target="tpu_custom_call" | custom-call | flops 3623878656 | bytes 28311552 | tf_op jit(solution)/shard_map/pallas_call | solution.py:376
  75.4 2.3 %collective-permute-done.26 = bf16[16,3072]{1,0:T(8,128)(2,1)S(1)} collective-permute-done((bf16[16,3072]{1,0:T(8,128)(2,1)S(1)}, bf16[16,3072]{1,0:T(8,128)(2,1)S(1)}, u32[]{:S(2)}, u32[]{:S(2)}) %collective-permute-start.26) | collective-permute-done | bytes 98336 | tf_op jit(solution)/shard_map/ppermute | solution.py:587
  80.1 3.4 %collective-permute-done.27 = bf16[16,6144]{1,0:T(8,128)(2,1)S(1)} collective-permute-done((bf16[16,6144]{1,0:T(8,128)(2,1)S(1)}, bf16[16,6144]{1,0:T(8,128)(2,1)S(1)}, u32[]{:S(2)}, u32[]{:S(2)}) %collective-permute-start.27) | collective-permute-done | bytes 196640 | tf_op jit(solution)/shard_map/ppermute | solution.py:587
  85.9 3.4 %collective-permute-done.29 = bf16[16,6144]{1,0:T(8,128)(2,1)S(1)} collective-permute-done((bf16[16,6144]{1,0:T(8,128)(2,1)S(1)}, bf16[16,6144]{1,0:T(8,128)(2,1)S(1)}, u32[]{:S(2)}, u32[]{:S(2)}) %collective-permute-start.29) | collective-permute-done | bytes 196640 | tf_op jit(solution)/shard_map/ppermute | solution.py:587
  90.8 1.6 %collective-permute-start.33 = (bf16[16,6144]{1,0:T(8,128)(2,1)S(1)}, bf16[16,6144]{1,0:T(8,128)(2,1)S(1)}, u32[]{:S(2)}, u32[]{:S(2)}) collective-permute-start(bf16[16,6144]{1,0:T(8,128)(2,1)S(1)} %get-tuple-element.119), channel_id=1, source_target_pairs={{0,4},{4,8},{8,12},{12,14},{14,10},{10,6},{6,2},{2,0},{1,5},{5,9},... | collective-permute-start | bytes 589832 | tf_op jit(solution)/shard_map/ppermute | solution.py:588
  92.4 3.5 %collective-permute-done.31.left_ref = bf16[16,6144]{1,0:T(8,128)(2,1)S(1)} collective-permute-done((bf16[16,6144]{1,0:T(8,128)(2,1)S(1)}, bf16[16,6144]{1,0:T(8,128)(2,1)S(1)}, u32[]{:S(2)}, u32[]{:S(2)}) %collective-permute-start.31) | collective-permute-done | bytes 196640 | tf_op jit(solution)/shard_map/ppermute | solution.py:587
  (141 shorter events, 33.6 us)
Async XLA Ops:
  3.1 10.0 %collective-permute-start = (bf16[528,128]{1,0:T(8,128)(2,1)}, bf16[528,128]{1,0:T(8,128)(2,1)S(1)}, u32[]{:S(2)}, u32[]{:S(2)}) collective-permute-start(bf16[528,128]{1,0:T(8,128)(2,1)} %get-tuple-element.60), channel_id=1, source_target_pairs={{0,2},{2,0},{4,6},{6,4},{8,10},{10,8},{12,14},{14,12},{1,3},{3,1},... | collective-permute-start | bytes 405512 | tf_op jit(solution)/shard_map/ppermute | solution.py:486
  6.2 13.0 %collective-permute-start.2 = (bf16[512,128]{1,0:T(8,128)(2,1)}, bf16[512,128]{1,0:T(8,128)(2,1)S(1)}, u32[]{:S(2)}, u32[]{:S(2)}) collective-permute-start(bf16[512,128]{1,0:T(8,128)(2,1)} %get-tuple-element.64), channel_id=1, source_target_pairs={{0,2},{2,0},{4,6},{6,4},{8,10},{10,8},{12,14},{14,12},{1,3},{3,1},... | collective-permute-start | bytes 393224 | tf_op jit(solution)/shard_map/ppermute | solution.py:486
  6.2 14.4 %collective-permute-start.1 = (bf16[512,128]{1,0:T(8,128)(2,1)}, bf16[512,128]{1,0:T(8,128)(2,1)S(1)}, u32[]{:S(2)}, u32[]{:S(2)}) collective-permute-start(bf16[512,128]{1,0:T(8,128)(2,1)} %get-tuple-element.63), channel_id=1, source_target_pairs={{0,2},{2,0},{4,6},{6,4},{8,10},{10,8},{12,14},{14,12},{1,3},{3,1},... | collective-permute-start | bytes 393224 | tf_op jit(solution)/shard_map/ppermute | solution.py:486
  13.4 9.3 %collective-permute-start.5 = (bf16[4,128,128]{2,1,0:T(8,128)(2,1)S(1)}, bf16[4,128,128]{2,1,0:T(8,128)(2,1)S(1)}, u32[]{:S(2)}, u32[]{:S(2)}) collective-permute-start(bf16[4,128,128]{2,1,0:T(8,128)(2,1)S(1)} %get-tuple-element.117), channel_id=1, source_target_pairs={{0,4},{2,6},{1,5},{3,7},{16,20},{18,22},{17,21},{19,23}} | collective-permute-start | bytes 393224 | tf_op jit(solution)/shard_map/ppermute | solution.py:513
  19.3 4.7 %collective-permute-start.4 = (bf16[4,128,128]{2,1,0:T(8,128)(2,1)S(1)}, bf16[4,128,128]{2,1,0:T(8,128)(2,1)S(1)}, u32[]{:S(2)}, u32[]{:S(2)}) collective-permute-start(bf16[4,128,128]{2,1,0:T(8,128)(2,1)S(1)} %get-tuple-element.115), channel_id=1, source_target_pairs={{0,4},{2,6},{1,5},{3,7},{16,20},{18,22},{17,21},{19,23}} | collective-permute-start | bytes 393224 | tf_op jit(solution)/shard_map/ppermute | solution.py:513
  22.1 9.4 %collective-permute-start.6 = (bf16[32,4736]{1,0:T(8,128)(2,1)S(1)}, bf16[32,4736]{1,0:T(8,128)(2,1)S(1)}, u32[]{:S(2)}, u32[]{:S(2)}) collective-permute-start(bf16[32,4736]{1,0:T(8,128)(2,1)S(1)} %get-tuple-element.73), channel_id=1, source_target_pairs={{0,2},{2,0},{4,6},{6,4},{8,10},{10,8},{12,14},{14,12},{1,3},{3,1},... | collective-permute-start | bytes 909320 | tf_op jit(solution)/shard_map/ppermute | solution.py:505
  22.8 5.6 %collective-permute-start.7 = (bf16[4,128,128]{2,1,0:T(8,128)(2,1)S(1)}, bf16[4,128,128]{2,1,0:T(8,128)(2,1)S(1)}, u32[]{:S(2)}, u32[]{:S(2)}) collective-permute-start(bf16[4,128,128]{2,1,0:T(8,128)(2,1)S(1)} %fusion.5), channel_id=1, source_target_pairs={{4,8},{6,10},{5,9},{7,11},{20,24},{22,26},{21,25},{23,27}} | collective-permute-start | bytes 393224 | tf_op jit(solution)/shard_map/ppermute | solution.py:513
  24.1 5.1 %collective-permute-start.10 = (bf16[4,128,128]{2,1,0:T(8,128)(2,1)S(1)}, bf16[4,128,128]{2,1,0:T(8,128)(2,1)S(1)}, u32[]{:S(2)}, u32[]{:S(2)}) collective-permute-start(bf16[4,128,128]{2,1,0:T(8,128)(2,1)S(1)} %fusion.7), channel_id=1, source_target_pairs={{4,8},{6,10},{5,9},{7,11},{20,24},{22,26},{21,25},{23,27}} | collective-permute-start | bytes 393224 | tf_op jit(solution)/shard_map/ppermute | solution.py:513
  31.0 9.4 %collective-permute-start.14 = (bf16[4,128,128]{2,1,0:T(8,128)(2,1)S(1)}, bf16[4,128,128]{2,1,0:T(8,128)(2,1)S(1)}, u32[]{:S(2)}, u32[]{:S(2)}) collective-permute-start(bf16[4,128,128]{2,1,0:T(8,128)(2,1)S(1)} %get-tuple-element.129.moved_ref), channel_id=1, source_target_pairs={{0,2},{2,0},{4,6},{6,4},{8,10},{10,8},{12,14},{14,12},{1,3},{3,1},... | collective-permute-start | bytes 393224 | tf_op jit(solution)/shard_map/ppermute | solution.py:650
  32.1 8.2 %collective-permute-start.15 = (bf16[4,128,128]{2,1,0:T(8,128)(2,1)S(1)}, bf16[4,128,128]{2,1,0:T(8,128)(2,1)S(1)}, u32[]{:S(2)}, u32[]{:S(2)}) collective-permute-start(bf16[4,128,128]{2,1,0:T(8,128)(2,1)S(1)} %get-tuple-element.127.moved_ref), channel_id=1, source_target_pairs={{0,2},{2,0},{4,6},{6,4},{8,10},{10,8},{12,14},{14,12},{1,3},{3,1},... | collective-permute-start | bytes 393224 | tf_op jit(solution)/shard_map/ppermute | solution.py:650
  34.3 6.0 %collective-permute-start.16 = (bf16[4,128,128]{2,1,0:T(8,128)(2,1)S(1)}, bf16[4,128,128]{2,1,0:T(8,128)(2,1)S(1)}, u32[]{:S(2)}, u32[]{:S(2)}) collective-permute-start(bf16[4,128,128]{2,1,0:T(8,128)(2,1)S(1)} %get-tuple-element.125.moved_ref), channel_id=1, source_target_pairs={{0,2},{2,0},{4,6},{6,4},{8,10},{10,8},{12,14},{14,12},{1,3},{3,1},... | collective-permute-start | bytes 393224 | tf_op jit(solution)/shard_map/ppermute | solution.py:650
  40.4 7.6 %collective-permute-start.17 = (bf16[32,3072]{1,0:T(8,128)(2,1)S(1)}, bf16[32,3072]{1,0:T(8,128)(2,1)S(1)}, u32[]{:S(2)}, u32[]{:S(2)}) collective-permute-start(bf16[32,3072]{1,0:T(8,128)(2,1)S(1)} %constant_dynamic-update-slice_fusion.refs_0_), channel_id=1, source_target_pairs={{0,4},{4,8},{8,12},{12,14},{14,10},{10,6},{6,2},{2,0},{1,5},{5,9},... | collective-permute-start | bytes 589832 | tf_op jit(solution)/shard_map/ppermute | solution.py:565
  43.5 6.9 %collective-permute-start.20 = (bf16[32,3072]{1,0:T(8,128)(2,1)S(1)}, bf16[32,3072]{1,0:T(8,128)(2,1)S(1)}, u32[]{:S(2)}, u32[]{:S(2)}) collective-permute-start(bf16[32,3072]{1,0:T(8,128)(2,1)S(1)} %constant_dynamic-update-slice_fusion.refs_0_), channel_id=1, source_target_pairs={{4,0},{8,4},{12,8},{14,12},{10,14},{6,10},{2,6},{0,2},{5,1},{9,5},... | collective-permute-start | bytes 589832 | tf_op jit(solution)/shard_map/ppermute | solution.py:566
  47.9 5.7 %collective-permute-start.19 = (bf16[32,3072]{1,0:T(8,128)(2,1)S(1)}, bf16[32,3072]{1,0:T(8,128)(2,1)S(1)}, u32[]{:S(2)}, u32[]{:S(2)}) collective-permute-start(bf16[32,3072]{1,0:T(8,128)(2,1)S(1)} %collective-permute-done.17.refs_1_), channel_id=1, source_target_pairs={{0,4},{4,8},{8,12},{12,14},{14,10},{10,6},{6,2},{2,0},{1,5},{5,9},... | collective-permute-start | bytes 589832 | tf_op jit(solution)/shard_map/ppermute | solution.py:565
  50.4 5.7 %collective-permute-start.22 = (bf16[32,3072]{1,0:T(8,128)(2,1)S(1)}, bf16[32,3072]{1,0:T(8,128)(2,1)S(1)}, u32[]{:S(2)}, u32[]{:S(2)}) collective-permute-start(bf16[32,3072]{1,0:T(8,128)(2,1)S(1)} %collective-permute-done.20.refs_6_), channel_id=1, source_target_pairs={{4,0},{8,4},{12,8},{14,12},{10,14},{6,10},{2,6},{0,2},{5,1},{9,5},... | collective-permute-start | bytes 589832 | tf_op jit(solution)/shard_map/ppermute | solution.py:566
  53.6 5.9 %collective-permute-start.21 = (bf16[32,3072]{1,0:T(8,128)(2,1)S(1)}, bf16[32,3072]{1,0:T(8,128)(2,1)S(1)}, u32[]{:S(2)}, u32[]{:S(2)}) collective-permute-start(bf16[32,3072]{1,0:T(8,128)(2,1)S(1)} %collective-permute-done.19.refs_2_), channel_id=1, source_target_pairs={{0,4},{4,8},{8,12},{12,14},{14,10},{10,6},{6,2},{2,0},{1,5},{5,9},... | collective-permute-start | bytes 589832 | tf_op jit(solution)/shard_map/ppermute | solution.py:565
  56.1 5.7 %collective-permute-start.24 = (bf16[32,3072]{1,0:T(8,128)(2,1)S(1)}, bf16[32,3072]{1,0:T(8,128)(2,1)S(1)}, u32[]{:S(2)}, u32[]{:S(2)}) collective-permute-start(bf16[32,3072]{1,0:T(8,128)(2,1)S(1)} %collective-permute-done.22.refs_7_), channel_id=1, source_target_pairs={{4,0},{8,4},{12,8},{14,12},{10,14},{6,10},{2,6},{0,2},{5,1},{9,5},... | collective-permute-start | bytes 589832 | tf_op jit(solution)/shard_map/ppermute | solution.py:566
  62.6 4.8 %collective-permute-start.25 = (bf16[32,1536]{1,0:T(8,128)(2,1)S(1)}, bf16[32,1536]{1,0:T(8,128)(2,1)S(1)}, u32[]{:S(2)}, u32[]{:S(2)}) collective-permute-start(bf16[32,1536]{1,0:T(8,128)(2,1)S(1)} %slice.110), channel_id=1, source_target_pairs={{4,0},{8,4},{12,8},{14,12},{10,14},{6,10},{2,6},{0,2},{5,1},{9,5},... | collective-permute-start | bytes 294920 | tf_op jit(solution)/shard_map/ppermute | solution.py:570
  77.8 5.7 %collective-permute-start.27 = (bf16[16,6144]{1,0:T(8,128)(2,1)S(1)}, bf16[16,6144]{1,0:T(8,128)(2,1)S(1)}, u32[]{:S(2)}, u32[]{:S(2)}) collective-permute-start(bf16[16,6144]{1,0:T(8,128)(2,1)S(1)} %pad_maximum_fusion), channel_id=1, source_target_pairs={{4,0},{8,4},{12,8},{14,12},{10,14},{6,10},{2,6},{0,2},{5,1},{9,5},... | collective-permute-start | bytes 589832 | tf_op jit(solution)/shard_map/ppermute | solution.py:587
  79.3 5.7 %collective-permute-start.30 = (bf16[16,6144]{1,0:T(8,128)(2,1)S(1)}, bf16[16,6144]{1,0:T(8,128)(2,1)S(1)}, u32[]{:S(2)}, u32[]{:S(2)}) collective-permute-start(bf16[16,6144]{1,0:T(8,128)(2,1)S(1)} %pad_maximum_fusion.1), channel_id=1, source_target_pairs={{0,4},{4,8},{8,12},{12,14},{14,10},{10,6},{6,2},{2,0},{1,5},{5,9},... | collective-permute-start | bytes 589832 | tf_op jit(solution)/shard_map/ppermute | solution.py:588
  83.6 5.7 %collective-permute-start.29 = (bf16[16,6144]{1,0:T(8,128)(2,1)S(1)}, bf16[16,6144]{1,0:T(8,128)(2,1)S(1)}, u32[]{:S(2)}, u32[]{:S(2)}) collective-permute-start(bf16[16,6144]{1,0:T(8,128)(2,1)S(1)} %fusion.2), channel_id=1, source_target_pairs={{4,0},{8,4},{12,8},{14,12},{10,14},{6,10},{2,6},{0,2},{5,1},{9,5},... | collective-permute-start | bytes 589832 | tf_op jit(solution)/shard_map/ppermute | solution.py:587
  85.0 5.7 %collective-permute-start.32 = (bf16[16,6144]{1,0:T(8,128)(2,1)S(1)}, bf16[16,6144]{1,0:T(8,128)(2,1)S(1)}, u32[]{:S(2)}, u32[]{:S(2)}) collective-permute-start(bf16[16,6144]{1,0:T(8,128)(2,1)S(1)} %fusion.1), channel_id=1, source_target_pairs={{0,4},{4,8},{8,12},{12,14},{14,10},{10,6},{6,2},{2,0},{1,5},{5,9},... | collective-permute-start | bytes 589832 | tf_op jit(solution)/shard_map/ppermute | solution.py:588
  89.4 6.5 %collective-permute-start.31 = (bf16[16,6144]{1,0:T(8,128)(2,1)S(1)}, bf16[16,6144]{1,0:T(8,128)(2,1)S(1)}, u32[]{:S(2)}, u32[]{:S(2)}) collective-permute-start(bf16[16,6144]{1,0:T(8,128)(2,1)S(1)} %fusion.3), channel_id=1, source_target_pairs={{4,0},{8,4},{12,8},{14,12},{10,14},{6,10},{2,6},{0,2},{5,1},{9,5},... | collective-permute-start | bytes 589832 | tf_op jit(solution)/shard_map/ppermute | solution.py:587
  90.8 5.7 %collective-permute-start.33 = (bf16[16,6144]{1,0:T(8,128)(2,1)S(1)}, bf16[16,6144]{1,0:T(8,128)(2,1)S(1)}, u32[]{:S(2)}, u32[]{:S(2)}) collective-permute-start(bf16[16,6144]{1,0:T(8,128)(2,1)S(1)} %get-tuple-element.119), channel_id=1, source_target_pairs={{0,4},{4,8},{8,12},{12,14},{14,10},{10,6},{6,2},{2,0},{1,5},{5,9},... | collective-permute-start | bytes 589832 | tf_op jit(solution)/shard_map/ppermute | solution.py:588
  (33 other events, 466.3 us)

commit v5 on v4

--- a/solution.py
+++ b/solution.py
@@ -321,98 +321,140 @@
     )
 
 
-def expert_kernel(order_ref, gain_ref, gate_ref, up_ref, down_ref, *refs):
-    *units, out_ref, square_ref, scaled_ref, hidden_ref = refs
-    width = gate_ref.shape[0]
-    count = order_ref.shape[0]
-    steps = count // 2
-    capacity = scaled_ref.shape[0] // count
-    quarter = width // 4
-
-    pieces = [(steps, 0, units[steps]), (steps, 1, units[steps + 1])]
-    for position, unit in [*enumerate(units[:steps]), *enumerate(units[steps + 2 :], steps + 1)]:
-        for side in range(2):
-            pieces.append((position, side, unit.at[:, side * quarter : (side + 1) * quarter]))
-
-    def block_of(position):
-        return order_ref[lax.axis_index("seq"), position]
-
-    def rows_of(position):
-        first = block_of(position) // 2 * (2 * capacity)
-        return pl.ds(pl.multiple_of(first, 2 * capacity), 2 * capacity)
-
-    square_ref[...] = jnp.zeros_like(square_ref)
-    for position, side, piece in pieces:
+def place_pieces(places, gain_ref, pieces, scaled_ref, square_ref):
+    quarter = scaled_ref.shape[1] // 4
+    for (position, side), piece in zip(places, pieces, strict=True):
+        height = piece.shape[0]
+        block = ring_block(2 * scaled_ref.shape[0] // height, position)
+        rows = pl.ds(pl.multiple_of(block // 2 * height, height), height)
+        first = ((lax.axis_index("exp") ^ side) * 2 + block % 2) * quarter
+        lanes = pl.ds(pl.multiple_of(first, quarter), quarter)
         value = piece[...].astype(F32)
         square = jnp.sum(value * value, axis=1, keepdims=True)
-        square_ref[rows_of(position), :] += jnp.broadcast_to(square, (2 * capacity, 128))
-        first = ((lax.axis_index("exp") ^ side) * 2 + block_of(position) % 2) * quarter
-        lanes = pl.ds(pl.multiple_of(first, quarter), quarter)
-        scaled_ref[rows_of(position), lanes] = (value * gain_ref[:, lanes]).astype(BF16)
+        square_ref[rows, :] += jnp.broadcast_to(square, (height, square_ref.shape[1]))
+        scaled_ref[rows, lanes] = (value * gain_ref[:, lanes]).astype(BF16)
+
+
+def early_kernel(places, gain_ref, *refs):
+    *pieces, scaled_ref, square_ref = refs
+    square_ref[...] = jnp.zeros_like(square_ref)
+    place_pieces(places, gain_ref, pieces, scaled_ref, square_ref)
+
+
+def early_rows(places, rows, gain, pieces):
+    return pl.pallas_call(
+        functools.partial(early_kernel, places),
+        out_shape=(
+            jax.ShapeDtypeStruct((rows, gain.shape[1]), BF16),
+            jax.ShapeDtypeStruct((rows, 128), F32),
+        ),
+        in_specs=[VMEM] * (1 + len(pieces)),
+        out_specs=(VMEM, VMEM),
+        compiler_params=grant(8),
+    )(gain, *pieces)
+
+
+def expert_kernel(places, gain_ref, gate_ref, up_ref, down_ref, early_ref, early_square_ref, *refs):
+    *pieces, out_ref, hidden_ref, scaled_ref, square_ref, block_ref = refs
+    width = gate_ref.shape[0]
+    capacity = CAP
+    count = scaled_ref.shape[0] // capacity
+    quarter = width // 4
+    scaled_ref[...] = early_ref[...]
+    square_ref[...] = early_square_ref[...]
+    place_pieces(places, gain_ref, pieces, scaled_ref, square_ref)
     inverse = lax.rsqrt(square_ref[...][:, :1] / width + 1e-06)
-
-    chunks = [slice(part * quarter, (part + 1) * quarter) for part in range(4)]
     gate_part, up_part = (0.0, 0.0)
-    for lanes in chunks:
+    for part in range(4):
+        lanes = slice(part * quarter, (part + 1) * quarter)
         rows = scaled_ref[:, lanes]
         gate_part += jnp.dot(rows, gate_ref[lanes], preferred_element_type=F32)
         up_part += jnp.dot(rows, up_ref[lanes], preferred_element_type=F32)
     gate_part, up_part = (gate_part * inverse, up_part * inverse)
-    hidden_ref[...] = (jax.nn.silu(gate_part) * up_part).astype(BF16)
-    hidden = jnp.concatenate(
-        [
-            hidden_ref[pl.ds(pl.multiple_of(block_of(position) * capacity, capacity), capacity)]
-            for position in range(count)
-        ],
-        axis=0,
-    )
-    for lanes in chunks:
+    block_ref[...] = (jax.nn.silu(gate_part) * up_part).astype(BF16)
+    for position in range(count):
+        block = ring_block(count, position)
+        hidden_ref[position * capacity : (position + 1) * capacity] = block_ref[
+            pl.ds(pl.multiple_of(block * capacity, capacity), capacity)
+        ]
+    hidden = hidden_ref[...]
+    for part in range(2):
+        lanes = slice(part * quarter, (part + 1) * quarter)
         out_ref[:, lanes] = jnp.dot(hidden, down_ref[:, lanes], preferred_element_type=F32)
 
 
-def expert_rows(order, gain, units, gate_weight, up_weight, down_weight):
+def expert_rows(places, gain, early, pieces, gate_weight, up_weight, down_weight):
     width, hidden_units = gate_weight.shape
-    rows = order.shape[0] * CAP
-    return pl.pallas_call(
-        expert_kernel,
-        out_shape=jax.ShapeDtypeStruct((rows, width), F32),
-        in_specs=[SMEM] + [VMEM] * (4 + len(units)),
-        out_specs=VMEM,
+    rows = early[0].shape[0]
+    return pl.pallas_call(
+        functools.partial(expert_kernel, places),
+        out_shape=(
+            jax.ShapeDtypeStruct((rows, width // 2), F32),
+            jax.ShapeDtypeStruct((rows, hidden_units), BF16),
+        ),
+        in_specs=[VMEM] * (6 + len(pieces)),
+        out_specs=(VMEM, VMEM),
         scratch_shapes=[
+            pltpu.VMEM((rows, width), BF16),
             pltpu.VMEM((rows, 128), F32),
-            pltpu.VMEM((rows, width), BF16),
             pltpu.VMEM((rows, hidden_units), BF16),
         ],
         compiler_params=grant(max(16, rows // 16)),
         cost_estimate=pl.CostEstimate(
-            flops=6 * rows * width * hidden_units,
-            bytes_accessed=6 * width * hidden_units,
+            flops=5 * rows * width * hidden_units,
+            bytes_accessed=5 * width * hidden_units,
             transcendentals=0,
         ),
-    )(order, gain, gate_weight, up_weight, down_weight, *units)
-
-
-def total_kernel(own_ref, left_ref, right_ref, kept_ref, sent_ref):
-    span = kept_ref.shape[1]
-    for side, out_ref in enumerate((kept_ref, sent_ref)):
-        lanes = pl.ds(pl.multiple_of((lax.axis_index("exp") ^ side) * span, span), span)
-        total = own_ref[:, lanes] + left_ref[:, lanes].astype(F32) + right_ref[:, lanes].astype(F32)
-        out_ref[...] = total.astype(BF16)
-
-
-def expert_total(own, from_left, from_right):
-    rows, width = own.shape
-    shape = jax.ShapeDtypeStruct((rows, width // 2), BF16)
+    )(gain, gate_weight, up_weight, down_weight, *early, *pieces)
+
+
+def rest_kernel(hidden_ref, down_ref, out_ref):
+    half = out_ref.shape[1]
+    for part in range(2):
+        lanes = slice(part * half // 2, (part + 1) * half // 2)
+        weights = down_ref[:, half + lanes.start : half + lanes.stop]
+        out_ref[:, lanes] = jnp.dot(hidden_ref[...], weights, preferred_element_type=F32)
+
+
+def expert_rest(hidden, down_weight):
+    rows, width = (hidden.shape[0], down_weight.shape[1])
+    return pl.pallas_call(
+        rest_kernel,
+        out_shape=jax.ShapeDtypeStruct((rows, width // 2), F32),
+        in_specs=[VMEM] * 2,
+        out_specs=VMEM,
+        compiler_params=grant(max(8, rows // 32)),
+        cost_estimate=pl.CostEstimate(
+            flops=rows * width * hidden.shape[1],
+            bytes_accessed=width * hidden.shape[1],
+            transcendentals=0,
+        ),
+    )(hidden, down_weight)
+
+
+def total_kernel(low_ref, high_ref, *refs):
+    *got_refs, kept_ref, sent_ref = refs
+    totals = []
+    for own_ref, first, second in ((low_ref, 0, 1), (high_ref, 2, 3)):
+        got = got_refs[first][...].astype(F32) + got_refs[second][...].astype(F32)
+        totals.append((own_ref[...] + got).astype(BF16))
+    low = lax.axis_index("exp") == 0
+    kept_ref[...] = jnp.where(low, totals[0], totals[1])
+    sent_ref[...] = jnp.where(low, totals[1], totals[0])
+
+
+def expert_total(low, high, *gots):
+    shape = jax.ShapeDtypeStruct(low.shape, BF16)
     return pl.pallas_call(
         total_kernel,
         out_shape=(shape, shape),
-        in_specs=[VMEM] * 3,
+        in_specs=[VMEM] * (2 + len(gots)),
         out_specs=(VMEM, VMEM),
         compiler_params=grant(4),
         cost_estimate=pl.CostEstimate(
-            flops=2 * rows * width, bytes_accessed=10 * rows * width, transcendentals=0
-        ),
-    )(own, from_left, from_right)
+            flops=4 * low.size, bytes_accessed=20 * low.size, transcendentals=0
+        ),
+    )(low, high, *gots)
 
 
 def share_kernel(span, sums_ref, got_sums_ref, route_ref, slot_ref, table_ref):
@@ -531,79 +573,83 @@
     return (finished, result[1], shared[1])
 
 
-def ring_order(count):
-    return list(range(0, count, 2)) + list(range(count - 1, 0, -2))
-
-
 def ring_pairs(count):
-    order = ring_order(count)
+    order = list(range(0, count, 2)) + list(range(count - 1, 0, -2))
     right = [(order[i], order[(i + 1) % count]) for i in range(count)]
     return (right, [(b, a) for a, b in right])
 
 
-def ring_blocks(count):
-    order = ring_order(count)
-    steps = count // 2
-    offsets = [-k for k in range(steps + 1)] + list(range(1, steps))
-    return jnp.array(
-        [
-            [order[(order.index(block) + offset) % count] for offset in offsets]
-            for block in range(count)
-        ],
-        jnp.int32,
-    )
-
-
-def ring_gather(unit, *holds):
-    count = lax.axis_size("seq")
-    right, left = ring_pairs(count)
-    middle = unit.shape[1] // 2
-    from_left, from_right = ([], [])
-    moving_right, moving_left = (unit, unit)
-    for step in range(count // 2 - 1):
-        hold = holds[step](moving_right) if step < len(holds) else ()
-        moving_right = after(lax.ppermute(moving_right, "seq", right), moving_left, *hold)
-        moving_left = after(lax.ppermute(moving_left, "seq", left), moving_right)
-        from_left.append(moving_right)
-        from_right.append(moving_left)
-    far_left = after(lax.ppermute(moving_right[:, :middle], "seq", right), moving_left)
-    far_right = lax.ppermute(moving_left[:, middle:], "seq", left)
-    return [unit, *from_left, far_left, far_right, *from_right]
-
-
-def ring_scatter(partial, rows, hold):
-    count = lax.axis_size("seq")
-    right, left = ring_pairs(count)
-    middle = partial.shape[1] // 2
-    steps = count // 2
-
-    def piece(position):
-        return partial[position * rows : (position + 1) * rows]
-
-    far = piece(steps)
-    to_left, to_right = (far[:, :middle].astype(BF16), far[:, middle:].astype(BF16))
-    for step in range(steps - 1, -1, -1):
-        marks = (to_right, hold) if step == steps - 1 else (to_right,)
-        moving_left = after(lax.ppermute(to_left, "seq", left), *marks)
-        arriving = lax.ppermute(to_right, "seq", right)
-        if step == 0:
-            return (piece(0), moving_left, arriving)
-        to_left, to_right = (piece(step), piece(steps + step))
-        if step == steps - 1:
-            to_left = jnp.concatenate(
-                [to_left[:, :middle] + moving_left.astype(F32), to_left[:, middle:]], axis=1
-            )
-        else:
-            to_left = to_left + moving_left.astype(F32)
-        to_left = to_left.astype(BF16)
-        moving_right = after(arriving, to_left).astype(F32)
-        if step == steps - 1:
-            to_right = jnp.concatenate(
-                [to_right[:, :middle], to_right[:, middle:] + moving_right], axis=1
-            )
-        else:
-            to_right = to_right + moving_right
-        to_right = to_right.astype(BF16)
+def ring_block(count, position):
+    block = lax.axis_index("seq")
+    here = jnp.where(block % 2 == 0, block // 2, count - 1 - block // 2)
+    offset = count - position if position <= count // 2 else position - count // 2
+    there = (here + offset) % count
+    return jnp.where(there < count // 2, 2 * there, 2 * (count - 1 - there) + 1)
+
+
+def ring_gather(halves, holds):
+    steps = lax.axis_size("seq") // 2
+    right, left = ring_pairs(2 * steps)
+    chains = [(0, right), (1, left), (1, right), (0, left)]
+    moving = [halves[half] for half, _ in chains]
+    brought = [list(halves)]
+    marks = list(halves)
+    for step in range(steps):
+        here = chains if step < steps - 1 else chains[:2]
+        gots = [lax.ppermute(moving[k], "seq", way) for k, (_, way) in enumerate(here)]
+        if step in holds:
+            marks = [*marks, *holds[step](brought)]
+        brought.append([])
+        for k, got in enumerate(gots):
+            moving[k] = after(got, *marks)
+            marks = [moving[k]]
+            brought[-1].append(moving[k])
+    return brought
+
+
+def ring_places(steps, step):
+    if step == 0:
+        return [(0, 0), (0, 1)]
+    to_left, to_right = (step, steps + step)
+    if step == steps:
+        return [(to_left, 0), (to_left, 1)]
+    return [(to_left, 0), (to_right, 1), (to_left, 1), (to_right, 0)]
+
+
+def ring_scatter(low, rest, rows, last):
+    steps = lax.axis_size("seq") // 2
+    right, left = ring_pairs(2 * steps)
+    partials = [low, None]
+
+    def piece(position, half):
+        return partials[half][position * rows : (position + 1) * rows]
+
+    chains = [
+        (0, left, [steps, *range(steps - 1, 0, -1)]),
+        (0, right, list(range(2 * steps - 1, steps, -1))),
+        (1, right, [steps, *range(2 * steps - 1, steps, -1)]),
+        (1, left, list(range(steps - 1, 0, -1))),
+    ]
+    sents = [piece(positions[0], 0).astype(BF16) for _, _, positions in chains[:2]]
+    partials[1] = rest(sents)
+    sents += [piece(positions[0], 1).astype(BF16) for _, _, positions in chains[2:]]
+    marks = list(sents)
+    for step in range(1, steps + 1):
+        gots = {
+            k: lax.ppermute(sents[k], "seq", way)
+            for k, (_, way, positions) in enumerate(chains)
+            if step <= len(positions)
+        }
+        if step == steps:
+            marks = [*marks, *last(marks)]
+        for k, got in gots.items():
+            half, _, positions = chains[k]
+            got = after(got, *marks)
+            if step < len(positions):
+                got = (piece(positions[step], half) + got.astype(F32)).astype(BF16)
+            sents[k] = got
+            marks = [got]
+    return (piece(0, 0), piece(0, 1), *sents)
 
 
 def shards(
@@ -660,18 +706,42 @@
     )
     rows_mine, rows_sent, kept, swapped = zip(*finished, strict=True)
     rows_got = lax.ppermute(jnp.concatenate(rows_sent, axis=1), "exp", exchange)
-    unit = jnp.concatenate([*rows_mine, after(rows_got, *swapped[:3])], axis=1)
+    halves = (jnp.concatenate(rows_mine, axis=1), after(rows_got, *swapped[:2]))
+
+    steps = count // 2
+    early = []
+
+    def places(first, last):
+        return sum([ring_places(steps, step) for step in range(first, last)], [])
+
+    def hold_rows(brought):
+        early.extend(early_rows(places(0, steps - 1), count * CAP, moe_gain, sum(brought, [])))
+        return early
+
+    brought = ring_gather(halves, {0: lambda brought: swapped, steps - 2: hold_rows})
+    low, hidden_units = expert_rows(
+        places(steps - 1, steps + 1),
+        moe_gain,
+        early,
+        sum(brought[steps - 1 :], []),
+        gate_weight[0],
+        up_weight[0],
+        down_weight[0],
+    )
+
+    def rest(marks):
+        return expert_rest(after(hidden_units, *marks), down_weight[0])
 
     held = []
 
-    def hold_hidden(mark):
+    def hold_hidden(marks):
         held.extend(
             hidden_block(
                 running,
                 queries,
                 within_own,
                 within_other,
-                after(residual, mark),
+                after(residual, *marks),
                 attn_gain,
                 moe_gain,
                 router.T,
@@ -682,18 +752,11 @@
         )
         return held
 
-    def hold_sums(mark):
-        held.append(lax.ppermute(after(held[1], mark), "exp", exchange))
-        return held[2:]
-
-    units = ring_gather(unit, hold_hidden, hold_sums)
-    hidden_half, sums, got_sums = held
-    partial = expert_rows(
-        ring_blocks(count), moe_gain, units, gate_weight[0], up_weight[0], down_weight[0]
-    )
+    sums_here = ring_scatter(low, rest, CAP, hold_hidden)
+    hidden_half, sums = held
+    got_sums = lax.ppermute(sums, "exp", exchange)
     table = share_table(queries.shape[1], sums, got_sums, route_rows, slot_rows)
-    own, from_right, from_left = ring_scatter(partial, CAP, table)
-    out_own, out_sent = expert_total(own, from_right, from_left)
+    out_own, out_sent = expert_total(*sums_here)
     out_got = lax.ppermute(out_sent, "exp", exchange)
     return mixed_block(table, hidden_half, out_own, out_got)
 

time: 99.7 us -> 90.4 us (0.907)
  waiting for transfers between devices: 34.8 us -> 13.9 us
  starting transfers between devices: 38.2 us -> 53.4 us
  local copies, waits for them, and re-layouts: 3.12 us -> 0.12 us
    ppermute x17 -> x29, waiting for transfers between devices: 27.5 us -> 13.3 us  [the longest x14 6.84 us: ring_gather(): lax.ppermute(moving[k], 'seq', way)]
    ppermute x17 -> x29, starting transfers between devices: 19.6 us -> 32.4 us  [the longest x14 17.7 us: ring_gather(): lax.ppermute(moving[k], 'seq', way)]
    ppermute x3, waiting for transfers between devices: 3.52 us -> 0.01 us  [finish(): return (*rows, kept, lax.ppermute(moved, 'seq', swap))]
    unnamed x47 -> x40, local copies, waits for them, and re-layouts: 3.07 us -> 0.09 us
    ppermute x1, waiting for transfers between devices: 1.29 us -> 0.01 us  [shards(): out_got = lax.ppermute(out_sent, 'exp', exchange)]
    ppermute x1, waiting for transfers between devices: 1.26 us -> 0.01 us  [shards(): rows_got = lax.ppermute(jnp.concatenate(rows_sent, axis=1), 'exp', exchange)]
    ppermute x9, waiting for transfers between devices: 1.17 us -> 0.02 us  [entering_state(): gots = [lax.ppermute(sent, 'seq', pairs) for sent in sents]]
    ppermute x1, starting transfers between devices: 0.57 us -> 1.58 us  [entering_state(): swapped = lax.ppermute(shared[0], 'seq', swap)]
  transfers between devices with their start and end apart: 35 -> 47, of which waited for: 20 -> 18; matrix products, arithmetic and copies ran while one was open for 2% -> 2% of each run, Pallas kernels for 11% -> 13%
where the time goes in v5:
time: 90.4 us; the launch traced here: 90.2 us
  starting transfers between devices  53.4 us (59%)
  Pallas kernels  19.8 us (22%)
  waiting for transfers between devices  13.9 us (15%)
  other arithmetic  2.19 us (2%)
    ppermute x14, starting transfers between devices, ring_gather(): lax.ppermute(moving[k], 'seq', way)  17.7 us
    ppermute x14, starting transfers between devices, ring_scatter(): lax.ppermute(sents[k], 'seq', way)  14.3 us
    ppermute x9, starting transfers between devices, entering_state(): gots = [lax.ppermute(sent, 'seq', pairs) for sent in sents]  10.6 us
    ppermute x14, waiting for transfers between devices, ring_gather(): lax.ppermute(moving[k], 'seq', way)  6.84 us
    ppermute x14, waiting for transfers between devices, ring_scatter(): lax.ppermute(sents[k], 'seq', way)  5.62 us
    ppermute x3, starting transfers between devices, entering_state(): arrived = after(lax.ppermute(sending[chunk], 'seq', swap), *marks)  5.14 us
    pallas_call x2, Pallas kernels, half_state(): pl.pallas_call(functools.partial(state_kernel, sent), out_shape=tuple(sha...  4.87 us
    pallas_call x2, Pallas kernels, within_block(): pl.pallas_call(functools.partial(within_kernel, sent), out_shape=(jax.Sha...  4.47 us
  transfers between devices with their start and end apart: 47, of which 18 were waited for; matrix products, arithmetic and copies ran while one was open for 2% of the time, Pallas kernels for 13%

profile of v5, /device:TPU:0, one launch (start us, length us, event | category | flops | bytes accessed | tf_op | source)
XLA Modules:
  0.0 90.2 jit_solution(322978401351192494)
XLA Ops:
  0.0 3.1 %shard_map.127 = (bf16[528,128]{1,0:T(8,128)(2,1)}, bf16[512,128]{1,0:T(8,128)(2,1)}, bf16[512,128]{1,0:T(8,128)(2,1)}) custom-call(f32[24,128]{1,0:T(8,128)} %bitcast.33, bf16[128,3072]{1,0:T(8,128)(2,1)} %key_ref.7, bf16[128,3072]{1,0:T(8,128)(2,1)} %value_ref.7), custom_call_target="tpu_custom_call" | custom-call | flops 50331648 | bytes 786432 | tf_op jit(solution)/shard_map/pallas_call | solution.py:102
  3.1 3.0 %collective-permute-start = (bf16[528,128]{1,0:T(8,128)(2,1)}, bf16[528,128]{1,0:T(8,128)(2,1)S(1)}, u32[]{:S(2)}, u32[]{:S(2)}) collective-permute-start(bf16[528,128]{1,0:T(8,128)(2,1)} %get-tuple-element.78), channel_id=1, source_target_pairs={{0,2},{2,0},{4,6},{6,4},{8,10},{10,8},{12,14},{14,12},{1,3},{3,1},... | collective-permute-start | bytes 405512 | tf_op jit(solution)/shard_map/ppermute | solution.py:528
  6.3 2.0 %collective-permute-start.1 = (bf16[512,128]{1,0:T(8,128)(2,1)}, bf16[512,128]{1,0:T(8,128)(2,1)S(1)}, u32[]{:S(2)}, u32[]{:S(2)}) collective-permute-start(bf16[512,128]{1,0:T(8,128)(2,1)} %get-tuple-element.81), channel_id=1, source_target_pairs={{0,2},{2,0},{4,6},{6,4},{8,10},{10,8},{12,14},{14,12},{1,3},{3,1},... | collective-permute-start | bytes 393224 | tf_op jit(solution)/shard_map/ppermute | solution.py:528
  8.3 1.8 %shard_map.128 = (f32[512,128]{1,0:T(8,128)S(1)}, f32[512,128]{1,0:T(8,128)S(1)}, f32[512,128]{1,0:T(8,128)S(1)}, f32[24,128]{1,0:T(8,128)S(1)}) custom-call(f32[24,128]{1,0:T(8,128)S(1)} %bitcast.34, bf16[128,3072]{1,0:T(8,128)(2,1)S(1)} %copy-done, bf16[128,3072]{1,0:T(8,128)(2,1)S(1)} %copy-done.1), custom_call_target="tpu_custom_call" | custom-call | flops 50331648 | bytes 786432 | tf_op jit(solution)/shard_map/pallas_call | solution.py:102
  11.1 4.0 %collective-permute-start.5 = (bf16[4,128,128]{2,1,0:T(8,128)(2,1)S(1)}, bf16[4,128,128]{2,1,0:T(8,128)(2,1)S(1)}, u32[]{:S(2)}, u32[]{:S(2)}) collective-permute-start(bf16[4,128,128]{2,1,0:T(8,128)(2,1)S(1)} %get-tuple-element.153), channel_id=1, source_target_pairs={{0,4},{2,6},{1,5},{3,7},{16,20},{18,22},{17,21},{19,23}} | collective-permute-start | bytes 393224 | tf_op jit(solution)/shard_map/ppermute | solution.py:555
  15.1 2.2 %shard_map.129 = (f32[128,1536]{1,0:T(8,128)S(1)}, bf16[32,4736]{1,0:T(8,128)(2,1)S(1)}) custom-call(f32[24,128]{1,0:T(8,128)S(1)} %get-tuple-element.80.run_ref, bf16[128,3072]{1,0:T(8,128)(2,1)S(1)} %copy-done.2, bf16[128,3072]{1,0:T(8,128)(2,1)S(1)} %copy-done, bf16[128,3072]{1,0:T(8,128)(2,1)S(1)} %copy-done.1, bf16[128,3072]{1,0:T(8,128)(2,1)S(1)} %copy-done.3, ...), custom_call_target="tpu_custom_call" | custom-call | flops 100663296 | bytes 2359296 | tf_op jit(solution)/shard_map/pallas_call | solution.py:182
  24.3 2.2 %shard_map.130 = (f32[128,1536]{1,0:T(8,128)S(1)}, bf16[32,4736]{1,0:T(8,128)(2,1)S(1)}) custom-call(f32[24,128]{1,0:T(8,128)S(1)} %get-tuple-element.80.run_ref, bf16[128,3072]{1,0:T(8,128)(2,1)S(1)} %copy-done.2, bf16[128,3072]{1,0:T(8,128)(2,1)S(1)} %copy-done, bf16[128,3072]{1,0:T(8,128)(2,1)S(1)} %copy-done.1, bf16[128,3072]{1,0:T(8,128)(2,1)S(1)} %copy-done.3, ...), custom_call_target="tpu_custom_call" | custom-call | flops 100663296 | bytes 2359296 | tf_op jit(solution)/shard_map/pallas_call | solution.py:182
  34.3 3.2 %collective-permute-start.16 = (bf16[32,1536]{1,0:T(8,128)(2,1)S(1)}, bf16[32,1536]{1,0:T(8,128)(2,1)S(1)}, u32[]{:S(2)}, u32[]{:S(2)}) collective-permute-start(bf16[32,1536]{1,0:T(8,128)(2,1)S(1)} %constant_dynamic-update-slice_fusion.refs_0_), channel_id=1, source_target_pairs={{0,4},{4,8},{8,12},{12,14},{14,10},{10,6},{6,2},{2,0},{1,5},{5,9},... | collective-permute-start | bytes 294920 | tf_op jit(solution)/shard_map/ppermute | solution.py:599
  37.6 2.5 %collective-permute-start.19 = (bf16[32,1536]{1,0:T(8,128)(2,1)S(1)}, bf16[32,1536]{1,0:T(8,128)(2,1)S(1)}, u32[]{:S(2)}, u32[]{:S(2)}) collective-permute-start(bf16[32,1536]{1,0:T(8,128)(2,1)S(1)} %collective-permute-done.13.refs_1_), channel_id=1, source_target_pairs={{0,4},{4,8},{8,12},{12,14},{14,10},{10,6},{6,2},{2,0},{1,5},{5,9},... | collective-permute-start | bytes 294920 | tf_op jit(solution)/shard_map/ppermute | solution.py:599
  40.8 1.9 %collective-permute-start.21 = (bf16[32,1536]{1,0:T(8,128)(2,1)S(1)}, bf16[32,1536]{1,0:T(8,128)(2,1)S(1)}, u32[]{:S(2)}, u32[]{:S(2)}) collective-permute-start(bf16[32,1536]{1,0:T(8,128)(2,1)S(1)} %collective-permute-done.16.refs_2_), channel_id=1, source_target_pairs={{0,4},{4,8},{8,12},{12,14},{14,10},{10,6},{6,2},{2,0},{1,5},{5,9},... | collective-permute-start | bytes 294920 | tf_op jit(solution)/shard_map/ppermute | solution.py:599
  44.1 2.0 %collective-permute-start.23 = (bf16[32,1536]{1,0:T(8,128)(2,1)S(1)}, bf16[32,1536]{1,0:T(8,128)(2,1)S(1)}, u32[]{:S(2)}, u32[]{:S(2)}) collective-permute-start(bf16[32,1536]{1,0:T(8,128)(2,1)S(1)} %collective-permute-done.19.refs_4_), channel_id=1, source_target_pairs={{0,4},{4,8},{8,12},{12,14},{14,10},{10,6},{6,2},{2,0},{1,5},{5,9},... | collective-permute-start | bytes 294920 | tf_op jit(solution)/shard_map/ppermute | solution.py:599
  46.7 1.8 %collective-permute-start.25 = (bf16[32,1536]{1,0:T(8,128)(2,1)S(1)}, bf16[32,1536]{1,0:T(8,128)(2,1)S(1)}, u32[]{:S(2)}, u32[]{:S(2)}) collective-permute-start(bf16[32,1536]{1,0:T(8,128)(2,1)S(1)} %collective-permute-done.21.refs_6_), channel_id=1, source_target_pairs={{0,4},{4,8},{8,12},{12,14},{14,10},{10,6},{6,2},{2,0},{1,5},{5,9},... | collective-permute-start | bytes 294920 | tf_op jit(solution)/shard_map/ppermute | solution.py:599
  49.8 1.9 %collective-permute-start.27 = (bf16[32,1536]{1,0:T(8,128)(2,1)S(1)}, bf16[32,1536]{1,0:T(8,128)(2,1)S(1)}, u32[]{:S(2)}, u32[]{:S(2)}) collective-permute-start(bf16[32,1536]{1,0:T(8,128)(2,1)S(1)} %collective-permute-done.23.refs_8_), channel_id=1, source_target_pairs={{0,4},{4,8},{8,12},{12,14},{14,10},{10,6},{6,2},{2,0},{1,5},{5,9},... | collective-permute-start | bytes 294920 | tf_op jit(solution)/shard_map/ppermute | solution.py:599
  52.4 1.9 %collective-permute-start.29 = (bf16[32,1536]{1,0:T(8,128)(2,1)S(1)}, bf16[32,1536]{1,0:T(8,128)(2,1)S(1)}, u32[]{:S(2)}, u32[]{:S(2)}) collective-permute-start(bf16[32,1536]{1,0:T(8,128)(2,1)S(1)} %collective-permute-done.25.refs_0_), channel_id=1, source_target_pairs={{0,4},{4,8},{8,12},{12,14},{14,10},{10,6},{6,2},{2,0},{1,5},{5,9},... | collective-permute-start | bytes 294920 | tf_op jit(solution)/shard_map/ppermute | solution.py:599
  55.0 1.7 %collective-permute-done.28.refs_3_ = bf16[32,1536]{1,0:T(8,128)(2,1)S(1)} collective-permute-done((bf16[32,1536]{1,0:T(8,128)(2,1)S(1)}, bf16[32,1536]{1,0:T(8,128)(2,1)S(1)}, u32[]{:S(2)}, u32[]{:S(2)}) %collective-permute-start.28) | collective-permute-done | bytes 98336 | tf_op jit(solution)/shard_map/ppermute | solution.py:599
  57.1 2.1 %collective-permute-done.30.refs_5_ = bf16[32,1536]{1,0:T(8,128)(2,1)S(1)} collective-permute-done((bf16[32,1536]{1,0:T(8,128)(2,1)S(1)}, bf16[32,1536]{1,0:T(8,128)(2,1)S(1)}, u32[]{:S(2)}, u32[]{:S(2)}) %collective-permute-start.30) | collective-permute-done | bytes 98336 | tf_op jit(solution)/shard_map/ppermute | solution.py:599
  59.3 3.8 %shard_map.135 = (f32[128,3072]{1,0:T(8,128)S(1)}, bf16[128,768]{1,0:T(8,128)(2,1)S(1)}) custom-call(f32[1,6144]{1,0:T(1,128)S(1)} %bitcast.27, bf16[6144,768]{1,0:T(8,128)(2,1)S(1)} %bitcast.21, bf16[6144,768]{1,0:T(8,128)(2,1)S(1)} %bitcast.24, bf16[768,6144]{1,0:T(8,128)(2,1)S(1)} %bitcast.17, bf16[128,6144]{1,0:T(8,128)(2,1)S(1)} %get-tuple-element.119.early_ref, ...), custom_call_target="tpu_custom_call" | custom-call | flops 3019898880 | bytes 23592960 | tf_op jit(solution)/shard_map/pallas_call | solution.py:389
  63.7 1.6 %collective-permute-start.33 = (bf16[16,3072]{1,0:T(8,128)(2,1)S(1)}, bf16[16,3072]{1,0:T(8,128)(2,1)S(1)}, u32[]{:S(2)}, u32[]{:S(2)}) collective-permute-start(bf16[16,3072]{1,0:T(8,128)(2,1)S(1)} %get-tuple-element.161), channel_id=1, source_target_pairs={{0,4},{4,8},{8,12},{12,14},{14,10},{10,6},{6,2},{2,0},{1,5},{5,9},... | collective-permute-start | bytes 294920 | tf_op jit(solution)/shard_map/ppermute | solution.py:639
  66.2 1.9 %collective-permute-start.32 = (bf16[16,3072]{1,0:T(8,128)(2,1)S(1)}, bf16[16,3072]{1,0:T(8,128)(2,1)S(1)}, u32[]{:S(2)}, u32[]{:S(2)}) collective-permute-start(bf16[16,3072]{1,0:T(8,128)(2,1)S(1)} %get-tuple-element.159), channel_id=1, source_target_pairs={{0,4},{4,8},{8,12},{12,14},{14,10},{10,6},{6,2},{2,0},{1,5},{5,9},... | collective-permute-start | bytes 294920 | tf_op jit(solution)/shard_map/ppermute | solution.py:639
  69.5 1.7 %collective-permute-start.37 = (bf16[16,3072]{1,0:T(8,128)(2,1)S(1)}, bf16[16,3072]{1,0:T(8,128)(2,1)S(1)}, u32[]{:S(2)}, u32[]{:S(2)}) collective-permute-start(bf16[16,3072]{1,0:T(8,128)(2,1)S(1)} %add_convert_fusion.6), channel_id=1, source_target_pairs={{0,4},{4,8},{8,12},{12,14},{14,10},{10,6},{6,2},{2,0},{1,5},{5,9},... | collective-permute-start | bytes 294920 | tf_op jit(solution)/shard_map/ppermute | solution.py:639
  71.1 1.9 %collective-permute-start.36 = (bf16[16,3072]{1,0:T(8,128)(2,1)S(1)}, bf16[16,3072]{1,0:T(8,128)(2,1)S(1)}, u32[]{:S(2)}, u32[]{:S(2)}) collective-permute-start(bf16[16,3072]{1,0:T(8,128)(2,1)S(1)} %fusion.8), channel_id=1, source_target_pairs={{0,4},{4,8},{8,12},{12,14},{14,10},{10,6},{6,2},{2,0},{1,5},{5,9},... | collective-permute-start | bytes 294920 | tf_op jit(solution)/shard_map/ppermute | solution.py:639
  75.8 1.8 %collective-permute-start.41 = (bf16[16,3072]{1,0:T(8,128)(2,1)S(1)}, bf16[16,3072]{1,0:T(8,128)(2,1)S(1)}, u32[]{:S(2)}, u32[]{:S(2)}) collective-permute-start(bf16[16,3072]{1,0:T(8,128)(2,1)S(1)} %add_convert_fusion.4), channel_id=1, source_target_pairs={{0,4},{4,8},{8,12},{12,14},{14,10},{10,6},{6,2},{2,0},{1,5},{5,9},... | collective-permute-start | bytes 294920 | tf_op jit(solution)/shard_map/ppermute | solution.py:639
  77.6 1.8 %collective-permute-start.40 = (bf16[16,3072]{1,0:T(8,128)(2,1)S(1)}, bf16[16,3072]{1,0:T(8,128)(2,1)S(1)}, u32[]{:S(2)}, u32[]{:S(2)}) collective-permute-start(bf16[16,3072]{1,0:T(8,128)(2,1)S(1)} %fusion.7), channel_id=1, source_target_pairs={{0,4},{4,8},{8,12},{12,14},{14,10},{10,6},{6,2},{2,0},{1,5},{5,9},... | collective-permute-start | bytes 294920 | tf_op jit(solution)/shard_map/ppermute | solution.py:639
  84.1 2.9 %shard_map.137 = (bf16[128,3072]{1,0:T(8,128)(2,1)S(1)}, f32[8,128]{1,0:T(8,128)S(1)}) custom-call(f32[24,128]{1,0:T(8,128)S(1)} %get-tuple-element.80.run_ref, bf16[128,3072]{1,0:T(8,128)(2,1)S(1)} %copy-done.2, f32[128,1536]{1,0:T(8,128)S(1)} %get-tuple-element.96.own_ref, f32[128,1536]{1,0:T(8,128)S(1)} %get-tuple-element.86.other_ref, ...), custom_call_target="tpu_custom_call" | custom-call | flops 100663296 | bytes 4718592 | tf_op jit(solution)/shard_map/pallas_call | solution.py:305
  (162 shorter events, 34.8 us)
Async XLA Ops:
  3.1 7.7 %collective-permute-start = (bf16[528,128]{1,0:T(8,128)(2,1)}, bf16[528,128]{1,0:T(8,128)(2,1)S(1)}, u32[]{:S(2)}, u32[]{:S(2)}) collective-permute-start(bf16[528,128]{1,0:T(8,128)(2,1)} %get-tuple-element.78), channel_id=1, source_target_pairs={{0,2},{2,0},{4,6},{6,4},{8,10},{10,8},{12,14},{14,12},{1,3},{3,1},... | collective-permute-start | bytes 405512 | tf_op jit(solution)/shard_map/ppermute | solution.py:528
  6.2 11.2 %collective-permute-start.2 = (bf16[512,128]{1,0:T(8,128)(2,1)}, bf16[512,128]{1,0:T(8,128)(2,1)S(1)}, u32[]{:S(2)}, u32[]{:S(2)}) collective-permute-start(bf16[512,128]{1,0:T(8,128)(2,1)} %get-tuple-element.82), channel_id=1, source_target_pairs={{0,2},{2,0},{4,6},{6,4},{8,10},{10,8},{12,14},{14,12},{1,3},{3,1},... | collective-permute-start | bytes 393224 | tf_op jit(solution)/shard_map/ppermute | solution.py:528
  6.3 12.6 %collective-permute-start.1 = (bf16[512,128]{1,0:T(8,128)(2,1)}, bf16[512,128]{1,0:T(8,128)(2,1)S(1)}, u32[]{:S(2)}, u32[]{:S(2)}) collective-permute-start(bf16[512,128]{1,0:T(8,128)(2,1)} %get-tuple-element.81), channel_id=1, source_target_pairs={{0,2},{2,0},{4,6},{6,4},{8,10},{10,8},{12,14},{14,12},{1,3},{3,1},... | collective-permute-start | bytes 393224 | tf_op jit(solution)/shard_map/ppermute | solution.py:528
  11.1 10.8 %collective-permute-start.5 = (bf16[4,128,128]{2,1,0:T(8,128)(2,1)S(1)}, bf16[4,128,128]{2,1,0:T(8,128)(2,1)S(1)}, u32[]{:S(2)}, u32[]{:S(2)}) collective-permute-start(bf16[4,128,128]{2,1,0:T(8,128)(2,1)S(1)} %get-tuple-element.153), channel_id=1, source_target_pairs={{0,4},{2,6},{1,5},{3,7},{16,20},{18,22},{17,21},{19,23}} | collective-permute-start | bytes 393224 | tf_op jit(solution)/shard_map/ppermute | solution.py:555
  20.3 10.0 %collective-permute-start.6 = (bf16[32,4736]{1,0:T(8,128)(2,1)S(1)}, bf16[32,4736]{1,0:T(8,128)(2,1)S(1)}, u32[]{:S(2)}, u32[]{:S(2)}) collective-permute-start(bf16[32,4736]{1,0:T(8,128)(2,1)S(1)} %get-tuple-element.91), channel_id=1, source_target_pairs={{0,2},{2,0},{4,6},{6,4},{8,10},{10,8},{12,14},{14,12},{1,3},{3,1},... | collective-permute-start | bytes 909320 | tf_op jit(solution)/shard_map/ppermute | solution.py:547
  29.0 8.4 %collective-permute-start.14 = (bf16[4,128,128]{2,1,0:T(8,128)(2,1)S(1)}, bf16[4,128,128]{2,1,0:T(8,128)(2,1)S(1)}, u32[]{:S(2)}, u32[]{:S(2)}) collective-permute-start(bf16[4,128,128]{2,1,0:T(8,128)(2,1)S(1)} %get-tuple-element.167.moved_ref), channel_id=1, source_target_pairs={{0,2},{2,0},{4,6},{6,4},{8,10},{10,8},{12,14},{14,12},{1,3},{3,1},... | collective-permute-start | bytes 393224 | tf_op jit(solution)/shard_map/ppermute | solution.py:696
  30.9 6.6 %collective-permute-start.15 = (bf16[4,128,128]{2,1,0:T(8,128)(2,1)S(1)}, bf16[4,128,128]{2,1,0:T(8,128)(2,1)S(1)}, u32[]{:S(2)}, u32[]{:S(2)}) collective-permute-start(bf16[4,128,128]{2,1,0:T(8,128)(2,1)S(1)} %get-tuple-element.165.moved_ref), channel_id=1, source_target_pairs={{0,2},{2,0},{4,6},{6,4},{8,10},{10,8},{12,14},{14,12},{1,3},{3,1},... | collective-permute-start | bytes 393224 | tf_op jit(solution)/shard_map/ppermute | solution.py:696
  32.4 8.4 %collective-permute-start.17 = (bf16[4,128,128]{2,1,0:T(8,128)(2,1)S(1)}, bf16[4,128,128]{2,1,0:T(8,128)(2,1)S(1)}, u32[]{:S(2)}, u32[]{:S(2)}) collective-permute-start(bf16[4,128,128]{2,1,0:T(8,128)(2,1)S(1)} %get-tuple-element.163.moved_ref), channel_id=1, source_target_pairs={{0,2},{2,0},{4,6},{6,4},{8,10},{10,8},{12,14},{14,12},{1,3},{3,1},... | collective-permute-start | bytes 393224 | tf_op jit(solution)/shard_map/ppermute | solution.py:696
  34.3 6.5 %collective-permute-start.16 = (bf16[32,1536]{1,0:T(8,128)(2,1)S(1)}, bf16[32,1536]{1,0:T(8,128)(2,1)S(1)}, u32[]{:S(2)}, u32[]{:S(2)}) collective-permute-start(bf16[32,1536]{1,0:T(8,128)(2,1)S(1)} %constant_dynamic-update-slice_fusion.refs_0_), channel_id=1, source_target_pairs={{0,4},{4,8},{8,12},{12,14},{14,10},{10,6},{6,2},{2,0},{1,5},{5,9},... | collective-permute-start | bytes 294920 | tf_op jit(solution)/shard_map/ppermute | solution.py:599
  37.5 5.7 %collective-permute-start.18 = (bf16[32,1536]{1,0:T(8,128)(2,1)S(1)}, bf16[32,1536]{1,0:T(8,128)(2,1)S(1)}, u32[]{:S(2)}, u32[]{:S(2)}) collective-permute-start(bf16[32,1536]{1,0:T(8,128)(2,1)S(1)} %collective-permute-done.13.refs_1_), channel_id=1, source_target_pairs={{4,0},{8,4},{12,8},{14,12},{10,14},{6,10},{2,6},{0,2},{5,1},{9,5},... | collective-permute-start | bytes 294920 | tf_op jit(solution)/shard_map/ppermute | solution.py:599
  37.6 6.5 %collective-permute-start.19 = (bf16[32,1536]{1,0:T(8,128)(2,1)S(1)}, bf16[32,1536]{1,0:T(8,128)(2,1)S(1)}, u32[]{:S(2)}, u32[]{:S(2)}) collective-permute-start(bf16[32,1536]{1,0:T(8,128)(2,1)S(1)} %collective-permute-done.13.refs_1_), channel_id=1, source_target_pairs={{0,4},{4,8},{8,12},{12,14},{14,10},{10,6},{6,2},{2,0},{1,5},{5,9},... | collective-permute-start | bytes 294920 | tf_op jit(solution)/shard_map/ppermute | solution.py:599
  40.1 6.0 %collective-permute-start.20 = (bf16[32,1536]{1,0:T(8,128)(2,1)S(1)}, bf16[32,1536]{1,0:T(8,128)(2,1)S(1)}, u32[]{:S(2)}, u32[]{:S(2)}) collective-permute-start(bf16[32,1536]{1,0:T(8,128)(2,1)S(1)} %constant_dynamic-update-slice_fusion.refs_0_), channel_id=1, source_target_pairs={{4,0},{8,4},{12,8},{14,12},{10,14},{6,10},{2,6},{0,2},{5,1},{9,5},... | collective-permute-start | bytes 294920 | tf_op jit(solution)/shard_map/ppermute | solution.py:599
  40.8 5.9 %collective-permute-start.21 = (bf16[32,1536]{1,0:T(8,128)(2,1)S(1)}, bf16[32,1536]{1,0:T(8,128)(2,1)S(1)}, u32[]{:S(2)}, u32[]{:S(2)}) collective-permute-start(bf16[32,1536]{1,0:T(8,128)(2,1)S(1)} %collective-permute-done.16.refs_2_), channel_id=1, source_target_pairs={{0,4},{4,8},{8,12},{12,14},{14,10},{10,6},{6,2},{2,0},{1,5},{5,9},... | collective-permute-start | bytes 294920 | tf_op jit(solution)/shard_map/ppermute | solution.py:599
  43.2 6.5 %collective-permute-start.22 = (bf16[32,1536]{1,0:T(8,128)(2,1)S(1)}, bf16[32,1536]{1,0:T(8,128)(2,1)S(1)}, u32[]{:S(2)}, u32[]{:S(2)}) collective-permute-start(bf16[32,1536]{1,0:T(8,128)(2,1)S(1)} %collective-permute-done.18.refs_3_), channel_id=1, source_target_pairs={{4,0},{8,4},{12,8},{14,12},{10,14},{6,10},{2,6},{0,2},{5,1},{9,5},... | collective-permute-start | bytes 294920 | tf_op jit(solution)/shard_map/ppermute | solution.py:599
  44.1 5.7 %collective-permute-start.23 = (bf16[32,1536]{1,0:T(8,128)(2,1)S(1)}, bf16[32,1536]{1,0:T(8,128)(2,1)S(1)}, u32[]{:S(2)}, u32[]{:S(2)}) collective-permute-start(bf16[32,1536]{1,0:T(8,128)(2,1)S(1)} %collective-permute-done.19.refs_4_), channel_id=1, source_target_pairs={{0,4},{4,8},{8,12},{12,14},{14,10},{10,6},{6,2},{2,0},{1,5},{5,9},... | collective-permute-start | bytes 294920 | tf_op jit(solution)/shard_map/ppermute | solution.py:599
  46.1 5.7 %collective-permute-start.24 = (bf16[32,1536]{1,0:T(8,128)(2,1)S(1)}, bf16[32,1536]{1,0:T(8,128)(2,1)S(1)}, u32[]{:S(2)}, u32[]{:S(2)}) collective-permute-start(bf16[32,1536]{1,0:T(8,128)(2,1)S(1)} %collective-permute-done.20.refs_5_), channel_id=1, source_target_pairs={{4,0},{8,4},{12,8},{14,12},{10,14},{6,10},{2,6},{0,2},{5,1},{9,5},... | collective-permute-start | bytes 294920 | tf_op jit(solution)/shard_map/ppermute | solution.py:599
  46.7 5.7 %collective-permute-start.25 = (bf16[32,1536]{1,0:T(8,128)(2,1)S(1)}, bf16[32,1536]{1,0:T(8,128)(2,1)S(1)}, u32[]{:S(2)}, u32[]{:S(2)}) collective-permute-start(bf16[32,1536]{1,0:T(8,128)(2,1)S(1)} %collective-permute-done.21.refs_6_), channel_id=1, source_target_pairs={{0,4},{4,8},{8,12},{12,14},{14,10},{10,6},{6,2},{2,0},{1,5},{5,9},... | collective-permute-start | bytes 294920 | tf_op jit(solution)/shard_map/ppermute | solution.py:599
  63.2 5.7 %collective-permute-start.34 = (bf16[16,3072]{1,0:T(8,128)(2,1)S(1)}, bf16[16,3072]{1,0:T(8,128)(2,1)S(1)}, u32[]{:S(2)}, u32[]{:S(2)}) collective-permute-start(bf16[16,3072]{1,0:T(8,128)(2,1)S(1)} %get-tuple-element.162), channel_id=1, source_target_pairs={{4,0},{8,4},{12,8},{14,12},{10,14},{6,10},{2,6},{0,2},{5,1},{9,5},... | collective-permute-start | bytes 294920 | tf_op jit(solution)/shard_map/ppermute | solution.py:639
  63.7 5.7 %collective-permute-start.33 = (bf16[16,3072]{1,0:T(8,128)(2,1)S(1)}, bf16[16,3072]{1,0:T(8,128)(2,1)S(1)}, u32[]{:S(2)}, u32[]{:S(2)}) collective-permute-start(bf16[16,3072]{1,0:T(8,128)(2,1)S(1)} %get-tuple-element.161), channel_id=1, source_target_pairs={{0,4},{4,8},{8,12},{12,14},{14,10},{10,6},{6,2},{2,0},{1,5},{5,9},... | collective-permute-start | bytes 294920 | tf_op jit(solution)/shard_map/ppermute | solution.py:639
  68.2 5.6 %collective-permute-start.31 = (bf16[16,3072]{1,0:T(8,128)(2,1)S(1)}, bf16[16,3072]{1,0:T(8,128)(2,1)S(1)}, u32[]{:S(2)}, u32[]{:S(2)}) collective-permute-start(bf16[16,3072]{1,0:T(8,128)(2,1)S(1)} %get-tuple-element.160), channel_id=1, source_target_pairs={{4,0},{8,4},{12,8},{14,12},{10,14},{6,10},{2,6},{0,2},{5,1},{9,5},... | collective-permute-start | bytes 294920 | tf_op jit(solution)/shard_map/ppermute | solution.py:639
  69.0 6.4 %collective-permute-start.38 = (bf16[16,3072]{1,0:T(8,128)(2,1)S(1)}, bf16[16,3072]{1,0:T(8,128)(2,1)S(1)}, u32[]{:S(2)}, u32[]{:S(2)}) collective-permute-start(bf16[16,3072]{1,0:T(8,128)(2,1)S(1)} %add_convert_fusion.7), channel_id=1, source_target_pairs={{4,0},{8,4},{12,8},{14,12},{10,14},{6,10},{2,6},{0,2},{5,1},{9,5},... | collective-permute-start | bytes 294920 | tf_op jit(solution)/shard_map/ppermute | solution.py:639
  69.5 6.3 %collective-permute-start.37 = (bf16[16,3072]{1,0:T(8,128)(2,1)S(1)}, bf16[16,3072]{1,0:T(8,128)(2,1)S(1)}, u32[]{:S(2)}, u32[]{:S(2)}) collective-permute-start(bf16[16,3072]{1,0:T(8,128)(2,1)S(1)} %add_convert_fusion.6), channel_id=1, source_target_pairs={{0,4},{4,8},{8,12},{12,14},{14,10},{10,6},{6,2},{2,0},{1,5},{5,9},... | collective-permute-start | bytes 294920 | tf_op jit(solution)/shard_map/ppermute | solution.py:639
  71.1 6.4 %collective-permute-start.36 = (bf16[16,3072]{1,0:T(8,128)(2,1)S(1)}, bf16[16,3072]{1,0:T(8,128)(2,1)S(1)}, u32[]{:S(2)}, u32[]{:S(2)}) collective-permute-start(bf16[16,3072]{1,0:T(8,128)(2,1)S(1)} %fusion.8), channel_id=1, source_target_pairs={{0,4},{4,8},{8,12},{12,14},{14,10},{10,6},{6,2},{2,0},{1,5},{5,9},... | collective-permute-start | bytes 294920 | tf_op jit(solution)/shard_map/ppermute | solution.py:639
  80.6 6.3 %collective-permute-start.44 = (bf16[16,3072]{1,0:T(8,128)(2,1)S(1)}, bf16[16,3072]{1,0:T(8,128)(2,1)S(1)}, u32[]{:S(2)}, u32[]{:S(2)}) collective-permute-start(bf16[16,3072]{1,0:T(8,128)(2,1)S(1)} %get-tuple-element.158), channel_id=1, source_target_pairs={{4,0},{8,4},{12,8},{14,12},{10,14},{6,10},{2,6},{0,2},{5,1},{9,5},... | collective-permute-start | bytes 294920 | tf_op jit(solution)/shard_map/ppermute | solution.py:639
  (42 other events, 421.5 us)

commit v6 on v5

--- a/solution.py
+++ b/solution.py
@@ -321,18 +321,41 @@
     )
 
 
+def far_side(count):
+    return ring_block(count, count // 2) % 2
+
+
+def quarter_of(count, late, side):
+    return (lax.axis_index("exp") ^ side) * 2 + (far_side(count) ^ 1 ^ late)
+
+
 def place_pieces(places, gain_ref, pieces, scaled_ref, square_ref):
     quarter = scaled_ref.shape[1] // 4
     for (position, side), piece in zip(places, pieces, strict=True):
         height = piece.shape[0]
-        block = ring_block(2 * scaled_ref.shape[0] // height, position)
+        count = 2 * scaled_ref.shape[0] // height
+        block = ring_block(count, position)
         rows = pl.ds(pl.multiple_of(block // 2 * height, height), height)
+        late = (block % 2) ^ far_side(count) ^ 1
+        lanes = pl.ds(pl.multiple_of((late * 2 + side) * quarter, quarter), quarter)
         first = ((lax.axis_index("exp") ^ side) * 2 + block % 2) * quarter
-        lanes = pl.ds(pl.multiple_of(first, quarter), quarter)
+        gain = gain_ref[:, pl.ds(pl.multiple_of(first, quarter), quarter)]
         value = piece[...].astype(F32)
         square = jnp.sum(value * value, axis=1, keepdims=True)
         square_ref[rows, :] += jnp.broadcast_to(square, (height, square_ref.shape[1]))
-        scaled_ref[rows, lanes] = (value * gain_ref[:, lanes]).astype(BF16)
+        scaled_ref[rows, lanes] = (value * gain).astype(BF16)
+
+
+def products(late, scaled_ref, gate_ref, up_ref):
+    quarter = scaled_ref.shape[1] // 4
+    gate_part, up_part = (0.0, 0.0)
+    for side in range(2):
+        rows = scaled_ref[:, (late * 2 + side) * quarter : (late * 2 + side + 1) * quarter]
+        first = quarter_of(scaled_ref.shape[0] // CAP, late, side) * quarter
+        here = pl.ds(pl.multiple_of(first, quarter), quarter)
+        gate_part += jnp.dot(rows, gate_ref[here, :], preferred_element_type=F32)
+        up_part += jnp.dot(rows, up_ref[here, :], preferred_element_type=F32)
+    return (gate_part, up_part)
 
 
 def early_kernel(places, gain_ref, *refs):
@@ -354,76 +377,97 @@
     )(gain, *pieces)
 
 
-def expert_kernel(places, gain_ref, gate_ref, up_ref, down_ref, early_ref, early_square_ref, *refs):
-    *pieces, out_ref, hidden_ref, scaled_ref, square_ref, block_ref = refs
+def partial_kernel(places, gain_ref, gate_ref, up_ref, early_ref, early_square_ref, *refs):
+    *pieces, scaled_ref, square_ref, gate_out_ref, up_out_ref = refs
+    scaled_ref[...] = early_ref[...]
+    square_ref[...] = early_square_ref[...]
+    place_pieces(places, gain_ref, pieces, scaled_ref, square_ref)
+    gate_out_ref[...], up_out_ref[...] = products(0, scaled_ref, gate_ref, up_ref)
+
+
+def partial_rows(places, gain, early, pieces, gate_weight, up_weight):
+    width, hidden_units = gate_weight.shape
+    rows = early[0].shape[0]
+    part = jax.ShapeDtypeStruct((rows, hidden_units), F32)
+    return pl.pallas_call(
+        functools.partial(partial_kernel, places),
+        out_shape=(
+            jax.ShapeDtypeStruct((rows, width), BF16),
+            jax.ShapeDtypeStruct((rows, 128), F32),
+            part,
+            part,
+        ),
+        in_specs=[VMEM] * (5 + len(pieces)),
+        out_specs=(VMEM,) * 4,
+        compiler_params=grant(max(6, rows // 16)),
+        cost_estimate=pl.CostEstimate(
+            flops=2 * rows * width * hidden_units,
+            bytes_accessed=2 * width * hidden_units,
+            transcendentals=0,
+        ),
+    )(gain, gate_weight, up_weight, *early, *pieces)
+
+
+def expert_kernel(
+    places, gain_ref, gate_ref, up_ref, early_ref, early_square_ref, gate_in_ref, up_in_ref, *refs
+):
+    *pieces, hidden_ref, scaled_ref, square_ref, block_ref = refs
     width = gate_ref.shape[0]
     capacity = CAP
     count = scaled_ref.shape[0] // capacity
-    quarter = width // 4
-    scaled_ref[...] = early_ref[...]
+    scaled_ref[:, width // 2 :] = early_ref[:, width // 2 :]
     square_ref[...] = early_square_ref[...]
     place_pieces(places, gain_ref, pieces, scaled_ref, square_ref)
     inverse = lax.rsqrt(square_ref[...][:, :1] / width + 1e-06)
-    gate_part, up_part = (0.0, 0.0)
-    for part in range(4):
-        lanes = slice(part * quarter, (part + 1) * quarter)
-        rows = scaled_ref[:, lanes]
-        gate_part += jnp.dot(rows, gate_ref[lanes], preferred_element_type=F32)
-        up_part += jnp.dot(rows, up_ref[lanes], preferred_element_type=F32)
-    gate_part, up_part = (gate_part * inverse, up_part * inverse)
+    gate_part, up_part = products(1, scaled_ref, gate_ref, up_ref)
+    gate_part = (gate_in_ref[...] + gate_part) * inverse
+    up_part = (up_in_ref[...] + up_part) * inverse
     block_ref[...] = (jax.nn.silu(gate_part) * up_part).astype(BF16)
     for position in range(count):
         block = ring_block(count, position)
         hidden_ref[position * capacity : (position + 1) * capacity] = block_ref[
             pl.ds(pl.multiple_of(block * capacity, capacity), capacity)
         ]
-    hidden = hidden_ref[...]
-    for part in range(2):
-        lanes = slice(part * quarter, (part + 1) * quarter)
-        out_ref[:, lanes] = jnp.dot(hidden, down_ref[:, lanes], preferred_element_type=F32)
-
-
-def expert_rows(places, gain, early, pieces, gate_weight, up_weight, down_weight):
+
+
+def expert_rows(places, gain, early, pieces, gate_weight, up_weight):
     width, hidden_units = gate_weight.shape
     rows = early[0].shape[0]
     return pl.pallas_call(
         functools.partial(expert_kernel, places),
-        out_shape=(
-            jax.ShapeDtypeStruct((rows, width // 2), F32),
-            jax.ShapeDtypeStruct((rows, hidden_units), BF16),
-        ),
-        in_specs=[VMEM] * (6 + len(pieces)),
-        out_specs=(VMEM, VMEM),
+        out_shape=jax.ShapeDtypeStruct((rows, hidden_units), BF16),
+        in_specs=[VMEM] * (7 + len(pieces)),
+        out_specs=VMEM,
         scratch_shapes=[
             pltpu.VMEM((rows, width), BF16),
             pltpu.VMEM((rows, 128), F32),
             pltpu.VMEM((rows, hidden_units), BF16),
         ],
-        compiler_params=grant(max(16, rows // 16)),
+        compiler_params=grant(max(6, rows // 16)),
         cost_estimate=pl.CostEstimate(
-            flops=5 * rows * width * hidden_units,
-            bytes_accessed=5 * width * hidden_units,
+            flops=2 * rows * width * hidden_units,
+            bytes_accessed=2 * width * hidden_units,
             transcendentals=0,
         ),
-    )(gain, gate_weight, up_weight, down_weight, *early, *pieces)
-
-
-def rest_kernel(hidden_ref, down_ref, out_ref):
-    half = out_ref.shape[1]
+    )(gain, gate_weight, up_weight, *early, *pieces)
+
+
+def down_kernel(half, hidden_ref, down_ref, out_ref):
+    width = out_ref.shape[1]
     for part in range(2):
-        lanes = slice(part * half // 2, (part + 1) * half // 2)
-        weights = down_ref[:, half + lanes.start : half + lanes.stop]
+        lanes = slice(part * width // 2, (part + 1) * width // 2)
+        weights = down_ref[:, half * width + lanes.start : half * width + lanes.stop]
         out_ref[:, lanes] = jnp.dot(hidden_ref[...], weights, preferred_element_type=F32)
 
 
-def expert_rest(hidden, down_weight):
+def expert_down(half, hidden, down_weight):
     rows, width = (hidden.shape[0], down_weight.shape[1])
     return pl.pallas_call(
-        rest_kernel,
+        functools.partial(down_kernel, half),
         out_shape=jax.ShapeDtypeStruct((rows, width // 2), F32),
         in_specs=[VMEM] * 2,
         out_specs=VMEM,
-        compiler_params=grant(max(8, rows // 32)),
+        compiler_params=grant(max(6, rows // 32)),
         cost_estimate=pl.CostEstimate(
             flops=rows * width * hidden.shape[1],
             bytes_accessed=width * hidden.shape[1],
@@ -635,10 +679,11 @@
     sents += [piece(positions[0], 1).astype(BF16) for _, _, positions in chains[2:]]
     marks = list(sents)
     for step in range(1, steps + 1):
+        order = (0, 2, 3, 1)
         gots = {
-            k: lax.ppermute(sents[k], "seq", way)
-            for k, (_, way, positions) in enumerate(chains)
-            if step <= len(positions)
+            k: lax.ppermute(sents[k], "seq", chains[k][1])
+            for k in order
+            if step <= len(chains[k][2])
         }
         if step == steps:
             marks = [*marks, *last(marks)]
@@ -711,26 +756,38 @@
     steps = count // 2
     early = []
 
-    def places(first, last):
-        return sum([ring_places(steps, step) for step in range(first, last)], [])
-
     def hold_rows(brought):
-        early.extend(early_rows(places(0, steps - 1), count * CAP, moe_gain, sum(brought, [])))
-        return early
-
-    brought = ring_gather(halves, {0: lambda brought: swapped, steps - 2: hold_rows})
-    low, hidden_units = expert_rows(
-        places(steps - 1, steps + 1),
+        places = sum([ring_places(steps, step) for step in range(steps - 1)], [])
+        early.append(early_rows(places, count * CAP, moe_gain, sum(brought, [])))
+        return early[-1]
+
+    def hold_partial(brought):
+        early.append(
+            partial_rows(
+                ring_places(steps, steps - 1),
+                moe_gain,
+                early[-1],
+                brought[-1],
+                gate_weight[0],
+                up_weight[0],
+            )
+        )
+        return early[-1]
+
+    holds = {0: lambda brought: swapped, steps - 2: hold_rows, steps - 1: hold_partial}
+    brought = ring_gather(halves, holds)
+    hidden_units = expert_rows(
+        ring_places(steps, steps),
         moe_gain,
-        early,
-        sum(brought[steps - 1 :], []),
+        early[-1],
+        brought[-1],
         gate_weight[0],
         up_weight[0],
-        down_weight[0],
     )
+    low = expert_down(0, hidden_units, down_weight[0])
 
     def rest(marks):
-        return expert_rest(after(hidden_units, *marks), down_weight[0])
+        return expert_down(1, after(hidden_units, *marks), down_weight[0])
 
     held = []
 

time: 90.4 us -> 89 us (0.985)
  waiting for transfers between devices: 13.9 us -> 10.7 us
  starting transfers between devices: 53.4 us -> 54.7 us
    ppermute x14, waiting for transfers between devices: 6.84 us -> 5.03 us  [ring_gather(): lax.ppermute(moving[k], 'seq', way)]
    ppermute x14, waiting for transfers between devices: 5.62 us -> 4.25 us  [ring_scatter(): lax.ppermute(sents[k], 'seq', chains[k][1])]
    ppermute x14, starting transfers between devices: 14.3 us -> 15.5 us  [ring_scatter(): lax.ppermute(sents[k], 'seq', chains[k][1])]
    pallas_call x2 -> x4, Pallas kernels: 4.58 us -> 4.89 us  [the longest x1 1.68 us: expert_rows(): pl.pallas_call(functools.partial(expert_kernel, places), out_shape=jax.Sh...]
  transfers between devices with their start and end apart: 47 -> 47, of which waited for: 18 -> 15; matrix products, arithmetic and copies ran while one was open for 2% -> 2% of each run, Pallas kernels for 13% -> 15%
where the time goes in v6:
time: 89 us; the launch traced here: 88.7 us
  starting transfers between devices  54.7 us (61%)
  Pallas kernels  20.2 us (23%)
  waiting for transfers between devices  10.7 us (12%)
  other arithmetic  2.22 us (2%)
    ppermute x14, starting transfers between devices, ring_gather(): lax.ppermute(moving[k], 'seq', way)  17.7 us
    ppermute x14, starting transfers between devices, ring_scatter(): lax.ppermute(sents[k], 'seq', chains[k][1])  15.5 us
    ppermute x9, starting transfers between devices, entering_state(): gots = [lax.ppermute(sent, 'seq', pairs) for sent in sents]  10.6 us
    ppermute x3, starting transfers between devices, entering_state(): arrived = after(lax.ppermute(sending[chunk], 'seq', swap), *marks)  5.14 us
    ppermute x14, waiting for transfers between devices, ring_gather(): lax.ppermute(moving[k], 'seq', way)  5.03 us
    pallas_call x2, Pallas kernels, half_state(): pl.pallas_call(functools.partial(state_kernel, sent), out_shape=tuple(sha...  4.87 us
    pallas_call x2, Pallas kernels, within_block(): pl.pallas_call(functools.partial(within_kernel, sent), out_shape=(jax.Sha...  4.47 us
    ppermute x14, waiting for transfers between devices, ring_scatter(): lax.ppermute(sents[k], 'seq', chains[k][1])  4.25 us
  transfers between devices with their start and end apart: 47, of which 15 were waited for; matrix products, arithmetic and copies ran while one was open for 2% of the time, Pallas kernels for 15%

profile of v6, /device:TPU:0, one launch (start us, length us, event | category | flops | bytes accessed | tf_op | source)
XLA Modules:
  0.0 88.7 jit_solution(10724432729125475921)
XLA Ops:
  0.0 3.1 %shard_map.127 = (bf16[528,128]{1,0:T(8,128)(2,1)}, bf16[512,128]{1,0:T(8,128)(2,1)}, bf16[512,128]{1,0:T(8,128)(2,1)}) custom-call(f32[24,128]{1,0:T(8,128)} %bitcast.36, bf16[128,3072]{1,0:T(8,128)(2,1)} %key_ref.7, bf16[128,3072]{1,0:T(8,128)(2,1)} %value_ref.7), custom_call_target="tpu_custom_call" | custom-call | flops 50331648 | bytes 786432 | tf_op jit(solution)/shard_map/pallas_call | solution.py:102
  3.1 3.0 %collective-permute-start = (bf16[528,128]{1,0:T(8,128)(2,1)}, bf16[528,128]{1,0:T(8,128)(2,1)S(1)}, u32[]{:S(2)}, u32[]{:S(2)}) collective-permute-start(bf16[528,128]{1,0:T(8,128)(2,1)} %get-tuple-element.80), channel_id=1, source_target_pairs={{0,2},{2,0},{4,6},{6,4},{8,10},{10,8},{12,14},{14,12},{1,3},{3,1},... | collective-permute-start | bytes 405512 | tf_op jit(solution)/shard_map/ppermute | solution.py:572
  6.3 2.0 %collective-permute-start.1 = (bf16[512,128]{1,0:T(8,128)(2,1)}, bf16[512,128]{1,0:T(8,128)(2,1)S(1)}, u32[]{:S(2)}, u32[]{:S(2)}) collective-permute-start(bf16[512,128]{1,0:T(8,128)(2,1)} %get-tuple-element.83), channel_id=1, source_target_pairs={{0,2},{2,0},{4,6},{6,4},{8,10},{10,8},{12,14},{14,12},{1,3},{3,1},... | collective-permute-start | bytes 393224 | tf_op jit(solution)/shard_map/ppermute | solution.py:572
  8.3 1.8 %shard_map.128 = (f32[512,128]{1,0:T(8,128)S(1)}, f32[512,128]{1,0:T(8,128)S(1)}, f32[512,128]{1,0:T(8,128)S(1)}, f32[24,128]{1,0:T(8,128)S(1)}) custom-call(f32[24,128]{1,0:T(8,128)S(1)} %bitcast.37, bf16[128,3072]{1,0:T(8,128)(2,1)S(1)} %copy-done, bf16[128,3072]{1,0:T(8,128)(2,1)S(1)} %copy-done.1), custom_call_target="tpu_custom_call" | custom-call | flops 50331648 | bytes 786432 | tf_op jit(solution)/shard_map/pallas_call | solution.py:102
  11.1 4.0 %collective-permute-start.5 = (bf16[4,128,128]{2,1,0:T(8,128)(2,1)S(1)}, bf16[4,128,128]{2,1,0:T(8,128)(2,1)S(1)}, u32[]{:S(2)}, u32[]{:S(2)}) collective-permute-start(bf16[4,128,128]{2,1,0:T(8,128)(2,1)S(1)} %get-tuple-element.157), channel_id=1, source_target_pairs={{0,4},{2,6},{1,5},{3,7},{16,20},{18,22},{17,21},{19,23}} | collective-permute-start | bytes 393224 | tf_op jit(solution)/shard_map/ppermute | solution.py:599
  15.1 2.2 %shard_map.129 = (f32[128,1536]{1,0:T(8,128)S(1)}, bf16[32,4736]{1,0:T(8,128)(2,1)S(1)}) custom-call(f32[24,128]{1,0:T(8,128)S(1)} %get-tuple-element.82.run_ref, bf16[128,3072]{1,0:T(8,128)(2,1)S(1)} %copy-done.2, bf16[128,3072]{1,0:T(8,128)(2,1)S(1)} %copy-done, bf16[128,3072]{1,0:T(8,128)(2,1)S(1)} %copy-done.1, bf16[128,3072]{1,0:T(8,128)(2,1)S(1)} %copy-done.3, ...), custom_call_target="tpu_custom_call" | custom-call | flops 100663296 | bytes 2359296 | tf_op jit(solution)/shard_map/pallas_call | solution.py:182
  24.3 2.2 %shard_map.130 = (f32[128,1536]{1,0:T(8,128)S(1)}, bf16[32,4736]{1,0:T(8,128)(2,1)S(1)}) custom-call(f32[24,128]{1,0:T(8,128)S(1)} %get-tuple-element.82.run_ref, bf16[128,3072]{1,0:T(8,128)(2,1)S(1)} %copy-done.2, bf16[128,3072]{1,0:T(8,128)(2,1)S(1)} %copy-done, bf16[128,3072]{1,0:T(8,128)(2,1)S(1)} %copy-done.1, bf16[128,3072]{1,0:T(8,128)(2,1)S(1)} %copy-done.3, ...), custom_call_target="tpu_custom_call" | custom-call | flops 100663296 | bytes 2359296 | tf_op jit(solution)/shard_map/pallas_call | solution.py:182
  34.3 3.2 %collective-permute-start.16 = (bf16[32,1536]{1,0:T(8,128)(2,1)S(1)}, bf16[32,1536]{1,0:T(8,128)(2,1)S(1)}, u32[]{:S(2)}, u32[]{:S(2)}) collective-permute-start(bf16[32,1536]{1,0:T(8,128)(2,1)S(1)} %constant_dynamic-update-slice_fusion.refs_0_), channel_id=1, source_target_pairs={{0,4},{4,8},{8,12},{12,14},{14,10},{10,6},{6,2},{2,0},{1,5},{5,9},... | collective-permute-start | bytes 294920 | tf_op jit(solution)/shard_map/ppermute | solution.py:643
  37.6 2.5 %collective-permute-start.19 = (bf16[32,1536]{1,0:T(8,128)(2,1)S(1)}, bf16[32,1536]{1,0:T(8,128)(2,1)S(1)}, u32[]{:S(2)}, u32[]{:S(2)}) collective-permute-start(bf16[32,1536]{1,0:T(8,128)(2,1)S(1)} %collective-permute-done.13.refs_1_), channel_id=1, source_target_pairs={{0,4},{4,8},{8,12},{12,14},{14,10},{10,6},{6,2},{2,0},{1,5},{5,9},... | collective-permute-start | bytes 294920 | tf_op jit(solution)/shard_map/ppermute | solution.py:643
  40.7 1.9 %collective-permute-start.21 = (bf16[32,1536]{1,0:T(8,128)(2,1)S(1)}, bf16[32,1536]{1,0:T(8,128)(2,1)S(1)}, u32[]{:S(2)}, u32[]{:S(2)}) collective-permute-start(bf16[32,1536]{1,0:T(8,128)(2,1)S(1)} %collective-permute-done.16.refs_2_), channel_id=1, source_target_pairs={{0,4},{4,8},{8,12},{12,14},{14,10},{10,6},{6,2},{2,0},{1,5},{5,9},... | collective-permute-start | bytes 294920 | tf_op jit(solution)/shard_map/ppermute | solution.py:643
  44.1 2.0 %collective-permute-start.23 = (bf16[32,1536]{1,0:T(8,128)(2,1)S(1)}, bf16[32,1536]{1,0:T(8,128)(2,1)S(1)}, u32[]{:S(2)}, u32[]{:S(2)}) collective-permute-start(bf16[32,1536]{1,0:T(8,128)(2,1)S(1)} %collective-permute-done.19.refs_4_), channel_id=1, source_target_pairs={{0,4},{4,8},{8,12},{12,14},{14,10},{10,6},{6,2},{2,0},{1,5},{5,9},... | collective-permute-start | bytes 294920 | tf_op jit(solution)/shard_map/ppermute | solution.py:643
  46.7 1.8 %collective-permute-start.25 = (bf16[32,1536]{1,0:T(8,128)(2,1)S(1)}, bf16[32,1536]{1,0:T(8,128)(2,1)S(1)}, u32[]{:S(2)}, u32[]{:S(2)}) collective-permute-start(bf16[32,1536]{1,0:T(8,128)(2,1)S(1)} %collective-permute-done.21.refs_6_), channel_id=1, source_target_pairs={{0,4},{4,8},{8,12},{12,14},{14,10},{10,6},{6,2},{2,0},{1,5},{5,9},... | collective-permute-start | bytes 294920 | tf_op jit(solution)/shard_map/ppermute | solution.py:643
  49.8 2.0 %collective-permute-start.27 = (bf16[32,1536]{1,0:T(8,128)(2,1)S(1)}, bf16[32,1536]{1,0:T(8,128)(2,1)S(1)}, u32[]{:S(2)}, u32[]{:S(2)}) collective-permute-start(bf16[32,1536]{1,0:T(8,128)(2,1)S(1)} %collective-permute-done.23.refs_8_), channel_id=1, source_target_pairs={{0,4},{4,8},{8,12},{12,14},{14,10},{10,6},{6,2},{2,0},{1,5},{5,9},... | collective-permute-start | bytes 294920 | tf_op jit(solution)/shard_map/ppermute | solution.py:643
  52.4 1.9 %collective-permute-start.29 = (bf16[32,1536]{1,0:T(8,128)(2,1)S(1)}, bf16[32,1536]{1,0:T(8,128)(2,1)S(1)}, u32[]{:S(2)}, u32[]{:S(2)}) collective-permute-start(bf16[32,1536]{1,0:T(8,128)(2,1)S(1)} %collective-permute-done.25.refs_0_), channel_id=1, source_target_pairs={{0,4},{4,8},{8,12},{12,14},{14,10},{10,6},{6,2},{2,0},{1,5},{5,9},... | collective-permute-start | bytes 294920 | tf_op jit(solution)/shard_map/ppermute | solution.py:643
  55.0 1.7 %collective-permute-done.28.refs_3_ = bf16[32,1536]{1,0:T(8,128)(2,1)S(1)} collective-permute-done((bf16[32,1536]{1,0:T(8,128)(2,1)S(1)}, bf16[32,1536]{1,0:T(8,128)(2,1)S(1)}, u32[]{:S(2)}, u32[]{:S(2)}) %collective-permute-start.28) | collective-permute-done | bytes 98336 | tf_op jit(solution)/shard_map/ppermute | solution.py:643
  56.8 1.6 %shard_map.135 = (bf16[128,6144]{1,0:T(8,128)(2,1)S(1)}, f32[128,128]{1,0:T(8,128)S(1)}, f32[128,768]{1,0:T(8,128)S(1)}, f32[128,768]{1,0:T(8,128)S(1)}) custom-call(f32[1,6144]{1,0:T(1,128)S(1)} %bitcast.29, bf16[6144,768]{1,0:T(8,128)(2,1)S(1)} %bitcast.21, bf16[6144,768]{1,0:T(8,128)(2,1)S(1)} %bitcast.25, ...), custom_call_target="tpu_custom_call" | custom-call | flops 1207959552 | bytes 9437184 | tf_op jit(solution)/shard_map/pallas_call | solution.py:392
  59.2 1.7 %shard_map.136.hidden_ref = bf16[128,768]{1,0:T(8,128)(2,1)S(1)} custom-call(f32[1,6144]{1,0:T(1,128)S(1)} %bitcast.30, bf16[6144,768]{1,0:T(8,128)(2,1)S(1)} %bitcast.22, bf16[6144,768]{1,0:T(8,128)(2,1)S(1)} %bitcast.26, bf16[128,6144]{1,0:T(8,128)(2,1)S(1)} %get-tuple-element.127.early_ref, f32[128,128]{1,0:T(8,128)S(1)} %get-tuple-element.128.early_square_ref, ...), custom_call_target="tpu_custom_call" | custom-call | flops 1207959552 | bytes 9437184 | tf_op jit(solution)/shard_map/pallas_call | solution.py:436
  64.8 2.0 %collective-permute-start.33 = (bf16[16,3072]{1,0:T(8,128)(2,1)S(1)}, bf16[16,3072]{1,0:T(8,128)(2,1)S(1)}, u32[]{:S(2)}, u32[]{:S(2)}) collective-permute-start(bf16[16,3072]{1,0:T(8,128)(2,1)S(1)} %get-tuple-element.163), channel_id=1, source_target_pairs={{0,4},{4,8},{8,12},{12,14},{14,10},{10,6},{6,2},{2,0},{1,5},{5,9},... | collective-permute-start | bytes 294920 | tf_op jit(solution)/shard_map/ppermute | solution.py:684
  69.7 1.8 %collective-permute-start.37 = (bf16[16,3072]{1,0:T(8,128)(2,1)S(1)}, bf16[16,3072]{1,0:T(8,128)(2,1)S(1)}, u32[]{:S(2)}, u32[]{:S(2)}) collective-permute-start(bf16[16,3072]{1,0:T(8,128)(2,1)S(1)} %fusion.12), channel_id=1, source_target_pairs={{0,4},{4,8},{8,12},{12,14},{14,10},{10,6},{6,2},{2,0},{1,5},{5,9},... | collective-permute-start | bytes 294920 | tf_op jit(solution)/shard_map/ppermute | solution.py:684
  72.6 2.0 %collective-permute-start.35 = (bf16[16,3072]{1,0:T(8,128)(2,1)S(1)}, bf16[16,3072]{1,0:T(8,128)(2,1)S(1)}, u32[]{:S(2)}, u32[]{:S(2)}) collective-permute-start(bf16[16,3072]{1,0:T(8,128)(2,1)S(1)} %fusion.14), channel_id=1, source_target_pairs={{0,4},{4,8},{8,12},{12,14},{14,10},{10,6},{6,2},{2,0},{1,5},{5,9},... | collective-permute-start | bytes 294920 | tf_op jit(solution)/shard_map/ppermute | solution.py:684
  74.8 2.3 %collective-permute-start.41 = (bf16[16,3072]{1,0:T(8,128)(2,1)S(1)}, bf16[16,3072]{1,0:T(8,128)(2,1)S(1)}, u32[]{:S(2)}, u32[]{:S(2)}) collective-permute-start(bf16[16,3072]{1,0:T(8,128)(2,1)S(1)} %fusion.9), channel_id=1, source_target_pairs={{0,4},{4,8},{8,12},{12,14},{14,10},{10,6},{6,2},{2,0},{1,5},{5,9},... | collective-permute-start | bytes 294920 | tf_op jit(solution)/shard_map/ppermute | solution.py:684
  78.0 2.3 %collective-permute-start.39 = (bf16[16,3072]{1,0:T(8,128)(2,1)S(1)}, bf16[16,3072]{1,0:T(8,128)(2,1)S(1)}, u32[]{:S(2)}, u32[]{:S(2)}) collective-permute-start(bf16[16,3072]{1,0:T(8,128)(2,1)S(1)} %fusion.15), channel_id=1, source_target_pairs={{0,4},{4,8},{8,12},{12,14},{14,10},{10,6},{6,2},{2,0},{1,5},{5,9},... | collective-permute-start | bytes 294920 | tf_op jit(solution)/shard_map/ppermute | solution.py:684
  80.5 2.1 %collective-permute-start.45 = (bf16[16,3072]{1,0:T(8,128)(2,1)S(1)}, bf16[16,3072]{1,0:T(8,128)(2,1)S(1)}, u32[]{:S(2)}, u32[]{:S(2)}) collective-permute-start(bf16[16,3072]{1,0:T(8,128)(2,1)S(1)} %get-tuple-element.160), channel_id=1, source_target_pairs={{0,4},{4,8},{8,12},{12,14},{14,10},{10,6},{6,2},{2,0},{1,5},{5,9},... | collective-permute-start | bytes 294920 | tf_op jit(solution)/shard_map/ppermute | solution.py:684
  82.8 2.8 %shard_map.139 = (bf16[128,3072]{1,0:T(8,128)(2,1)S(1)}, f32[8,128]{1,0:T(8,128)S(1)}) custom-call(f32[24,128]{1,0:T(8,128)S(1)} %get-tuple-element.82.run_ref, bf16[128,3072]{1,0:T(8,128)(2,1)S(1)} %copy-done.2, f32[128,1536]{1,0:T(8,128)S(1)} %get-tuple-element.98.own_ref, f32[128,1536]{1,0:T(8,128)S(1)} %get-tuple-element.88.other_ref, ...), custom_call_target="tpu_custom_call" | custom-call | flops 100663296 | bytes 4718592 | tf_op jit(solution)/shard_map/pallas_call | solution.py:305
  (164 shorter events, 34.1 us)
Async XLA Ops:
  3.1 7.7 %collective-permute-start = (bf16[528,128]{1,0:T(8,128)(2,1)}, bf16[528,128]{1,0:T(8,128)(2,1)S(1)}, u32[]{:S(2)}, u32[]{:S(2)}) collective-permute-start(bf16[528,128]{1,0:T(8,128)(2,1)} %get-tuple-element.80), channel_id=1, source_target_pairs={{0,2},{2,0},{4,6},{6,4},{8,10},{10,8},{12,14},{14,12},{1,3},{3,1},... | collective-permute-start | bytes 405512 | tf_op jit(solution)/shard_map/ppermute | solution.py:572
  6.2 11.2 %collective-permute-start.2 = (bf16[512,128]{1,0:T(8,128)(2,1)}, bf16[512,128]{1,0:T(8,128)(2,1)S(1)}, u32[]{:S(2)}, u32[]{:S(2)}) collective-permute-start(bf16[512,128]{1,0:T(8,128)(2,1)} %get-tuple-element.84), channel_id=1, source_target_pairs={{0,2},{2,0},{4,6},{6,4},{8,10},{10,8},{12,14},{14,12},{1,3},{3,1},... | collective-permute-start | bytes 393224 | tf_op jit(solution)/shard_map/ppermute | solution.py:572
  6.3 12.6 %collective-permute-start.1 = (bf16[512,128]{1,0:T(8,128)(2,1)}, bf16[512,128]{1,0:T(8,128)(2,1)S(1)}, u32[]{:S(2)}, u32[]{:S(2)}) collective-permute-start(bf16[512,128]{1,0:T(8,128)(2,1)} %get-tuple-element.83), channel_id=1, source_target_pairs={{0,2},{2,0},{4,6},{6,4},{8,10},{10,8},{12,14},{14,12},{1,3},{3,1},... | collective-permute-start | bytes 393224 | tf_op jit(solution)/shard_map/ppermute | solution.py:572
  11.1 10.8 %collective-permute-start.5 = (bf16[4,128,128]{2,1,0:T(8,128)(2,1)S(1)}, bf16[4,128,128]{2,1,0:T(8,128)(2,1)S(1)}, u32[]{:S(2)}, u32[]{:S(2)}) collective-permute-start(bf16[4,128,128]{2,1,0:T(8,128)(2,1)S(1)} %get-tuple-element.157), channel_id=1, source_target_pairs={{0,4},{2,6},{1,5},{3,7},{16,20},{18,22},{17,21},{19,23}} | collective-permute-start | bytes 393224 | tf_op jit(solution)/shard_map/ppermute | solution.py:599
  20.3 10.0 %collective-permute-start.6 = (bf16[32,4736]{1,0:T(8,128)(2,1)S(1)}, bf16[32,4736]{1,0:T(8,128)(2,1)S(1)}, u32[]{:S(2)}, u32[]{:S(2)}) collective-permute-start(bf16[32,4736]{1,0:T(8,128)(2,1)S(1)} %get-tuple-element.93), channel_id=1, source_target_pairs={{0,2},{2,0},{4,6},{6,4},{8,10},{10,8},{12,14},{14,12},{1,3},{3,1},... | collective-permute-start | bytes 909320 | tf_op jit(solution)/shard_map/ppermute | solution.py:591
  29.0 8.4 %collective-permute-start.14 = (bf16[4,128,128]{2,1,0:T(8,128)(2,1)S(1)}, bf16[4,128,128]{2,1,0:T(8,128)(2,1)S(1)}, u32[]{:S(2)}, u32[]{:S(2)}) collective-permute-start(bf16[4,128,128]{2,1,0:T(8,128)(2,1)S(1)} %get-tuple-element.171.moved_ref), channel_id=1, source_target_pairs={{0,2},{2,0},{4,6},{6,4},{8,10},{10,8},{12,14},{14,12},{1,3},{3,1},... | collective-permute-start | bytes 393224 | tf_op jit(solution)/shard_map/ppermute | solution.py:741
  30.9 6.6 %collective-permute-start.15 = (bf16[4,128,128]{2,1,0:T(8,128)(2,1)S(1)}, bf16[4,128,128]{2,1,0:T(8,128)(2,1)S(1)}, u32[]{:S(2)}, u32[]{:S(2)}) collective-permute-start(bf16[4,128,128]{2,1,0:T(8,128)(2,1)S(1)} %get-tuple-element.169.moved_ref), channel_id=1, source_target_pairs={{0,2},{2,0},{4,6},{6,4},{8,10},{10,8},{12,14},{14,12},{1,3},{3,1},... | collective-permute-start | bytes 393224 | tf_op jit(solution)/shard_map/ppermute | solution.py:741
  32.4 8.3 %collective-permute-start.17 = (bf16[4,128,128]{2,1,0:T(8,128)(2,1)S(1)}, bf16[4,128,128]{2,1,0:T(8,128)(2,1)S(1)}, u32[]{:S(2)}, u32[]{:S(2)}) collective-permute-start(bf16[4,128,128]{2,1,0:T(8,128)(2,1)S(1)} %get-tuple-element.167.moved_ref), channel_id=1, source_target_pairs={{0,2},{2,0},{4,6},{6,4},{8,10},{10,8},{12,14},{14,12},{1,3},{3,1},... | collective-permute-start | bytes 393224 | tf_op jit(solution)/shard_map/ppermute | solution.py:741
  34.3 6.5 %collective-permute-start.16 = (bf16[32,1536]{1,0:T(8,128)(2,1)S(1)}, bf16[32,1536]{1,0:T(8,128)(2,1)S(1)}, u32[]{:S(2)}, u32[]{:S(2)}) collective-permute-start(bf16[32,1536]{1,0:T(8,128)(2,1)S(1)} %constant_dynamic-update-slice_fusion.refs_0_), channel_id=1, source_target_pairs={{0,4},{4,8},{8,12},{12,14},{14,10},{10,6},{6,2},{2,0},{1,5},{5,9},... | collective-permute-start | bytes 294920 | tf_op jit(solution)/shard_map/ppermute | solution.py:643
  37.5 5.7 %collective-permute-start.18 = (bf16[32,1536]{1,0:T(8,128)(2,1)S(1)}, bf16[32,1536]{1,0:T(8,128)(2,1)S(1)}, u32[]{:S(2)}, u32[]{:S(2)}) collective-permute-start(bf16[32,1536]{1,0:T(8,128)(2,1)S(1)} %collective-permute-done.13.refs_1_), channel_id=1, source_target_pairs={{4,0},{8,4},{12,8},{14,12},{10,14},{6,10},{2,6},{0,2},{5,1},{9,5},... | collective-permute-start | bytes 294920 | tf_op jit(solution)/shard_map/ppermute | solution.py:643
  37.6 6.5 %collective-permute-start.19 = (bf16[32,1536]{1,0:T(8,128)(2,1)S(1)}, bf16[32,1536]{1,0:T(8,128)(2,1)S(1)}, u32[]{:S(2)}, u32[]{:S(2)}) collective-permute-start(bf16[32,1536]{1,0:T(8,128)(2,1)S(1)} %collective-permute-done.13.refs_1_), channel_id=1, source_target_pairs={{0,4},{4,8},{8,12},{12,14},{14,10},{10,6},{6,2},{2,0},{1,5},{5,9},... | collective-permute-start | bytes 294920 | tf_op jit(solution)/shard_map/ppermute | solution.py:643
  40.1 6.0 %collective-permute-start.20 = (bf16[32,1536]{1,0:T(8,128)(2,1)S(1)}, bf16[32,1536]{1,0:T(8,128)(2,1)S(1)}, u32[]{:S(2)}, u32[]{:S(2)}) collective-permute-start(bf16[32,1536]{1,0:T(8,128)(2,1)S(1)} %constant_dynamic-update-slice_fusion.refs_0_), channel_id=1, source_target_pairs={{4,0},{8,4},{12,8},{14,12},{10,14},{6,10},{2,6},{0,2},{5,1},{9,5},... | collective-permute-start | bytes 294920 | tf_op jit(solution)/shard_map/ppermute | solution.py:643
  40.7 6.0 %collective-permute-start.21 = (bf16[32,1536]{1,0:T(8,128)(2,1)S(1)}, bf16[32,1536]{1,0:T(8,128)(2,1)S(1)}, u32[]{:S(2)}, u32[]{:S(2)}) collective-permute-start(bf16[32,1536]{1,0:T(8,128)(2,1)S(1)} %collective-permute-done.16.refs_2_), channel_id=1, source_target_pairs={{0,4},{4,8},{8,12},{12,14},{14,10},{10,6},{6,2},{2,0},{1,5},{5,9},... | collective-permute-start | bytes 294920 | tf_op jit(solution)/shard_map/ppermute | solution.py:643
  43.1 6.5 %collective-permute-start.22 = (bf16[32,1536]{1,0:T(8,128)(2,1)S(1)}, bf16[32,1536]{1,0:T(8,128)(2,1)S(1)}, u32[]{:S(2)}, u32[]{:S(2)}) collective-permute-start(bf16[32,1536]{1,0:T(8,128)(2,1)S(1)} %collective-permute-done.18.refs_3_), channel_id=1, source_target_pairs={{4,0},{8,4},{12,8},{14,12},{10,14},{6,10},{2,6},{0,2},{5,1},{9,5},... | collective-permute-start | bytes 294920 | tf_op jit(solution)/shard_map/ppermute | solution.py:643
  44.1 5.6 %collective-permute-start.23 = (bf16[32,1536]{1,0:T(8,128)(2,1)S(1)}, bf16[32,1536]{1,0:T(8,128)(2,1)S(1)}, u32[]{:S(2)}, u32[]{:S(2)}) collective-permute-start(bf16[32,1536]{1,0:T(8,128)(2,1)S(1)} %collective-permute-done.19.refs_4_), channel_id=1, source_target_pairs={{0,4},{4,8},{8,12},{12,14},{14,10},{10,6},{6,2},{2,0},{1,5},{5,9},... | collective-permute-start | bytes 294920 | tf_op jit(solution)/shard_map/ppermute | solution.py:643
  46.1 5.7 %collective-permute-start.24 = (bf16[32,1536]{1,0:T(8,128)(2,1)S(1)}, bf16[32,1536]{1,0:T(8,128)(2,1)S(1)}, u32[]{:S(2)}, u32[]{:S(2)}) collective-permute-start(bf16[32,1536]{1,0:T(8,128)(2,1)S(1)} %collective-permute-done.20.refs_5_), channel_id=1, source_target_pairs={{4,0},{8,4},{12,8},{14,12},{10,14},{6,10},{2,6},{0,2},{5,1},{9,5},... | collective-permute-start | bytes 294920 | tf_op jit(solution)/shard_map/ppermute | solution.py:643
  46.7 5.7 %collective-permute-start.25 = (bf16[32,1536]{1,0:T(8,128)(2,1)S(1)}, bf16[32,1536]{1,0:T(8,128)(2,1)S(1)}, u32[]{:S(2)}, u32[]{:S(2)}) collective-permute-start(bf16[32,1536]{1,0:T(8,128)(2,1)S(1)} %collective-permute-done.21.refs_6_), channel_id=1, source_target_pairs={{0,4},{4,8},{8,12},{12,14},{14,10},{10,6},{6,2},{2,0},{1,5},{5,9},... | collective-permute-start | bytes 294920 | tf_op jit(solution)/shard_map/ppermute | solution.py:643
  52.4 6.0 %collective-permute-start.29 = (bf16[32,1536]{1,0:T(8,128)(2,1)S(1)}, bf16[32,1536]{1,0:T(8,128)(2,1)S(1)}, u32[]{:S(2)}, u32[]{:S(2)}) collective-permute-start(bf16[32,1536]{1,0:T(8,128)(2,1)S(1)} %collective-permute-done.25.refs_0_), channel_id=1, source_target_pairs={{0,4},{4,8},{8,12},{12,14},{14,10},{10,6},{6,2},{2,0},{1,5},{5,9},... | collective-permute-start | bytes 294920 | tf_op jit(solution)/shard_map/ppermute | solution.py:643
  61.8 5.7 %collective-permute-start.34 = (bf16[16,3072]{1,0:T(8,128)(2,1)S(1)}, bf16[16,3072]{1,0:T(8,128)(2,1)S(1)}, u32[]{:S(2)}, u32[]{:S(2)}) collective-permute-start(bf16[16,3072]{1,0:T(8,128)(2,1)S(1)} %get-tuple-element.165), channel_id=1, source_target_pairs={{4,0},{8,4},{12,8},{14,12},{10,14},{6,10},{2,6},{0,2},{5,1},{9,5},... | collective-permute-start | bytes 294920 | tf_op jit(solution)/shard_map/ppermute | solution.py:684
  62.4 10.2 %collective-permute-start.31 = (bf16[16,3072]{1,0:T(8,128)(2,1)S(1)}, bf16[16,3072]{1,0:T(8,128)(2,1)S(1)}, u32[]{:S(2)}, u32[]{:S(2)}) collective-permute-start(bf16[16,3072]{1,0:T(8,128)(2,1)S(1)} %get-tuple-element.166), channel_id=1, source_target_pairs={{0,4},{4,8},{8,12},{12,14},{14,10},{10,6},{6,2},{2,0},{1,5},{5,9},... | collective-permute-start | bytes 294920 | tf_op jit(solution)/shard_map/ppermute | solution.py:684
  66.8 5.6 %collective-permute-start.32 = (bf16[16,3072]{1,0:T(8,128)(2,1)S(1)}, bf16[16,3072]{1,0:T(8,128)(2,1)S(1)}, u32[]{:S(2)}, u32[]{:S(2)}) collective-permute-start(bf16[16,3072]{1,0:T(8,128)(2,1)S(1)} %get-tuple-element.164), channel_id=1, source_target_pairs={{4,0},{8,4},{12,8},{14,12},{10,14},{6,10},{2,6},{0,2},{5,1},{9,5},... | collective-permute-start | bytes 294920 | tf_op jit(solution)/shard_map/ppermute | solution.py:684
  67.6 7.0 %collective-permute-start.38 = (bf16[16,3072]{1,0:T(8,128)(2,1)S(1)}, bf16[16,3072]{1,0:T(8,128)(2,1)S(1)}, u32[]{:S(2)}, u32[]{:S(2)}) collective-permute-start(bf16[16,3072]{1,0:T(8,128)(2,1)S(1)} %fusion.11), channel_id=1, source_target_pairs={{4,0},{8,4},{12,8},{14,12},{10,14},{6,10},{2,6},{0,2},{5,1},{9,5},... | collective-permute-start | bytes 294920 | tf_op jit(solution)/shard_map/ppermute | solution.py:684
  74.6 5.7 %collective-permute-start.42 = (bf16[16,3072]{1,0:T(8,128)(2,1)S(1)}, bf16[16,3072]{1,0:T(8,128)(2,1)S(1)}, u32[]{:S(2)}, u32[]{:S(2)}) collective-permute-start(bf16[16,3072]{1,0:T(8,128)(2,1)S(1)} %fusion.8), channel_id=1, source_target_pairs={{4,0},{8,4},{12,8},{14,12},{10,14},{6,10},{2,6},{0,2},{5,1},{9,5},... | collective-permute-start | bytes 294920 | tf_op jit(solution)/shard_map/ppermute | solution.py:684
  74.8 5.6 %collective-permute-start.41 = (bf16[16,3072]{1,0:T(8,128)(2,1)S(1)}, bf16[16,3072]{1,0:T(8,128)(2,1)S(1)}, u32[]{:S(2)}, u32[]{:S(2)}) collective-permute-start(bf16[16,3072]{1,0:T(8,128)(2,1)S(1)} %fusion.9), channel_id=1, source_target_pairs={{0,4},{4,8},{8,12},{12,14},{14,10},{10,6},{6,2},{2,0},{1,5},{5,9},... | collective-permute-start | bytes 294920 | tf_op jit(solution)/shard_map/ppermute | solution.py:684
  (42 other events, 341.2 us)

commit v7 on v6

--- a/solution.py
+++ b/solution.py
@@ -62,9 +62,10 @@
         copies.append(pair)
     log_copy.wait()
     running = running_sums(log[...])
-    total = running[:, length - 1 :]
-    rest = as_columns(jnp.exp(total - running))
-    rest = jnp.where(side == 0, rest[:, :half], rest[:, half:heads])
+    columns = as_columns(running)
+    columns = jnp.where(side == 0, columns[:, :half], columns[:, half:heads])
+    totals = columns[length - 1 :, :]
+    rest = jnp.exp(totals - columns)
     for head in range(half):
         chunk, place = divmod(head, part)
         if place == 0:
@@ -78,8 +79,6 @@
         rows = slice(place * width, (place + 1) * width)
         outs[chunk][rows, :] = state.astype(outs[chunk].dtype)
     if sent:
-        totals = as_columns(jnp.broadcast_to(total, (heads, length)))[:1]
-        totals = jnp.where(side == 0, totals[:, :half], totals[:, half:heads])
         first = totals.astype(BF16).astype(F32)
         second = (totals - first).astype(BF16).astype(F32)
         third = totals - first - second
@@ -240,42 +239,38 @@
 
 
 def hidden_kernel(
+    sent,
     run_ref,
     query_ref,
-    own_ref,
-    other_ref,
+    within_ref,
     residual_ref,
     gain_ref,
     moe_gain_ref,
     router_ref,
     route_ref,
+    before_ref,
     *refs,
 ):
     *state_refs, hidden_ref, sums_ref = refs
     heads, length = run_ref.shape
-    span = query_ref.shape[1]
-    width = span // heads
+    span = hidden_ref.shape[1]
     half, part = (heads // 2, state_refs[0].shape[0])
-    grown = as_columns(jnp.exp(run_ref[...]))
-    even = lax.axis_index("seq") % 2 == 0
+    width = span // half
+    side = (lax.axis_index("seq") + sent) % 2
+    grown = as_columns(jnp.exp(jnp.where(side == 0, run_ref[:half, :], run_ref[half:, :])))
     squares = jnp.zeros((length, width), F32)
-    for head in range(heads):
-        lanes = slice(head * width, (head + 1) * width)
-        chunk, place = divmod(head % half, part)
-        kept, swapped = (state_refs[chunk][place], state_refs[CHUNKS + chunk][place])
-        here = slice(head % half * width, (head % half + 1) * width)
-        own, other = (own_ref[:, here], other_ref[:, here])
-        if head >= half:
-            kept, swapped, own, other = (swapped, kept, other, own)
-        state, within = (jnp.where(even, kept, swapped), jnp.where(even, own, other))
+    for head in range(half):
+        here = slice(head * width, (head + 1) * width)
+        lanes = pl.ds(pl.multiple_of((side * half + head) * width, width), width)
+        state = state_refs[head // part][head % part]
         carried = jnp.dot(query_ref[:, lanes], state, preferred_element_type=F32)
-        raw = within + carried * grown[:, head : head + 1]
+        raw = within_ref[:, here] + carried * grown[:, head : head + 1]
         normed = raw * lax.rsqrt(jnp.mean(raw * raw, axis=1, keepdims=True) + 1e-05)
         hidden = (residual_ref[:, lanes].astype(F32) + normed * gain_ref[:, lanes]).astype(BF16)
-        hidden_ref[:, lanes] = hidden
+        hidden_ref[:, here] = hidden
         value = hidden.astype(F32)
         squares += value * value
-    here = pl.ds(pl.multiple_of(lax.axis_index("exp") * span, span), span)
+    here = pl.ds(pl.multiple_of((lax.axis_index("exp") * 2 + side) * span, span), span)
     weights = router_ref[:, here].astype(F32) * moe_gain_ref[:, here]
     first = weights.astype(BF16)
     second = (weights - first.astype(F32)).astype(BF16)
@@ -292,33 +287,30 @@
     for choice in range(2):
         here = slice(choice, choice + 1)
         chosen = jnp.where(route_ref[here, :] == expert, logits, 0.0)
-        sums_ref[here, :] = jnp.sum(chosen, axis=0, keepdims=True)
-    sums_ref[2:3, :] = jnp.sum(squares.T, axis=0, keepdims=True)
+        sums_ref[here, :] = before_ref[here, :] + jnp.sum(chosen, axis=0, keepdims=True)
+    sums_ref[2:3, :] = before_ref[2:3, :] + jnp.sum(squares.T, axis=0, keepdims=True)
     sums_ref[3:, :] = jnp.zeros((sums_ref.shape[0] - 3, length), F32)
 
 
 def hidden_block(
-    running, query_rows, own, other, residual, gain, moe_gain, router, routes, kept, swapped
+    sent, running, query_rows, within, residual, gain, moe_gain, router, routes, before, states
 ):
     heads, length = running.shape
-    wide = query_rows.shape[1]
-    return pl.pallas_call(
-        hidden_kernel,
+    return pl.pallas_call(
+        functools.partial(hidden_kernel, sent),
         out_shape=(
-            jax.ShapeDtypeStruct((length, wide), BF16),
-            jax.ShapeDtypeStruct((8, length), F32),
-        ),
-        in_specs=[VMEM] * (9 + 2 * CHUNKS),
+            jax.ShapeDtypeStruct(within.shape, BF16),
+            jax.ShapeDtypeStruct(before.shape, F32),
+        ),
+        in_specs=[VMEM] * (9 + CHUNKS),
         out_specs=(VMEM, VMEM),
-        compiler_params=grant(16),
+        compiler_params=grant(8),
         cost_estimate=pl.CostEstimate(
-            flops=2 * length * wide * (wide // heads),
-            bytes_accessed=12 * length * wide,
+            flops=4 * within.size * within.shape[1] // heads,
+            bytes_accessed=12 * within.size,
             transcendentals=0,
         ),
-    )(
-        running, query_rows, own, other, residual, gain, moe_gain, router, routes, *kept, *swapped
-    )
+    )(running, query_rows, within, residual, gain, moe_gain, router, routes, before, *states)
 
 
 def far_side(count):
@@ -453,11 +445,13 @@
 
 
 def down_kernel(half, hidden_ref, down_ref, out_ref):
-    width = out_ref.shape[1]
+    quarter = out_ref.shape[1] // 2
     for part in range(2):
-        lanes = slice(part * width // 2, (part + 1) * width // 2)
-        weights = down_ref[:, half * width + lanes.start : half * width + lanes.stop]
-        out_ref[:, lanes] = jnp.dot(hidden_ref[...], weights, preferred_element_type=F32)
+        first = ((lax.axis_index("exp") ^ half) * 2 + part) * quarter
+        weights = down_ref[:, pl.ds(pl.multiple_of(first, quarter), quarter)]
+        out_ref[:, part * quarter : (part + 1) * quarter] = jnp.dot(
+            hidden_ref[...], weights, preferred_element_type=F32
+        )
 
 
 def expert_down(half, hidden, down_weight):
@@ -474,31 +468,6 @@
             transcendentals=0,
         ),
     )(hidden, down_weight)
-
-
-def total_kernel(low_ref, high_ref, *refs):
-    *got_refs, kept_ref, sent_ref = refs
-    totals = []
-    for own_ref, first, second in ((low_ref, 0, 1), (high_ref, 2, 3)):
-        got = got_refs[first][...].astype(F32) + got_refs[second][...].astype(F32)
-        totals.append((own_ref[...] + got).astype(BF16))
-    low = lax.axis_index("exp") == 0
-    kept_ref[...] = jnp.where(low, totals[0], totals[1])
-    sent_ref[...] = jnp.where(low, totals[1], totals[0])
-
-
-def expert_total(low, high, *gots):
-    shape = jax.ShapeDtypeStruct(low.shape, BF16)
-    return pl.pallas_call(
-        total_kernel,
-        out_shape=(shape, shape),
-        in_specs=[VMEM] * (2 + len(gots)),
-        out_specs=(VMEM, VMEM),
-        compiler_params=grant(4),
-        cost_estimate=pl.CostEstimate(
-            flops=4 * low.size, bytes_accessed=20 * low.size, transcendentals=0
-        ),
-    )(low, high, *gots)
 
 
 def share_kernel(span, sums_ref, got_sums_ref, route_ref, slot_ref, table_ref):
@@ -524,14 +493,24 @@
     )(sums, got_sums, routes, slots)
 
 
-def mixed_kernel(table_ref, hidden_ref, own_ref, got_ref, out_ref, held_ref, sems):
-    span = own_ref.shape[1]
+def mixed_kernel(table_ref, kept_ref, swapped_ref, *refs):
+    *part_refs, out_ref, held_ref, sems = refs
+    span = out_ref.shape[1]
+    even = lax.axis_index("seq") % 2 == 0
     copies = []
     for part in range(4):
         lanes = slice(part * span // 4, (part + 1) * span // 4)
-        outs = jnp.concatenate([own_ref[:, lanes], got_ref[:, lanes]] * 2, axis=0)
+        parts = [ref[:, lanes].astype(F32) for ref in part_refs]
+        own, other = [
+            (first + second + third).astype(BF16)
+            for first, second, third in (parts[:3], parts[3:])
+        ]
+        outs = jnp.concatenate([own, other] * 2, axis=0)
         mixed = jnp.dot(table_ref[...], outs, preferred_element_type=F32)
-        held_ref[:, lanes] = (hidden_ref[:, lanes].astype(F32) + mixed).astype(BF16)
+        here = slice(part % 2 * span // 4, (part % 2 + 1) * span // 4)
+        halves = (kept_ref[:, here], swapped_ref[:, here])
+        hidden = jnp.where(even, halves[part // 2], halves[1 - part // 2])
+        held_ref[:, lanes] = (hidden.astype(F32) + mixed).astype(BF16)
         copies.append(
             pltpu.make_async_copy(held_ref.at[:, lanes], out_ref.at[:, lanes], sems.at[part])
         )
@@ -540,20 +519,21 @@
         copy.wait()
 
 
-def mixed_block(table, hidden, own, got):
+def mixed_block(table, kept, swapped, parts):
+    shape = (kept.shape[0], 2 * kept.shape[1])
     return pl.pallas_call(
         mixed_kernel,
-        out_shape=jax.ShapeDtypeStruct(hidden.shape, BF16),
-        in_specs=[VMEM] * 4,
+        out_shape=jax.ShapeDtypeStruct(shape, BF16),
+        in_specs=[VMEM] * (3 + len(parts)),
         out_specs=HBM,
-        scratch_shapes=[pltpu.VMEM(hidden.shape, BF16), pltpu.SemaphoreType.DMA((4,))],
+        scratch_shapes=[pltpu.VMEM(shape, BF16), pltpu.SemaphoreType.DMA((4,))],
         compiler_params=grant(8),
         cost_estimate=pl.CostEstimate(
-            flops=8 * hidden.size * own.shape[0],
-            bytes_accessed=4 * hidden.size,
+            flops=16 * kept.size * CAP,
+            bytes_accessed=8 * kept.size,
             transcendentals=0,
         ),
-    )(table, hidden, own, got)
+    )(table, kept, swapped, *parts)
 
 
 def after(value, *others):
@@ -660,13 +640,19 @@
     return [(to_left, 0), (to_right, 1), (to_left, 1), (to_right, 0)]
 
 
-def ring_scatter(low, rest, rows, last):
+def ring_scatter(own, rest, rows, holds):
     steps = lax.axis_size("seq") // 2
     right, left = ring_pairs(2 * steps)
-    partials = [low, None]
+    partials = [own, None]
 
     def piece(position, half):
         return partials[half][position * rows : (position + 1) * rows]
+
+    def move(sent, half, way, last):
+        if half == 0 or not last:
+            return lax.ppermute(sent, "seq", way)
+        across = [(2 * a + core, 2 * b + 1 - core) for a, b in way for core in range(2)]
+        return lax.ppermute(sent, ("seq", "exp"), across)
 
     chains = [
         (0, left, [steps, *range(steps - 1, 0, -1)]),
@@ -677,16 +663,19 @@
     sents = [piece(positions[0], 0).astype(BF16) for _, _, positions in chains[:2]]
     partials[1] = rest(sents)
     sents += [piece(positions[0], 1).astype(BF16) for _, _, positions in chains[2:]]
+    here = piece(0, 1).astype(BF16)
     marks = list(sents)
     for step in range(1, steps + 1):
-        order = (0, 2, 3, 1)
-        gots = {
-            k: lax.ppermute(sents[k], "seq", chains[k][1])
-            for k in order
-            if step <= len(chains[k][2])
-        }
-        if step == steps:
-            marks = [*marks, *last(marks)]
+        gots = {}
+        for k in (0, 2, 3, 1):
+            half, way, positions = chains[k]
+            if step <= len(positions):
+                gots[k] = move(sents[k], half, way, step == len(positions))
+        if step == 2:
+            here = lax.ppermute(here, "exp", [(0, 1), (1, 0)])
+            marks = [*marks, here]
+        if step in holds:
+            marks = [*marks, *holds[step]([sents[k] for k in gots])]
         for k, got in gots.items():
             half, _, positions = chains[k]
             got = after(got, *marks)
@@ -694,7 +683,7 @@
                 got = (piece(positions[step], half) + got.astype(F32)).astype(BF16)
             sents[k] = got
             marks = [got]
-    return (piece(0, 0), piece(0, 1), *sents)
+    return (piece(0, 0), sents[0], sents[1], here, sents[2], sents[3])
 
 
 def shards(
@@ -751,7 +740,28 @@
     )
     rows_mine, rows_sent, kept, swapped = zip(*finished, strict=True)
     rows_got = lax.ppermute(jnp.concatenate(rows_sent, axis=1), "exp", exchange)
-    halves = (jnp.concatenate(rows_mine, axis=1), after(rows_got, *swapped[:2]))
+
+    def all_rows(sent, mark, within, before, entering):
+        return hidden_block(
+            sent,
+            running,
+            queries,
+            within,
+            after(residual, *mark),
+            attn_gain,
+            moe_gain,
+            router.T,
+            route_rows,
+            before,
+            entering,
+        )
+
+    zeros = jnp.zeros((8, running.shape[1]), F32)
+    hidden_own, sums = all_rows(False, rows_sent, within_own, zeros, kept)
+    halves = (
+        jnp.concatenate(rows_mine, axis=1),
+        after(rows_got, *swapped[:2], hidden_own, sums),
+    )
 
     steps = count // 2
     early = []
@@ -784,7 +794,7 @@
         gate_weight[0],
         up_weight[0],
     )
-    low = expert_down(0, hidden_units, down_weight[0])
+    own = expert_down(0, hidden_units, down_weight[0])
 
     def rest(marks):
         return expert_down(1, after(hidden_units, *marks), down_weight[0])
@@ -792,30 +802,16 @@
     held = []
 
     def hold_hidden(marks):
-        held.extend(
-            hidden_block(
-                running,
-                queries,
-                within_own,
-                within_other,
-                after(residual, *marks),
-                attn_gain,
-                moe_gain,
-                router.T,
-                route_rows,
-                kept,
-                swapped,
-            )
+        held.extend(all_rows(True, marks, within_other, sums, swapped))
+        got_sums = lax.ppermute(held[1], "exp", exchange)
+        held.append(
+            share_table(queries.shape[1], held[1], got_sums, route_rows, slot_rows)
         )
         return held
 
-    sums_here = ring_scatter(low, rest, CAP, hold_hidden)
-    hidden_half, sums = held
-    got_sums = lax.ppermute(sums, "exp", exchange)
-    table = share_table(queries.shape[1], sums, got_sums, route_rows, slot_rows)
-    out_own, out_sent = expert_total(*sums_here)
-    out_got = lax.ppermute(out_sent, "exp", exchange)
-    return mixed_block(table, hidden_half, out_own, out_got)
+    parts = ring_scatter(own, rest, CAP, {steps: hold_hidden})
+    hidden_other, _, table = held
+    return mixed_block(table, hidden_own, hidden_other, parts)
 
 
 def solution(mesh):

time: 89 us -> 88.2 us (level)
  starting transfers between devices: 54.7 us -> 53.2 us
    ppermute x16, starting transfers between devices: 16.1 us -> 14.5 us  [the longest x12 12.4 us: move(): return lax.ppermute(sent, 'seq', way)]
  transfers between devices with their start and end apart: 47 -> 47, of which waited for: 15 -> 15; matrix products, arithmetic and copies ran while one was open for 2% -> 2% of each run, Pallas kernels for 15% -> 16%
where the time goes in v7:
time: 88.2 us; the launch traced here: 87.9 us
  starting transfers between devices  53.2 us (60%)
  Pallas kernels  20.4 us (23%)
  waiting for transfers between devices  11.2 us (13%)
  other arithmetic  2.19 us (2%)
    ppermute x14, starting transfers between devices, ring_gather(): lax.ppermute(moving[k], 'seq', way)  17.8 us
    ppermute x12, starting transfers between devices, move(): return lax.ppermute(sent, 'seq', way)  12.4 us
    ppermute x9, starting transfers between devices, entering_state(): gots = [lax.ppermute(sent, 'seq', pairs) for sent in sents]  10.6 us
    ppermute x14, waiting for transfers between devices, ring_gather(): lax.ppermute(moving[k], 'seq', way)  5.2 us
    ppermute x3, starting transfers between devices, entering_state(): arrived = after(lax.ppermute(sending[chunk], 'seq', swap), *marks)  5.14 us
    pallas_call x2, Pallas kernels, half_state(): pl.pallas_call(functools.partial(state_kernel, sent), out_shape=tuple(sha...  4.76 us
    pallas_call x2, Pallas kernels, within_block(): pl.pallas_call(functools.partial(within_kernel, sent), out_shape=(jax.Sha...  4.48 us
    ppermute x12, waiting for transfers between devices, move(): return lax.ppermute(sent, 'seq', way)  4.37 us
  transfers between devices with their start and end apart: 47, of which 15 were waited for; matrix products, arithmetic and copies ran while one was open for 2% of the time, Pallas kernels for 16%

profile of v7, /device:TPU:0, one launch (start us, length us, event | category | flops | bytes accessed | tf_op | source)
XLA Modules:
  0.0 87.9 jit_solution(12697821537129653307)
XLA Ops:
  0.0 3.0 %shard_map.127 = (bf16[528,128]{1,0:T(8,128)(2,1)}, bf16[512,128]{1,0:T(8,128)(2,1)}, bf16[512,128]{1,0:T(8,128)(2,1)}) custom-call(f32[24,128]{1,0:T(8,128)} %bitcast.39, bf16[128,3072]{1,0:T(8,128)(2,1)} %key_ref.7, bf16[128,3072]{1,0:T(8,128)(2,1)} %value_ref.7), custom_call_target="tpu_custom_call" | custom-call | flops 50331648 | bytes 786432 | tf_op jit(solution)/shard_map/pallas_call | solution.py:101
  3.1 3.0 %collective-permute-start = (bf16[528,128]{1,0:T(8,128)(2,1)}, bf16[528,128]{1,0:T(8,128)(2,1)S(1)}, u32[]{:S(2)}, u32[]{:S(2)}) collective-permute-start(bf16[528,128]{1,0:T(8,128)(2,1)} %get-tuple-element.81), channel_id=1, source_target_pairs={{0,2},{2,0},{4,6},{6,4},{8,10},{10,8},{12,14},{14,12},{1,3},{3,1},... | collective-permute-start | bytes 405512 | tf_op jit(solution)/shard_map/ppermute | solution.py:552
  6.2 2.0 %collective-permute-start.1 = (bf16[512,128]{1,0:T(8,128)(2,1)}, bf16[512,128]{1,0:T(8,128)(2,1)S(1)}, u32[]{:S(2)}, u32[]{:S(2)}) collective-permute-start(bf16[512,128]{1,0:T(8,128)(2,1)} %get-tuple-element.87), channel_id=1, source_target_pairs={{0,2},{2,0},{4,6},{6,4},{8,10},{10,8},{12,14},{14,12},{1,3},{3,1},... | collective-permute-start | bytes 393224 | tf_op jit(solution)/shard_map/ppermute | solution.py:552
  8.2 1.7 %shard_map.128 = (f32[512,128]{1,0:T(8,128)S(1)}, f32[512,128]{1,0:T(8,128)S(1)}, f32[512,128]{1,0:T(8,128)S(1)}, f32[24,128]{1,0:T(8,128)S(1)}) custom-call(f32[24,128]{1,0:T(8,128)S(1)} %bitcast.40, bf16[128,3072]{1,0:T(8,128)(2,1)S(1)} %copy-done, bf16[128,3072]{1,0:T(8,128)(2,1)S(1)} %copy-done.1), custom_call_target="tpu_custom_call" | custom-call | flops 50331648 | bytes 786432 | tf_op jit(solution)/shard_map/pallas_call | solution.py:101
  11.0 4.0 %collective-permute-start.5 = (bf16[4,128,128]{2,1,0:T(8,128)(2,1)S(1)}, bf16[4,128,128]{2,1,0:T(8,128)(2,1)S(1)}, u32[]{:S(2)}, u32[]{:S(2)}) collective-permute-start(bf16[4,128,128]{2,1,0:T(8,128)(2,1)S(1)} %get-tuple-element.159), channel_id=1, source_target_pairs={{0,4},{2,6},{1,5},{3,7},{16,20},{18,22},{17,21},{19,23}} | collective-permute-start | bytes 393224 | tf_op jit(solution)/shard_map/ppermute | solution.py:579
  15.1 2.2 %shard_map.129 = (f32[128,1536]{1,0:T(8,128)S(1)}, bf16[32,4736]{1,0:T(8,128)(2,1)S(1)}) custom-call(f32[24,128]{1,0:T(8,128)S(1)} %get-tuple-element.83.run_ref, bf16[128,3072]{1,0:T(8,128)(2,1)S(1)} %copy-done.2, bf16[128,3072]{1,0:T(8,128)(2,1)S(1)} %copy-done, bf16[128,3072]{1,0:T(8,128)(2,1)S(1)} %copy-done.1, bf16[128,3072]{1,0:T(8,128)(2,1)S(1)} %copy-done.3, ...), custom_call_target="tpu_custom_call" | custom-call | flops 100663296 | bytes 2359296 | tf_op jit(solution)/shard_map/pallas_call | solution.py:181
  24.2 2.2 %shard_map.130 = (f32[128,1536]{1,0:T(8,128)S(1)}, bf16[32,4736]{1,0:T(8,128)(2,1)S(1)}) custom-call(f32[24,128]{1,0:T(8,128)S(1)} %get-tuple-element.83.run_ref, bf16[128,3072]{1,0:T(8,128)(2,1)S(1)} %copy-done.2, bf16[128,3072]{1,0:T(8,128)(2,1)S(1)} %copy-done, bf16[128,3072]{1,0:T(8,128)(2,1)S(1)} %copy-done.1, bf16[128,3072]{1,0:T(8,128)(2,1)S(1)} %copy-done.3, ...), custom_call_target="tpu_custom_call" | custom-call | flops 100663296 | bytes 2359296 | tf_op jit(solution)/shard_map/pallas_call | solution.py:181
  34.2 3.2 %collective-permute-start.16 = (bf16[32,1536]{1,0:T(8,128)(2,1)S(1)}, bf16[32,1536]{1,0:T(8,128)(2,1)S(1)}, u32[]{:S(2)}, u32[]{:S(2)}) collective-permute-start(bf16[32,1536]{1,0:T(8,128)(2,1)S(1)} %constant_dynamic-update-slice_fusion.refs_0_), channel_id=1, source_target_pairs={{0,4},{4,8},{8,12},{12,14},{14,10},{10,6},{6,2},{2,0},{1,5},{5,9},... | collective-permute-start | bytes 294920 | tf_op jit(solution)/shard_map/ppermute | solution.py:623
  39.1 2.6 %collective-permute-start.19 = (bf16[32,1536]{1,0:T(8,128)(2,1)S(1)}, bf16[32,1536]{1,0:T(8,128)(2,1)S(1)}, u32[]{:S(2)}, u32[]{:S(2)}) collective-permute-start(bf16[32,1536]{1,0:T(8,128)(2,1)S(1)} %collective-permute-done.13.refs_1_), channel_id=1, source_target_pairs={{0,4},{4,8},{8,12},{12,14},{14,10},{10,6},{6,2},{2,0},{1,5},{5,9},... | collective-permute-start | bytes 294920 | tf_op jit(solution)/shard_map/ppermute | solution.py:623
  41.7 2.5 %collective-permute-start.21 = (bf16[32,1536]{1,0:T(8,128)(2,1)S(1)}, bf16[32,1536]{1,0:T(8,128)(2,1)S(1)}, u32[]{:S(2)}, u32[]{:S(2)}) collective-permute-start(bf16[32,1536]{1,0:T(8,128)(2,1)S(1)} %collective-permute-done.16.refs_2_), channel_id=1, source_target_pairs={{0,4},{4,8},{8,12},{12,14},{14,10},{10,6},{6,2},{2,0},{1,5},{5,9},... | collective-permute-start | bytes 294920 | tf_op jit(solution)/shard_map/ppermute | solution.py:623
  44.7 2.9 %collective-permute-start.23 = (bf16[32,1536]{1,0:T(8,128)(2,1)S(1)}, bf16[32,1536]{1,0:T(8,128)(2,1)S(1)}, u32[]{:S(2)}, u32[]{:S(2)}) collective-permute-start(bf16[32,1536]{1,0:T(8,128)(2,1)S(1)} %collective-permute-done.19.refs_4_), channel_id=1, source_target_pairs={{0,4},{4,8},{8,12},{12,14},{14,10},{10,6},{6,2},{2,0},{1,5},{5,9},... | collective-permute-start | bytes 294920 | tf_op jit(solution)/shard_map/ppermute | solution.py:623
  47.7 2.1 %collective-permute-start.25 = (bf16[32,1536]{1,0:T(8,128)(2,1)S(1)}, bf16[32,1536]{1,0:T(8,128)(2,1)S(1)}, u32[]{:S(2)}, u32[]{:S(2)}) collective-permute-start(bf16[32,1536]{1,0:T(8,128)(2,1)S(1)} %collective-permute-done.21.refs_6_), channel_id=1, source_target_pairs={{0,4},{4,8},{8,12},{12,14},{14,10},{10,6},{6,2},{2,0},{1,5},{5,9},... | collective-permute-start | bytes 294920 | tf_op jit(solution)/shard_map/ppermute | solution.py:623
  50.9 2.2 %collective-permute-start.27 = (bf16[32,1536]{1,0:T(8,128)(2,1)S(1)}, bf16[32,1536]{1,0:T(8,128)(2,1)S(1)}, u32[]{:S(2)}, u32[]{:S(2)}) collective-permute-start(bf16[32,1536]{1,0:T(8,128)(2,1)S(1)} %collective-permute-done.23.refs_8_), channel_id=1, source_target_pairs={{0,4},{4,8},{8,12},{12,14},{14,10},{10,6},{6,2},{2,0},{1,5},{5,9},... | collective-permute-start | bytes 294920 | tf_op jit(solution)/shard_map/ppermute | solution.py:623
  53.6 2.2 %collective-permute-start.29 = (bf16[32,1536]{1,0:T(8,128)(2,1)S(1)}, bf16[32,1536]{1,0:T(8,128)(2,1)S(1)}, u32[]{:S(2)}, u32[]{:S(2)}) collective-permute-start(bf16[32,1536]{1,0:T(8,128)(2,1)S(1)} %collective-permute-done.25.refs_0_), channel_id=1, source_target_pairs={{0,4},{4,8},{8,12},{12,14},{14,10},{10,6},{6,2},{2,0},{1,5},{5,9},... | collective-permute-start | bytes 294920 | tf_op jit(solution)/shard_map/ppermute | solution.py:623
  56.6 2.0 %collective-permute-done.28.refs_3_ = bf16[32,1536]{1,0:T(8,128)(2,1)S(1)} collective-permute-done((bf16[32,1536]{1,0:T(8,128)(2,1)S(1)}, bf16[32,1536]{1,0:T(8,128)(2,1)S(1)}, u32[]{:S(2)}, u32[]{:S(2)}) %collective-permute-start.28) | collective-permute-done | bytes 98336 | tf_op jit(solution)/shard_map/ppermute | solution.py:623
  58.6 1.6 %shard_map.136 = (bf16[128,6144]{1,0:T(8,128)(2,1)S(1)}, f32[128,128]{1,0:T(8,128)S(1)}, f32[128,768]{1,0:T(8,128)S(1)}, f32[128,768]{1,0:T(8,128)S(1)}) custom-call(f32[1,6144]{1,0:T(1,128)S(1)} %bitcast.31, bf16[6144,768]{1,0:T(8,128)(2,1)S(1)} %bitcast.21, bf16[6144,768]{1,0:T(8,128)(2,1)S(1)} %bitcast.25, ...), custom_call_target="tpu_custom_call" | custom-call | flops 1207959552 | bytes 9437184 | tf_op jit(solution)/shard_map/pallas_call | solution.py:384
  61.0 1.7 %shard_map.137.hidden_ref = bf16[128,768]{1,0:T(8,128)(2,1)S(1)} custom-call(f32[1,6144]{1,0:T(1,128)S(1)} %bitcast.32, bf16[6144,768]{1,0:T(8,128)(2,1)S(1)} %bitcast.22, bf16[6144,768]{1,0:T(8,128)(2,1)S(1)} %bitcast.26, bf16[128,6144]{1,0:T(8,128)(2,1)S(1)} %get-tuple-element.131.early_ref, f32[128,128]{1,0:T(8,128)S(1)} %get-tuple-element.132.early_square_ref, ...), custom_call_target="tpu_custom_call" | custom-call | flops 1207959552 | bytes 9437184 | tf_op jit(solution)/shard_map/pallas_call | solution.py:428
  63.8 2.0 %collective-permute-start.33 = (bf16[16,3072]{1,0:T(8,128)(2,1)S(1)}, bf16[16,3072]{1,0:T(8,128)(2,1)S(1)}, u32[]{:S(2)}, u32[]{:S(2)}) collective-permute-start(bf16[16,3072]{1,0:T(8,128)(2,1)S(1)} %get-tuple-element.166), channel_id=1, source_target_pairs={{0,4},{4,8},{8,12},{12,14},{14,10},{10,6},{6,2},{2,0},{1,5},{5,9},... | collective-permute-start | bytes 294920 | tf_op jit(solution)/shard_map/ppermute | solution.py:653
  66.8 1.8 %collective-permute-start.35 = (bf16[16,3072]{1,0:T(8,128)(2,1)S(1)}, bf16[16,3072]{1,0:T(8,128)(2,1)S(1)}, u32[]{:S(2)}, u32[]{:S(2)}) collective-permute-start(bf16[16,3072]{1,0:T(8,128)(2,1)S(1)} %get-tuple-element.165), channel_id=1, source_target_pairs={{0,4},{4,8},{8,12},{12,14},{14,10},{10,6},{6,2},{2,0},{1,5},{5,9},... | collective-permute-start | bytes 294920 | tf_op jit(solution)/shard_map/ppermute | solution.py:653
  69.4 2.0 %collective-permute-done.35 = bf16[16,3072]{1,0:T(8,128)(2,1)S(1)} collective-permute-done((bf16[16,3072]{1,0:T(8,128)(2,1)S(1)}, bf16[16,3072]{1,0:T(8,128)(2,1)S(1)}, u32[]{:S(2)}, u32[]{:S(2)}) %collective-permute-start.35) | collective-permute-done | bytes 98336 | tf_op jit(solution)/shard_map/ppermute | solution.py:653
  71.5 1.8 %collective-permute-start.40 = (bf16[16,3072]{1,0:T(8,128)(2,1)S(1)}, bf16[16,3072]{1,0:T(8,128)(2,1)S(1)}, u32[]{:S(2)}, u32[]{:S(2)}) collective-permute-start(bf16[16,3072]{1,0:T(8,128)(2,1)S(1)} %fusion.10), channel_id=1, source_target_pairs={{0,4},{4,8},{8,12},{12,14},{14,10},{10,6},{6,2},{2,0},{1,5},{5,9},... | collective-permute-start | bytes 294920 | tf_op jit(solution)/shard_map/ppermute | solution.py:653
  74.6 1.8 %collective-permute-start.38 = (bf16[16,3072]{1,0:T(8,128)(2,1)S(1)}, bf16[16,3072]{1,0:T(8,128)(2,1)S(1)}, u32[]{:S(2)}, u32[]{:S(2)}) collective-permute-start(bf16[16,3072]{1,0:T(8,128)(2,1)S(1)} %fusion.12), channel_id=1, source_target_pairs={{0,4},{4,8},{8,12},{12,14},{14,10},{10,6},{6,2},{2,0},{1,5},{5,9},... | collective-permute-start | bytes 294920 | tf_op jit(solution)/shard_map/ppermute | solution.py:653
  76.8 1.8 %collective-permute-start.41 = (bf16[16,3072]{1,0:T(8,128)(2,1)S(1)}, bf16[16,3072]{1,0:T(8,128)(2,1)S(1)}, u32[]{:S(2)}, u32[]{:S(2)}) collective-permute-start(bf16[16,3072]{1,0:T(8,128)(2,1)S(1)} %fusion.7), channel_id=1, source_target_pairs={{0,4},{4,8},{8,12},{12,14},{14,10},{10,6},{6,2},{2,0},{1,5},{5,9},... | collective-permute-start | bytes 294920 | tf_op jit(solution)/shard_map/ppermute | solution.py:653
  79.3 1.8 %collective-permute-start.44 = (bf16[16,3072]{1,0:T(8,128)(2,1)S(1)}, bf16[16,3072]{1,0:T(8,128)(2,1)S(1)}, u32[]{:S(2)}, u32[]{:S(2)}) collective-permute-start(bf16[16,3072]{1,0:T(8,128)(2,1)S(1)} %get-tuple-element.162), channel_id=1, source_target_pairs={{0,4},{4,8},{8,12},{12,14},{14,10},{10,6},{6,2},{2,0},{1,5},{5,9},... | collective-permute-start | bytes 294920 | tf_op jit(solution)/shard_map/ppermute | solution.py:653
  (165 shorter events, 32.6 us)
Async XLA Ops:
  3.1 7.7 %collective-permute-start = (bf16[528,128]{1,0:T(8,128)(2,1)}, bf16[528,128]{1,0:T(8,128)(2,1)S(1)}, u32[]{:S(2)}, u32[]{:S(2)}) collective-permute-start(bf16[528,128]{1,0:T(8,128)(2,1)} %get-tuple-element.81), channel_id=1, source_target_pairs={{0,2},{2,0},{4,6},{6,4},{8,10},{10,8},{12,14},{14,12},{1,3},{3,1},... | collective-permute-start | bytes 405512 | tf_op jit(solution)/shard_map/ppermute | solution.py:552
  6.1 11.2 %collective-permute-start.2 = (bf16[512,128]{1,0:T(8,128)(2,1)}, bf16[512,128]{1,0:T(8,128)(2,1)S(1)}, u32[]{:S(2)}, u32[]{:S(2)}) collective-permute-start(bf16[512,128]{1,0:T(8,128)(2,1)} %get-tuple-element.88), channel_id=1, source_target_pairs={{0,2},{2,0},{4,6},{6,4},{8,10},{10,8},{12,14},{14,12},{1,3},{3,1},... | collective-permute-start | bytes 393224 | tf_op jit(solution)/shard_map/ppermute | solution.py:552
  6.2 12.6 %collective-permute-start.1 = (bf16[512,128]{1,0:T(8,128)(2,1)}, bf16[512,128]{1,0:T(8,128)(2,1)S(1)}, u32[]{:S(2)}, u32[]{:S(2)}) collective-permute-start(bf16[512,128]{1,0:T(8,128)(2,1)} %get-tuple-element.87), channel_id=1, source_target_pairs={{0,2},{2,0},{4,6},{6,4},{8,10},{10,8},{12,14},{14,12},{1,3},{3,1},... | collective-permute-start | bytes 393224 | tf_op jit(solution)/shard_map/ppermute | solution.py:552
  11.0 10.9 %collective-permute-start.5 = (bf16[4,128,128]{2,1,0:T(8,128)(2,1)S(1)}, bf16[4,128,128]{2,1,0:T(8,128)(2,1)S(1)}, u32[]{:S(2)}, u32[]{:S(2)}) collective-permute-start(bf16[4,128,128]{2,1,0:T(8,128)(2,1)S(1)} %get-tuple-element.159), channel_id=1, source_target_pairs={{0,4},{2,6},{1,5},{3,7},{16,20},{18,22},{17,21},{19,23}} | collective-permute-start | bytes 393224 | tf_op jit(solution)/shard_map/ppermute | solution.py:579
  20.3 10.0 %collective-permute-start.6 = (bf16[32,4736]{1,0:T(8,128)(2,1)S(1)}, bf16[32,4736]{1,0:T(8,128)(2,1)S(1)}, u32[]{:S(2)}, u32[]{:S(2)}) collective-permute-start(bf16[32,4736]{1,0:T(8,128)(2,1)S(1)} %get-tuple-element.94), channel_id=1, source_target_pairs={{0,2},{2,0},{4,6},{6,4},{8,10},{10,8},{12,14},{14,12},{1,3},{3,1},... | collective-permute-start | bytes 909320 | tf_op jit(solution)/shard_map/ppermute | solution.py:571
  29.0 10.0 %collective-permute-start.14 = (bf16[4,128,128]{2,1,0:T(8,128)(2,1)S(1)}, bf16[4,128,128]{2,1,0:T(8,128)(2,1)S(1)}, u32[]{:S(2)}, u32[]{:S(2)}) collective-permute-start(bf16[4,128,128]{2,1,0:T(8,128)(2,1)S(1)} %get-tuple-element.172.moved_ref), channel_id=1, source_target_pairs={{0,2},{2,0},{4,6},{6,4},{8,10},{10,8},{12,14},{14,12},{1,3},{3,1},... | collective-permute-start | bytes 393224 | tf_op jit(solution)/shard_map/ppermute | solution.py:730
  30.8 8.2 %collective-permute-start.15 = (bf16[4,128,128]{2,1,0:T(8,128)(2,1)S(1)}, bf16[4,128,128]{2,1,0:T(8,128)(2,1)S(1)}, u32[]{:S(2)}, u32[]{:S(2)}) collective-permute-start(bf16[4,128,128]{2,1,0:T(8,128)(2,1)S(1)} %get-tuple-element.170.moved_ref), channel_id=1, source_target_pairs={{0,2},{2,0},{4,6},{6,4},{8,10},{10,8},{12,14},{14,12},{1,3},{3,1},... | collective-permute-start | bytes 393224 | tf_op jit(solution)/shard_map/ppermute | solution.py:730
  32.4 9.3 %collective-permute-start.17 = (bf16[4,128,128]{2,1,0:T(8,128)(2,1)S(1)}, bf16[4,128,128]{2,1,0:T(8,128)(2,1)S(1)}, u32[]{:S(2)}, u32[]{:S(2)}) collective-permute-start(bf16[4,128,128]{2,1,0:T(8,128)(2,1)S(1)} %get-tuple-element.168.moved_ref), channel_id=1, source_target_pairs={{0,2},{2,0},{4,6},{6,4},{8,10},{10,8},{12,14},{14,12},{1,3},{3,1},... | collective-permute-start | bytes 393224 | tf_op jit(solution)/shard_map/ppermute | solution.py:730
  34.2 7.4 %collective-permute-start.16 = (bf16[32,1536]{1,0:T(8,128)(2,1)S(1)}, bf16[32,1536]{1,0:T(8,128)(2,1)S(1)}, u32[]{:S(2)}, u32[]{:S(2)}) collective-permute-start(bf16[32,1536]{1,0:T(8,128)(2,1)S(1)} %constant_dynamic-update-slice_fusion.refs_0_), channel_id=1, source_target_pairs={{0,4},{4,8},{8,12},{12,14},{14,10},{10,6},{6,2},{2,0},{1,5},{5,9},... | collective-permute-start | bytes 294920 | tf_op jit(solution)/shard_map/ppermute | solution.py:623
  39.0 5.7 %collective-permute-start.18 = (bf16[32,1536]{1,0:T(8,128)(2,1)S(1)}, bf16[32,1536]{1,0:T(8,128)(2,1)S(1)}, u32[]{:S(2)}, u32[]{:S(2)}) collective-permute-start(bf16[32,1536]{1,0:T(8,128)(2,1)S(1)} %collective-permute-done.13.refs_1_), channel_id=1, source_target_pairs={{4,0},{8,4},{12,8},{14,12},{10,14},{6,10},{2,6},{0,2},{5,1},{9,5},... | collective-permute-start | bytes 294920 | tf_op jit(solution)/shard_map/ppermute | solution.py:623
  39.1 5.6 %collective-permute-start.19 = (bf16[32,1536]{1,0:T(8,128)(2,1)S(1)}, bf16[32,1536]{1,0:T(8,128)(2,1)S(1)}, u32[]{:S(2)}, u32[]{:S(2)}) collective-permute-start(bf16[32,1536]{1,0:T(8,128)(2,1)S(1)} %collective-permute-done.13.refs_1_), channel_id=1, source_target_pairs={{0,4},{4,8},{8,12},{12,14},{14,10},{10,6},{6,2},{2,0},{1,5},{5,9},... | collective-permute-start | bytes 294920 | tf_op jit(solution)/shard_map/ppermute | solution.py:623
  41.7 6.0 %collective-permute-start.20 = (bf16[32,1536]{1,0:T(8,128)(2,1)S(1)}, bf16[32,1536]{1,0:T(8,128)(2,1)S(1)}, u32[]{:S(2)}, u32[]{:S(2)}) collective-permute-start(bf16[32,1536]{1,0:T(8,128)(2,1)S(1)} %constant_dynamic-update-slice_fusion.refs_0_), channel_id=1, source_target_pairs={{4,0},{8,4},{12,8},{14,12},{10,14},{6,10},{2,6},{0,2},{5,1},{9,5},... | collective-permute-start | bytes 294920 | tf_op jit(solution)/shard_map/ppermute | solution.py:623
  41.7 6.0 %collective-permute-start.21 = (bf16[32,1536]{1,0:T(8,128)(2,1)S(1)}, bf16[32,1536]{1,0:T(8,128)(2,1)S(1)}, u32[]{:S(2)}, u32[]{:S(2)}) collective-permute-start(bf16[32,1536]{1,0:T(8,128)(2,1)S(1)} %collective-permute-done.16.refs_2_), channel_id=1, source_target_pairs={{0,4},{4,8},{8,12},{12,14},{14,10},{10,6},{6,2},{2,0},{1,5},{5,9},... | collective-permute-start | bytes 294920 | tf_op jit(solution)/shard_map/ppermute | solution.py:623
  44.7 6.2 %collective-permute-start.22 = (bf16[32,1536]{1,0:T(8,128)(2,1)S(1)}, bf16[32,1536]{1,0:T(8,128)(2,1)S(1)}, u32[]{:S(2)}, u32[]{:S(2)}) collective-permute-start(bf16[32,1536]{1,0:T(8,128)(2,1)S(1)} %collective-permute-done.18.refs_3_), channel_id=1, source_target_pairs={{4,0},{8,4},{12,8},{14,12},{10,14},{6,10},{2,6},{0,2},{5,1},{9,5},... | collective-permute-start | bytes 294920 | tf_op jit(solution)/shard_map/ppermute | solution.py:623
  44.7 6.2 %collective-permute-start.23 = (bf16[32,1536]{1,0:T(8,128)(2,1)S(1)}, bf16[32,1536]{1,0:T(8,128)(2,1)S(1)}, u32[]{:S(2)}, u32[]{:S(2)}) collective-permute-start(bf16[32,1536]{1,0:T(8,128)(2,1)S(1)} %collective-permute-done.19.refs_4_), channel_id=1, source_target_pairs={{0,4},{4,8},{8,12},{12,14},{14,10},{10,6},{6,2},{2,0},{1,5},{5,9},... | collective-permute-start | bytes 294920 | tf_op jit(solution)/shard_map/ppermute | solution.py:623
  47.7 6.0 %collective-permute-start.25 = (bf16[32,1536]{1,0:T(8,128)(2,1)S(1)}, bf16[32,1536]{1,0:T(8,128)(2,1)S(1)}, u32[]{:S(2)}, u32[]{:S(2)}) collective-permute-start(bf16[32,1536]{1,0:T(8,128)(2,1)S(1)} %collective-permute-done.21.refs_6_), channel_id=1, source_target_pairs={{0,4},{4,8},{8,12},{12,14},{14,10},{10,6},{6,2},{2,0},{1,5},{5,9},... | collective-permute-start | bytes 294920 | tf_op jit(solution)/shard_map/ppermute | solution.py:623
  50.9 5.7 %collective-permute-start.27 = (bf16[32,1536]{1,0:T(8,128)(2,1)S(1)}, bf16[32,1536]{1,0:T(8,128)(2,1)S(1)}, u32[]{:S(2)}, u32[]{:S(2)}) collective-permute-start(bf16[32,1536]{1,0:T(8,128)(2,1)S(1)} %collective-permute-done.23.refs_8_), channel_id=1, source_target_pairs={{0,4},{4,8},{8,12},{12,14},{14,10},{10,6},{6,2},{2,0},{1,5},{5,9},... | collective-permute-start | bytes 294920 | tf_op jit(solution)/shard_map/ppermute | solution.py:623
  53.6 6.6 %collective-permute-start.29 = (bf16[32,1536]{1,0:T(8,128)(2,1)S(1)}, bf16[32,1536]{1,0:T(8,128)(2,1)S(1)}, u32[]{:S(2)}, u32[]{:S(2)}) collective-permute-start(bf16[32,1536]{1,0:T(8,128)(2,1)S(1)} %collective-permute-done.25.refs_0_), channel_id=1, source_target_pairs={{0,4},{4,8},{8,12},{12,14},{14,10},{10,6},{6,2},{2,0},{1,5},{5,9},... | collective-permute-start | bytes 294920 | tf_op jit(solution)/shard_map/ppermute | solution.py:623
  63.8 10.8 %collective-permute-start.33 = (bf16[16,3072]{1,0:T(8,128)(2,1)S(1)}, bf16[16,3072]{1,0:T(8,128)(2,1)S(1)}, u32[]{:S(2)}, u32[]{:S(2)}) collective-permute-start(bf16[16,3072]{1,0:T(8,128)(2,1)S(1)} %get-tuple-element.166), channel_id=1, source_target_pairs={{0,4},{4,8},{8,12},{12,14},{14,10},{10,6},{6,2},{2,0},{1,5},{5,9},... | collective-permute-start | bytes 294920 | tf_op jit(solution)/shard_map/ppermute | solution.py:653
  68.6 5.7 %collective-permute-start.34 = (bf16[16,3072]{1,0:T(8,128)(2,1)S(1)}, bf16[16,3072]{1,0:T(8,128)(2,1)S(1)}, u32[]{:S(2)}, u32[]{:S(2)}) collective-permute-start(bf16[16,3072]{1,0:T(8,128)(2,1)S(1)} %get-tuple-element.164), channel_id=1, source_target_pairs={{4,0},{8,4},{12,8},{14,12},{10,14},{6,10},{2,6},{0,2},{5,1},{9,5},... | collective-permute-start | bytes 294920 | tf_op jit(solution)/shard_map/ppermute | solution.py:653
  68.8 7.6 %collective-permute-start.36 = (bf16[16,3072]{1,0:T(8,128)(2,1)S(1)}, bf16[16,3072]{1,0:T(8,128)(2,1)S(1)}, u32[]{:S(2)}, u32[]{:S(2)}) collective-permute-start(bf16[16,3072]{1,0:T(8,128)(2,1)S(1)} %get-tuple-element.163), channel_id=1, source_target_pairs={{0,1},{1,0},{2,3},{3,2},{4,5},{5,4},{6,7},{7,6},{8,9},{9,8},{10,11... | collective-permute-start | bytes 294920 | tf_op jit(solution)/shard_map/ppermute | solution.py:675
  69.4 7.1 %collective-permute-start.32 = (bf16[16,3072]{1,0:T(8,128)(2,1)S(1)}, bf16[16,3072]{1,0:T(8,128)(2,1)S(1)}, u32[]{:S(2)}, u32[]{:S(2)}) collective-permute-start(bf16[16,3072]{1,0:T(8,128)(2,1)S(1)} %fusion.13), channel_id=1, source_target_pairs={{4,0},{8,4},{12,8},{14,12},{10,14},{6,10},{2,6},{0,2},{5,1},{9,5},... | collective-permute-start | bytes 294920 | tf_op jit(solution)/shard_map/ppermute | solution.py:653
  79.2 5.9 %collective-permute-start.45 = (bf16[16,3072]{1,0:T(8,128)(2,1)S(1)}, bf16[16,3072]{1,0:T(8,128)(2,1)S(1)}, u32[]{:S(2)}, u32[]{:S(2)}) collective-permute-start(bf16[16,3072]{1,0:T(8,128)(2,1)S(1)} %fusion.8), channel_id=1, source_target_pairs={{4,1},{5,0},{8,5},{9,4},{12,9},{13,8},{14,13},{15,12},{10,15},{11,... | collective-permute-start | bytes 294920 | tf_op jit(solution)/shard_map/ppermute | solution.py:655
  79.3 5.8 %collective-permute-start.44 = (bf16[16,3072]{1,0:T(8,128)(2,1)S(1)}, bf16[16,3072]{1,0:T(8,128)(2,1)S(1)}, u32[]{:S(2)}, u32[]{:S(2)}) collective-permute-start(bf16[16,3072]{1,0:T(8,128)(2,1)S(1)} %get-tuple-element.162), channel_id=1, source_target_pairs={{0,4},{4,8},{8,12},{12,14},{14,10},{10,6},{6,2},{2,0},{1,5},{5,9},... | collective-permute-start | bytes 294920 | tf_op jit(solution)/shard_map/ppermute | solution.py:653
  (42 other events, 337.0 us)

commit v8 on v7

--- a/solution.py
+++ b/solution.py
@@ -611,16 +611,25 @@
     return jnp.where(there < count // 2, 2 * there, 2 * (count - 1 - there) + 1)
 
 
-def ring_gather(halves, holds):
+def move(sent, way, across):
+    if not across:
+        return lax.ppermute(sent, "seq", way)
+    pairs = [(2 * a + core, 2 * b + 1 - core) for a, b in way for core in range(2)]
+    return lax.ppermute(sent, ("seq", "exp"), pairs)
+
+
+def ring_gather(halves, second, holds):
     steps = lax.axis_size("seq") // 2
     right, left = ring_pairs(2 * steps)
     chains = [(0, right), (1, left), (1, right), (0, left)]
     moving = [halves[half] for half, _ in chains]
-    brought = [list(halves)]
+    brought = [[halves[0], second]]
     marks = list(halves)
     for step in range(steps):
         here = chains if step < steps - 1 else chains[:2]
-        gots = [lax.ppermute(moving[k], "seq", way) for k, (_, way) in enumerate(here)]
+        gots = [
+            move(moving[k], way, half == 1 and step == 0) for k, (half, way) in enumerate(here)
+        ]
         if step in holds:
             marks = [*marks, *holds[step](brought)]
         brought.append([])
@@ -647,12 +656,6 @@
 
     def piece(position, half):
         return partials[half][position * rows : (position + 1) * rows]
-
-    def move(sent, half, way, last):
-        if half == 0 or not last:
-            return lax.ppermute(sent, "seq", way)
-        across = [(2 * a + core, 2 * b + 1 - core) for a, b in way for core in range(2)]
-        return lax.ppermute(sent, ("seq", "exp"), across)
 
     chains = [
         (0, left, [steps, *range(steps - 1, 0, -1)]),
@@ -670,7 +673,7 @@
         for k in (0, 2, 3, 1):
             half, way, positions = chains[k]
             if step <= len(positions):
-                gots[k] = move(sents[k], half, way, step == len(positions))
+                gots[k] = move(sents[k], way, half == 1 and step == len(positions))
         if step == 2:
             here = lax.ppermute(here, "exp", [(0, 1), (1, 0)])
             marks = [*marks, here]
@@ -739,7 +742,8 @@
         finish,
     )
     rows_mine, rows_sent, kept, swapped = zip(*finished, strict=True)
-    rows_got = lax.ppermute(jnp.concatenate(rows_sent, axis=1), "exp", exchange)
+    rows_sent = jnp.concatenate(rows_sent, axis=1)
+    rows_got = lax.ppermute(rows_sent, "exp", exchange)
 
     def all_rows(sent, mark, within, before, entering):
         return hidden_block(
@@ -757,11 +761,9 @@
         )
 
     zeros = jnp.zeros((8, running.shape[1]), F32)
-    hidden_own, sums = all_rows(False, rows_sent, within_own, zeros, kept)
-    halves = (
-        jnp.concatenate(rows_mine, axis=1),
-        after(rows_got, *swapped[:2], hidden_own, sums),
-    )
+    hidden_own, sums = all_rows(False, [rows_sent], within_own, zeros, kept)
+    halves = (jnp.concatenate(rows_mine, axis=1), rows_sent)
+    second = after(rows_got, *swapped[:2], hidden_own, sums)
 
     steps = count // 2
     early = []
@@ -784,8 +786,8 @@
         )
         return early[-1]
 
-    holds = {0: lambda brought: swapped, steps - 2: hold_rows, steps - 1: hold_partial}
-    brought = ring_gather(halves, holds)
+    holds = {0: lambda brought: (second, *swapped), steps - 2: hold_rows, steps - 1: hold_partial}
+    brought = ring_gather(halves, second, holds)
     hidden_units = expert_rows(
         ring_places(steps, steps),
         moe_gain,

time: 88.2 us -> 86.9 us (0.985)
  waiting for transfers between devices: 11.2 us -> 9.12 us
    ppermute x12 -> x24, starting transfers between devices: 12.4 us -> 28.7 us  [move(): return lax.ppermute(sent, 'seq', way)]
    ppermute x17 -> x5, starting transfers between devices: 19.2 us -> 3.68 us  [the longest x4 3.61 us: move(): return lax.ppermute(sent, ('seq', 'exp'), pairs)]
    ppermute x17 -> x5, waiting for transfers between devices: 5.39 us -> 0.19 us  [the longest x4 0.19 us: move(): return lax.ppermute(sent, ('seq', 'exp'), pairs)]
    ppermute x12 -> x24, waiting for transfers between devices: 4.37 us -> 7.46 us  [move(): return lax.ppermute(sent, 'seq', way)]
  transfers between devices with their start and end apart: 47 -> 47, of which waited for: 15 -> 13; matrix products, arithmetic and copies ran while one was open for 2% -> 2% of each run, Pallas kernels for 16% -> 16%
where the time goes in v8:
time: 86.9 us; the launch traced here: 86.7 us
  starting transfers between devices  53.9 us (62%)
  Pallas kernels  20.4 us (23%)
  waiting for transfers between devices  9.12 us (10%)
  other arithmetic  2.19 us (3%)
    ppermute x24, starting transfers between devices, move(): return lax.ppermute(sent, 'seq', way)  28.7 us
    ppermute x9, starting transfers between devices, entering_state(): gots = [lax.ppermute(sent, 'seq', pairs) for sent in sents]  10.6 us
    ppermute x24, waiting for transfers between devices, move(): return lax.ppermute(sent, 'seq', way)  7.46 us
    ppermute x3, starting transfers between devices, entering_state(): arrived = after(lax.ppermute(sending[chunk], 'seq', swap), *marks)  5.14 us
    pallas_call x2, Pallas kernels, half_state(): pl.pallas_call(functools.partial(state_kernel, sent), out_shape=tuple(sha...  4.75 us
    pallas_call x2, Pallas kernels, within_block(): pl.pallas_call(functools.partial(within_kernel, sent), out_shape=(jax.Sha...  4.47 us
    ppermute x4, starting transfers between devices, move(): return lax.ppermute(sent, ('seq', 'exp'), pairs)  3.61 us
    ppermute x3, starting transfers between devices, finish(): return (*rows, kept, lax.ppermute(moved, 'seq', swap))  3.41 us
  transfers between devices with their start and end apart: 47, of which 13 were waited for; matrix products, arithmetic and copies ran while one was open for 2% of the time, Pallas kernels for 16%

profile of v8, /device:TPU:0, one launch (start us, length us, event | category | flops | bytes accessed | tf_op | source)
XLA Modules:
  0.0 86.7 jit_solution(4678998621040752428)
XLA Ops:
  0.0 3.0 %shard_map.127 = (bf16[528,128]{1,0:T(8,128)(2,1)}, bf16[512,128]{1,0:T(8,128)(2,1)}, bf16[512,128]{1,0:T(8,128)(2,1)}) custom-call(f32[24,128]{1,0:T(8,128)} %bitcast.39, bf16[128,3072]{1,0:T(8,128)(2,1)} %key_ref.7, bf16[128,3072]{1,0:T(8,128)(2,1)} %value_ref.7), custom_call_target="tpu_custom_call" | custom-call | flops 50331648 | bytes 786432 | tf_op jit(solution)/shard_map/pallas_call | solution.py:101
  3.1 3.0 %collective-permute-start = (bf16[528,128]{1,0:T(8,128)(2,1)}, bf16[528,128]{1,0:T(8,128)(2,1)S(1)}, u32[]{:S(2)}, u32[]{:S(2)}) collective-permute-start(bf16[528,128]{1,0:T(8,128)(2,1)} %get-tuple-element.81), channel_id=1, source_target_pairs={{0,2},{2,0},{4,6},{6,4},{8,10},{10,8},{12,14},{14,12},{1,3},{3,1},... | collective-permute-start | bytes 405512 | tf_op jit(solution)/shard_map/ppermute | solution.py:552
  6.2 2.0 %collective-permute-start.1 = (bf16[512,128]{1,0:T(8,128)(2,1)}, bf16[512,128]{1,0:T(8,128)(2,1)S(1)}, u32[]{:S(2)}, u32[]{:S(2)}) collective-permute-start(bf16[512,128]{1,0:T(8,128)(2,1)} %get-tuple-element.87), channel_id=1, source_target_pairs={{0,2},{2,0},{4,6},{6,4},{8,10},{10,8},{12,14},{14,12},{1,3},{3,1},... | collective-permute-start | bytes 393224 | tf_op jit(solution)/shard_map/ppermute | solution.py:552
  8.2 1.7 %shard_map.128 = (f32[512,128]{1,0:T(8,128)S(1)}, f32[512,128]{1,0:T(8,128)S(1)}, f32[512,128]{1,0:T(8,128)S(1)}, f32[24,128]{1,0:T(8,128)S(1)}) custom-call(f32[24,128]{1,0:T(8,128)S(1)} %bitcast.40, bf16[128,3072]{1,0:T(8,128)(2,1)S(1)} %copy-done, bf16[128,3072]{1,0:T(8,128)(2,1)S(1)} %copy-done.1), custom_call_target="tpu_custom_call" | custom-call | flops 50331648 | bytes 786432 | tf_op jit(solution)/shard_map/pallas_call | solution.py:101
  11.0 4.0 %collective-permute-start.5 = (bf16[4,128,128]{2,1,0:T(8,128)(2,1)S(1)}, bf16[4,128,128]{2,1,0:T(8,128)(2,1)S(1)}, u32[]{:S(2)}, u32[]{:S(2)}) collective-permute-start(bf16[4,128,128]{2,1,0:T(8,128)(2,1)S(1)} %get-tuple-element.159), channel_id=1, source_target_pairs={{0,4},{2,6},{1,5},{3,7},{16,20},{18,22},{17,21},{19,23}} | collective-permute-start | bytes 393224 | tf_op jit(solution)/shard_map/ppermute | solution.py:579
  15.1 2.2 %shard_map.129 = (f32[128,1536]{1,0:T(8,128)S(1)}, bf16[32,4736]{1,0:T(8,128)(2,1)S(1)}) custom-call(f32[24,128]{1,0:T(8,128)S(1)} %get-tuple-element.83.run_ref, bf16[128,3072]{1,0:T(8,128)(2,1)S(1)} %copy-done.2, bf16[128,3072]{1,0:T(8,128)(2,1)S(1)} %copy-done, bf16[128,3072]{1,0:T(8,128)(2,1)S(1)} %copy-done.1, bf16[128,3072]{1,0:T(8,128)(2,1)S(1)} %copy-done.3, ...), custom_call_target="tpu_custom_call" | custom-call | flops 100663296 | bytes 2359296 | tf_op jit(solution)/shard_map/pallas_call | solution.py:181
  20.3 1.6 %collective-permute-start.6 = (bf16[32,4736]{1,0:T(8,128)(2,1)S(1)}, bf16[32,4736]{1,0:T(8,128)(2,1)S(1)}, u32[]{:S(2)}, u32[]{:S(2)}) collective-permute-start(bf16[32,4736]{1,0:T(8,128)(2,1)S(1)} %get-tuple-element.94), channel_id=1, source_target_pairs={{0,2},{2,0},{4,6},{6,4},{8,10},{10,8},{12,14},{14,12},{1,3},{3,1},... | collective-permute-start | bytes 909320 | tf_op jit(solution)/shard_map/ppermute | solution.py:571
  24.2 2.2 %shard_map.130 = (f32[128,1536]{1,0:T(8,128)S(1)}, bf16[32,4736]{1,0:T(8,128)(2,1)S(1)}) custom-call(f32[24,128]{1,0:T(8,128)S(1)} %get-tuple-element.83.run_ref, bf16[128,3072]{1,0:T(8,128)(2,1)S(1)} %copy-done.2, bf16[128,3072]{1,0:T(8,128)(2,1)S(1)} %copy-done, bf16[128,3072]{1,0:T(8,128)(2,1)S(1)} %copy-done.1, bf16[128,3072]{1,0:T(8,128)(2,1)S(1)} %copy-done.3, ...), custom_call_target="tpu_custom_call" | custom-call | flops 100663296 | bytes 2359296 | tf_op jit(solution)/shard_map/pallas_call | solution.py:181
  34.2 3.2 %collective-permute-start.16 = (bf16[32,1536]{1,0:T(8,128)(2,1)S(1)}, bf16[32,1536]{1,0:T(8,128)(2,1)S(1)}, u32[]{:S(2)}, u32[]{:S(2)}) collective-permute-start(bf16[32,1536]{1,0:T(8,128)(2,1)S(1)} %constant_dynamic-update-slice_fusion.refs_0_), channel_id=1, source_target_pairs={{0,4},{4,8},{8,12},{12,14},{14,10},{10,6},{6,2},{2,0},{1,5},{5,9},... | collective-permute-start | bytes 294920 | tf_op jit(solution)/shard_map/ppermute | solution.py:616
  37.4 2.3 %collective-permute-start.19 = (bf16[32,1536]{1,0:T(8,128)(2,1)S(1)}, bf16[32,1536]{1,0:T(8,128)(2,1)S(1)}, u32[]{:S(2)}, u32[]{:S(2)}) collective-permute-start(bf16[32,1536]{1,0:T(8,128)(2,1)S(1)} %constant_dynamic-update-slice_fusion.3), channel_id=1, source_target_pairs={{0,5},{1,4},{4,9},{5,8},{8,13},{9,12},{12,15},{13,14},{14,11},{15,... | collective-permute-start | bytes 294920 | tf_op jit(solution)/shard_map/ppermute | solution.py:618
  39.8 1.6 %shard_map.134 = (bf16[128,1536]{1,0:T(8,128)(2,1)S(1)}, f32[8,128]{1,0:T(8,128)S(1)}) custom-call(f32[24,128]{1,0:T(8,128)S(1)} %get-tuple-element.83.run_ref, bf16[128,3072]{1,0:T(8,128)(2,1)S(1)} %copy-done.2, f32[128,1536]{1,0:T(8,128)S(1)} %get-tuple-element.100.within_ref, bf16[128,3072]{1,0:T(8,128)(2,1)S(1)} %copy-done.3, f32[1,3072]{1,0:T(1,128)S(1)} %bitcast.37, ...), custom_call_target="tpu_custom_call" | custom-call | flops 50331648 | bytes 2359296 | tf_op jit(solution)/shard_map/pallas_call | solution.py:299
  41.4 2.5 %collective-permute-start.21 = (bf16[32,1536]{1,0:T(8,128)(2,1)S(1)}, bf16[32,1536]{1,0:T(8,128)(2,1)S(1)}, u32[]{:S(2)}, u32[]{:S(2)}) collective-permute-start(bf16[32,1536]{1,0:T(8,128)(2,1)S(1)} %collective-permute-done.16.refs_2_), channel_id=1, source_target_pairs={{0,4},{4,8},{8,12},{12,14},{14,10},{10,6},{6,2},{2,0},{1,5},{5,9},... | collective-permute-start | bytes 294920 | tf_op jit(solution)/shard_map/ppermute | solution.py:616
  43.9 2.1 %collective-permute-start.23 = (bf16[32,1536]{1,0:T(8,128)(2,1)S(1)}, bf16[32,1536]{1,0:T(8,128)(2,1)S(1)}, u32[]{:S(2)}, u32[]{:S(2)}) collective-permute-start(bf16[32,1536]{1,0:T(8,128)(2,1)S(1)} %collective-permute-done.19.refs_4_), channel_id=1, source_target_pairs={{0,4},{4,8},{8,12},{12,14},{14,10},{10,6},{6,2},{2,0},{1,5},{5,9},... | collective-permute-start | bytes 294920 | tf_op jit(solution)/shard_map/ppermute | solution.py:616
  46.5 2.6 %collective-permute-start.25 = (bf16[32,1536]{1,0:T(8,128)(2,1)S(1)}, bf16[32,1536]{1,0:T(8,128)(2,1)S(1)}, u32[]{:S(2)}, u32[]{:S(2)}) collective-permute-start(bf16[32,1536]{1,0:T(8,128)(2,1)S(1)} %collective-permute-done.21.refs_6_), channel_id=1, source_target_pairs={{0,4},{4,8},{8,12},{12,14},{14,10},{10,6},{6,2},{2,0},{1,5},{5,9},... | collective-permute-start | bytes 294920 | tf_op jit(solution)/shard_map/ppermute | solution.py:616
  49.6 2.1 %collective-permute-start.27 = (bf16[32,1536]{1,0:T(8,128)(2,1)S(1)}, bf16[32,1536]{1,0:T(8,128)(2,1)S(1)}, u32[]{:S(2)}, u32[]{:S(2)}) collective-permute-start(bf16[32,1536]{1,0:T(8,128)(2,1)S(1)} %collective-permute-done.23.refs_8_), channel_id=1, source_target_pairs={{0,4},{4,8},{8,12},{12,14},{14,10},{10,6},{6,2},{2,0},{1,5},{5,9},... | collective-permute-start | bytes 294920 | tf_op jit(solution)/shard_map/ppermute | solution.py:616
  52.3 1.8 %collective-permute-start.29 = (bf16[32,1536]{1,0:T(8,128)(2,1)S(1)}, bf16[32,1536]{1,0:T(8,128)(2,1)S(1)}, u32[]{:S(2)}, u32[]{:S(2)}) collective-permute-start(bf16[32,1536]{1,0:T(8,128)(2,1)S(1)} %collective-permute-done.25.refs_0_), channel_id=1, source_target_pairs={{0,4},{4,8},{8,12},{12,14},{14,10},{10,6},{6,2},{2,0},{1,5},{5,9},... | collective-permute-start | bytes 294920 | tf_op jit(solution)/shard_map/ppermute | solution.py:616
  56.8 1.7 %shard_map.136 = (bf16[128,6144]{1,0:T(8,128)(2,1)S(1)}, f32[128,128]{1,0:T(8,128)S(1)}, f32[128,768]{1,0:T(8,128)S(1)}, f32[128,768]{1,0:T(8,128)S(1)}) custom-call(f32[1,6144]{1,0:T(1,128)S(1)} %bitcast.31, bf16[6144,768]{1,0:T(8,128)(2,1)S(1)} %bitcast.21, bf16[6144,768]{1,0:T(8,128)(2,1)S(1)} %bitcast.25, ...), custom_call_target="tpu_custom_call" | custom-call | flops 1207959552 | bytes 9437184 | tf_op jit(solution)/shard_map/pallas_call | solution.py:384
  59.3 1.7 %shard_map.137.hidden_ref = bf16[128,768]{1,0:T(8,128)(2,1)S(1)} custom-call(f32[1,6144]{1,0:T(1,128)S(1)} %bitcast.32, bf16[6144,768]{1,0:T(8,128)(2,1)S(1)} %bitcast.22, bf16[6144,768]{1,0:T(8,128)(2,1)S(1)} %bitcast.26, bf16[128,6144]{1,0:T(8,128)(2,1)S(1)} %get-tuple-element.131.early_ref, f32[128,128]{1,0:T(8,128)S(1)} %get-tuple-element.132.early_square_ref, ...), custom_call_target="tpu_custom_call" | custom-call | flops 1207959552 | bytes 9437184 | tf_op jit(solution)/shard_map/pallas_call | solution.py:428
  65.2 2.1 %collective-permute-start.35 = (bf16[16,3072]{1,0:T(8,128)(2,1)S(1)}, bf16[16,3072]{1,0:T(8,128)(2,1)S(1)}, u32[]{:S(2)}, u32[]{:S(2)}) collective-permute-start(bf16[16,3072]{1,0:T(8,128)(2,1)S(1)} %get-tuple-element.165), channel_id=1, source_target_pairs={{0,4},{4,8},{8,12},{12,14},{14,10},{10,6},{6,2},{2,0},{1,5},{5,9},... | collective-permute-start | bytes 294920 | tf_op jit(solution)/shard_map/ppermute | solution.py:616
  68.1 1.7 %collective-permute-done.35 = bf16[16,3072]{1,0:T(8,128)(2,1)S(1)} collective-permute-done((bf16[16,3072]{1,0:T(8,128)(2,1)S(1)}, bf16[16,3072]{1,0:T(8,128)(2,1)S(1)}, u32[]{:S(2)}, u32[]{:S(2)}) %collective-permute-start.35) | collective-permute-done | bytes 98336 | tf_op jit(solution)/shard_map/ppermute | solution.py:616
  69.9 2.1 %collective-permute-start.40 = (bf16[16,3072]{1,0:T(8,128)(2,1)S(1)}, bf16[16,3072]{1,0:T(8,128)(2,1)S(1)}, u32[]{:S(2)}, u32[]{:S(2)}) collective-permute-start(bf16[16,3072]{1,0:T(8,128)(2,1)S(1)} %fusion.10), channel_id=1, source_target_pairs={{0,4},{4,8},{8,12},{12,14},{14,10},{10,6},{6,2},{2,0},{1,5},{5,9},... | collective-permute-start | bytes 294920 | tf_op jit(solution)/shard_map/ppermute | solution.py:616
  73.1 2.1 %collective-permute-start.38 = (bf16[16,3072]{1,0:T(8,128)(2,1)S(1)}, bf16[16,3072]{1,0:T(8,128)(2,1)S(1)}, u32[]{:S(2)}, u32[]{:S(2)}) collective-permute-start(bf16[16,3072]{1,0:T(8,128)(2,1)S(1)} %fusion.12), channel_id=1, source_target_pairs={{0,4},{4,8},{8,12},{12,14},{14,10},{10,6},{6,2},{2,0},{1,5},{5,9},... | collective-permute-start | bytes 294920 | tf_op jit(solution)/shard_map/ppermute | solution.py:616
  75.3 2.1 %collective-permute-start.41 = (bf16[16,3072]{1,0:T(8,128)(2,1)S(1)}, bf16[16,3072]{1,0:T(8,128)(2,1)S(1)}, u32[]{:S(2)}, u32[]{:S(2)}) collective-permute-start(bf16[16,3072]{1,0:T(8,128)(2,1)S(1)} %fusion.7), channel_id=1, source_target_pairs={{0,4},{4,8},{8,12},{12,14},{14,10},{10,6},{6,2},{2,0},{1,5},{5,9},... | collective-permute-start | bytes 294920 | tf_op jit(solution)/shard_map/ppermute | solution.py:616
  78.0 1.8 %collective-permute-start.44 = (bf16[16,3072]{1,0:T(8,128)(2,1)S(1)}, bf16[16,3072]{1,0:T(8,128)(2,1)S(1)}, u32[]{:S(2)}, u32[]{:S(2)}) collective-permute-start(bf16[16,3072]{1,0:T(8,128)(2,1)S(1)} %get-tuple-element.162), channel_id=1, source_target_pairs={{0,4},{4,8},{8,12},{12,14},{14,10},{10,6},{6,2},{2,0},{1,5},{5,9},... | collective-permute-start | bytes 294920 | tf_op jit(solution)/shard_map/ppermute | solution.py:616
  (166 shorter events, 32.6 us)
Async XLA Ops:
  3.1 7.7 %collective-permute-start = (bf16[528,128]{1,0:T(8,128)(2,1)}, bf16[528,128]{1,0:T(8,128)(2,1)S(1)}, u32[]{:S(2)}, u32[]{:S(2)}) collective-permute-start(bf16[528,128]{1,0:T(8,128)(2,1)} %get-tuple-element.81), channel_id=1, source_target_pairs={{0,2},{2,0},{4,6},{6,4},{8,10},{10,8},{12,14},{14,12},{1,3},{3,1},... | collective-permute-start | bytes 405512 | tf_op jit(solution)/shard_map/ppermute | solution.py:552
  6.1 11.2 %collective-permute-start.2 = (bf16[512,128]{1,0:T(8,128)(2,1)}, bf16[512,128]{1,0:T(8,128)(2,1)S(1)}, u32[]{:S(2)}, u32[]{:S(2)}) collective-permute-start(bf16[512,128]{1,0:T(8,128)(2,1)} %get-tuple-element.88), channel_id=1, source_target_pairs={{0,2},{2,0},{4,6},{6,4},{8,10},{10,8},{12,14},{14,12},{1,3},{3,1},... | collective-permute-start | bytes 393224 | tf_op jit(solution)/shard_map/ppermute | solution.py:552
  6.2 12.6 %collective-permute-start.1 = (bf16[512,128]{1,0:T(8,128)(2,1)}, bf16[512,128]{1,0:T(8,128)(2,1)S(1)}, u32[]{:S(2)}, u32[]{:S(2)}) collective-permute-start(bf16[512,128]{1,0:T(8,128)(2,1)} %get-tuple-element.87), channel_id=1, source_target_pairs={{0,2},{2,0},{4,6},{6,4},{8,10},{10,8},{12,14},{14,12},{1,3},{3,1},... | collective-permute-start | bytes 393224 | tf_op jit(solution)/shard_map/ppermute | solution.py:552
  11.0 10.9 %collective-permute-start.5 = (bf16[4,128,128]{2,1,0:T(8,128)(2,1)S(1)}, bf16[4,128,128]{2,1,0:T(8,128)(2,1)S(1)}, u32[]{:S(2)}, u32[]{:S(2)}) collective-permute-start(bf16[4,128,128]{2,1,0:T(8,128)(2,1)S(1)} %get-tuple-element.159), channel_id=1, source_target_pairs={{0,4},{2,6},{1,5},{3,7},{16,20},{18,22},{17,21},{19,23}} | collective-permute-start | bytes 393224 | tf_op jit(solution)/shard_map/ppermute | solution.py:579
  20.3 10.0 %collective-permute-start.6 = (bf16[32,4736]{1,0:T(8,128)(2,1)S(1)}, bf16[32,4736]{1,0:T(8,128)(2,1)S(1)}, u32[]{:S(2)}, u32[]{:S(2)}) collective-permute-start(bf16[32,4736]{1,0:T(8,128)(2,1)S(1)} %get-tuple-element.94), channel_id=1, source_target_pairs={{0,2},{2,0},{4,6},{6,4},{8,10},{10,8},{12,14},{14,12},{1,3},{3,1},... | collective-permute-start | bytes 909320 | tf_op jit(solution)/shard_map/ppermute | solution.py:571
  29.0 10.8 %collective-permute-start.14 = (bf16[4,128,128]{2,1,0:T(8,128)(2,1)S(1)}, bf16[4,128,128]{2,1,0:T(8,128)(2,1)S(1)}, u32[]{:S(2)}, u32[]{:S(2)}) collective-permute-start(bf16[4,128,128]{2,1,0:T(8,128)(2,1)S(1)} %get-tuple-element.172.moved_ref), channel_id=1, source_target_pairs={{0,2},{2,0},{4,6},{6,4},{8,10},{10,8},{12,14},{14,12},{1,3},{3,1},... | collective-permute-start | bytes 393224 | tf_op jit(solution)/shard_map/ppermute | solution.py:733
  30.9 6.6 %collective-permute-start.15 = (bf16[4,128,128]{2,1,0:T(8,128)(2,1)S(1)}, bf16[4,128,128]{2,1,0:T(8,128)(2,1)S(1)}, u32[]{:S(2)}, u32[]{:S(2)}) collective-permute-start(bf16[4,128,128]{2,1,0:T(8,128)(2,1)S(1)} %get-tuple-element.170.moved_ref), channel_id=1, source_target_pairs={{0,2},{2,0},{4,6},{6,4},{8,10},{10,8},{12,14},{14,12},{1,3},{3,1},... | collective-permute-start | bytes 393224 | tf_op jit(solution)/shard_map/ppermute | solution.py:733
  32.4 9.0 %collective-permute-start.17 = (bf16[4,128,128]{2,1,0:T(8,128)(2,1)S(1)}, bf16[4,128,128]{2,1,0:T(8,128)(2,1)S(1)}, u32[]{:S(2)}, u32[]{:S(2)}) collective-permute-start(bf16[4,128,128]{2,1,0:T(8,128)(2,1)S(1)} %get-tuple-element.168.moved_ref), channel_id=1, source_target_pairs={{0,2},{2,0},{4,6},{6,4},{8,10},{10,8},{12,14},{14,12},{1,3},{3,1},... | collective-permute-start | bytes 393224 | tf_op jit(solution)/shard_map/ppermute | solution.py:733
  34.2 7.1 %collective-permute-start.16 = (bf16[32,1536]{1,0:T(8,128)(2,1)S(1)}, bf16[32,1536]{1,0:T(8,128)(2,1)S(1)}, u32[]{:S(2)}, u32[]{:S(2)}) collective-permute-start(bf16[32,1536]{1,0:T(8,128)(2,1)S(1)} %constant_dynamic-update-slice_fusion.refs_0_), channel_id=1, source_target_pairs={{0,4},{4,8},{8,12},{12,14},{14,10},{10,6},{6,2},{2,0},{1,5},{5,9},... | collective-permute-start | bytes 294920 | tf_op jit(solution)/shard_map/ppermute | solution.py:616
  37.4 6.5 %collective-permute-start.18 = (bf16[32,1536]{1,0:T(8,128)(2,1)S(1)}, bf16[32,1536]{1,0:T(8,128)(2,1)S(1)}, u32[]{:S(2)}, u32[]{:S(2)}) collective-permute-start(bf16[32,1536]{1,0:T(8,128)(2,1)S(1)} %constant_dynamic-update-slice_fusion.3), channel_id=1, source_target_pairs={{4,1},{5,0},{8,5},{9,4},{12,9},{13,8},{14,13},{15,12},{10,15},{11,... | collective-permute-start | bytes 294920 | tf_op jit(solution)/shard_map/ppermute | solution.py:618
  37.4 6.5 %collective-permute-start.19 = (bf16[32,1536]{1,0:T(8,128)(2,1)S(1)}, bf16[32,1536]{1,0:T(8,128)(2,1)S(1)}, u32[]{:S(2)}, u32[]{:S(2)}) collective-permute-start(bf16[32,1536]{1,0:T(8,128)(2,1)S(1)} %constant_dynamic-update-slice_fusion.3), channel_id=1, source_target_pairs={{0,5},{1,4},{4,9},{5,8},{8,13},{9,12},{12,15},{13,14},{14,11},{15,... | collective-permute-start | bytes 294920 | tf_op jit(solution)/shard_map/ppermute | solution.py:618
  39.7 6.3 %collective-permute-start.20 = (bf16[32,1536]{1,0:T(8,128)(2,1)S(1)}, bf16[32,1536]{1,0:T(8,128)(2,1)S(1)}, u32[]{:S(2)}, u32[]{:S(2)}) collective-permute-start(bf16[32,1536]{1,0:T(8,128)(2,1)S(1)} %constant_dynamic-update-slice_fusion.refs_0_), channel_id=1, source_target_pairs={{4,0},{8,4},{12,8},{14,12},{10,14},{6,10},{2,6},{0,2},{5,1},{9,5},... | collective-permute-start | bytes 294920 | tf_op jit(solution)/shard_map/ppermute | solution.py:616
  43.9 5.7 %collective-permute-start.22 = (bf16[32,1536]{1,0:T(8,128)(2,1)S(1)}, bf16[32,1536]{1,0:T(8,128)(2,1)S(1)}, u32[]{:S(2)}, u32[]{:S(2)}) collective-permute-start(bf16[32,1536]{1,0:T(8,128)(2,1)S(1)} %collective-permute-done.18.refs_3_), channel_id=1, source_target_pairs={{4,0},{8,4},{12,8},{14,12},{10,14},{6,10},{2,6},{0,2},{5,1},{9,5},... | collective-permute-start | bytes 294920 | tf_op jit(solution)/shard_map/ppermute | solution.py:616
  43.9 5.7 %collective-permute-start.23 = (bf16[32,1536]{1,0:T(8,128)(2,1)S(1)}, bf16[32,1536]{1,0:T(8,128)(2,1)S(1)}, u32[]{:S(2)}, u32[]{:S(2)}) collective-permute-start(bf16[32,1536]{1,0:T(8,128)(2,1)S(1)} %collective-permute-done.19.refs_4_), channel_id=1, source_target_pairs={{0,4},{4,8},{8,12},{12,14},{14,10},{10,6},{6,2},{2,0},{1,5},{5,9},... | collective-permute-start | bytes 294920 | tf_op jit(solution)/shard_map/ppermute | solution.py:616
  46.0 5.7 %collective-permute-start.24 = (bf16[32,1536]{1,0:T(8,128)(2,1)S(1)}, bf16[32,1536]{1,0:T(8,128)(2,1)S(1)}, u32[]{:S(2)}, u32[]{:S(2)}) collective-permute-start(bf16[32,1536]{1,0:T(8,128)(2,1)S(1)} %collective-permute-done.20.refs_5_), channel_id=1, source_target_pairs={{4,0},{8,4},{12,8},{14,12},{10,14},{6,10},{2,6},{0,2},{5,1},{9,5},... | collective-permute-start | bytes 294920 | tf_op jit(solution)/shard_map/ppermute | solution.py:616
  46.5 5.9 %collective-permute-start.25 = (bf16[32,1536]{1,0:T(8,128)(2,1)S(1)}, bf16[32,1536]{1,0:T(8,128)(2,1)S(1)}, u32[]{:S(2)}, u32[]{:S(2)}) collective-permute-start(bf16[32,1536]{1,0:T(8,128)(2,1)S(1)} %collective-permute-done.21.refs_6_), channel_id=1, source_target_pairs={{0,4},{4,8},{8,12},{12,14},{14,10},{10,6},{6,2},{2,0},{1,5},{5,9},... | collective-permute-start | bytes 294920 | tf_op jit(solution)/shard_map/ppermute | solution.py:616
  49.6 5.6 %collective-permute-start.27 = (bf16[32,1536]{1,0:T(8,128)(2,1)S(1)}, bf16[32,1536]{1,0:T(8,128)(2,1)S(1)}, u32[]{:S(2)}, u32[]{:S(2)}) collective-permute-start(bf16[32,1536]{1,0:T(8,128)(2,1)S(1)} %collective-permute-done.23.refs_8_), channel_id=1, source_target_pairs={{0,4},{4,8},{8,12},{12,14},{14,10},{10,6},{6,2},{2,0},{1,5},{5,9},... | collective-permute-start | bytes 294920 | tf_op jit(solution)/shard_map/ppermute | solution.py:616
  52.3 6.1 %collective-permute-start.29 = (bf16[32,1536]{1,0:T(8,128)(2,1)S(1)}, bf16[32,1536]{1,0:T(8,128)(2,1)S(1)}, u32[]{:S(2)}, u32[]{:S(2)}) collective-permute-start(bf16[32,1536]{1,0:T(8,128)(2,1)S(1)} %collective-permute-done.25.refs_0_), channel_id=1, source_target_pairs={{0,4},{4,8},{8,12},{12,14},{14,10},{10,6},{6,2},{2,0},{1,5},{5,9},... | collective-permute-start | bytes 294920 | tf_op jit(solution)/shard_map/ppermute | solution.py:616
  63.0 10.1 %collective-permute-start.33 = (bf16[16,3072]{1,0:T(8,128)(2,1)S(1)}, bf16[16,3072]{1,0:T(8,128)(2,1)S(1)}, u32[]{:S(2)}, u32[]{:S(2)}) collective-permute-start(bf16[16,3072]{1,0:T(8,128)(2,1)S(1)} %get-tuple-element.166), channel_id=1, source_target_pairs={{0,4},{4,8},{8,12},{12,14},{14,10},{10,6},{6,2},{2,0},{1,5},{5,9},... | collective-permute-start | bytes 294920 | tf_op jit(solution)/shard_map/ppermute | solution.py:616
  67.3 5.7 %collective-permute-start.34 = (bf16[16,3072]{1,0:T(8,128)(2,1)S(1)}, bf16[16,3072]{1,0:T(8,128)(2,1)S(1)}, u32[]{:S(2)}, u32[]{:S(2)}) collective-permute-start(bf16[16,3072]{1,0:T(8,128)(2,1)S(1)} %get-tuple-element.164), channel_id=1, source_target_pairs={{4,0},{8,4},{12,8},{14,12},{10,14},{6,10},{2,6},{0,2},{5,1},{9,5},... | collective-permute-start | bytes 294920 | tf_op jit(solution)/shard_map/ppermute | solution.py:616
  67.3 7.9 %collective-permute-start.36 = (bf16[16,3072]{1,0:T(8,128)(2,1)S(1)}, bf16[16,3072]{1,0:T(8,128)(2,1)S(1)}, u32[]{:S(2)}, u32[]{:S(2)}) collective-permute-start(bf16[16,3072]{1,0:T(8,128)(2,1)S(1)} %get-tuple-element.163), channel_id=1, source_target_pairs={{0,1},{1,0},{2,3},{3,2},{4,5},{5,4},{6,7},{7,6},{8,9},{9,8},{10,11... | collective-permute-start | bytes 294920 | tf_op jit(solution)/shard_map/ppermute | solution.py:678
  67.3 7.8 %collective-permute-start.32 = (bf16[16,3072]{1,0:T(8,128)(2,1)S(1)}, bf16[16,3072]{1,0:T(8,128)(2,1)S(1)}, u32[]{:S(2)}, u32[]{:S(2)}) collective-permute-start(bf16[16,3072]{1,0:T(8,128)(2,1)S(1)} %fusion.13), channel_id=1, source_target_pairs={{4,0},{8,4},{12,8},{14,12},{10,14},{6,10},{2,6},{0,2},{5,1},{9,5},... | collective-permute-start | bytes 294920 | tf_op jit(solution)/shard_map/ppermute | solution.py:616
  77.9 5.9 %collective-permute-start.45 = (bf16[16,3072]{1,0:T(8,128)(2,1)S(1)}, bf16[16,3072]{1,0:T(8,128)(2,1)S(1)}, u32[]{:S(2)}, u32[]{:S(2)}) collective-permute-start(bf16[16,3072]{1,0:T(8,128)(2,1)S(1)} %fusion.8), channel_id=1, source_target_pairs={{4,1},{5,0},{8,5},{9,4},{12,9},{13,8},{14,13},{15,12},{10,15},{11,... | collective-permute-start | bytes 294920 | tf_op jit(solution)/shard_map/ppermute | solution.py:618
  78.0 5.8 %collective-permute-start.44 = (bf16[16,3072]{1,0:T(8,128)(2,1)S(1)}, bf16[16,3072]{1,0:T(8,128)(2,1)S(1)}, u32[]{:S(2)}, u32[]{:S(2)}) collective-permute-start(bf16[16,3072]{1,0:T(8,128)(2,1)S(1)} %get-tuple-element.162), channel_id=1, source_target_pairs={{0,4},{4,8},{8,12},{12,14},{14,10},{10,6},{6,2},{2,0},{1,5},{5,9},... | collective-permute-start | bytes 294920 | tf_op jit(solution)/shard_map/ppermute | solution.py:616
  (42 other events, 328.5 us)
